TPU v7x, 512 devices: a whole 4x8x8 slice. The times are simulated.
512 devices in a mesh: section: 2 (over z_hi), seq: 32 (over y, z_lo), grp: 8 (over x, core).
Axes of the slice: x: 4, y: 8, z: 8 (z_hi: 2, z_lo: 4; z = z_hi * 4 + z_lo), core: 2. Of those that a mesh axis runs over, the one named last changes fastest.
Arguments:
- rows: bfloat16 [2, 8192, 3072], P('section', 'seq', 'grp'), may hold values from -1.5 to 1.5
- queries: bfloat16 [2, 8192, 2048], P('section', 'seq', 'grp'), may hold values from -6 to 6
- keys: bfloat16 [2, 8192, 2048], P('section', 'seq', 'grp'), may hold values from -6 to 6
- values: bfloat16 [2, 8192, 2048], P('section', 'seq', 'grp'), may hold values from -6 to 6
- text_kv: bfloat16 [2, 2, 256, 2048], P('section', None, 'grp'), may hold values from -6 to 6
- text_count: int32 [2], P('section'), may hold values from 32 to 256
- out_weight: bfloat16 [2, 2048, 3072], P('section', 'grp'), may hold values from -0.1875 to 0.1875
- gate: float32 [2, 3072], P('section', 'grp'), may hold values from 1 to 8
- band: int32 [64, 2], replicated, may hold values from 0 to 63, as said below
- tile_order: int32 [64], replicated, may hold values from 0 to 63, as said below
Outputs:
- handed: bfloat16 [2, 8192, 3072], P('section', 'seq', 'grp')
Inputs may be any that keep to these rules, and one draw needn't show every extreme that they name: band[t, 0] <= t <= band[t, 1], and each side reaches at most 8 tiles from t; some tile reaches exactly 8 below itself. `tile_order`: a permutation of the tiles that moves each tile only within its aligned block of 4 stored positions.
All inputs are finite; a program needn't handle non-finite values.
Results may differ from a plain program's by a relative error of at most 0.0058.
Values may be sent and summed in bfloat16 or wider, within the bound.
No kernel may reach another device: no remote copies, remote signals or barrier semaphores. Data moves between devices by JAX's collectives and lax.ppermute only.
A program may use at most 64 MiB of HBM per device.

v0:
```python
import math

import jax
import jax.numpy as jnp
from jax import lax
from jax.sharding import PartitionSpec as P

HD = 128
TILE = 128


def shifted(block, axis, distance):
    devices = range(lax.axis_size(axis))
    route = [(i - distance, i) for i in devices if i - distance in devices]
    return lax.ppermute(block, axis, route)


def from_behind(block, axis, distance):
    devices = range(lax.axis_size(axis))
    route = [((i - distance) % len(devices), i) for i in devices]
    return lax.ppermute(block, axis, route)


def unit_norm(values_in, head_count):
    shaped = values_in.astype(jnp.float32).reshape(values_in.shape[:-1] + (head_count, HD))
    normed = shaped * lax.rsqrt(jnp.mean(shaped * shaped, axis=-1, keepdims=True) + 1e-06)
    return normed.reshape(values_in.shape).astype(jnp.bfloat16)


def body(rows, queries, keys, values, text_kv, text_count, out_weight, gate, band, tile_order):
    tok_rows = queries.shape[1]
    col_width = queries.shape[2]
    head_count = col_width // HD
    score_scale = HD ** (-0.5)
    query_n = unit_norm(queries[0], head_count).reshape(tok_rows, head_count, HD)
    key_n = unit_norm(keys[0], head_count)
    value_own = values[0]
    gathered = lax.all_gather(text_kv[0], "grp", axis=1, tiled=True)
    panels = lax.dynamic_slice_in_dim(gathered, lax.axis_index("grp") * col_width, col_width, 2)
    text_slots = panels.shape[1]
    text_key = unit_norm(panels[0], head_count).reshape(text_slots, head_count, HD)
    text_value = panels[1].reshape(text_slots, head_count, HD)
    tile_total = band.shape[0]
    tile_ids = jnp.arange(tile_total, dtype=jnp.int32)
    per_device = tok_rows // TILE
    own_tiles = lax.dynamic_slice_in_dim(
        tile_order, lax.axis_index("seq") * per_device, per_device, 0
    )
    own_pick = own_tiles[:, None] == tile_ids[None, :]
    low_row = jnp.repeat(jnp.sum(jnp.where(own_pick, band[None, :, 0], 0), axis=1), TILE)
    high_row = jnp.repeat(jnp.sum(jnp.where(own_pick, band[None, :, 1], 0), axis=1), TILE)
    text_live = jnp.arange(text_slots, dtype=jnp.int32) < text_count[0]
    text_scores = (
        jnp.einsum("qhd,khd->hqk", query_n, text_key, preferred_element_type=jnp.float32)
        * score_scale
    )
    exp_text = jnp.where(text_live[None, None, :], jnp.exp(text_scores), 0.0)
    start_den = jnp.sum(exp_text, axis=-1)
    start_num = jnp.einsum(
        "hqk,khd->qhd",
        exp_text.astype(jnp.bfloat16),
        text_value,
        preferred_element_type=jnp.float32,
    )

    def fold_keys(carry, piece, start, present):
        key_piece, value_piece = piece
        piece_rows = key_piece.shape[0]
        block_rows = math.gcd(piece_rows, 2048)
        block_count = piece_rows // block_rows
        key_blocks = key_piece.reshape(block_count, block_rows, head_count, HD)
        value_blocks = value_piece.reshape(block_count, block_rows, head_count, HD)
        block_starts = start + jnp.arange(block_count, dtype=jnp.int32) * block_rows

        def one_block(state_now, item_triple):
            key_block, value_block, first_row = item_triple
            positions = (first_row + jnp.arange(block_rows, dtype=jnp.int32)) // TILE
            onehot = positions[:, None] == tile_ids[None, :]
            key_tile = jnp.sum(jnp.where(onehot, tile_order[None, :], 0), axis=1)
            allowed = (
                (key_tile[None, :] >= low_row[:, None])
                & (key_tile[None, :] <= high_row[:, None])
                & present
            )
            numerator, denominator = state_now
            scores = (
                jnp.einsum("qhd,khd->hqk", query_n, key_block, preferred_element_type=jnp.float32)
                * score_scale
            )
            exp_video = jnp.where(allowed[None, :, :], jnp.exp(scores), 0.0)
            numerator = numerator + jnp.einsum(
                "hqk,khd->qhd",
                exp_video.astype(jnp.bfloat16),
                value_block,
                preferred_element_type=jnp.float32,
            )
            state_now = (numerator, denominator + jnp.sum(exp_video, axis=-1))
            return (state_now, None)

        carry, unused = lax.scan(one_block, carry, (key_blocks, value_blocks, block_starts))
        return carry

    seq_count = lax.axis_size("seq")
    seq_index = lax.axis_index("seq")
    band_reach = min(8, tile_total // 2)
    reach = min(seq_count - 1, (band_reach + 3 * per_device - 2) // per_device)
    state = fold_keys((start_num, start_den), (key_n, value_own), seq_index * tok_rows, True)
    for offset in list(range(-reach, 0)) + list(range(1, reach + 1)):
        near_piece = shifted((key_n, value_own), "seq", offset)
        source = seq_index - offset
        add_present = (source >= 0) & (source < seq_count)
        state = fold_keys(
            state, near_piece, jnp.clip(source, 0, seq_count - 1) * tok_rows, add_present
        )
    numerator, denominator = state
    attention = (
        (numerator / denominator.T[:, :, None]).astype(jnp.bfloat16).reshape(tok_rows, col_width)
    )
    weight = out_weight[0]
    own_share = lax.psum_scatter(
        lax.dot_general(
            weight, attention, (((0,), (1,)), ((), ())), preferred_element_type=jnp.float32
        ),
        "grp",
        scatter_dimension=0,
        tiled=True,
    )
    result = (rows[0].astype(jnp.float32) + gate[0][None, :] * own_share.T).astype(jnp.bfloat16)
    handed = from_behind(result, "section", 1)
    return handed[None]


def solution(mesh):
    placed = (
        P("section", "seq", "grp"),
        P("section", "seq", "grp"),
        P("section", "seq", "grp"),
        P("section", "seq", "grp"),
        P("section", None, "grp", None),
        P("section"),
        P("section", "grp", None),
        P("section", "grp"),
        P(),
        P(),
    )
    return jax.shard_map(
        body, mesh=mesh, in_specs=placed, out_specs=P("section", "seq", "grp"), check_vma=False
    )
```

profile of v0, /device:TPU:7, one launch (start us, length us, event | category | flops | bytes accessed | tf_op | source)
XLA Modules:
  0.0 251.0 jit_solution(9507375020034661087)
XLA Ops:
  6.5 7.0 %collective-permute-start.23 = (bf16[256,256]{1,0:T(8,128)(2,1)}, bf16[256,256]{1,0:T(8,128)(2,1)S(1)}, u32[]{:S(2)}, u32[]{:S(2)}) collective-permute-start(bf16[256,256]{1,0:T(8,128)(2,1)} %bitcast.195), channel_id=1, source_target_pairs={{0,48},{8,56},{16,64},{24,72},{32,80},{40,88},{48,96},{56,104},{64... | collective-permute-start | bytes 393224 | tf_op jit(solution)/shard_map/ppermute | solution.py:15
  13.5 5.0 %collective-permute-start.21 = (bf16[256,256]{1,0:T(8,128)(2,1)}, bf16[256,256]{1,0:T(8,128)(2,1)S(1)}, u32[]{:S(2)}, u32[]{:S(2)}) collective-permute-start(bf16[256,256]{1,0:T(8,128)(2,1)} %bitcast.196), channel_id=1, source_target_pairs={{0,40},{8,48},{16,56},{24,64},{32,72},{40,80},{48,88},{56,96},{64,... | collective-permute-start | bytes 393224 | tf_op jit(solution)/shard_map/ppermute | solution.py:15
  18.5 3.2 %collective-permute-start.19 = (bf16[256,256]{1,0:T(8,128)(2,1)}, bf16[256,256]{1,0:T(8,128)(2,1)S(1)}, u32[]{:S(2)}, u32[]{:S(2)}) collective-permute-start(bf16[256,256]{1,0:T(8,128)(2,1)} %bitcast.197), channel_id=1, source_target_pairs={{0,32},{8,40},{16,48},{24,56},{32,64},{40,72},{48,80},{56,88},{64,... | collective-permute-start | bytes 393224 | tf_op jit(solution)/shard_map/ppermute | solution.py:15
  21.7 5.3 %collective-permute-start.17 = (bf16[256,256]{1,0:T(8,128)(2,1)}, bf16[256,256]{1,0:T(8,128)(2,1)S(1)}, u32[]{:S(2)}, u32[]{:S(2)}) collective-permute-start(bf16[256,256]{1,0:T(8,128)(2,1)} %bitcast.198), channel_id=1, source_target_pairs={{0,24},{8,32},{16,40},{24,48},{32,56},{40,64},{48,72},{56,80},{64,... | collective-permute-start | bytes 393224 | tf_op jit(solution)/shard_map/ppermute | solution.py:15
  28.9 1.9 collective-permute-start.22
  33.1 1.4 and_and_fusion.11
  37.1 2.4 collective-permute-start.20
  39.8 1.9 collective-permute-done.20
  41.7 4.1 %collective-permute-start.18 = (bf16[256,256]{0,1:T(8,128)(2,1)}, bf16[256,256]{0,1:T(8,128)(2,1)S(1)}, u32[]{:S(2)}, u32[]{:S(2)}) collective-permute-start(bf16[256,256]{0,1:T(8,128)(2,1)} %fusion.45), channel_id=1, source_target_pairs={{0,32},{8,40},{16,48},{24,56},{32,64},{40,72},{48,80},{56,88},{64,... | collective-permute-start | bytes 393224 | tf_op jit(solution)/shard_map/ppermute | solution.py:15
  46.2 1.9 collective-permute-done.18
  48.1 7.1 %collective-permute-start.16 = (bf16[256,256]{0,1:T(8,128)(2,1)}, bf16[256,256]{0,1:T(8,128)(2,1)S(1)}, u32[]{:S(2)}, u32[]{:S(2)}) collective-permute-start(bf16[256,256]{0,1:T(8,128)(2,1)} %fusion.45), channel_id=1, source_target_pairs={{0,24},{8,32},{16,40},{24,48},{32,56},{40,64},{48,72},{56,80},{64,... | collective-permute-start | bytes 393224 | tf_op jit(solution)/shard_map/ppermute | solution.py:15
  58.8 1.6 fusion.65
  60.4 4.8 %collective-permute-done = bf16[256,256]{0,1:T(8,128)(2,1)S(1)} collective-permute-done((bf16[256,256]{0,1:T(8,128)(2,1)}, bf16[256,256]{0,1:T(8,128)(2,1)S(1)}, u32[]{:S(2)}, u32[]{:S(2)}) %collective-permute-start) | collective-permute-done | bytes 131104 | tf_op jit(solution)/shard_map/ppermute | solution.py:15
  65.2 1.3 collective-permute-start.2
  66.5 1.6 fusion.73
  68.1 6.4 %collective-permute-done.2 = bf16[256,256]{0,1:T(8,128)(2,1)S(1)} collective-permute-done((bf16[256,256]{0,1:T(8,128)(2,1)}, bf16[256,256]{0,1:T(8,128)(2,1)S(1)}, u32[]{:S(2)}, u32[]{:S(2)}) %collective-permute-start.2) | collective-permute-done | bytes 131104 | tf_op jit(solution)/shard_map/ppermute | solution.py:15
  74.5 1.3 collective-permute-start.4
  75.8 1.6 fusion.72
  77.5 4.6 %collective-permute-start.15 = (bf16[256,256]{1,0:T(8,128)(2,1)S(1)}, bf16[256,256]{1,0:T(8,128)(2,1)S(1)}, u32[]{:S(2)}, u32[]{:S(2)}) collective-permute-start(bf16[256,256]{1,0:T(8,128)(2,1)S(1)} %bitcast.199), channel_id=1, source_target_pairs={{0,16},{8,24},{16,32},{24,40},{32,48},{40,56},{48,64},{56,72},{64,... | collective-permute-start | bytes 393224 | tf_op jit(solution)/shard_map/ppermute | solution.py:15
  82.1 5.8 %collective-permute-start.13 = (bf16[256,256]{1,0:T(8,128)(2,1)S(1)}, bf16[256,256]{1,0:T(8,128)(2,1)S(1)}, u32[]{:S(2)}, u32[]{:S(2)}) collective-permute-start(bf16[256,256]{1,0:T(8,128)(2,1)S(1)} %bitcast.200), channel_id=1, source_target_pairs={{0,8},{8,16},{16,24},{24,32},{32,40},{40,48},{48,56},{56,64},{64,7... | collective-permute-start | bytes 393224 | tf_op jit(solution)/shard_map/ppermute | solution.py:15
  87.9 1.3 collective-permute-start.11
  89.2 1.3 collective-permute-start.9
  90.6 1.3 collective-permute-start.6
  91.9 1.6 fusion.71
  93.5 1.3 collective-permute-start.7
  94.8 1.3 collective-permute-start.5
  96.1 1.3 collective-permute-start.3
  97.4 1.3 collective-permute-start.1
  101.1 1.6 fusion.70
  104.3 1.6 copy.341
  106.0 1.7 copy.338
  107.6 7.1 %collective-permute-start.14 = (bf16[256,256]{0,1:T(8,128)(2,1)}, bf16[256,256]{0,1:T(8,128)(2,1)}, u32[]{:S(2)}, u32[]{:S(2)}) collective-permute-start(bf16[256,256]{0,1:T(8,128)(2,1)} %fusion.45), channel_id=1, source_target_pairs={{0,16},{8,24},{16,32},{24,40},{32,48},{40,56},{48,64},{56,72},{64,... | collective-permute-start | bytes 393224 | tf_op jit(solution)/shard_map/ppermute | solution.py:15
  114.8 1.7 copy.335
  116.4 3.9 %collective-permute-start.12 = (bf16[256,256]{0,1:T(8,128)(2,1)}, bf16[256,256]{0,1:T(8,128)(2,1)}, u32[]{:S(2)}, u32[]{:S(2)}) collective-permute-start(bf16[256,256]{0,1:T(8,128)(2,1)} %fusion.45), channel_id=1, source_target_pairs={{0,8},{8,16},{16,24},{24,32},{32,40},{40,48},{48,56},{56,64},{64,7... | collective-permute-start | bytes 393224 | tf_op jit(solution)/shard_map/ppermute | solution.py:15
  120.3 1.7 copy.332
  122.0 1.3 collective-permute-start.10
  124.3 1.6 copy.326
  125.9 1.8 fusion.69
  128.7 1.8 fusion.68
  130.6 1.9 fusion.67
  132.5 1.9 fusion.66
  140.1 1.7 dynamic-slice_convert_fusion
  144.3 1.7 copy.312
  146.0 1.4 fusion.74
  150.7 2.3 convolution_bitcast_fusion
  153.7 73.8 %reduce-scatter.2.cloned.1.call-done = f32[384,256]{0,1:T(8,128)} async-done(((f32[3072,256]{0,1:T(8,128)}), f32[384,256]{0,1:T(8,128)}) %reduce-scatter.2.cloned.1.call-update) | async-done | bytes 393232 | tf_op jit(solution)/shard_map/reduce_scatter | solution.py:120
  228.5 6.7 %collective-permute-start.24 = (bf16[256,384]{1,0:T(8,128)(2,1)S(1)}, bf16[256,384]{1,0:T(8,128)(2,1)S(1)}, u32[]{:S(2)}, u32[]{:S(2)}) collective-permute-start(bf16[256,384]{1,0:T(8,128)(2,1)S(1)} %fusion.44), channel_id=1, source_target_pairs={{256,0},{0,256},{257,1},{1,257},{258,2},{2,258},{259,3},{3,259},{2... | collective-permute-start | bytes 589832 | tf_op jit(solution)/shard_map/ppermute | solution.py:21
  235.2 8.2 %collective-permute-done.24 = bf16[256,384]{1,0:T(8,128)(2,1)S(1)} collective-permute-done((bf16[256,384]{1,0:T(8,128)(2,1)S(1)}, bf16[256,384]{1,0:T(8,128)(2,1)S(1)}, u32[]{:S(2)}, u32[]{:S(2)}) %collective-permute-start.24) | collective-permute-done | bytes 196640 | tf_op jit(solution)/shard_map/ppermute | solution.py:21
  (144 shorter events, 29.7 us)
Async XLA Ops:
  6.5 144.2 %copy-start = (bf16[1,256,3072]{2,1,0:T(8,128)(2,1)S(1)}, bf16[1,256,3072]{2,1,0:T(8,128)(2,1)}, u32[]{:S(2)}) copy-start(bf16[1,256,3072]{2,1,0:T(8,128)(2,1)} %param.16) | copy-start | bytes 4718596
  6.5 25.6 %copy-start.28 = (s32[64,2]{0,1:T(2,128)S(1)}, s32[64,2]{0,1:T(2,128)}, u32[]{:S(2)}) copy-start(s32[64,2]{0,1:T(2,128)} %param.18) | copy-start | bytes 1540
  6.5 25.7 %copy-start.29 = (s32[64]{0:T(128)S(1)}, s32[64]{0:T(128)}, u32[]{:S(2)}) copy-start(s32[64]{0:T(128)} %param.19) | copy-start | bytes 772
  6.5 133.6 %all-gather.3.cloned.1.call-start = ((), (), s32[]{:S(2)}) async-start(), calls=%async_computation.2 | async-start | bytes 2359296 | tf_op jit(solution)/shard_map/all_gather | solution.py:38
  6.5 70.9 %collective-permute-start.23 = (bf16[256,256]{1,0:T(8,128)(2,1)}, bf16[256,256]{1,0:T(8,128)(2,1)S(1)}, u32[]{:S(2)}, u32[]{:S(2)}) collective-permute-start(bf16[256,256]{1,0:T(8,128)(2,1)} %bitcast.195), channel_id=1, source_target_pairs={{0,48},{8,56},{16,64},{24,72},{32,80},{40,88},{48,96},{56,104},{64... | collective-permute-start | bytes 393224 | tf_op jit(solution)/shard_map/ppermute | solution.py:15
  13.5 68.6 %collective-permute-start.21 = (bf16[256,256]{1,0:T(8,128)(2,1)}, bf16[256,256]{1,0:T(8,128)(2,1)S(1)}, u32[]{:S(2)}, u32[]{:S(2)}) collective-permute-start(bf16[256,256]{1,0:T(8,128)(2,1)} %bitcast.196), channel_id=1, source_target_pairs={{0,40},{8,48},{16,56},{24,64},{32,72},{40,80},{48,88},{56,96},{64,... | collective-permute-start | bytes 393224 | tf_op jit(solution)/shard_map/ppermute | solution.py:15
  18.5 69.4 %collective-permute-start.19 = (bf16[256,256]{1,0:T(8,128)(2,1)}, bf16[256,256]{1,0:T(8,128)(2,1)S(1)}, u32[]{:S(2)}, u32[]{:S(2)}) collective-permute-start(bf16[256,256]{1,0:T(8,128)(2,1)} %bitcast.197), channel_id=1, source_target_pairs={{0,32},{8,40},{16,48},{24,56},{32,64},{40,72},{48,80},{56,88},{64,... | collective-permute-start | bytes 393224 | tf_op jit(solution)/shard_map/ppermute | solution.py:15
  21.7 67.5 %collective-permute-start.17 = (bf16[256,256]{1,0:T(8,128)(2,1)}, bf16[256,256]{1,0:T(8,128)(2,1)S(1)}, u32[]{:S(2)}, u32[]{:S(2)}) collective-permute-start(bf16[256,256]{1,0:T(8,128)(2,1)} %bitcast.198), channel_id=1, source_target_pairs={{0,24},{8,32},{16,40},{24,48},{32,56},{40,64},{48,72},{56,80},{64,... | collective-permute-start | bytes 393224 | tf_op jit(solution)/shard_map/ppermute | solution.py:15
  27.1 8.7 %copy-start.19 = (bf16[1,256,256]{2,1,0:T(8,128)(2,1)S(1)}, bf16[1,256,256]{2,1,0:T(8,128)(2,1)}, u32[]{:S(2)}) copy-start(bf16[1,256,256]{2,1,0:T(8,128)(2,1)} %param.13) | copy-start | bytes 393220
  27.1 200.4 %reduce-scatter.2.cloned.1.call-start = ((), (), s32[]{:S(2)}) async-start(), calls=%async_computation.1 | async-start | bytes 3538944 | tf_op jit(solution)/shard_map/reduce_scatter | solution.py:120
  28.9 8.2 %collective-permute-start.22 = (bf16[256,256]{0,1:T(8,128)(2,1)}, bf16[256,256]{0,1:T(8,128)(2,1)S(1)}, u32[]{:S(2)}, u32[]{:S(2)}) collective-permute-start(bf16[256,256]{0,1:T(8,128)(2,1)} %fusion.45), channel_id=1, source_target_pairs={{0,48},{8,56},{16,64},{24,72},{32,80},{40,88},{48,96},{56,104},{64... | collective-permute-start | bytes 393224 | tf_op jit(solution)/shard_map/ppermute | solution.py:15
  32.8 99.6 %copy-start.18 = (bf16[256,2,128]{2,0,1:T(8,128)(2,1)}, bf16[256,2,128]{2,0,1:T(8,128)(2,1)S(1)}, u32[]{:S(2)}) copy-start(bf16[256,2,128]{2,0,1:T(8,128)(2,1)S(1)} %multiply_convert_fusion.2) | copy-start | bytes 393220
  37.1 4.6 %collective-permute-start.20 = (bf16[256,256]{0,1:T(8,128)(2,1)}, bf16[256,256]{0,1:T(8,128)(2,1)S(1)}, u32[]{:S(2)}, u32[]{:S(2)}) collective-permute-start(bf16[256,256]{0,1:T(8,128)(2,1)} %fusion.45), channel_id=1, source_target_pairs={{0,40},{8,48},{16,56},{24,64},{32,72},{40,80},{48,88},{56,96},{64,... | collective-permute-start | bytes 393224 | tf_op jit(solution)/shard_map/ppermute | solution.py:15
  41.7 6.4 %collective-permute-start.18 = (bf16[256,256]{0,1:T(8,128)(2,1)}, bf16[256,256]{0,1:T(8,128)(2,1)S(1)}, u32[]{:S(2)}, u32[]{:S(2)}) collective-permute-start(bf16[256,256]{0,1:T(8,128)(2,1)} %fusion.45), channel_id=1, source_target_pairs={{0,32},{8,40},{16,48},{24,56},{32,64},{40,72},{48,80},{56,88},{64,... | collective-permute-start | bytes 393224 | tf_op jit(solution)/shard_map/ppermute | solution.py:15
  46.2 45.7 %copy-start.26 = (pred[256,256]{0,1:T(8,128)(4,1)S(1)}, pred[256,256]{0,1:T(8,128)(4,1)}, u32[]{:S(2)}) copy-start(pred[256,256]{0,1:T(8,128)(4,1)} %get-tuple-element.357) | copy-start | bytes 196612
  48.1 9.4 %collective-permute-start.16 = (bf16[256,256]{0,1:T(8,128)(2,1)}, bf16[256,256]{0,1:T(8,128)(2,1)S(1)}, u32[]{:S(2)}, u32[]{:S(2)}) collective-permute-start(bf16[256,256]{0,1:T(8,128)(2,1)} %fusion.45), channel_id=1, source_target_pairs={{0,24},{8,32},{16,40},{24,48},{32,56},{40,64},{48,72},{56,80},{64,... | collective-permute-start | bytes 393224 | tf_op jit(solution)/shard_map/ppermute | solution.py:15
  56.3 44.8 %copy-start.25 = (pred[256,256]{0,1:T(8,128)(4,1)S(1)}, pred[256,256]{0,1:T(8,128)(4,1)}, u32[]{:S(2)}) copy-start(pred[256,256]{0,1:T(8,128)(4,1)} %get-tuple-element.358) | copy-start | bytes 196612
  57.5 7.7 %collective-permute-start = (bf16[256,256]{0,1:T(8,128)(2,1)}, bf16[256,256]{0,1:T(8,128)(2,1)S(1)}, u32[]{:S(2)}, u32[]{:S(2)}) collective-permute-start(bf16[256,256]{0,1:T(8,128)(2,1)} %fusion.45), channel_id=1, source_target_pairs={{48,0},{56,8},{64,16},{72,24},{80,32},{88,40},{96,48},{104,56},{11... | collective-permute-start | bytes 393224 | tf_op jit(solution)/shard_map/ppermute | solution.py:15
  65.2 9.3 %collective-permute-start.2 = (bf16[256,256]{0,1:T(8,128)(2,1)}, bf16[256,256]{0,1:T(8,128)(2,1)S(1)}, u32[]{:S(2)}, u32[]{:S(2)}) collective-permute-start(bf16[256,256]{0,1:T(8,128)(2,1)} %fusion.45), channel_id=1, source_target_pairs={{40,0},{48,8},{56,16},{64,24},{72,32},{80,40},{88,48},{96,56},{104... | collective-permute-start | bytes 393224 | tf_op jit(solution)/shard_map/ppermute | solution.py:15
  74.5 16.0 %collective-permute-start.4 = (bf16[256,256]{0,1:T(8,128)(2,1)}, bf16[256,256]{0,1:T(8,128)(2,1)S(1)}, u32[]{:S(2)}, u32[]{:S(2)}) collective-permute-start(bf16[256,256]{0,1:T(8,128)(2,1)} %fusion.45), channel_id=1, source_target_pairs={{32,0},{40,8},{48,16},{56,24},{64,32},{72,40},{80,48},{88,56},{96,... | collective-permute-start | bytes 393224 | tf_op jit(solution)/shard_map/ppermute | solution.py:15
  77.5 16.0 %collective-permute-start.15 = (bf16[256,256]{1,0:T(8,128)(2,1)S(1)}, bf16[256,256]{1,0:T(8,128)(2,1)S(1)}, u32[]{:S(2)}, u32[]{:S(2)}) collective-permute-start(bf16[256,256]{1,0:T(8,128)(2,1)S(1)} %bitcast.199), channel_id=1, source_target_pairs={{0,16},{8,24},{16,32},{24,40},{32,48},{40,56},{48,64},{56,72},{64,... | collective-permute-start | bytes 393224 | tf_op jit(solution)/shard_map/ppermute | solution.py:15
  82.1 12.7 %collective-permute-start.13 = (bf16[256,256]{1,0:T(8,128)(2,1)S(1)}, bf16[256,256]{1,0:T(8,128)(2,1)S(1)}, u32[]{:S(2)}, u32[]{:S(2)}) collective-permute-start(bf16[256,256]{1,0:T(8,128)(2,1)S(1)} %bitcast.200), channel_id=1, source_target_pairs={{0,8},{8,16},{16,24},{24,32},{32,40},{40,48},{48,56},{56,64},{64,7... | collective-permute-start | bytes 393224 | tf_op jit(solution)/shard_map/ppermute | solution.py:15
  87.9 8.2 %collective-permute-start.11 = (bf16[256,256]{1,0:T(8,128)(2,1)S(1)}, bf16[256,256]{1,0:T(8,128)(2,1)S(1)}, u32[]{:S(2)}, u32[]{:S(2)}) collective-permute-start(bf16[256,256]{1,0:T(8,128)(2,1)S(1)} %bitcast.201), channel_id=1, source_target_pairs={{8,0},{16,8},{24,16},{32,24},{40,32},{48,40},{56,48},{64,56},{72,6... | collective-permute-start | bytes 393224 | tf_op jit(solution)/shard_map/ppermute | solution.py:15
  89.2 8.2 %collective-permute-start.9 = (bf16[256,256]{1,0:T(8,128)(2,1)S(1)}, bf16[256,256]{1,0:T(8,128)(2,1)S(1)}, u32[]{:S(2)}, u32[]{:S(2)}) collective-permute-start(bf16[256,256]{1,0:T(8,128)(2,1)S(1)} %bitcast.202), channel_id=1, source_target_pairs={{16,0},{24,8},{32,16},{40,24},{48,32},{56,40},{64,48},{72,56},{80,... | collective-permute-start | bytes 393224 | tf_op jit(solution)/shard_map/ppermute | solution.py:15
  90.6 9.2 %collective-permute-start.6 = (bf16[256,256]{0,1:T(8,128)(2,1)}, bf16[256,256]{0,1:T(8,128)(2,1)S(1)}, u32[]{:S(2)}, u32[]{:S(2)}) collective-permute-start(bf16[256,256]{0,1:T(8,128)(2,1)} %fusion.45), channel_id=1, source_target_pairs={{24,0},{32,8},{40,16},{48,24},{56,32},{64,40},{72,48},{80,56},{88,... | collective-permute-start | bytes 393224 | tf_op jit(solution)/shard_map/ppermute | solution.py:15
  93.5 14.2 %collective-permute-start.7 = (bf16[256,256]{1,0:T(8,128)(2,1)S(1)}, bf16[256,256]{1,0:T(8,128)(2,1)}, u32[]{:S(2)}, u32[]{:S(2)}) collective-permute-start(bf16[256,256]{1,0:T(8,128)(2,1)S(1)} %bitcast.203), channel_id=1, source_target_pairs={{24,0},{32,8},{40,16},{48,24},{56,32},{64,40},{72,48},{80,56},{88,... | collective-permute-start | bytes 393224 | tf_op jit(solution)/shard_map/ppermute | solution.py:15
  94.8 7.9 %copy-start.20 = (bf16[256,256]{1,0:T(8,128)(2,1)}, bf16[256,256]{1,0:T(8,128)(2,1)S(1)}, u32[]{:S(2)}) copy-start(bf16[256,256]{1,0:T(8,128)(2,1)S(1)} %collective-permute-done.13) | copy-start | bytes 393220
  94.8 21.6 %collective-permute-start.5 = (bf16[256,256]{1,0:T(8,128)(2,1)S(1)}, bf16[256,256]{1,0:T(8,128)(2,1)}, u32[]{:S(2)}, u32[]{:S(2)}) collective-permute-start(bf16[256,256]{1,0:T(8,128)(2,1)S(1)} %bitcast.204), channel_id=1, source_target_pairs={{32,0},{40,8},{48,16},{56,24},{64,32},{72,40},{80,48},{88,56},{96,... | collective-permute-start | bytes 393224 | tf_op jit(solution)/shard_map/ppermute | solution.py:15
  96.1 5.0 %copy-start.21 = (bf16[256,256]{1,0:T(8,128)(2,1)}, bf16[256,256]{1,0:T(8,128)(2,1)S(1)}, u32[]{:S(2)}) copy-start(bf16[256,256]{1,0:T(8,128)(2,1)S(1)} %collective-permute-done.11) | copy-start | bytes 393220
  96.1 25.9 %collective-permute-start.3 = (bf16[256,256]{1,0:T(8,128)(2,1)S(1)}, bf16[256,256]{1,0:T(8,128)(2,1)}, u32[]{:S(2)}, u32[]{:S(2)}) collective-permute-start(bf16[256,256]{1,0:T(8,128)(2,1)S(1)} %bitcast.205), channel_id=1, source_target_pairs={{40,0},{48,8},{56,16},{64,24},{72,32},{80,40},{88,48},{96,56},{104... | collective-permute-start | bytes 393224 | tf_op jit(solution)/shard_map/ppermute | solution.py:15
  97.4 5.7 %copy-start.22 = (bf16[256,256]{1,0:T(8,128)(2,1)}, bf16[256,256]{1,0:T(8,128)(2,1)S(1)}, u32[]{:S(2)}) copy-start(bf16[256,256]{1,0:T(8,128)(2,1)S(1)} %collective-permute-done.9) | copy-start | bytes 393220
  97.4 26.8 %collective-permute-start.1 = (bf16[256,256]{1,0:T(8,128)(2,1)S(1)}, bf16[256,256]{1,0:T(8,128)(2,1)}, u32[]{:S(2)}, u32[]{:S(2)}) collective-permute-start(bf16[256,256]{1,0:T(8,128)(2,1)S(1)} %bitcast.206), channel_id=1, source_target_pairs={{48,0},{56,8},{64,16},{72,24},{80,32},{88,40},{96,48},{104,56},{11... | collective-permute-start | bytes 393224 | tf_op jit(solution)/shard_map/ppermute | solution.py:15
  99.8 26.1 %collective-permute-start.8 = (bf16[256,256]{0,1:T(8,128)(2,1)}, bf16[256,256]{0,1:T(8,128)(2,1)}, u32[]{:S(2)}, u32[]{:S(2)}) collective-permute-start(bf16[256,256]{0,1:T(8,128)(2,1)} %fusion.45), channel_id=1, source_target_pairs={{16,0},{24,8},{32,16},{40,24},{48,32},{56,40},{64,48},{72,56},{80,... | collective-permute-start | bytes 393224 | tf_op jit(solution)/shard_map/ppermute | solution.py:15
  103.3 25.5 %copy-start.24 = (pred[256,256]{0,1:T(8,128)(4,1)S(1)}, pred[256,256]{0,1:T(8,128)(4,1)}, u32[]{:S(2)}) copy-start(pred[256,256]{0,1:T(8,128)(4,1)} %get-tuple-element.360) | copy-start | bytes 196612
  105.9 26.5 %copy-start.23 = (pred[256,256]{0,1:T(8,128)(4,1)S(1)}, pred[256,256]{0,1:T(8,128)(4,1)}, u32[]{:S(2)}) copy-start(pred[256,256]{0,1:T(8,128)(4,1)} %get-tuple-element.362) | copy-start | bytes 196612
  107.6 24.8 %collective-permute-start.14 = (bf16[256,256]{0,1:T(8,128)(2,1)}, bf16[256,256]{0,1:T(8,128)(2,1)}, u32[]{:S(2)}, u32[]{:S(2)}) collective-permute-start(bf16[256,256]{0,1:T(8,128)(2,1)} %fusion.45), channel_id=1, source_target_pairs={{0,16},{8,24},{16,32},{24,40},{32,48},{40,56},{48,64},{56,72},{64,... | collective-permute-start | bytes 393224 | tf_op jit(solution)/shard_map/ppermute | solution.py:15
  116.4 14.2 %collective-permute-start.12 = (bf16[256,256]{0,1:T(8,128)(2,1)}, bf16[256,256]{0,1:T(8,128)(2,1)}, u32[]{:S(2)}, u32[]{:S(2)}) collective-permute-start(bf16[256,256]{0,1:T(8,128)(2,1)} %fusion.45), channel_id=1, source_target_pairs={{0,8},{8,16},{16,24},{24,32},{32,40},{40,48},{48,56},{56,64},{64,7... | collective-permute-start | bytes 393224 | tf_op jit(solution)/shard_map/ppermute | solution.py:15
  122.0 6.8 %collective-permute-start.10 = (bf16[256,256]{0,1:T(8,128)(2,1)}, bf16[256,256]{0,1:T(8,128)(2,1)}, u32[]{:S(2)}, u32[]{:S(2)}) collective-permute-start(bf16[256,256]{0,1:T(8,128)(2,1)} %fusion.45), channel_id=1, source_target_pairs={{8,0},{16,8},{24,16},{32,24},{40,32},{48,40},{56,48},{64,56},{72,6... | collective-permute-start | bytes 393224 | tf_op jit(solution)/shard_map/ppermute | solution.py:15
  128.7 6.0 %copy-start.12 = (bf16[2,256,256]{1,2,0:T(8,128)(2,1)S(1)}, bf16[2,256,256]{1,2,0:T(8,128)(2,1)}, u32[]{:S(2)}) copy-start(bf16[2,256,256]{1,2,0:T(8,128)(2,1)} %get-tuple-element.387) | copy-start | bytes 786436
  130.6 4.6 %copy-start.14 = (bf16[2,256,256]{1,2,0:T(8,128)(2,1)S(1)}, bf16[2,256,256]{1,2,0:T(8,128)(2,1)}, u32[]{:S(2)}) copy-start(bf16[2,256,256]{1,2,0:T(8,128)(2,1)} %get-tuple-element.415) | copy-start | bytes 786436
  144.3 6.1 %copy-start.1 = (f32[256,2,128]{0,2,1:T(8,128)S(1)}, f32[256,2,128]{0,2,1:T(8,128)}, u32[]{:S(2)}) copy-start(f32[256,2,128]{0,2,1:T(8,128)} %convolution_bitcast_fusion.9) | copy-start | bytes 786436
  146.0 4.4 %copy-start.3 = (f32[256,2,128]{0,2,1:T(8,128)S(1)}, f32[256,2,128]{0,2,1:T(8,128)}, u32[]{:S(2)}) copy-start(f32[256,2,128]{0,2,1:T(8,128)} %convolution_bitcast_fusion.7) | copy-start | bytes 786436
  146.0 4.4 %copy-start.4 = (f32[256,2,128]{0,2,1:T(8,128)S(1)}, f32[256,2,128]{0,2,1:T(8,128)}, u32[]{:S(2)}) copy-start(f32[256,2,128]{0,2,1:T(8,128)} %convolution_bitcast_fusion.6) | copy-start | bytes 786436
  146.0 4.4 %copy-start.5 = (f32[256,2,128]{0,2,1:T(8,128)S(1)}, f32[256,2,128]{0,2,1:T(8,128)}, u32[]{:S(2)}) copy-start(f32[256,2,128]{0,2,1:T(8,128)} %convolution_bitcast_fusion.5) | copy-start | bytes 786436
  146.0 4.4 %copy-start.6 = (bf16[256,256]{0,1:T(8,128)(2,1)S(1)}, bf16[256,256]{0,1:T(8,128)(2,1)}, u32[]{:S(2)}) copy-start(bf16[256,256]{0,1:T(8,128)(2,1)} %copy.326) | copy-start | bytes 393220
  146.0 4.4 %copy-start.11 = (bf16[2,256,256]{1,2,0:T(8,128)(2,1)S(1)}, bf16[2,256,256]{1,2,0:T(8,128)(2,1)}, u32[]{:S(2)}) copy-start(bf16[2,256,256]{1,2,0:T(8,128)(2,1)} %get-tuple-element.429) | copy-start | bytes 786436
  153.0 74.5 %copy-start.17 = (bf16[1,256,384]{2,1,0:T(8,128)(2,1)S(1)}, bf16[1,256,384]{2,1,0:T(8,128)(2,1)}, u32[]{:S(2)}) copy-start(bf16[1,256,384]{2,1,0:T(8,128)(2,1)} %param.10) | copy-start | bytes 589828
  228.5 14.9 %collective-permute-start.24 = (bf16[256,384]{1,0:T(8,128)(2,1)S(1)}, bf16[256,384]{1,0:T(8,128)(2,1)S(1)}, u32[]{:S(2)}, u32[]{:S(2)}) collective-permute-start(bf16[256,384]{1,0:T(8,128)(2,1)S(1)} %fusion.44), channel_id=1, source_target_pairs={{256,0},{0,256},{257,1},{1,257},{258,2},{2,258},{259,3},{3,259},{2... | collective-permute-start | bytes 589832 | tf_op jit(solution)/shard_map/ppermute | solution.py:21
  (9 other events, 22.3 us)
Sparse Core Ops, SparseCore 0:
  27.2 28.8 all-gather.2
  153.2 74.2 reduce-scatter.1
where the time goes:
time: 252 us; the launch traced here: 251 us
  waiting for transfers between devices  100 us (40%)
  starting transfers between devices  79.7 us (32%)
  matrix products  29.9 us (12%)
  local copies, waits for them, and re-layouts  17.4 us (7%)
  between operations  15 us (6%)
  other arithmetic  8.55 us (3%)
    reduce_scatter x1, waiting for transfers between devices, body(): lax.psum_scatter(lax.dot_general(weight, attention, (((0,), (1,)), ((), (...  73.8 us
    ppermute x24, starting transfers between devices, shifted(): return lax.ppermute(block, axis, route)  72.9 us
    ppermute x24, waiting for transfers between devices, shifted(): return lax.ppermute(block, axis, route)  18.3 us
    dot_general x13, matrix products, one_block(): jnp.einsum('qhd,khd->hqk', query_n, key_block, preferred_element_type=jnp...  18.2 us
    ppermute x12, local copies, waits for them, and re-layouts, shifted(): return lax.ppermute(block, axis, route)  10.8 us
    ppermute x1, waiting for transfers between devices, from_behind(): return lax.ppermute(block, axis, route)  8.21 us
    dot_general x13, matrix products, one_block(): jnp.einsum('hqk,khd->qhd', exp_video.astype(jnp.bfloat16), value_block, p...  7.04 us
    ppermute x1, starting transfers between devices, from_behind(): return lax.ppermute(block, axis, route)  6.72 us
  transfers between devices with their start and end apart: 27, of which 9 were waited for; matrix products, arithmetic and copies ran while one was open for 16% of the time, Pallas kernels for 0%

commit v1 on v0

v1 whole, which is shorter than its diff:
```python
import math

import jax
import jax.numpy as jnp
from jax import lax
from jax.experimental import pallas as pl
from jax.experimental.pallas import tpu as pltpu
from jax.sharding import PartitionSpec as P

HD = 128
TILE = 128
BLOCK = 256
PAIR = 2 * BLOCK
CHIPS = 4
FAR = -30000.0
EXP2_SCALE = HD ** (-0.5) * math.log2(math.e)
BF16 = jnp.bfloat16
F32 = jnp.float32
SMEM = pl.BlockSpec(memory_space=pltpu.SMEM)
VMEM = pl.BlockSpec(memory_space=pltpu.VMEM)
ANY = pl.BlockSpec(memory_space=pl.ANY)


def params():
    return pltpu.CompilerParams(vmem_limit_bytes=32 * 1024 * 1024)


def normed(block):
    wide = block.astype(F32)
    return (wide * lax.rsqrt(jnp.mean(wide * wide, axis=-1, keepdims=True) + 1e-06)).astype(BF16)


def split_heads(place, q_ref, k_ref, v_ref, pair_ref, near_ref, cross_ref, mine_ref):
    first = place[1] == 0

    def pick(a, b):
        return jnp.where(first, a, b)

    def halves(ref, prepare):
        a = prepare(ref[0, :, :HD])
        b = prepare(ref[0, :, HD:])
        return pick(a, b), pick(b, a)

    key_own, key_other = halves(k_ref, normed)
    value_own, value_other = halves(v_ref, lambda x: x)
    query_own, query_other = halves(q_ref, normed)
    pair_ref[0] = key_other
    pair_ref[1] = value_other
    pair_ref[2] = query_other
    cross_ref[0] = key_other
    cross_ref[1] = value_other
    near_ref[0] = key_own
    near_ref[1] = value_own
    mine_ref[...] = query_own


def regroup(place, w_ref, t_ref, own_ref, one_ref, two_ref, three_ref, text_ref, sems):
    chip, core, odd = place[2], place[3], place[1]
    width = w_ref.shape[2] // (2 * CHIPS)
    copies = []
    for ahead, out in enumerate((own_ref, one_ref, two_ref, three_ref)):
        target = lax.rem(chip + ahead, CHIPS)
        for half in range(2):
            side = core if half == 0 else 1 - core
            start = pl.multiple_of((target * 2 + side) * width, 128)
            copies.append((w_ref.at[0, :, pl.ds(start, width)], out.at[:, pl.ds(half * width, width)]))
    for group in range(2 * CHIPS):
        start = pl.multiple_of((2 * group + odd) * HD, 128)
        copies.append((t_ref.at[0, :, :, pl.ds(start, HD)], text_ref.at[group]))
    started = [
        pltpu.make_async_copy(source, target, sems.at[i])
        for i, (source, target) in enumerate(copies)
    ]
    for copy in started:
        copy.start()
    for copy in started:
        copy.wait()


def tile_at(place, order, pair, slot):
    return order[pair * 4 + ((slot // 2) ^ place[1]) * 2 + slot % 2]


def mask_lanes(place, order, band, pairs, text_lane):
    total = order.shape[0] // 4
    lane = lax.broadcasted_iota(jnp.int32, (TILE, HD), 1)
    key_tiles = []
    for pair in pairs:
        inside = (pair >= 0) & (pair < total)
        held = jnp.clip(pair, 0, total - 1)
        key_tiles += [(inside, tile_at(place, order, held, slot)) for slot in range(4)]
    rows = []
    for slot in range(4):
        tile = tile_at(place, order, place[0], slot)
        low, high = band[tile, 0], band[tile, 1]
        row = jnp.where(lane == text_lane, F32(FAR), F32(0.0))
        for index, (inside, key_tile) in enumerate(key_tiles):
            seen = inside & (key_tile >= low) & (key_tile <= high)
            row = jnp.where(lane == index, jnp.where(seen, F32(0.0), F32(FAR)), row)
        rows.append(row.astype(BF16))
    return jnp.concatenate(rows, axis=0)


def add_keys(total, query, key, key_lanes, value):
    scores = lax.dot_general(
        query,
        jnp.concatenate([key, key_lanes], axis=1),
        (((1,), (1,)), ((), ())),
        preferred_element_type=F32,
    )
    weights = jnp.exp2(scores * EXP2_SCALE).astype(BF16)
    wide = jnp.concatenate([value, jnp.ones_like(value)], axis=1)
    part = lax.dot_general(weights, wide, (((1,), (0,)), ((), ())), preferred_element_type=F32)
    return part if total is None else total + part


def video_lanes(index):
    shape = (PAIR, HD)
    row = lax.broadcasted_iota(jnp.int32, shape, 0)
    lane = lax.broadcasted_iota(jnp.int32, shape, 1)
    return jnp.where(lane == 4 * index + row // TILE, F32(1.0), F32(0.0)).astype(BF16)


def pair_arrays(low_ref, high_ref):
    key = jnp.concatenate([low_ref[0], high_ref[0]], axis=0)
    value = jnp.concatenate([low_ref[1], high_ref[1]], axis=0)
    return key, value


def near_keys(
    place, order, band, count, mine_ref, near_ref, pair_ref, far_ref, cross_ref, text_ref, total_ref
):
    query = jnp.concatenate([mine_ref[...], pair_ref[2]], axis=0)
    pairs = (place[0], place[0] ^ 1)
    query = jnp.concatenate([query, mask_lanes(place, order, band, pairs, HD - 1)], axis=1)
    total = add_keys(None, query, *with_lanes(pair_arrays(near_ref, pair_ref), 0))
    total = add_keys(total, query, *with_lanes(pair_arrays(far_ref, cross_ref), 1))
    text = text_ref[...]
    slots = text.shape[0] * text.shape[2]
    text_key = normed(text[:, 0].reshape(slots, HD))
    text_value = text[:, 1].reshape(slots, HD)
    slot = lax.broadcasted_iota(jnp.int32, (slots, HD), 0)
    lane = lax.broadcasted_iota(jnp.int32, (slots, HD), 1)
    dead = (lane == HD - 1) & (slot >= count[0])
    text_lanes = jnp.where(dead, F32(1.0), F32(0.0)).astype(BF16)
    total_ref[...] = add_keys(total, query, text_key, text_lanes, text_value)


def with_lanes(arrays, index):
    key, value = arrays
    return key, video_lanes(index), value


def far_keys(
    place, order, band, mine_ref, pair_ref, total_ref, below_ref, above_ref, next_ref, out_ref
):
    query = jnp.concatenate([mine_ref[...], pair_ref[2]], axis=0)
    own = place[0]
    beside = own - 1 + 2 * lax.rem(own, 2)
    lanes = mask_lanes(place, order, band, (own - 2, own + 2, beside), -1)
    query = jnp.concatenate([query, lanes], axis=1)
    total = total_ref[...]
    for index, ref in enumerate((below_ref, above_ref, next_ref)):
        total = add_keys(total, query, *with_lanes(pair_arrays(ref.at[0], ref.at[1]), index))
    result = (total[:, :HD] / total[:, HD:]).astype(BF16)
    odd = place[1]
    for chip in range(CHIPS):
        out_ref[odd * CHIPS + chip] = result[:BLOCK]
        out_ref[(1 - odd) * CHIPS + chip] = result[BLOCK:]


def project(place, heads_ref, own_ref, one_ref, two_ref, three_ref, kept_ref, sent_ref):
    total = None
    for behind, weight_ref in enumerate((own_ref, one_ref, two_ref, three_ref)):
        source = lax.rem(place[2] + CHIPS - behind, CHIPS)
        heads = jnp.concatenate([heads_ref[source], heads_ref[CHIPS + source]], axis=1)
        part = jnp.dot(heads, weight_ref[...], preferred_element_type=F32)
        total = part if total is None else total + part
    width = kept_ref.shape[1]
    kept_ref[...] = total[:, :width]
    sent_ref[...] = total[:, width:].astype(BF16)


def body(rows, queries, keys, values, text_kv, text_count, out_weight, gate, band, tile_order):
    seq_count = lax.axis_size("seq")
    seq = lax.axis_index("seq")
    grp = lax.axis_index("grp")
    place = jnp.stack([seq // 2, seq % 2, grp // 2, grp % 2]).astype(jnp.int32)
    shape = jax.ShapeDtypeStruct
    width = gate.shape[1]

    pair_out, near, cross_out, mine = pl.pallas_call(
        split_heads,
        out_shape=(
            shape((3, BLOCK, HD), BF16),
            shape((2, BLOCK, HD), BF16),
            shape((2, BLOCK, HD), BF16),
            shape((BLOCK, HD), BF16),
        ),
        in_specs=[SMEM, VMEM, VMEM, VMEM],
        compiler_params=params(),
        cost_estimate=pl.CostEstimate(flops=10**6, bytes_accessed=10**6, transcendentals=0),
    )(place, queries, keys, values)

    def swapped(block, mask):
        return lax.ppermute(block, "seq", [(i, i ^ mask) for i in range(seq_count)])

    pair_in = swapped(pair_out, 1)
    far_in = swapped(near, 2)
    cross_in = swapped(cross_out, 3)

    blocks = [shape((BLOCK, 2 * width), BF16)] * CHIPS
    weight_own, *weight_out, text_out = pl.pallas_call(
        regroup,
        out_shape=(*blocks, shape((2 * CHIPS, 2, text_kv.shape[2], HD), BF16)),
        in_specs=[SMEM, ANY, ANY],
        out_specs=(ANY,) * 5,
        scratch_shapes=[pltpu.SemaphoreType.DMA((4 * CHIPS,))],
        compiler_params=params(),
        cost_estimate=pl.CostEstimate(flops=0, bytes_accessed=4 * 10**6, transcendentals=0),
    )(place, out_weight, text_kv)
    weight_in = [
        lax.ppermute(
            block,
            "grp",
            [(g, (g + 2 * (ahead + 1)) % (2 * CHIPS)) for g in range(2 * CHIPS)],
        )
        for ahead, block in enumerate(weight_out)
    ]
    text_in = lax.all_to_all(text_out, "grp", 0, 0)

    own_pair = jnp.stack([near, pair_in[:2]])
    other_pair = jnp.stack([far_in, cross_in])
    up = [(i, i + 4) for i in range(seq_count - 4)]
    down = [(i + 4, i) for i in range(seq_count - 4)]
    below = lax.ppermute(own_pair, "seq", up)
    above = lax.ppermute(own_pair, "seq", down)
    mixed = [(i, j) for i, j in up if i % 4 < 2] + [(i, j) for i, j in down if i % 4 >= 2]
    beside = lax.ppermute(other_pair, "seq", mixed)

    total = pl.pallas_call(
        near_keys,
        out_shape=shape((PAIR, 2 * HD), F32),
        in_specs=[SMEM] * 4 + [VMEM] * 6,
        compiler_params=params(),
        cost_estimate=pl.CostEstimate(
            flops=4 * PAIR * (2 * PAIR + 256) * 256, bytes_accessed=2 * 10**6, transcendentals=10**6
        ),
    )(place, tile_order, band, text_count, mine, near, pair_in, far_in, cross_in, text_in)
    attention = pl.pallas_call(
        far_keys,
        out_shape=shape((2 * CHIPS, BLOCK, HD), BF16),
        in_specs=[SMEM] * 3 + [VMEM] * 6,
        compiler_params=params(),
        cost_estimate=pl.CostEstimate(
            flops=4 * PAIR * 3 * PAIR * 256, bytes_accessed=2 * 10**6, transcendentals=10**6
        ),
    )(place, tile_order, band, mine, pair_in, total, below, above, beside)

    groups = [
        [(2 * pair + odd) * 2 * CHIPS + 2 * chip + core for odd in range(2) for chip in range(CHIPS)]
        for pair in range(seq_count // 2)
        for core in range(2)
    ]
    heads = lax.all_to_all(attention, ("seq", "grp"), 0, 0, axis_index_groups=groups)
    kept, sent = pl.pallas_call(
        project,
        out_shape=(shape((BLOCK, width), F32), shape((BLOCK, width), BF16)),
        in_specs=[SMEM] + [VMEM] * 5,
        compiler_params=params(),
        cost_estimate=pl.CostEstimate(
            flops=2 * BLOCK * 1024 * 768, bytes_accessed=3 * 10**6, transcendentals=0
        ),
    )(place, heads, weight_own, *weight_in)
    other = lax.ppermute(sent, "grp", [(g, g ^ 1) for g in range(2 * CHIPS)])
    share = kept + other.astype(F32)
    result = (rows[0].astype(F32) + gate[0][None, :] * share).astype(BF16)
    handed = lax.ppermute(result, "section", [(0, 1), (1, 0)])
    return handed[None]


def solution(mesh):
    placed = (
        P("section", "seq", "grp"),
        P("section", "seq", "grp"),
        P("section", "seq", "grp"),
        P("section", "seq", "grp"),
        P("section", None, "grp", None),
        P("section"),
        P("section", "grp", None),
        P("section", "grp"),
        P(),
        P(),
    )
    return jax.shard_map(
        body, mesh=mesh, in_specs=placed, out_specs=P("section", "seq", "grp"), check_vma=False
    )
```

time: 252 us -> 105 us (0.42)
  the two profiles are of different devices: /device:TPU:7 before, /device:TPU:88 now
where the time goes in v1:
time: 105 us; the launch traced here: 104 us
  starting transfers between devices  52.8 us (50%)
  waiting for transfers between devices  35.5 us (34%)
  Pallas kernels  8.87 us (8%)
  local copies, waits for them, and re-layouts  4.57 us (4%)
  other arithmetic  1.62 us (2%)
    ppermute x3, waiting for transfers between devices, body(): lax.ppermute(block, 'grp', [(g, (g + 2 * (ahead + 1)) % (2 * CHIPS)) for...  14.2 us
    ppermute x3, starting transfers between devices, swapped(): return lax.ppermute(block, 'seq', [(i, i ^ mask) for i in range(seq_count)])  11.4 us
    ppermute x3, starting transfers between devices, body(): lax.ppermute(block, 'grp', [(g, (g + 2 * (ahead + 1)) % (2 * CHIPS)) for...  11.3 us
    ppermute x1, waiting for transfers between devices, body(): handed = lax.ppermute(result, 'section', [(0, 1), (1, 0)])  9.55 us
    ppermute x1, starting transfers between devices, body(): handed = lax.ppermute(result, 'section', [(0, 1), (1, 0)])  9.18 us
    all_to_all x1, waiting for transfers between devices, body(): text_in = lax.all_to_all(text_out, 'grp', 0, 0)  5.38 us
    ppermute x3, waiting for transfers between devices, swapped(): return lax.ppermute(block, 'seq', [(i, i ^ mask) for i in range(seq_count)])  4.99 us
    ppermute x1, starting transfers between devices, body(): beside = lax.ppermute(other_pair, 'seq', mixed)  4.82 us
  transfers between devices with their start and end apart: 13, of which 7 were waited for; matrix products, arithmetic and copies ran while one was open for 2% of the time, Pallas kernels for 4%

profile of v1, /device:TPU:88, one launch (start us, length us, event | category | flops | bytes accessed | tf_op | source)
XLA Modules:
  0.0 104.3 jit_solution(16459693026926145719)
XLA Ops:
  0.0 0.1 pad_add_fusion.place
  0.1 1.0 copy-done.2
  1.1 0.9 copy-done.3
  2.0 0.9 copy-done.4
  2.9 0.8 shard_map.100
  3.7 0.0 copy-start.5
  3.7 6.1 %collective-permute-start.1 = (bf16[2,256,128]{2,1,0:T(8,128)(2,1)S(1)}, bf16[2,256,128]{2,1,0:T(8,128)(2,1)S(1)}, u32[]{:S(2)}, u32[]{:S(2)}) collective-permute-start(bf16[2,256,128]{2,1,0:T(8,128)(2,1)S(1)} %get-tuple-element.18.near_ref), channel_id=1, source_target_pairs={{0,16},{8,24},{16,0},{24,8},{32,48},{40,56},{48,32},{56,40},{64,80... | collective-permute-start | bytes 393224 | tf_op jit(solution)/shard_map/ppermute | solution.py:206
  9.8 1.9 %collective-permute-start.2 = (bf16[2,256,128]{2,1,0:T(8,128)(2,1)S(1)}, bf16[2,256,128]{2,1,0:T(8,128)(2,1)S(1)}, u32[]{:S(2)}, u32[]{:S(2)}) collective-permute-start(bf16[2,256,128]{2,1,0:T(8,128)(2,1)S(1)} %get-tuple-element.19), channel_id=1, source_target_pairs={{0,24},{8,16},{16,8},{24,0},{32,56},{40,48},{48,40},{56,32},{64,88... | collective-permute-start | bytes 393224 | tf_op jit(solution)/shard_map/ppermute | solution.py:206
  11.7 3.4 %collective-permute-start = (bf16[3,256,128]{2,1,0:T(8,128)(2,1)S(1)}, bf16[3,256,128]{2,1,0:T(8,128)(2,1)S(1)}, u32[]{:S(2)}, u32[]{:S(2)}) collective-permute-start(bf16[3,256,128]{2,1,0:T(8,128)(2,1)S(1)} %get-tuple-element.17), channel_id=1, source_target_pairs={{0,8},{8,0},{16,24},{24,16},{32,40},{40,32},{48,56},{56,48},{64,72... | collective-permute-start | bytes 589832 | tf_op jit(solution)/shard_map/ppermute | solution.py:206
  15.1 2.3 %collective-permute-done.1.far_ref = bf16[2,256,128]{2,1,0:T(8,128)(2,1)S(1)} collective-permute-done((bf16[2,256,128]{2,1,0:T(8,128)(2,1)S(1)}, bf16[2,256,128]{2,1,0:T(8,128)(2,1)S(1)}, u32[]{:S(2)}, u32[]{:S(2)}) %collective-permute-start.1) | collective-permute-done | bytes 131104 | tf_op jit(solution)/shard_map/ppermute | solution.py:206
  17.4 2.7 %collective-permute-done.2.cross_ref = bf16[2,256,128]{2,1,0:T(8,128)(2,1)S(1)} collective-permute-done((bf16[2,256,128]{2,1,0:T(8,128)(2,1)S(1)}, bf16[2,256,128]{2,1,0:T(8,128)(2,1)S(1)}, u32[]{:S(2)}, u32[]{:S(2)}) %collective-permute-start.2) | collective-permute-done | bytes 131104 | tf_op jit(solution)/shard_map/ppermute | solution.py:206
  20.1 0.7 pad_maximum_fusion.1
  20.8 4.8 %collective-permute-start.5 = (bf16[2,2,256,128]{3,2,1,0:T(8,128)(2,1)}, bf16[2,2,256,128]{3,2,1,0:T(8,128)(2,1)}, u32[]{:S(2)}, u32[]{:S(2)}) collective-permute-start(bf16[2,2,256,128]{3,2,1,0:T(8,128)(2,1)} %pad_maximum_fusion.1), channel_id=1, source_target_pairs={{0,32},{8,40},{32,64},{40,72},{64,96},{72,104},{96,128},{104,136},... | collective-permute-start | bytes 786440 | tf_op jit(solution)/shard_map/ppermute | solution.py:239
  25.6 0.0 collective-permute-done.pair_ref
  25.7 0.7 pad_maximum_fusion
  26.4 2.6 %collective-permute-start.3 = (bf16[2,2,256,128]{3,2,1,0:T(8,128)(2,1)}, bf16[2,2,256,128]{3,2,1,0:T(8,128)(2,1)}, u32[]{:S(2)}, u32[]{:S(2)}) collective-permute-start(bf16[2,2,256,128]{3,2,1,0:T(8,128)(2,1)} %pad_maximum_fusion), channel_id=1, source_target_pairs={{0,32},{8,40},{16,48},{24,56},{32,64},{40,72},{48,80},{56,88},{64,... | collective-permute-start | bytes 786440 | tf_op jit(solution)/shard_map/ppermute | solution.py:236
  29.0 0.0 copy-done.5
  29.0 3.3 %collective-permute-start.4 = (bf16[2,2,256,128]{3,2,1,0:T(8,128)(2,1)}, bf16[2,2,256,128]{3,2,1,0:T(8,128)(2,1)}, u32[]{:S(2)}, u32[]{:S(2)}) collective-permute-start(bf16[2,2,256,128]{3,2,1,0:T(8,128)(2,1)} %pad_maximum_fusion), channel_id=1, source_target_pairs={{32,0},{40,8},{48,16},{56,24},{64,32},{72,40},{80,48},{88,56},{96,... | collective-permute-start | bytes 786440 | tf_op jit(solution)/shard_map/ppermute | solution.py:237
  32.2 0.0 copy-done
  32.2 0.0 copy-start.1
  32.3 0.9 copy-done.1
  33.2 1.5 %shard_map.101 = (bf16[256,768]{1,0:T(8,128)(2,1)S(1)}, bf16[256,768]{1,0:T(8,128)(2,1)}, bf16[256,768]{1,0:T(8,128)(2,1)S(1)}, bf16[256,768]{1,0:T(8,128)(2,1)S(1)}, bf16[8,2,32,128]{3,2,1,0:T(8,128)(2,1)}) custom-call(s32[4]{0:T(128)S(1)} %pad_add_fusion.place, bf16[1,256,3072]{2,1,0:T(8,128)(2,1)S(1)} %copy-done, bf16[1,2,32,2048]{3,2,1,0:T(8,128)(2,1)S(1)} %copy-done.1), custom_call_target="tpu_custom_call" | custom-call | bytes 4000000 | tf_op jit(solution)/shard_map/pallas_call | solution.py:213
  34.7 4.3 %all-to-all-start = ((bf16[8,2,32,128]{3,2,1,0:T(8,128)(2,1)}), bf16[8,2,32,128]{3,2,1,0:T(8,128)(2,1)S(1)}, u32[]{:S(2)}, u32[]{:S(2)}) async-start(bf16[8,2,32,128]{3,2,1,0:T(8,128)(2,1)} %get-tuple-element.20), calls=%async_computation | async-start | bytes 262144 | tf_op jit(solution)/shard_map/all_to_all | solution.py:230
  39.1 0.0 copy-done.10
  39.1 0.1 copy.12.band
  39.8 5.4 %all-to-all-done.text_ref = bf16[8,2,32,128]{3,2,1,0:T(8,128)(2,1)S(1)} async-done(((bf16[8,2,32,128]{3,2,1,0:T(8,128)(2,1)}), bf16[8,2,32,128]{3,2,1,0:T(8,128)(2,1)S(1)}, u32[]{:S(2)}, u32[]{:S(2)}) %all-to-all-start) | async-done | bytes 131104 | tf_op jit(solution)/shard_map/all_to_all | solution.py:230
  45.2 0.0 copy-done.7
  45.2 2.4 %shard_map.102.total_ref = f32[512,256]{1,0:T(8,128)S(1)} custom-call(s32[4]{0:T(128)S(1)} %pad_add_fusion.place, s32[64]{0:T(128)S(1)} %copy-done.7, s32[64,2]{1,0:T(8,128)S(1)} %copy.12.band, s32[1]{0:T(128)S(6)} %copy.14.count, bf16[256,128]{1,0:T(8,128)(2,1)S(1)} %copy-done.6, bf16[2,256,128]{2,1,0:T(8,128)(2,1)S(1)} %get-tuple-element.18.near_ref, ...), custom_call_target="tpu_custom_call" | custom-call | flops 671088640 | bytes 2000000 | tf_op jit(solution)/shard_map/pallas_call | solution.py:241
  47.6 0.0 collective-permute-done.5.next_ref
  47.6 0.0 collective-permute-done.3.below_ref
  47.6 0.0 collective-permute-done.4.above_ref
  47.6 3.1 %shard_map.103 = bf16[8,256,128]{2,1,0:T(8,128)(2,1)} custom-call(s32[4]{0:T(128)S(1)} %pad_add_fusion.place, s32[64]{0:T(128)S(1)} %copy-done.7, s32[64,2]{1,0:T(8,128)S(1)} %copy.12.band, bf16[256,128]{1,0:T(8,128)(2,1)S(1)} %copy-done.6, bf16[3,256,128]{2,1,0:T(8,128)(2,1)S(1)} %collective-permute-done.pair_ref, f32[512,256]{1,0:T(8,128)S(1)} %shard_map.102.total_ref, ...), custom_call_target="tpu_custom_call" | custom-call | flops 805306368 | bytes 2000000 | tf_op jit(solution)/shard_map/pallas_call | solution.py:250
  50.7 4.0 %all-to-all-start.1 = ((bf16[8,256,128]{2,1,0:T(8,128)(2,1)}), bf16[8,256,128]{2,1,0:T(8,128)(2,1)S(1)}, u32[]{:S(2)}, u32[]{:S(2)}) async-start(bf16[8,256,128]{2,1,0:T(8,128)(2,1)} %shard_map.103), calls=%async_computation.1 | async-start | bytes 1048576 | tf_op jit(solution)/shard_map/all_to_all | solution.py:265
  54.7 3.4 %collective-permute-start.6 = (bf16[256,768]{1,0:T(8,128)(2,1)}, bf16[256,768]{1,0:T(8,128)(2,1)S(1)}, u32[]{:S(2)}, u32[]{:S(2)}) collective-permute-start(bf16[256,768]{1,0:T(8,128)(2,1)} %get-tuple-element.22), channel_id=1, source_target_pairs={{0,2},{1,3},{2,4},{3,5},{4,6},{5,7},{6,0},{7,1},{8,10},{9,11},{10,... | collective-permute-start | bytes 1179656 | tf_op jit(solution)/shard_map/ppermute | solution.py:223
  58.1 4.6 %collective-permute-start.7 = (bf16[256,768]{1,0:T(8,128)(2,1)S(1)}, bf16[256,768]{1,0:T(8,128)(2,1)S(1)}, u32[]{:S(2)}, u32[]{:S(2)}) collective-permute-start(bf16[256,768]{1,0:T(8,128)(2,1)S(1)} %get-tuple-element.23), channel_id=1, source_target_pairs={{0,4},{1,5},{2,6},{3,7},{4,0},{5,1},{6,2},{7,3},{8,12},{9,13},{10,... | collective-permute-start | bytes 1179656 | tf_op jit(solution)/shard_map/ppermute | solution.py:223
  62.7 3.4 %collective-permute-start.8 = (bf16[256,768]{1,0:T(8,128)(2,1)S(1)}, bf16[256,768]{1,0:T(8,128)(2,1)S(1)}, u32[]{:S(2)}, u32[]{:S(2)}) collective-permute-start(bf16[256,768]{1,0:T(8,128)(2,1)S(1)} %get-tuple-element.24), channel_id=1, source_target_pairs={{0,6},{1,7},{2,0},{3,1},{4,2},{5,3},{6,4},{7,5},{8,14},{9,15},{10,... | collective-permute-start | bytes 1179656 | tf_op jit(solution)/shard_map/ppermute | solution.py:223
  66.1 6.1 %collective-permute-done.6.one_ref = bf16[256,768]{1,0:T(8,128)(2,1)S(1)} collective-permute-done((bf16[256,768]{1,0:T(8,128)(2,1)}, bf16[256,768]{1,0:T(8,128)(2,1)S(1)}, u32[]{:S(2)}, u32[]{:S(2)}) %collective-permute-start.6) | collective-permute-done | bytes 393248 | tf_op jit(solution)/shard_map/ppermute | solution.py:223
  72.1 8.2 %collective-permute-done.7.two_ref = bf16[256,768]{1,0:T(8,128)(2,1)S(1)} collective-permute-done((bf16[256,768]{1,0:T(8,128)(2,1)S(1)}, bf16[256,768]{1,0:T(8,128)(2,1)S(1)}, u32[]{:S(2)}, u32[]{:S(2)}) %collective-permute-start.7) | collective-permute-done | bytes 393248 | tf_op jit(solution)/shard_map/ppermute | solution.py:223
  80.3 0.0 collective-permute-done.8.three_ref
  80.3 0.0 all-to-all-done.1.heads_ref
  80.3 1.1 %shard_map.104 = (f32[256,384]{1,0:T(8,128)S(1)}, bf16[256,384]{1,0:T(8,128)(2,1)S(1)}) custom-call(s32[4]{0:T(128)S(1)} %pad_add_fusion.place, bf16[8,256,128]{2,1,0:T(8,128)(2,1)S(1)} %all-to-all-done.1.heads_ref, bf16[256,768]{1,0:T(8,128)(2,1)S(1)} %get-tuple-element.21.own_ref, bf16[256,768]{1,0:T(8,128)(2,1)S(1)} %collective-permute-done.6.one_ref, ...), custom_call_target="tpu_custom_call" | custom-call | flops 402653184 | bytes 3000000 | tf_op jit(solution)/shard_map/pallas_call | solution.py:266
  81.4 1.9 %collective-permute-start.9 = (bf16[256,384]{1,0:T(8,128)(2,1)S(1)}, bf16[256,384]{1,0:T(8,128)(2,1)S(1)}, u32[]{:S(2)}, u32[]{:S(2)}) collective-permute-start(bf16[256,384]{1,0:T(8,128)(2,1)S(1)} %get-tuple-element.26), channel_id=1, source_target_pairs={{0,1},{1,0},{2,3},{3,2},{4,5},{5,4},{6,7},{7,6},{8,9},{9,8},{10,11... | collective-permute-start | bytes 589832 | tf_op jit(solution)/shard_map/ppermute | solution.py:275
  83.4 1.4 %collective-permute-done.9 = bf16[256,384]{1,0:T(8,128)(2,1)S(1)} collective-permute-done((bf16[256,384]{1,0:T(8,128)(2,1)S(1)}, bf16[256,384]{1,0:T(8,128)(2,1)S(1)}, u32[]{:S(2)}, u32[]{:S(2)}) %collective-permute-start.9) | collective-permute-done | bytes 196640 | tf_op jit(solution)/shard_map/ppermute | solution.py:275
  84.8 0.0 copy-done.8
  84.8 0.1 fusion
  84.9 9.2 %collective-permute-start.10 = (bf16[256,384]{1,0:T(8,128)(2,1)S(1)}, bf16[256,384]{1,0:T(8,128)(2,1)S(1)}, u32[]{:S(2)}, u32[]{:S(2)}) collective-permute-start(bf16[256,384]{1,0:T(8,128)(2,1)S(1)} %fusion), channel_id=1, source_target_pairs={{0,256},{256,0},{1,257},{257,1},{2,258},{258,2},{3,259},{259,3},{4... | collective-permute-start | bytes 589832 | tf_op jit(solution)/shard_map/ppermute | solution.py:278
  94.0 9.5 %collective-permute-done.10 = bf16[256,384]{1,0:T(8,128)(2,1)S(1)} collective-permute-done((bf16[256,384]{1,0:T(8,128)(2,1)S(1)}, bf16[256,384]{1,0:T(8,128)(2,1)S(1)}, u32[]{:S(2)}, u32[]{:S(2)}) %collective-permute-start.10) | collective-permute-done | bytes 196640 | tf_op jit(solution)/shard_map/ppermute | solution.py:278
  103.6 0.7 copy.15
  (13 shorter events, 0.0 us)
Async XLA Ops:
  0.0 32.2 %copy-start = (bf16[1,256,3072]{2,1,0:T(8,128)(2,1)S(1)}, bf16[1,256,3072]{2,1,0:T(8,128)(2,1)}, u32[]{:S(2)}) copy-start(bf16[1,256,3072]{2,1,0:T(8,128)(2,1)} %w_ref.1) | copy-start | bytes 4718596
  0.1 1.0 copy-start.2
  1.1 0.9 copy-start.3
  2.0 0.9 copy-start.4
  3.7 25.3 %copy-start.5 = (bf16[256,128]{1,0:T(8,128)(2,1)}, bf16[256,128]{1,0:T(8,128)(2,1)S(1)}, u32[]{:S(2)}) copy-start(bf16[256,128]{1,0:T(8,128)(2,1)S(1)} %get-tuple-element.16.mine_ref) | copy-start | bytes 196612
  3.7 13.7 %collective-permute-start.1 = (bf16[2,256,128]{2,1,0:T(8,128)(2,1)S(1)}, bf16[2,256,128]{2,1,0:T(8,128)(2,1)S(1)}, u32[]{:S(2)}, u32[]{:S(2)}) collective-permute-start(bf16[2,256,128]{2,1,0:T(8,128)(2,1)S(1)} %get-tuple-element.18.near_ref), channel_id=1, source_target_pairs={{0,16},{8,24},{16,0},{24,8},{32,48},{40,56},{48,32},{56,40},{64,80... | collective-permute-start | bytes 393224 | tf_op jit(solution)/shard_map/ppermute | solution.py:206
  9.8 10.3 %collective-permute-start.2 = (bf16[2,256,128]{2,1,0:T(8,128)(2,1)S(1)}, bf16[2,256,128]{2,1,0:T(8,128)(2,1)S(1)}, u32[]{:S(2)}, u32[]{:S(2)}) collective-permute-start(bf16[2,256,128]{2,1,0:T(8,128)(2,1)S(1)} %get-tuple-element.19), channel_id=1, source_target_pairs={{0,24},{8,16},{16,8},{24,0},{32,56},{40,48},{48,40},{56,32},{64,88... | collective-permute-start | bytes 393224 | tf_op jit(solution)/shard_map/ppermute | solution.py:206
  11.7 13.9 %collective-permute-start = (bf16[3,256,128]{2,1,0:T(8,128)(2,1)S(1)}, bf16[3,256,128]{2,1,0:T(8,128)(2,1)S(1)}, u32[]{:S(2)}, u32[]{:S(2)}) collective-permute-start(bf16[3,256,128]{2,1,0:T(8,128)(2,1)S(1)} %get-tuple-element.17), channel_id=1, source_target_pairs={{0,8},{8,0},{16,24},{24,16},{32,40},{40,32},{48,56},{56,48},{64,72... | collective-permute-start | bytes 589832 | tf_op jit(solution)/shard_map/ppermute | solution.py:206
  20.8 18.3 %copy-start.10 = (s32[64,2]{0,1:T(2,128)S(1)}, s32[64,2]{0,1:T(2,128)}, u32[]{:S(2)}) copy-start(s32[64,2]{0,1:T(2,128)} %param.18) | copy-start | bytes 1540
  20.8 24.4 %copy-start.7 = (s32[64]{0:T(128)S(1)}, s32[64]{0:T(128)}, u32[]{:S(2)}) copy-start(s32[64]{0:T(128)} %order.3) | copy-start | bytes 772
  20.8 26.7 %collective-permute-start.5 = (bf16[2,2,256,128]{3,2,1,0:T(8,128)(2,1)}, bf16[2,2,256,128]{3,2,1,0:T(8,128)(2,1)}, u32[]{:S(2)}, u32[]{:S(2)}) collective-permute-start(bf16[2,2,256,128]{3,2,1,0:T(8,128)(2,1)} %pad_maximum_fusion.1), channel_id=1, source_target_pairs={{0,32},{8,40},{32,64},{40,72},{64,96},{72,104},{96,128},{104,136},... | collective-permute-start | bytes 786440 | tf_op jit(solution)/shard_map/ppermute | solution.py:239
  26.4 21.2 %collective-permute-start.3 = (bf16[2,2,256,128]{3,2,1,0:T(8,128)(2,1)}, bf16[2,2,256,128]{3,2,1,0:T(8,128)(2,1)}, u32[]{:S(2)}, u32[]{:S(2)}) collective-permute-start(bf16[2,2,256,128]{3,2,1,0:T(8,128)(2,1)} %pad_maximum_fusion), channel_id=1, source_target_pairs={{0,32},{8,40},{16,48},{24,56},{32,64},{40,72},{48,80},{56,88},{64,... | collective-permute-start | bytes 786440 | tf_op jit(solution)/shard_map/ppermute | solution.py:236
  29.0 18.6 %collective-permute-start.4 = (bf16[2,2,256,128]{3,2,1,0:T(8,128)(2,1)}, bf16[2,2,256,128]{3,2,1,0:T(8,128)(2,1)}, u32[]{:S(2)}, u32[]{:S(2)}) collective-permute-start(bf16[2,2,256,128]{3,2,1,0:T(8,128)(2,1)} %pad_maximum_fusion), channel_id=1, source_target_pairs={{32,0},{40,8},{48,16},{56,24},{64,32},{72,40},{80,48},{88,56},{96,... | collective-permute-start | bytes 786440 | tf_op jit(solution)/shard_map/ppermute | solution.py:237
  32.2 1.0 copy-start.1
  33.2 12.0 %copy-start.6 = (bf16[256,128]{1,0:T(8,128)(2,1)S(1)}, bf16[256,128]{1,0:T(8,128)(2,1)}, u32[]{:S(2)}) copy-start(bf16[256,128]{1,0:T(8,128)(2,1)} %copy-done.5) | copy-start | bytes 196612
  34.7 10.4 %all-to-all-start = ((bf16[8,2,32,128]{3,2,1,0:T(8,128)(2,1)}), bf16[8,2,32,128]{3,2,1,0:T(8,128)(2,1)S(1)}, u32[]{:S(2)}, u32[]{:S(2)}) async-start(bf16[8,2,32,128]{3,2,1,0:T(8,128)(2,1)} %get-tuple-element.20), calls=%async_computation | async-start | bytes 262144 | tf_op jit(solution)/shard_map/all_to_all | solution.py:230
  50.7 32.7 %copy-start.9 = (f32[1,384]{1,0:T(1,128)S(1)}, f32[1,384]{1,0:T(1,128)}, u32[]{:S(2)}) copy-start(f32[1,384]{1,0:T(1,128)} %param.17) | copy-start | bytes 4612
  50.7 34.1 %copy-start.8 = (bf16[1,256,384]{2,1,0:T(8,128)(2,1)S(1)}, bf16[1,256,384]{2,1,0:T(8,128)(2,1)}, u32[]{:S(2)}) copy-start(bf16[1,256,384]{2,1,0:T(8,128)(2,1)} %param.10) | copy-start | bytes 589828
  50.7 29.6 %all-to-all-start.1 = ((bf16[8,256,128]{2,1,0:T(8,128)(2,1)}), bf16[8,256,128]{2,1,0:T(8,128)(2,1)S(1)}, u32[]{:S(2)}, u32[]{:S(2)}) async-start(bf16[8,256,128]{2,1,0:T(8,128)(2,1)} %shard_map.103), calls=%async_computation.1 | async-start | bytes 1048576 | tf_op jit(solution)/shard_map/all_to_all | solution.py:265
  54.7 17.4 %collective-permute-start.6 = (bf16[256,768]{1,0:T(8,128)(2,1)}, bf16[256,768]{1,0:T(8,128)(2,1)S(1)}, u32[]{:S(2)}, u32[]{:S(2)}) collective-permute-start(bf16[256,768]{1,0:T(8,128)(2,1)} %get-tuple-element.22), channel_id=1, source_target_pairs={{0,2},{1,3},{2,4},{3,5},{4,6},{5,7},{6,0},{7,1},{8,10},{9,11},{10,... | collective-permute-start | bytes 1179656 | tf_op jit(solution)/shard_map/ppermute | solution.py:223
  58.1 22.2 %collective-permute-start.7 = (bf16[256,768]{1,0:T(8,128)(2,1)S(1)}, bf16[256,768]{1,0:T(8,128)(2,1)S(1)}, u32[]{:S(2)}, u32[]{:S(2)}) collective-permute-start(bf16[256,768]{1,0:T(8,128)(2,1)S(1)} %get-tuple-element.23), channel_id=1, source_target_pairs={{0,4},{1,5},{2,6},{3,7},{4,0},{5,1},{6,2},{7,3},{8,12},{9,13},{10,... | collective-permute-start | bytes 1179656 | tf_op jit(solution)/shard_map/ppermute | solution.py:223
  62.7 17.6 %collective-permute-start.8 = (bf16[256,768]{1,0:T(8,128)(2,1)S(1)}, bf16[256,768]{1,0:T(8,128)(2,1)S(1)}, u32[]{:S(2)}, u32[]{:S(2)}) collective-permute-start(bf16[256,768]{1,0:T(8,128)(2,1)S(1)} %get-tuple-element.24), channel_id=1, source_target_pairs={{0,6},{1,7},{2,0},{3,1},{4,2},{5,3},{6,4},{7,5},{8,14},{9,15},{10,... | collective-permute-start | bytes 1179656 | tf_op jit(solution)/shard_map/ppermute | solution.py:223
  81.4 3.3 %collective-permute-start.9 = (bf16[256,384]{1,0:T(8,128)(2,1)S(1)}, bf16[256,384]{1,0:T(8,128)(2,1)S(1)}, u32[]{:S(2)}, u32[]{:S(2)}) collective-permute-start(bf16[256,384]{1,0:T(8,128)(2,1)S(1)} %get-tuple-element.26), channel_id=1, source_target_pairs={{0,1},{1,0},{2,3},{3,2},{4,5},{5,4},{6,7},{7,6},{8,9},{9,8},{10,11... | collective-permute-start | bytes 589832 | tf_op jit(solution)/shard_map/ppermute | solution.py:275
  84.9 18.7 %collective-permute-start.10 = (bf16[256,384]{1,0:T(8,128)(2,1)S(1)}, bf16[256,384]{1,0:T(8,128)(2,1)S(1)}, u32[]{:S(2)}, u32[]{:S(2)}) collective-permute-start(bf16[256,384]{1,0:T(8,128)(2,1)S(1)} %fusion), channel_id=1, source_target_pairs={{0,256},{256,0},{1,257},{257,1},{2,258},{258,2},{3,259},{259,3},{4... | collective-permute-start | bytes 589832 | tf_op jit(solution)/shard_map/ppermute | solution.py:278

commit v2 on v1

v2 whole, which is shorter than its diff:
```python
import math

import jax
import jax.numpy as jnp
from jax import lax
from jax.experimental import pallas as pl
from jax.experimental.pallas import tpu as pltpu
from jax.sharding import PartitionSpec as P

HD = 128
TILE = 128
BLOCK = 256
PAIR = 2 * BLOCK
CHIPS = 4
FAR = -30000.0
EXP2_SCALE = HD ** (-0.5) * math.log2(math.e)
BF16 = jnp.bfloat16
F32 = jnp.float32
SMEM = pl.BlockSpec(memory_space=pltpu.SMEM)
VMEM = pl.BlockSpec(memory_space=pltpu.VMEM)
ANY = pl.BlockSpec(memory_space=pl.ANY)
HBM = pl.BlockSpec(memory_space=pltpu.HBM)


def params(mib=32):
    return pltpu.CompilerParams(vmem_limit_bytes=mib * 1024 * 1024)


def normed(block):
    wide = block.astype(F32)
    return (wide * lax.rsqrt(jnp.mean(wide * wide, axis=-1, keepdims=True) + 1e-06)).astype(BF16)


def start_out(
    place, q_ref, k_ref, v_ref, w_ref, t_ref, spread_ref, pair_ref, near_ref, cross_ref, mine_ref,
    q_in, k_in, v_in, in_sems, out_sems,
):
    odd, chip, core = place[1], place[2], place[3]
    rows, width = w_ref.shape[1], w_ref.shape[2] // (2 * CHIPS)
    slots = t_ref.shape[2]
    loads = [
        pltpu.make_async_copy(source.at[0], target, in_sems.at[i])
        for i, (source, target) in enumerate(((k_ref, k_in), (v_ref, v_in), (q_ref, q_in)))
    ]
    for load in loads:
        load.start()
    copies = []
    for target in range(CHIPS):
        for half in range(2):
            side = target * 2 + (core if half == 0 else 1 - core)
            columns = pl.ds(pl.multiple_of(side * width, 128), width)
            copies.append((
                w_ref.at[0, :, columns],
                spread_ref.at[target, pl.ds(0, rows), pl.ds(half * width, width)],
            ))
            columns = pl.ds(pl.multiple_of((side * 2 + odd) * HD, 128), HD)
            for kind in range(2):
                copies.append((
                    t_ref.at[0, kind, :, columns],
                    spread_ref.at[target, pl.ds(rows, slots), pl.ds((2 * half + kind) * HD, HD)],
                ))
    copies = [
        pltpu.make_async_copy(source, target, out_sems.at[i])
        for i, (source, target) in enumerate(copies)
    ]
    for copy in copies:
        copy.start()

    def halves(load, ref, prepare):
        load.wait()
        a, b = prepare(ref[:, :HD]), prepare(ref[:, HD:])
        return jnp.where(odd == 0, a, b), jnp.where(odd == 0, b, a)

    key_own, key_other = halves(loads[0], k_in, normed)
    pair_ref[0] = key_other
    cross_ref[0] = key_other
    near_ref[0] = key_own
    value_own, value_other = halves(loads[1], v_in, lambda x: x)
    pair_ref[1] = value_other
    cross_ref[1] = value_other
    near_ref[1] = value_own
    query_own, query_other = halves(loads[2], q_in, normed)
    pair_ref[2] = query_other
    mine_ref[...] = query_own
    for copy in copies:
        copy.wait()


def tile_at(place, order, pair, slot):
    return order[pair * 4 + ((slot // 2) ^ place[1]) * 2 + slot % 2]


def mask_lanes(place, order, band, pairs, text_lane):
    total = order.shape[0] // 4
    lane = lax.broadcasted_iota(jnp.int32, (TILE, HD), 1)
    key_tiles = []
    for pair in pairs:
        inside = (pair >= 0) & (pair < total)
        held = jnp.clip(pair, 0, total - 1)
        key_tiles += [(inside, tile_at(place, order, held, slot)) for slot in range(4)]
    rows = []
    for slot in range(4):
        tile = tile_at(place, order, place[0], slot)
        low, high = band[tile, 0], band[tile, 1]
        row = jnp.where(lane == text_lane, F32(FAR), F32(0.0))
        for index, (inside, key_tile) in enumerate(key_tiles):
            seen = inside & (key_tile >= low) & (key_tile <= high)
            row = jnp.where(lane == index, jnp.where(seen, F32(0.0), F32(FAR)), row)
        rows.append(row.astype(BF16))
    return jnp.concatenate(rows, axis=0)


def add_keys(total, query, key, key_lanes, value):
    scores = lax.dot_general(
        query,
        jnp.concatenate([key, key_lanes], axis=1),
        (((1,), (1,)), ((), ())),
        preferred_element_type=F32,
    )
    weights = jnp.exp2(scores * EXP2_SCALE).astype(BF16)
    wide = jnp.concatenate([value, jnp.ones_like(value)], axis=1)
    part = lax.dot_general(weights, wide, (((1,), (0,)), ((), ())), preferred_element_type=F32)
    return part if total is None else total + part


def video_lanes(index):
    shape = (PAIR, HD)
    row = lax.broadcasted_iota(jnp.int32, shape, 0)
    lane = lax.broadcasted_iota(jnp.int32, shape, 1)
    return jnp.where(lane == 4 * index + row // TILE, F32(1.0), F32(0.0)).astype(BF16)


def pair_arrays(low_ref, high_ref):
    key = jnp.concatenate([low_ref[0], high_ref[0]], axis=0)
    value = jnp.concatenate([low_ref[1], high_ref[1]], axis=0)
    return key, value


def with_lanes(arrays, index):
    key, value = arrays
    return key, video_lanes(index), value


def masked_query(place, order, band, mine_ref, pair_ref, pairs, text_lane):
    query = jnp.concatenate([mine_ref[...], pair_ref[2]], axis=0)
    return jnp.concatenate([query, mask_lanes(place, order, band, pairs, text_lane)], axis=1)


def near_keys(place, order, band, mine_ref, near_ref, pair_ref, far_ref, cross_ref, total_ref):
    pairs = (place[0], place[0] ^ 1)
    query = masked_query(place, order, band, mine_ref, pair_ref, pairs, -1)
    total = add_keys(None, query, *with_lanes(pair_arrays(near_ref, pair_ref), 0))
    total_ref[...] = add_keys(total, query, *with_lanes(pair_arrays(far_ref, cross_ref), 1))


def text_arrays(text_ref, side, count):
    text = text_ref[...]
    chips, held, _ = text.shape
    key = normed(text[:, :, :HD].reshape(chips * held, HD))
    value = text[:, :, HD:].reshape(chips * held, HD)
    row = lax.broadcasted_iota(jnp.int32, key.shape, 0)
    lane = lax.broadcasted_iota(jnp.int32, key.shape, 1)
    slot = (2 * (row // held) + side) * held + row % held
    dead = (lane == HD - 1) & (slot >= count[0])
    return key, jnp.where(dead, F32(1.0), F32(0.0)).astype(BF16), value


def middle_keys(
    place, order, band, count, mine_ref, pair_ref, sum_ref, below_ref, above_ref, own_text, core_text,
    total_ref,
):
    pairs = (place[0] - 2, place[0] + 2)
    query = masked_query(place, order, band, mine_ref, pair_ref, pairs, HD - 1)
    total = sum_ref[...]
    for index, ref in enumerate((below_ref, above_ref)):
        total = add_keys(total, query, *with_lanes(pair_arrays(ref.at[0], ref.at[1]), index))
    total = add_keys(total, query, *text_arrays(own_text, place[3], count))
    total_ref[...] = add_keys(total, query, *text_arrays(core_text, 1 - place[3], count))


def last_keys(place, order, band, mine_ref, pair_ref, sum_ref, beside_ref, out_ref, held, sems):
    loads = [
        pltpu.make_async_copy(beside_ref.at[block, kind], held.at[kind, block], sems.at[kind, block])
        for kind in range(2)
        for block in range(2)
    ]
    for load in loads:
        load.start()
    own, odd = place[0], place[1]
    beside = own - 1 + 2 * lax.rem(own, 2)
    query = masked_query(place, order, band, mine_ref, pair_ref, (beside,), -1)
    for load in loads:
        load.wait()
    key = jnp.concatenate([held[0, 0], held[0, 1]], axis=0)
    value = jnp.concatenate([held[1, 0], held[1, 1]], axis=0)
    total = add_keys(sum_ref[...], query, key, video_lanes(0), value)
    result = (total[:, :HD] / total[:, HD:]).astype(BF16)
    for chip in range(CHIPS):
        out_ref[odd * CHIPS + chip] = result[BLOCK:]
        out_ref[(1 - odd) * CHIPS + chip] = result[:BLOCK]


def project(heads_ref, weight_ref, kept_ref, sent_ref):
    total = None
    depth = 2 * HD
    for chip in range(CHIPS):
        heads = jnp.concatenate([heads_ref[chip], heads_ref[CHIPS + chip]], axis=1)
        part = jnp.dot(heads, weight_ref[chip, :depth], preferred_element_type=F32)
        total = part if total is None else total + part
    width = kept_ref.shape[1]
    kept_ref[...] = total[:, :width]
    sent_ref[...] = total[:, width:].astype(BF16)


def body(rows, queries, keys, values, text_kv, text_count, out_weight, gate, band, tile_order):
    seq_count = lax.axis_size("seq")
    seq = lax.axis_index("seq")
    grp = lax.axis_index("grp")
    place = jnp.stack([seq // 2, seq % 2, grp // 2, grp % 2]).astype(jnp.int32)
    shape = jax.ShapeDtypeStruct
    width = gate.shape[1]
    depth, slots = out_weight.shape[1], text_kv.shape[2]

    spread, pair_out, near, cross_out, mine = pl.pallas_call(
        start_out,
        out_shape=(
            shape((CHIPS, depth + slots, 2 * width), BF16),
            shape((3, BLOCK, HD), BF16),
            shape((2, BLOCK, HD), BF16),
            shape((2, BLOCK, HD), BF16),
            shape((BLOCK, HD), BF16),
        ),
        in_specs=[SMEM] + [HBM] * 5,
        out_specs=(ANY,) + (VMEM,) * 4,
        scratch_shapes=[pltpu.VMEM((BLOCK, 2 * HD), BF16)] * 3
        + [pltpu.SemaphoreType.DMA((3,)), pltpu.SemaphoreType.DMA((6 * CHIPS,))],
        compiler_params=params(60),
        cost_estimate=pl.CostEstimate(flops=10**6, bytes_accessed=4 * 10**6, transcendentals=0),
    )(place, queries, keys, values, out_weight, text_kv)

    by_core = [[2 * chip + core for chip in range(CHIPS)] for core in range(2)]
    spread = lax.all_to_all(spread, "grp", 0, 0, axis_index_groups=by_core)

    def swapped(block, mask):
        return lax.ppermute(block, "seq", [(i, i ^ mask) for i in range(seq_count)])

    pair_in = swapped(pair_out, 1)
    far_in = swapped(near, 2)
    cross_in = swapped(cross_out, 3)
    rows_in = swapped(rows[0], 1)

    own_pair = jnp.stack([near, pair_in[:2]])
    other_pair = jnp.stack([far_in, cross_in])
    up = [(i, i + 4) for i in range(seq_count - 4)]
    down = [(i + 4, i) for i in range(seq_count - 4)]
    below = lax.ppermute(own_pair, "seq", up)
    above = lax.ppermute(own_pair, "seq", down)
    mixed = [(i, j) for i, j in up if i % 4 < 2] + [(i, j) for i, j in down if i % 4 >= 2]
    beside = lax.ppermute(other_pair, "seq", mixed)

    def cost(pieces):
        size = 4 * PAIR * pieces * PAIR * 256
        return pl.CostEstimate(flops=size, bytes_accessed=10**6, transcendentals=PAIR * pieces * PAIR)

    sums = shape((PAIR, 2 * HD), F32)
    total = pl.pallas_call(
        near_keys,
        out_shape=sums,
        in_specs=[SMEM] * 3 + [VMEM] * 5,
        compiler_params=params(),
        cost_estimate=cost(2),
    )(place, tile_order, band, mine, near, pair_in, far_in, cross_in)
    total, rows_in, spread = lax.optimization_barrier((total, rows_in, spread))
    own_text = spread[:, depth:, : 2 * HD]
    core_text = lax.ppermute(
        spread[:, depth:, 2 * HD : 4 * HD], "grp", [(g, g ^ 1) for g in range(2 * CHIPS)]
    )
    total = pl.pallas_call(
        middle_keys,
        out_shape=sums,
        in_specs=[SMEM] * 4 + [VMEM] * 7,
        compiler_params=params(),
        cost_estimate=cost(2),
    )(place, tile_order, band, text_count, mine, pair_in, total, below, above, own_text, core_text)
    attention = pl.pallas_call(
        last_keys,
        out_shape=shape((2 * CHIPS, BLOCK, HD), BF16),
        in_specs=[SMEM] * 3 + [VMEM] * 3 + [ANY],
        scratch_shapes=[pltpu.VMEM((2, 2, BLOCK, HD), BF16), pltpu.SemaphoreType.DMA((2, 2))],
        compiler_params=params(),
        cost_estimate=cost(1),
    )(place, tile_order, band, mine, pair_in, total, beside)

    groups = [
        [(2 * pair + odd) * 2 * CHIPS + 2 * chip + core for odd in range(2) for chip in range(CHIPS)]
        for pair in range(seq_count // 2)
        for core in range(2)
    ]
    heads = lax.all_to_all(attention, ("seq", "grp"), 0, 0, axis_index_groups=groups)
    kept, sent = pl.pallas_call(
        project,
        out_shape=(shape((BLOCK, width), F32), shape((BLOCK, width), BF16)),
        in_specs=[VMEM] * 2,
        compiler_params=params(),
        cost_estimate=pl.CostEstimate(
            flops=2 * BLOCK * 1024 * 768, bytes_accessed=3 * 10**6, transcendentals=0
        ),
    )(heads, spread)
    other = lax.ppermute(sent, "grp", [(g, g ^ 1) for g in range(2 * CHIPS)])
    share = kept + other.astype(F32)
    result = (rows_in.astype(F32) + gate[0][None, :] * share).astype(BF16)
    across = [
        (part * seq_count + i, (1 - part) * seq_count + (i ^ 1))
        for part in range(2)
        for i in range(seq_count)
    ]
    handed = lax.ppermute(result, ("section", "seq"), across)
    return handed[None]


def solution(mesh):
    placed = (
        P("section", "seq", "grp"),
        P("section", "seq", "grp"),
        P("section", "seq", "grp"),
        P("section", "seq", "grp"),
        P("section", None, "grp", None),
        P("section"),
        P("section", "grp", None),
        P("section", "grp"),
        P(),
        P(),
    )
    return jax.shard_map(
        body, mesh=mesh, in_specs=placed, out_specs=P("section", "seq", "grp"), check_vma=False
    )
```

time: 105 us -> 142 us (1.35)
  the two profiles are of different devices: /device:TPU:88 before, /device:TPU:24 now
where the time goes in v2:
time: 142 us; the launch traced here: 141 us
  Pallas kernels  61.7 us (43%)
  starting transfers between devices  44.2 us (31%)
  blocking collectives  14.7 us (10%)
  waiting for transfers between devices  12.4 us (9%)
  local copies, waits for them, and re-layouts  3.93 us (3%)
  other arithmetic  3.13 us (2%)
    pallas_call x1, Pallas kernels, body(): pl.pallas_call(start_out, out_shape=(shape((CHIPS, depth + slots, 2 * wid...  54.4 us
    ppermute x4, starting transfers between devices, swapped(): return lax.ppermute(block, 'seq', [(i, i ^ mask) for i in range(seq_count)])  15.7 us
    all_to_all x1, blocking collectives, body(): lax.all_to_all(attention, ('seq', 'grp'), 0, 0, axis_index_groups=groups)  14.7 us
    ppermute x1, starting transfers between devices, body(): handed = lax.ppermute(result, ('section', 'seq'), across)  8.53 us
    ppermute x1, waiting for transfers between devices, body(): handed = lax.ppermute(result, ('section', 'seq'), across)  8.41 us
    ppermute x1, starting transfers between devices, body(): below = lax.ppermute(own_pair, 'seq', up)  5.13 us
    ppermute x1, starting transfers between devices, body(): beside = lax.ppermute(other_pair, 'seq', mixed)  4.68 us
    all_to_all x1, starting transfers between devices, body(): spread = lax.all_to_all(spread, 'grp', 0, 0, axis_index_groups=by_core)  4.44 us
  transfers between devices with their start and end apart: 11, of which 4 were waited for; matrix products, arithmetic and copies ran while one was open for 1% of the time, Pallas kernels for 3%

profile of v2, /device:TPU:24, one launch (start us, length us, event | category | flops | bytes accessed | tf_op | source)
XLA Modules:
  0.0 141.0 jit_solution(11846740802009798818)
XLA Ops:
  0.0 0.7 pad_add_fusion.place
  0.7 54.4 %shard_map.100 = (bf16[4,288,768]{2,1,0:T(8,128)(2,1)}, bf16[3,256,128]{2,1,0:T(8,128)(2,1)}, bf16[2,256,128]{2,1,0:T(8,128)(2,1)}, bf16[2,256,128]{2,1,0:T(8,128)(2,1)}, bf16[256,128]{1,0:T(8,128)(2,1)}) custom-call(s32[4]{0:T(128)} %pad_add_fusion.place, bf16[1,256,256]{2,1,0:T(8,128)(2,1)} %q_ref.1, bf16[1,256,256]{2,1,0:T(8,128)(2,1)} %k_ref.1, ...), custom_call_target="tpu_custom_call" | custom-call | flops 1000000 | bytes 4000000 | tf_op jit(solution)/shard_map/pallas_call | solution.py:224
  55.1 0.0 copy-start.11
  55.1 0.0 copy-start.1
  55.1 0.0 copy-start.10
  55.1 0.0 copy-start.9
  55.1 0.0 copy-start
  55.1 0.0 copy-start.6
  55.1 0.0 copy-start.7
  55.2 4.4 %all-to-all-start = ((bf16[4,288,768]{2,1,0:T(8,128)(2,1)}), bf16[4,288,768]{2,1,0:T(8,128)(2,1)S(1)}, u32[]{:S(2)}, u32[]{:S(2)}) async-start(bf16[4,288,768]{2,1,0:T(8,128)(2,1)} %get-tuple-element.19), calls=%async_computation | async-start | bytes 3538944 | tf_op jit(solution)/shard_map/all_to_all | solution.py:242
  59.6 0.0 copy-done.11
  59.6 7.9 %collective-permute-start.2 = (bf16[2,256,128]{2,1,0:T(8,128)(2,1)S(1)}, bf16[2,256,128]{2,1,0:T(8,128)(2,1)S(1)}, u32[]{:S(2)}, u32[]{:S(2)}) collective-permute-start(bf16[2,256,128]{2,1,0:T(8,128)(2,1)S(1)} %copy-done.11), channel_id=1, source_target_pairs={{0,24},{8,16},{16,8},{24,0},{32,56},{40,48},{48,40},{56,32},{64,88... | collective-permute-start | bytes 393224 | tf_op jit(solution)/shard_map/ppermute | solution.py:245
  67.5 1.9 %collective-permute-start.1 = (bf16[2,256,128]{2,1,0:T(8,128)(2,1)S(1)}, bf16[2,256,128]{2,1,0:T(8,128)(2,1)S(1)}, u32[]{:S(2)}, u32[]{:S(2)}) collective-permute-start(bf16[2,256,128]{2,1,0:T(8,128)(2,1)S(1)} %copy-done.1), channel_id=1, source_target_pairs={{0,16},{8,24},{16,0},{24,8},{32,48},{40,56},{48,32},{56,40},{64,80... | collective-permute-start | bytes 393224 | tf_op jit(solution)/shard_map/ppermute | solution.py:245
  69.4 2.5 %collective-permute-start = (bf16[3,256,128]{2,1,0:T(8,128)(2,1)S(1)}, bf16[3,256,128]{2,1,0:T(8,128)(2,1)S(1)}, u32[]{:S(2)}, u32[]{:S(2)}) collective-permute-start(bf16[3,256,128]{2,1,0:T(8,128)(2,1)S(1)} %copy-done.10), channel_id=1, source_target_pairs={{0,8},{8,0},{16,24},{24,16},{32,40},{40,32},{48,56},{56,48},{64,72... | collective-permute-start | bytes 589832 | tf_op jit(solution)/shard_map/ppermute | solution.py:245
  71.9 3.4 %collective-permute-start.3 = (bf16[256,384]{1,0:T(8,128)(2,1)}, bf16[256,384]{1,0:T(8,128)(2,1)}, u32[]{:S(2)}, u32[]{:S(2)}) collective-permute-start(bf16[256,384]{1,0:T(8,128)(2,1)} %bitcast.4), channel_id=1, source_target_pairs={{0,8},{8,0},{16,24},{24,16},{32,40},{40,32},{48,56},{56,48},{64,72... | collective-permute-start | bytes 589832 | tf_op jit(solution)/shard_map/ppermute | solution.py:245
  75.3 0.1 copy.11.band
  75.4 0.0 collective-permute-done.2.cross_ref
  75.4 2.0 %collective-permute-done.1.far_ref = bf16[2,256,128]{2,1,0:T(8,128)(2,1)S(1)} collective-permute-done((bf16[2,256,128]{2,1,0:T(8,128)(2,1)S(1)}, bf16[2,256,128]{2,1,0:T(8,128)(2,1)S(1)}, u32[]{:S(2)}, u32[]{:S(2)}) %collective-permute-start.1) | collective-permute-done | bytes 131104 | tf_op jit(solution)/shard_map/ppermute | solution.py:245
  77.4 0.7 pad_maximum_fusion.1
  78.2 0.6 copy-done.2
  78.8 0.7 copy-done.4
  79.4 4.7 %collective-permute-start.7 = (bf16[2,2,256,128]{3,2,1,0:T(8,128)(2,1)}, bf16[2,2,256,128]{3,2,1,0:T(8,128)(2,1)S(1)}, u32[]{:S(2)}, u32[]{:S(2)}) collective-permute-start(bf16[2,2,256,128]{3,2,1,0:T(8,128)(2,1)} %pad_maximum_fusion.1), channel_id=1, source_target_pairs={{0,32},{8,40},{32,64},{40,72},{64,96},{72,104},{96,128},{104,136},... | collective-permute-start | bytes 786440 | tf_op jit(solution)/shard_map/ppermute | solution.py:259
  84.1 0.0 collective-permute-done.pair_ref
  84.2 0.7 pad_maximum_fusion
  84.9 1.9 %collective-permute-start.5 = (bf16[2,2,256,128]{3,2,1,0:T(8,128)(2,1)}, bf16[2,2,256,128]{3,2,1,0:T(8,128)(2,1)S(1)}, u32[]{:S(2)}, u32[]{:S(2)}) collective-permute-start(bf16[2,2,256,128]{3,2,1,0:T(8,128)(2,1)} %pad_maximum_fusion), channel_id=1, source_target_pairs={{32,0},{40,8},{48,16},{56,24},{64,32},{72,40},{80,48},{88,56},{96,... | collective-permute-start | bytes 786440 | tf_op jit(solution)/shard_map/ppermute | solution.py:257
  86.8 5.1 %collective-permute-start.4 = (bf16[2,2,256,128]{3,2,1,0:T(8,128)(2,1)}, bf16[2,2,256,128]{3,2,1,0:T(8,128)(2,1)S(1)}, u32[]{:S(2)}, u32[]{:S(2)}) collective-permute-start(bf16[2,2,256,128]{3,2,1,0:T(8,128)(2,1)} %pad_maximum_fusion), channel_id=1, source_target_pairs={{0,32},{8,40},{16,48},{24,56},{32,64},{40,72},{48,80},{56,88},{64,... | collective-permute-start | bytes 786440 | tf_op jit(solution)/shard_map/ppermute | solution.py:256
  92.0 0.9 copy-done.3
  92.9 0.9 copy-done.5
  93.8 2.2 %shard_map.101.sum_ref = f32[512,256]{1,0:T(8,128)S(1)} custom-call(s32[4]{0:T(128)S(1)} %copy-done.6, s32[64]{0:T(128)S(1)} %copy-done.7, s32[64,2]{1,0:T(8,128)S(1)} %copy.11.band, bf16[256,128]{1,0:T(8,128)(2,1)S(1)} %copy-done, bf16[2,256,128]{2,1,0:T(8,128)(2,1)S(1)} %copy-done.1, bf16[3,256,128]{2,1,0:T(8,128)(2,1)S(1)} %collective-permute-done.pair_ref, ...), custom_call_target="tpu_custom_call" | custom-call | flops 536870912 | bytes 1000000 | tf_op jit(solution)/shard_map/pallas_call | solution.py:266
  96.0 0.0 collective-permute-done.3
  96.0 0.0 all-to-all-done.weight_ref
  96.0 1.9 %collective-permute-start.6 = (bf16[4,32,256]{2,1,0:T(8,128)(2,1)S(1)}, bf16[4,32,256]{2,1,0:T(8,128)(2,1)S(1)}, u32[]{:S(2)}, u32[]{:S(2)}) collective-permute-start(bf16[4,32,256]{2,1,0:T(8,128)(2,1)S(1)} %get-tuple-element.25), channel_id=1, source_target_pairs={{0,1},{1,0},{2,3},{3,2},{4,5},{5,4},{6,7},{7,6},{8,9},{9,8},{10,11... | collective-permute-start | bytes 196616 | tf_op jit(solution)/shard_map/ppermute | solution.py:275
  98.6 0.0 collective-permute-done.5.above_ref
  98.6 0.0 collective-permute-done.4.below_ref
  98.6 0.6 collective-permute-done.6.core_text
  99.2 2.4 %shard_map.102.sum_ref = f32[512,256]{1,0:T(8,128)S(1)} custom-call(s32[4]{0:T(128)S(1)} %copy-done.6, s32[64]{0:T(128)S(1)} %copy-done.7, s32[64,2]{1,0:T(8,128)S(1)} %copy.11.band, s32[1]{0:T(128)S(6)} %copy.15.count, bf16[256,128]{1,0:T(8,128)(2,1)S(1)} %copy-done, bf16[3,256,128]{2,1,0:T(8,128)(2,1)S(1)} %collective-permute-done.pair_ref, ...), custom_call_target="tpu_custom_call" | custom-call | flops 536870912 | bytes 1000000 | tf_op jit(solution)/shard_map/pallas_call | solution.py:278
  101.6 0.0 collective-permute-done.7.beside_ref
  101.6 2.1 %shard_map.103 = bf16[8,256,128]{2,1,0:T(8,128)(2,1)S(1)} custom-call(s32[4]{0:T(128)S(1)} %copy-done.6, s32[64]{0:T(128)S(1)} %copy-done.7, s32[64,2]{1,0:T(8,128)S(1)} %copy.11.band, bf16[256,128]{1,0:T(8,128)(2,1)S(1)} %copy-done, bf16[3,256,128]{2,1,0:T(8,128)(2,1)S(1)} %collective-permute-done.pair_ref, f32[512,256]{1,0:T(8,128)S(1)} %shard_map.102.sum_ref, ...), custom_call_target="tpu_custom_call" | custom-call | flops 268435456 | bytes 1000000 | tf_op jit(solution)/shard_map/pallas_call | solution.py:285
  103.7 0.0 copy-start.8
  103.7 14.7 %all_to_all.10.heads_ref = bf16[8,256,128]{2,1,0:T(8,128)(2,1)S(1)} all-to-all(bf16[8,256,128]{2,1,0:T(8,128)(2,1)S(1)} %shard_map.103), channel_id=1, replica_groups={{0,2,4,6,8,10,12,14},{1,3,5,7,9,11,13,15},{16,18,20,22,24,26,28,30},{17..., dimensions={0} | all-to-all | bytes 1048576 | tf_op jit(solution)/shard_map/all_to_all | solution.py:299
  118.4 0.6 shard_map.104
  119.0 1.9 %collective-permute-start.8 = (bf16[256,384]{1,0:T(8,128)(2,1)S(1)}, bf16[256,384]{1,0:T(8,128)(2,1)S(1)}, u32[]{:S(2)}, u32[]{:S(2)}) collective-permute-start(bf16[256,384]{1,0:T(8,128)(2,1)S(1)} %get-tuple-element.24), channel_id=1, source_target_pairs={{0,1},{1,0},{2,3},{3,2},{4,5},{5,4},{6,7},{7,6},{8,9},{9,8},{10,11... | collective-permute-start | bytes 589832 | tf_op jit(solution)/shard_map/ppermute | solution.py:309
  120.9 0.0 copy-done.8
  120.9 1.4 collective-permute-done.8
  122.3 1.0 add_convert_fusion
  123.3 8.5 %collective-permute-start.9 = (bf16[256,384]{1,0:T(8,128)(2,1)S(1)}, bf16[256,384]{1,0:T(8,128)(2,1)S(1)}, u32[]{:S(2)}, u32[]{:S(2)}) collective-permute-start(bf16[256,384]{1,0:T(8,128)(2,1)S(1)} %add_convert_fusion), channel_id=1, source_target_pairs={{0,264},{8,256},{16,280},{24,272},{32,296},{40,288},{48,312},{56,3... | collective-permute-start | bytes 589832 | tf_op jit(solution)/shard_map/ppermute | solution.py:317
  131.9 8.4 %collective-permute-done.9 = bf16[256,384]{1,0:T(8,128)(2,1)S(1)} collective-permute-done((bf16[256,384]{1,0:T(8,128)(2,1)S(1)}, bf16[256,384]{1,0:T(8,128)(2,1)S(1)}, u32[]{:S(2)}, u32[]{:S(2)}) %collective-permute-start.9) | collective-permute-done | bytes 196640 | tf_op jit(solution)/shard_map/ppermute | solution.py:317
  140.3 0.7 copy.16
  (13 shorter events, 0.1 us)
Async XLA Ops:
  55.1 4.5 %copy-start.11 = (bf16[2,256,128]{2,1,0:T(8,128)(2,1)S(1)}, bf16[2,256,128]{2,1,0:T(8,128)(2,1)}, u32[]{:S(2)}) copy-start(bf16[2,256,128]{2,1,0:T(8,128)(2,1)} %get-tuple-element.18) | copy-start | bytes 393220
  55.1 12.4 %copy-start.1 = (bf16[2,256,128]{2,1,0:T(8,128)(2,1)S(1)}, bf16[2,256,128]{2,1,0:T(8,128)(2,1)}, u32[]{:S(2)}) copy-start(bf16[2,256,128]{2,1,0:T(8,128)(2,1)} %get-tuple-element.16.near_ref) | copy-start | bytes 393220
  55.1 14.3 %copy-start.10 = (bf16[3,256,128]{2,1,0:T(8,128)(2,1)S(1)}, bf16[3,256,128]{2,1,0:T(8,128)(2,1)}, u32[]{:S(2)}) copy-start(bf16[3,256,128]{2,1,0:T(8,128)(2,1)} %get-tuple-element.17) | copy-start | bytes 589828
  55.1 20.2 %copy-start.9 = (s32[64,2]{0,1:T(2,128)S(1)}, s32[64,2]{0,1:T(2,128)}, u32[]{:S(2)}) copy-start(s32[64,2]{0,1:T(2,128)} %param.18) | copy-start | bytes 1540
  55.1 36.8 %copy-start = (bf16[256,128]{1,0:T(8,128)(2,1)S(1)}, bf16[256,128]{1,0:T(8,128)(2,1)}, u32[]{:S(2)}) copy-start(bf16[256,128]{1,0:T(8,128)(2,1)} %get-tuple-element.15.mine_ref) | copy-start | bytes 196612
  55.1 36.8 %copy-start.6 = (s32[4]{0:T(128)S(1)}, s32[4]{0:T(128)}, u32[]{:S(2)}) copy-start(s32[4]{0:T(128)} %pad_add_fusion.place) | copy-start | bytes 52
  55.1 36.8 %copy-start.7 = (s32[64]{0:T(128)S(1)}, s32[64]{0:T(128)}, u32[]{:S(2)}) copy-start(s32[64]{0:T(128)} %order.5) | copy-start | bytes 772
  55.2 40.8 %all-to-all-start = ((bf16[4,288,768]{2,1,0:T(8,128)(2,1)}), bf16[4,288,768]{2,1,0:T(8,128)(2,1)S(1)}, u32[]{:S(2)}, u32[]{:S(2)}) async-start(bf16[4,288,768]{2,1,0:T(8,128)(2,1)} %get-tuple-element.19), calls=%async_computation | async-start | bytes 3538944 | tf_op jit(solution)/shard_map/all_to_all | solution.py:242
  59.6 15.8 %collective-permute-start.2 = (bf16[2,256,128]{2,1,0:T(8,128)(2,1)S(1)}, bf16[2,256,128]{2,1,0:T(8,128)(2,1)S(1)}, u32[]{:S(2)}, u32[]{:S(2)}) collective-permute-start(bf16[2,256,128]{2,1,0:T(8,128)(2,1)S(1)} %copy-done.11), channel_id=1, source_target_pairs={{0,24},{8,16},{16,8},{24,0},{32,56},{40,48},{48,40},{56,32},{64,88... | collective-permute-start | bytes 393224 | tf_op jit(solution)/shard_map/ppermute | solution.py:245
  67.5 9.9 %collective-permute-start.1 = (bf16[2,256,128]{2,1,0:T(8,128)(2,1)S(1)}, bf16[2,256,128]{2,1,0:T(8,128)(2,1)S(1)}, u32[]{:S(2)}, u32[]{:S(2)}) collective-permute-start(bf16[2,256,128]{2,1,0:T(8,128)(2,1)S(1)} %copy-done.1), channel_id=1, source_target_pairs={{0,16},{8,24},{16,0},{24,8},{32,48},{40,56},{48,32},{56,40},{64,80... | collective-permute-start | bytes 393224 | tf_op jit(solution)/shard_map/ppermute | solution.py:245
  69.4 14.7 %collective-permute-start = (bf16[3,256,128]{2,1,0:T(8,128)(2,1)S(1)}, bf16[3,256,128]{2,1,0:T(8,128)(2,1)S(1)}, u32[]{:S(2)}, u32[]{:S(2)}) collective-permute-start(bf16[3,256,128]{2,1,0:T(8,128)(2,1)S(1)} %copy-done.10), channel_id=1, source_target_pairs={{0,8},{8,0},{16,24},{24,16},{32,40},{40,32},{48,56},{56,48},{64,72... | collective-permute-start | bytes 589832 | tf_op jit(solution)/shard_map/ppermute | solution.py:245
  71.9 24.1 %collective-permute-start.3 = (bf16[256,384]{1,0:T(8,128)(2,1)}, bf16[256,384]{1,0:T(8,128)(2,1)}, u32[]{:S(2)}, u32[]{:S(2)}) collective-permute-start(bf16[256,384]{1,0:T(8,128)(2,1)} %bitcast.4), channel_id=1, source_target_pairs={{0,8},{8,0},{16,24},{24,16},{32,40},{40,32},{48,56},{56,48},{64,72... | collective-permute-start | bytes 589832 | tf_op jit(solution)/shard_map/ppermute | solution.py:245
  78.2 0.6 copy-start.2
  78.8 0.7 copy-start.4
  79.4 22.1 %collective-permute-start.7 = (bf16[2,2,256,128]{3,2,1,0:T(8,128)(2,1)}, bf16[2,2,256,128]{3,2,1,0:T(8,128)(2,1)S(1)}, u32[]{:S(2)}, u32[]{:S(2)}) collective-permute-start(bf16[2,2,256,128]{3,2,1,0:T(8,128)(2,1)} %pad_maximum_fusion.1), channel_id=1, source_target_pairs={{0,32},{8,40},{32,64},{40,72},{64,96},{72,104},{96,128},{104,136},... | collective-permute-start | bytes 786440 | tf_op jit(solution)/shard_map/ppermute | solution.py:259
  84.9 13.7 %collective-permute-start.5 = (bf16[2,2,256,128]{3,2,1,0:T(8,128)(2,1)}, bf16[2,2,256,128]{3,2,1,0:T(8,128)(2,1)S(1)}, u32[]{:S(2)}, u32[]{:S(2)}) collective-permute-start(bf16[2,2,256,128]{3,2,1,0:T(8,128)(2,1)} %pad_maximum_fusion), channel_id=1, source_target_pairs={{32,0},{40,8},{48,16},{56,24},{64,32},{72,40},{80,48},{88,56},{96,... | collective-permute-start | bytes 786440 | tf_op jit(solution)/shard_map/ppermute | solution.py:257
  86.8 11.8 %collective-permute-start.4 = (bf16[2,2,256,128]{3,2,1,0:T(8,128)(2,1)}, bf16[2,2,256,128]{3,2,1,0:T(8,128)(2,1)S(1)}, u32[]{:S(2)}, u32[]{:S(2)}) collective-permute-start(bf16[2,2,256,128]{3,2,1,0:T(8,128)(2,1)} %pad_maximum_fusion), channel_id=1, source_target_pairs={{0,32},{8,40},{16,48},{24,56},{32,64},{40,72},{48,80},{56,88},{64,... | collective-permute-start | bytes 786440 | tf_op jit(solution)/shard_map/ppermute | solution.py:256
  92.0 0.9 copy-start.3
  92.9 0.9 copy-start.5
  96.0 3.1 %collective-permute-start.6 = (bf16[4,32,256]{2,1,0:T(8,128)(2,1)S(1)}, bf16[4,32,256]{2,1,0:T(8,128)(2,1)S(1)}, u32[]{:S(2)}, u32[]{:S(2)}) collective-permute-start(bf16[4,32,256]{2,1,0:T(8,128)(2,1)S(1)} %get-tuple-element.25), channel_id=1, source_target_pairs={{0,1},{1,0},{2,3},{3,2},{4,5},{5,4},{6,7},{7,6},{8,9},{9,8},{10,11... | collective-permute-start | bytes 196616 | tf_op jit(solution)/shard_map/ppermute | solution.py:275
  103.7 17.2 %copy-start.8 = (f32[1,384]{1,0:T(1,128)S(1)}, f32[1,384]{1,0:T(1,128)}, u32[]{:S(2)}) copy-start(f32[1,384]{1,0:T(1,128)} %param.17) | copy-start | bytes 4612
  119.0 3.3 %collective-permute-start.8 = (bf16[256,384]{1,0:T(8,128)(2,1)S(1)}, bf16[256,384]{1,0:T(8,128)(2,1)S(1)}, u32[]{:S(2)}, u32[]{:S(2)}) collective-permute-start(bf16[256,384]{1,0:T(8,128)(2,1)S(1)} %get-tuple-element.24), channel_id=1, source_target_pairs={{0,1},{1,0},{2,3},{3,2},{4,5},{5,4},{6,7},{7,6},{8,9},{9,8},{10,11... | collective-permute-start | bytes 589832 | tf_op jit(solution)/shard_map/ppermute | solution.py:309
  123.3 17.0 %collective-permute-start.9 = (bf16[256,384]{1,0:T(8,128)(2,1)S(1)}, bf16[256,384]{1,0:T(8,128)(2,1)S(1)}, u32[]{:S(2)}, u32[]{:S(2)}) collective-permute-start(bf16[256,384]{1,0:T(8,128)(2,1)S(1)} %add_convert_fusion), channel_id=1, source_target_pairs={{0,264},{8,256},{16,280},{24,272},{32,296},{40,288},{48,312},{56,3... | collective-permute-start | bytes 589832 | tf_op jit(solution)/shard_map/ppermute | solution.py:317

commit v3 on v2

v3 whole, which is shorter than its diff:
```python
import math

import jax
import jax.numpy as jnp
from jax import lax
from jax.experimental import pallas as pl
from jax.experimental.pallas import tpu as pltpu
from jax.sharding import PartitionSpec as P

HD = 128
TILE = 128
BLOCK = 256
PAIR = 2 * BLOCK
CHIPS = 4
FAR = -30000.0
EXP2_SCALE = HD ** (-0.5) * math.log2(math.e)
PIECES = 5
TEXT_LANE = 4 * PIECES
COUNT_LANE, ODD_LANE, CORE_LANE = 32, 33, 34
BF16 = jnp.bfloat16
F32 = jnp.float32
SMEM = pl.BlockSpec(memory_space=pltpu.SMEM)
VMEM = pl.BlockSpec(memory_space=pltpu.VMEM)
HBM = pl.BlockSpec(memory_space=pltpu.HBM)


def params(mib=16):
    return pltpu.CompilerParams(vmem_limit_bytes=mib * 1024 * 1024)


def normed(block):
    wide = block.astype(F32)
    return (wide * lax.rsqrt(jnp.mean(wide * wide, axis=-1, keepdims=True) + 1e-06)).astype(BF16)


def start_out(
    place, order, band, count, q_ref, k_ref, v_ref, r_ref, w_ref, t_ref,
    spread_ref, near_ref, cross_ref, along_ref, mine_ref, mask_ref,
    q_in, k_in, v_in, sems, w_sems,
):
    odd, core = place[1], place[3]
    depth, width = w_ref.shape[1], w_ref.shape[2] // (2 * CHIPS)
    slots = t_ref.shape[2]
    loads = [
        pltpu.make_async_copy(source.at[0], target, sems.at[i])
        for i, (source, target) in enumerate((
            (k_ref, k_in), (v_ref, v_in), (q_ref, q_in), (r_ref, along_ref.at[:, pl.ds(0, width)])
        ))
    ]
    copies = []
    for target in range(CHIPS):
        for half in range(2):
            side = target * 2 + (core if half == 0 else 1 - core)
            columns = pl.ds(pl.multiple_of(side * width, 128), width)
            copies.append((
                w_ref.at[0, :, columns],
                spread_ref.at[target, pl.ds(0, depth), pl.ds(half * width, width)],
            ))
            columns = pl.ds(pl.multiple_of((side * 2 + odd) * HD, 128), HD)
            for kind in range(2):
                copies.append((
                    t_ref.at[0, kind, :, columns],
                    spread_ref.at[target, pl.ds(depth, slots), pl.ds((2 * half + kind) * HD, HD)],
                ))
    copies = [
        pltpu.make_async_copy(source, target, w_sems.at[i])
        for i, (source, target) in enumerate(copies)
    ]
    for copy in loads + copies:
        copy.start()
    spread_ref[:, depth:, 4 * HD :] = jnp.zeros((CHIPS, slots, 2 * width - 4 * HD), BF16)
    mask_ref[...] = mask_rows(place, order, band, count)

    def halves(load, ref, prepare):
        load.wait()
        a, b = prepare(ref[:, :HD]), prepare(ref[:, HD:])
        return jnp.where(odd == 0, a, b), jnp.where(odd == 0, b, a)

    near_ref[0], cross_ref[0] = halves(loads[0], k_in, normed)
    near_ref[1], cross_ref[1] = halves(loads[1], v_in, lambda x: x)
    mine_ref[...], along_ref[:, width:] = halves(loads[2], q_in, normed)
    loads[3].wait()
    for copy in copies:
        copy.wait()


def mask_rows(place, order, band, count):
    own, odd = place[0], place[1]
    total = order.shape[0] // 4

    def tile_at(pair, slot):
        return order[pair * 4 + ((slot // 2) ^ odd) * 2 + slot % 2]

    lane = lax.broadcasted_iota(jnp.int32, (8, HD), 1)
    row = lax.broadcasted_iota(jnp.int32, (8, HD), 0)
    low = jnp.zeros((8, HD), jnp.int32)
    high = jnp.zeros((8, HD), jnp.int32)
    for slot in range(4):
        tile = tile_at(own, slot)
        low = jnp.where(row == slot, band[tile, 0], low)
        high = jnp.where(row == slot, band[tile, 1], high)
    held = jnp.full((8, HD), -1, jnp.int32)
    beside = own - 1 + 2 * lax.rem(own, 2)
    for piece, pair in enumerate((own, own ^ 1, own - 2, own + 2, beside)):
        inside = (pair >= 0) & (pair < total)
        kept = jnp.clip(pair, 0, total - 1)
        for slot in range(4):
            tile = jnp.where(inside, tile_at(kept, slot), -1)
            held = jnp.where(lane == 4 * piece + slot, tile, held)
    seen = (held >= low) & (held <= high)
    result = jnp.where((lane <= TEXT_LANE) & jnp.logical_not(seen), F32(FAR), F32(0.0))
    for at, value in ((COUNT_LANE, count[0]), (ODD_LANE, odd), (CORE_LANE, place[3])):
        result = jnp.where(lane == at, value.astype(F32), result)
    return result


def masked_query(mask_ref, mine_ref, along_ref):
    query = jnp.concatenate([mine_ref[...], along_ref[:, along_ref.shape[1] - HD :]], axis=0)
    lane = lax.broadcasted_iota(jnp.int32, (TILE, HD), 1)
    lanes = [
        jnp.where(lane <= TEXT_LANE, mask_ref[slot : slot + 1, :], F32(0.0)).astype(BF16)
        for slot in range(4)
    ]
    return jnp.concatenate([query, jnp.concatenate(lanes, axis=0)], axis=1)


def add_keys(total, query, key, key_lanes, value):
    scores = lax.dot_general(
        query,
        jnp.concatenate([key, key_lanes], axis=1),
        (((1,), (1,)), ((), ())),
        preferred_element_type=F32,
    )
    weights = jnp.exp2(scores * EXP2_SCALE).astype(BF16)
    wide = jnp.concatenate([value, jnp.ones_like(value)], axis=1)
    part = lax.dot_general(weights, wide, (((1,), (0,)), ((), ())), preferred_element_type=F32)
    return part if total is None else total + part


def piece_arrays(index, low_ref, high_ref):
    shape = (PAIR, HD)
    row = lax.broadcasted_iota(jnp.int32, shape, 0)
    lane = lax.broadcasted_iota(jnp.int32, shape, 1)
    lanes = jnp.where(lane == 4 * index + row // TILE, F32(1.0), F32(0.0)).astype(BF16)
    key = jnp.concatenate([low_ref[0], high_ref[0]], axis=0)
    value = jnp.concatenate([low_ref[1], high_ref[1]], axis=0)
    return key, lanes, value


def text_arrays(mask_ref, text_ref, other_core):
    text = text_ref[...]
    chips, held, _ = text.shape
    key = normed(text[:, :, :HD].reshape(chips * held, HD))
    value = text[:, :, HD:].reshape(chips * held, HD)
    row = lax.broadcasted_iota(jnp.int32, key.shape, 0)
    lane = lax.broadcasted_iota(jnp.int32, key.shape, 1)
    core = mask_ref[0:1, CORE_LANE : CORE_LANE + 1]
    side = 1.0 - core if other_core else core
    slot = (2 * (row // held) * held + row % held).astype(F32) + side * held
    dead = (lane == TEXT_LANE) & (slot >= mask_ref[0:1, COUNT_LANE : COUNT_LANE + 1])
    return key, jnp.where(dead, F32(1.0), F32(0.0)).astype(BF16), value


def first_keys(
    mask_ref, mine_ref, along_ref, near_ref, pair_ref, far_ref, cross_ref, below_ref, above_ref,
    own_text, core_text, total_ref,
):
    query = masked_query(mask_ref, mine_ref, along_ref)
    total = add_keys(None, query, *piece_arrays(0, near_ref, pair_ref))
    total = add_keys(total, query, *piece_arrays(1, far_ref, cross_ref))
    total = add_keys(total, query, *piece_arrays(2, below_ref.at[0], below_ref.at[1]))
    total = add_keys(total, query, *piece_arrays(3, above_ref.at[0], above_ref.at[1]))
    total = add_keys(total, query, *text_arrays(mask_ref, own_text, False))
    total_ref[...] = add_keys(total, query, *text_arrays(mask_ref, core_text, True))


def last_keys(mask_ref, mine_ref, along_ref, sum_ref, beside_ref, out_ref):
    query = masked_query(mask_ref, mine_ref, along_ref)
    pieces = piece_arrays(PIECES - 1, beside_ref.at[0], beside_ref.at[1])
    total = add_keys(sum_ref[...], query, *pieces)
    result = total[:, :HD] / total[:, HD:]
    odd = mask_ref[0:1, ODD_LANE : ODD_LANE + 1] > 0.5
    own, other = result[:BLOCK], result[BLOCK:]
    to_even = jnp.where(odd, own, other).astype(BF16)
    to_odd = jnp.where(odd, other, own).astype(BF16)
    for chip in range(CHIPS):
        out_ref[chip] = to_even
        out_ref[CHIPS + chip] = to_odd


def project(heads_ref, weight_ref, along_ref, gate_ref, kept_ref, sent_ref):
    total = None
    depth, width = 2 * HD, kept_ref.shape[1]
    for chip in range(CHIPS):
        heads = jnp.concatenate([heads_ref[chip], heads_ref[CHIPS + chip]], axis=1)
        part = jnp.dot(heads, weight_ref[chip, :depth], preferred_element_type=F32)
        total = part if total is None else total + part
    kept_ref[...] = along_ref[:, :width].astype(F32) + gate_ref[...] * total[:, :width]
    sent_ref[...] = total[:, width:].astype(BF16)


def body(rows, queries, keys, values, text_kv, text_count, out_weight, gate, band, tile_order):
    seq_count = lax.axis_size("seq")
    seq = lax.axis_index("seq")
    grp = lax.axis_index("grp")
    place = jnp.stack([seq >> 1, seq & 1, grp >> 1, grp & 1]).astype(jnp.int32)
    shape = jax.ShapeDtypeStruct
    width = gate.shape[1]
    depth, slots = out_weight.shape[1], text_kv.shape[2]

    spread, near, cross_out, along, mine, mask = pl.pallas_call(
        start_out,
        out_shape=(
            shape((CHIPS, depth + slots, 2 * width), BF16),
            shape((2, BLOCK, HD), BF16),
            shape((2, BLOCK, HD), BF16),
            shape((BLOCK, width + HD), BF16),
            shape((BLOCK, HD), BF16),
            shape((8, HD), F32),
        ),
        in_specs=[SMEM] * 4 + [HBM] * 6,
        out_specs=(VMEM,) * 6,
        scratch_shapes=[pltpu.VMEM((BLOCK, 2 * HD), BF16)] * 3
        + [pltpu.SemaphoreType.DMA((4,)), pltpu.SemaphoreType.DMA((6 * CHIPS,))],
        compiler_params=params(60),
        cost_estimate=pl.CostEstimate(flops=10**6, bytes_accessed=4 * 10**6, transcendentals=0),
    )(place, tile_order, band, text_count, queries, keys, values, rows, out_weight, text_kv)

    by_core = [[2 * chip + core for chip in range(CHIPS)] for core in range(2)]
    spread = lax.all_to_all(spread, "grp", 0, 0, axis_index_groups=by_core)

    def swapped(block, mask):
        return lax.ppermute(block, "seq", [(i, i ^ mask) for i in range(seq_count)])

    pair_in = swapped(cross_out, 1)
    far_in = swapped(near, 2)
    cross_in = swapped(cross_out, 3)
    along_in = swapped(along, 1)

    own_pair = jnp.stack([near, pair_in])
    other_pair = jnp.stack([far_in, cross_in])
    up = [(i, i + 4) for i in range(seq_count - 4)]
    down = [(i + 4, i) for i in range(seq_count - 4)]
    below = lax.ppermute(own_pair, "seq", up)
    above = lax.ppermute(own_pair, "seq", down)
    mixed = [(i, j) for i, j in up if i % 4 < 2] + [(i, j) for i, j in down if i % 4 >= 2]
    beside = lax.ppermute(other_pair, "seq", mixed)

    own_text = spread[:, depth:, : 2 * HD]
    core_text = lax.ppermute(
        spread[:, depth:, 2 * HD : 4 * HD], "grp", [(g, g ^ 1) for g in range(2 * CHIPS)]
    )

    def cost(pieces):
        size = 4 * PAIR * pieces * PAIR * 256
        return pl.CostEstimate(flops=size, bytes_accessed=10**6, transcendentals=PAIR * pieces * PAIR)

    total = pl.pallas_call(
        first_keys,
        out_shape=shape((PAIR, 2 * HD), F32),
        in_specs=[VMEM] * 11,
        compiler_params=params(),
        cost_estimate=cost(5),
    )(mask, mine, along_in, near, pair_in, far_in, cross_in, below, above, own_text, core_text)
    attention = pl.pallas_call(
        last_keys,
        out_shape=shape((2 * CHIPS, BLOCK, HD), BF16),
        in_specs=[VMEM] * 5,
        compiler_params=params(),
        cost_estimate=cost(1),
    )(mask, mine, along_in, total, beside)

    groups = [
        [(2 * pair + odd) * 2 * CHIPS + 2 * chip + core for odd in range(2) for chip in range(CHIPS)]
        for pair in range(seq_count // 2)
        for core in range(2)
    ]
    heads = lax.all_to_all(attention, ("seq", "grp"), 0, 0, axis_index_groups=groups)
    kept, sent = pl.pallas_call(
        project,
        out_shape=(shape((BLOCK, width), F32), shape((BLOCK, width), BF16)),
        in_specs=[VMEM] * 4,
        compiler_params=params(),
        cost_estimate=pl.CostEstimate(
            flops=2 * BLOCK * 1024 * 768, bytes_accessed=3 * 10**6, transcendentals=0
        ),
    )(heads, spread, along_in, gate)
    other = lax.ppermute(sent, "grp", [(g, g ^ 1) for g in range(2 * CHIPS)])
    result = (kept + gate * other.astype(F32)).astype(BF16)
    across = [
        (part * seq_count + i, (1 - part) * seq_count + (i ^ 1))
        for part in range(2)
        for i in range(seq_count)
    ]
    handed = lax.ppermute(result, ("section", "seq"), across)
    return handed[None]


def solution(mesh):
    placed = (
        P("section", "seq", "grp"),
        P("section", "seq", "grp"),
        P("section", "seq", "grp"),
        P("section", "seq", "grp"),
        P("section", None, "grp", None),
        P("section"),
        P("section", "grp", None),
        P("section", "grp"),
        P(),
        P(),
    )
    return jax.shard_map(
        body, mesh=mesh, in_specs=placed, out_specs=P("section", "seq", "grp"), check_vma=False
    )
```

time: 142 us -> 82.4 us (0.58)
  Pallas kernels: 61.7 us -> 8.09 us
  starting transfers between devices: 44.2 us -> 41.7 us
  local copies, waits for them, and re-layouts: 3.93 us -> 2.08 us
    pallas_call x1, Pallas kernels: 54.4 us -> 4.79 us  [body(): pl.pallas_call(start_out, out_shape=(shape((CHIPS, depth + slots, 2 * wid...]
    pallas_call x2 -> x1, Pallas kernels: 4.57 us -> 2.11 us  [body(): pl.pallas_call(first_keys, out_shape=shape((PAIR, 2 * HD), F32), in_specs...]
    ppermute x4, waiting for transfers between devices: 2.01 us -> 0.01 us  [swapped(): return lax.ppermute(block, 'seq', [(i, i ^ mask) for i in range(seq_count)])]
    unnamed x26 -> x12, local copies, waits for them, and re-layouts: 3.91 us -> 2.07 us
    pallas_call x1, Pallas kernels: 2.14 us -> 0.6 us  [body(): pl.pallas_call(last_keys, out_shape=shape((2 * CHIPS, BLOCK, HD), BF16),...]
  transfers between devices with their start and end apart: 11 -> 11, of which waited for: 4 -> 4; matrix products, arithmetic and copies ran while one was open for 1% -> 2% of each run, Pallas kernels for 3% -> 3%
where the time goes in v3:
time: 82.4 us; the launch traced here: 81.8 us
  starting transfers between devices  41.7 us (51%)
  blocking collectives  15.4 us (19%)
  waiting for transfers between devices  11.5 us (14%)
  Pallas kernels  8.09 us (10%)
  other arithmetic  2.16 us (3%)
  local copies, waits for them, and re-layouts  2.08 us (3%)
  between operations  0.87 us (1%)
    all_to_all x1, blocking collectives, body(): lax.all_to_all(attention, ('seq', 'grp'), 0, 0, axis_index_groups=groups)  15.4 us
    ppermute x4, starting transfers between devices, swapped(): return lax.ppermute(block, 'seq', [(i, i ^ mask) for i in range(seq_count)])  14.7 us
    ppermute x1, waiting for transfers between devices, body(): handed = lax.ppermute(result, ('section', 'seq'), across)  8.69 us
    ppermute x1, starting transfers between devices, body(): handed = lax.ppermute(result, ('section', 'seq'), across)  7.89 us
    pallas_call x1, Pallas kernels, body(): pl.pallas_call(start_out, out_shape=(shape((CHIPS, depth + slots, 2 * wid...  4.79 us
    ppermute x1, starting transfers between devices, body(): below = lax.ppermute(own_pair, 'seq', up)  4.69 us
    all_to_all x1, starting transfers between devices, body(): spread = lax.all_to_all(spread, 'grp', 0, 0, axis_index_groups=by_core)  4.44 us
    ppermute x1, starting transfers between devices, body(): beside = lax.ppermute(other_pair, 'seq', mixed)  3.76 us
  transfers between devices with their start and end apart: 11, of which 4 were waited for; matrix products, arithmetic and copies ran while one was open for 2% of the time, Pallas kernels for 3%

profile of v3, /device:TPU:24, one launch (start us, length us, event | category | flops | bytes accessed | tf_op | source)
XLA Modules:
  0.0 81.8 jit_solution(5239712601567099233)
XLA Ops:
  0.7 1.4 %copy.11.band = s32[64,2]{1,0:T(8,128)} copy(s32[64,2]{0,1:T(2,128)} %param.18) | data formatting | bytes 1024 | tf_op args[8]
  2.0 0.6 pad_add_fusion.place
  2.7 4.8 %shard_map.100 = (bf16[4,288,768]{2,1,0:T(8,128)(2,1)}, bf16[2,256,128]{2,1,0:T(8,128)(2,1)}, bf16[2,256,128]{2,1,0:T(8,128)(2,1)}, bf16[256,512]{1,0:T(8,128)(2...) custom-call(s32[4]{0:T(128)} %pad_add_fusion.place, s32[64]{0:T(128)} %order.1, s32[64,2]{1,0:T(8,128)} %copy.11.band, ...), custom_call_target="tpu_custom_call" | custom-call | flops 1000000 | bytes 4000000 | tf_op jit(solution)/shard_map/pallas_call | solution.py:211
  7.5 0.0 copy-start.4
  7.5 0.0 copy-start
  7.5 0.0 copy-start.1
  7.5 0.0 copy-start.3
  7.5 4.4 %all-to-all-start = ((bf16[4,288,768]{2,1,0:T(8,128)(2,1)}), bf16[4,288,768]{2,1,0:T(8,128)(2,1)S(1)}, u32[]{:S(2)}, u32[]{:S(2)}) async-start(bf16[4,288,768]{2,1,0:T(8,128)(2,1)} %get-tuple-element.18), calls=%async_computation | async-start | bytes 3538944 | tf_op jit(solution)/shard_map/all_to_all | solution.py:230
  11.9 0.0 copy-done.4
  11.9 4.3 %collective-permute-start.1 = (bf16[2,256,128]{2,1,0:T(8,128)(2,1)S(1)}, bf16[2,256,128]{2,1,0:T(8,128)(2,1)S(1)}, u32[]{:S(2)}, u32[]{:S(2)}) collective-permute-start(bf16[2,256,128]{2,1,0:T(8,128)(2,1)S(1)} %copy-done.4), channel_id=1, source_target_pairs={{0,8},{8,0},{16,24},{24,16},{32,40},{40,32},{48,56},{56,48},{64,72... | collective-permute-start | bytes 393224 | tf_op jit(solution)/shard_map/ppermute | solution.py:233
  16.2 5.5 %collective-permute-start.3 = (bf16[2,256,128]{2,1,0:T(8,128)(2,1)S(1)}, bf16[2,256,128]{2,1,0:T(8,128)(2,1)S(1)}, u32[]{:S(2)}, u32[]{:S(2)}) collective-permute-start(bf16[2,256,128]{2,1,0:T(8,128)(2,1)S(1)} %copy-done.4), channel_id=1, source_target_pairs={{0,24},{8,16},{16,8},{24,0},{32,56},{40,48},{48,40},{56,32},{64,88... | collective-permute-start | bytes 393224 | tf_op jit(solution)/shard_map/ppermute | solution.py:233
  21.8 0.0 copy-done
  21.8 2.5 %collective-permute-start.2 = (bf16[2,256,128]{2,1,0:T(8,128)(2,1)S(1)}, bf16[2,256,128]{2,1,0:T(8,128)(2,1)S(1)}, u32[]{:S(2)}, u32[]{:S(2)}) collective-permute-start(bf16[2,256,128]{2,1,0:T(8,128)(2,1)S(1)} %copy-done), channel_id=1, source_target_pairs={{0,16},{8,24},{16,0},{24,8},{32,48},{40,56},{48,32},{56,40},{64,80... | collective-permute-start | bytes 393224 | tf_op jit(solution)/shard_map/ppermute | solution.py:233
  24.3 2.5 %collective-permute-start = (bf16[256,512]{1,0:T(8,128)(2,1)}, bf16[256,512]{1,0:T(8,128)(2,1)S(1)}, u32[]{:S(2)}, u32[]{:S(2)}) collective-permute-start(bf16[256,512]{1,0:T(8,128)(2,1)} %get-tuple-element.15), channel_id=1, source_target_pairs={{0,8},{8,0},{16,24},{24,16},{32,40},{40,32},{48,56},{56,48},{64,72... | collective-permute-start | bytes 786440 | tf_op jit(solution)/shard_map/ppermute | solution.py:233
  26.7 0.0 collective-permute-done.1.pair_ref
  26.7 0.7 pad_maximum_fusion
  27.5 2.3 %collective-permute-start.5 = (bf16[2,2,256,128]{3,2,1,0:T(8,128)(2,1)}, bf16[2,2,256,128]{3,2,1,0:T(8,128)(2,1)S(1)}, u32[]{:S(2)}, u32[]{:S(2)}) collective-permute-start(bf16[2,2,256,128]{3,2,1,0:T(8,128)(2,1)} %pad_maximum_fusion), channel_id=1, source_target_pairs={{32,0},{40,8},{48,16},{56,24},{64,32},{72,40},{80,48},{88,56},{96,... | collective-permute-start | bytes 786440 | tf_op jit(solution)/shard_map/ppermute | solution.py:245
  29.8 4.7 %collective-permute-start.4 = (bf16[2,2,256,128]{3,2,1,0:T(8,128)(2,1)}, bf16[2,2,256,128]{3,2,1,0:T(8,128)(2,1)S(1)}, u32[]{:S(2)}, u32[]{:S(2)}) collective-permute-start(bf16[2,2,256,128]{3,2,1,0:T(8,128)(2,1)} %pad_maximum_fusion), channel_id=1, source_target_pairs={{0,32},{8,40},{16,48},{24,56},{32,64},{40,72},{48,80},{56,88},{64,... | collective-permute-start | bytes 786440 | tf_op jit(solution)/shard_map/ppermute | solution.py:244
  34.5 0.0 collective-permute-done.3.cross_ref
  34.5 0.0 collective-permute-done.2.far_ref
  34.5 0.7 pad_maximum_fusion.1
  35.3 3.8 %collective-permute-start.7 = (bf16[2,2,256,128]{3,2,1,0:T(8,128)(2,1)}, bf16[2,2,256,128]{3,2,1,0:T(8,128)(2,1)S(1)}, u32[]{:S(2)}, u32[]{:S(2)}) collective-permute-start(bf16[2,2,256,128]{3,2,1,0:T(8,128)(2,1)} %pad_maximum_fusion.1), channel_id=1, source_target_pairs={{0,32},{8,40},{32,64},{40,72},{64,96},{72,104},{96,128},{104,136},... | collective-permute-start | bytes 786440 | tf_op jit(solution)/shard_map/ppermute | solution.py:247
  39.0 0.0 all-to-all-done.weight_ref
  39.1 1.9 %collective-permute-start.6 = (bf16[4,32,256]{2,1,0:T(8,128)(2,1)S(1)}, bf16[4,32,256]{2,1,0:T(8,128)(2,1)S(1)}, u32[]{:S(2)}, u32[]{:S(2)}) collective-permute-start(bf16[4,32,256]{2,1,0:T(8,128)(2,1)S(1)} %get-tuple-element.21), channel_id=1, source_target_pairs={{0,1},{1,0},{2,3},{3,2},{4,5},{5,4},{6,7},{7,6},{8,9},{9,8},{10,11... | collective-permute-start | bytes 196616 | tf_op jit(solution)/shard_map/ppermute | solution.py:250
  41.0 0.0 collective-permute-done.along_ref
  41.0 0.0 collective-permute-done.5.above_ref
  41.0 0.0 collective-permute-done.4.below_ref
  41.0 1.2 %collective-permute-done.6.core_text = bf16[4,32,256]{2,1,0:T(8,128)(2,1)S(1)} collective-permute-done((bf16[4,32,256]{2,1,0:T(8,128)(2,1)S(1)}, bf16[4,32,256]{2,1,0:T(8,128)(2,1)S(1)}, u32[]{:S(2)}, u32[]{:S(2)}) %collective-permute-start.6) | collective-permute-done | bytes 65568 | tf_op jit(solution)/shard_map/ppermute | solution.py:250
  42.2 0.0 copy-done.1
  42.2 0.0 copy-done.3
  42.2 2.1 %shard_map.101.sum_ref = f32[512,256]{1,0:T(8,128)S(1)} custom-call(f32[8,128]{1,0:T(8,128)S(1)} %copy-done.3, bf16[256,128]{1,0:T(8,128)(2,1)S(1)} %copy-done.1, bf16[256,512]{1,0:T(8,128)(2,1)S(1)} %collective-permute-done.along_ref, bf16[2,256,128]{2,1,0:T(8,128)(2,1)S(1)} %copy-done, bf16[2,256,128]{2,1,0:T(8,128)(2,1)S(1)} %collective-permute-done.1.pair_ref, ...), custom_call_target="tpu_custom_call" | custom-call | flops 1342177280 | bytes 1000000 | tf_op jit(solution)/shard_map/pallas_call | solution.py:258
  44.3 0.0 copy-start.2
  44.3 0.3 collective-permute-done.7.beside_ref
  44.6 0.6 shard_map.102
  45.2 15.4 %all_to_all.10.heads_ref = bf16[8,256,128]{2,1,0:T(8,128)(2,1)S(1)} all-to-all(bf16[8,256,128]{2,1,0:T(8,128)(2,1)S(1)} %shard_map.102), channel_id=1, replica_groups={{0,2,4,6,8,10,12,14},{1,3,5,7,9,11,13,15},{16,18,20,22,24,26,28,30},{17..., dimensions={0} | all-to-all | bytes 1048576 | tf_op jit(solution)/shard_map/all_to_all | solution.py:278
  60.6 0.0 copy-done.2
  60.6 0.6 shard_map.103
  61.2 1.9 %collective-permute-start.8 = (bf16[256,384]{1,0:T(8,128)(2,1)S(1)}, bf16[256,384]{1,0:T(8,128)(2,1)S(1)}, u32[]{:S(2)}, u32[]{:S(2)}) collective-permute-start(bf16[256,384]{1,0:T(8,128)(2,1)S(1)} %get-tuple-element.20), channel_id=1, source_target_pairs={{0,1},{1,0},{2,3},{3,2},{4,5},{5,4},{6,7},{7,6},{8,9},{9,8},{10,11... | collective-permute-start | bytes 589832 | tf_op jit(solution)/shard_map/ppermute | solution.py:288
  63.1 1.4 %collective-permute-done.8 = bf16[256,384]{1,0:T(8,128)(2,1)S(1)} collective-permute-done((bf16[256,384]{1,0:T(8,128)(2,1)S(1)}, bf16[256,384]{1,0:T(8,128)(2,1)S(1)}, u32[]{:S(2)}, u32[]{:S(2)}) %collective-permute-start.8) | collective-permute-done | bytes 196640 | tf_op jit(solution)/shard_map/ppermute | solution.py:288
  64.5 0.1 add_convert_fusion
  64.6 7.9 %collective-permute-start.9 = (bf16[256,384]{1,0:T(8,128)(2,1)S(1)}, bf16[256,384]{1,0:T(8,128)(2,1)S(1)}, u32[]{:S(2)}, u32[]{:S(2)}) collective-permute-start(bf16[256,384]{1,0:T(8,128)(2,1)S(1)} %add_convert_fusion), channel_id=1, source_target_pairs={{0,264},{8,256},{16,280},{24,272},{32,296},{40,288},{48,312},{56,3... | collective-permute-start | bytes 589832 | tf_op jit(solution)/shard_map/ppermute | solution.py:295
  72.5 8.7 %collective-permute-done.9 = bf16[256,384]{1,0:T(8,128)(2,1)S(1)} collective-permute-done((bf16[256,384]{1,0:T(8,128)(2,1)S(1)}, bf16[256,384]{1,0:T(8,128)(2,1)S(1)}, u32[]{:S(2)}, u32[]{:S(2)}) %collective-permute-start.9) | collective-permute-done | bytes 196640 | tf_op jit(solution)/shard_map/ppermute | solution.py:295
  81.1 0.7 copy.14
  (2 shorter events, 0.0 us)
Async XLA Ops:
  7.5 4.5 %copy-start.4 = (bf16[2,256,128]{2,1,0:T(8,128)(2,1)S(1)}, bf16[2,256,128]{2,1,0:T(8,128)(2,1)}, u32[]{:S(2)}) copy-start(bf16[2,256,128]{2,1,0:T(8,128)(2,1)} %get-tuple-element.17) | copy-start | bytes 393220
  7.5 14.3 %copy-start = (bf16[2,256,128]{2,1,0:T(8,128)(2,1)S(1)}, bf16[2,256,128]{2,1,0:T(8,128)(2,1)}, u32[]{:S(2)}) copy-start(bf16[2,256,128]{2,1,0:T(8,128)(2,1)} %get-tuple-element.16.near_ref) | copy-start | bytes 393220
  7.5 34.7 %copy-start.1 = (bf16[256,128]{1,0:T(8,128)(2,1)S(1)}, bf16[256,128]{1,0:T(8,128)(2,1)}, u32[]{:S(2)}) copy-start(bf16[256,128]{1,0:T(8,128)(2,1)} %get-tuple-element.14.mine_ref) | copy-start | bytes 196612
  7.5 34.7 %copy-start.3 = (f32[8,128]{1,0:T(8,128)S(1)}, f32[8,128]{1,0:T(8,128)}, u32[]{:S(2)}) copy-start(f32[8,128]{1,0:T(8,128)} %get-tuple-element.13.mask_ref) | copy-start | bytes 12292
  7.5 31.5 %all-to-all-start = ((bf16[4,288,768]{2,1,0:T(8,128)(2,1)}), bf16[4,288,768]{2,1,0:T(8,128)(2,1)S(1)}, u32[]{:S(2)}, u32[]{:S(2)}) async-start(bf16[4,288,768]{2,1,0:T(8,128)(2,1)} %get-tuple-element.18), calls=%async_computation | async-start | bytes 3538944 | tf_op jit(solution)/shard_map/all_to_all | solution.py:230
  11.9 14.8 %collective-permute-start.1 = (bf16[2,256,128]{2,1,0:T(8,128)(2,1)S(1)}, bf16[2,256,128]{2,1,0:T(8,128)(2,1)S(1)}, u32[]{:S(2)}, u32[]{:S(2)}) collective-permute-start(bf16[2,256,128]{2,1,0:T(8,128)(2,1)S(1)} %copy-done.4), channel_id=1, source_target_pairs={{0,8},{8,0},{16,24},{24,16},{32,40},{40,32},{48,56},{56,48},{64,72... | collective-permute-start | bytes 393224 | tf_op jit(solution)/shard_map/ppermute | solution.py:233
  16.2 18.3 %collective-permute-start.3 = (bf16[2,256,128]{2,1,0:T(8,128)(2,1)S(1)}, bf16[2,256,128]{2,1,0:T(8,128)(2,1)S(1)}, u32[]{:S(2)}, u32[]{:S(2)}) collective-permute-start(bf16[2,256,128]{2,1,0:T(8,128)(2,1)S(1)} %copy-done.4), channel_id=1, source_target_pairs={{0,24},{8,16},{16,8},{24,0},{32,56},{40,48},{48,40},{56,32},{64,88... | collective-permute-start | bytes 393224 | tf_op jit(solution)/shard_map/ppermute | solution.py:233
  21.8 12.8 %collective-permute-start.2 = (bf16[2,256,128]{2,1,0:T(8,128)(2,1)S(1)}, bf16[2,256,128]{2,1,0:T(8,128)(2,1)S(1)}, u32[]{:S(2)}, u32[]{:S(2)}) collective-permute-start(bf16[2,256,128]{2,1,0:T(8,128)(2,1)S(1)} %copy-done), channel_id=1, source_target_pairs={{0,16},{8,24},{16,0},{24,8},{32,48},{40,56},{48,32},{56,40},{64,80... | collective-permute-start | bytes 393224 | tf_op jit(solution)/shard_map/ppermute | solution.py:233
  24.3 16.7 %collective-permute-start = (bf16[256,512]{1,0:T(8,128)(2,1)}, bf16[256,512]{1,0:T(8,128)(2,1)S(1)}, u32[]{:S(2)}, u32[]{:S(2)}) collective-permute-start(bf16[256,512]{1,0:T(8,128)(2,1)} %get-tuple-element.15), channel_id=1, source_target_pairs={{0,8},{8,0},{16,24},{24,16},{32,40},{40,32},{48,56},{56,48},{64,72... | collective-permute-start | bytes 786440 | tf_op jit(solution)/shard_map/ppermute | solution.py:233
  27.5 13.5 %collective-permute-start.5 = (bf16[2,2,256,128]{3,2,1,0:T(8,128)(2,1)}, bf16[2,2,256,128]{3,2,1,0:T(8,128)(2,1)S(1)}, u32[]{:S(2)}, u32[]{:S(2)}) collective-permute-start(bf16[2,2,256,128]{3,2,1,0:T(8,128)(2,1)} %pad_maximum_fusion), channel_id=1, source_target_pairs={{32,0},{40,8},{48,16},{56,24},{64,32},{72,40},{80,48},{88,56},{96,... | collective-permute-start | bytes 786440 | tf_op jit(solution)/shard_map/ppermute | solution.py:245
  29.8 11.2 %collective-permute-start.4 = (bf16[2,2,256,128]{3,2,1,0:T(8,128)(2,1)}, bf16[2,2,256,128]{3,2,1,0:T(8,128)(2,1)S(1)}, u32[]{:S(2)}, u32[]{:S(2)}) collective-permute-start(bf16[2,2,256,128]{3,2,1,0:T(8,128)(2,1)} %pad_maximum_fusion), channel_id=1, source_target_pairs={{0,32},{8,40},{16,48},{24,56},{32,64},{40,72},{48,80},{56,88},{64,... | collective-permute-start | bytes 786440 | tf_op jit(solution)/shard_map/ppermute | solution.py:244
  35.3 9.3 %collective-permute-start.7 = (bf16[2,2,256,128]{3,2,1,0:T(8,128)(2,1)}, bf16[2,2,256,128]{3,2,1,0:T(8,128)(2,1)S(1)}, u32[]{:S(2)}, u32[]{:S(2)}) collective-permute-start(bf16[2,2,256,128]{3,2,1,0:T(8,128)(2,1)} %pad_maximum_fusion.1), channel_id=1, source_target_pairs={{0,32},{8,40},{32,64},{40,72},{64,96},{72,104},{96,128},{104,136},... | collective-permute-start | bytes 786440 | tf_op jit(solution)/shard_map/ppermute | solution.py:247
  39.1 3.1 %collective-permute-start.6 = (bf16[4,32,256]{2,1,0:T(8,128)(2,1)S(1)}, bf16[4,32,256]{2,1,0:T(8,128)(2,1)S(1)}, u32[]{:S(2)}, u32[]{:S(2)}) collective-permute-start(bf16[4,32,256]{2,1,0:T(8,128)(2,1)S(1)} %get-tuple-element.21), channel_id=1, source_target_pairs={{0,1},{1,0},{2,3},{3,2},{4,5},{5,4},{6,7},{7,6},{8,9},{9,8},{10,11... | collective-permute-start | bytes 196616 | tf_op jit(solution)/shard_map/ppermute | solution.py:250
  44.3 16.2 %copy-start.2 = (f32[1,384]{1,0:T(1,128)S(1)}, f32[1,384]{1,0:T(1,128)}, u32[]{:S(2)}) copy-start(f32[1,384]{1,0:T(1,128)} %gate_ref.1) | copy-start | bytes 4612
  61.2 3.3 %collective-permute-start.8 = (bf16[256,384]{1,0:T(8,128)(2,1)S(1)}, bf16[256,384]{1,0:T(8,128)(2,1)S(1)}, u32[]{:S(2)}, u32[]{:S(2)}) collective-permute-start(bf16[256,384]{1,0:T(8,128)(2,1)S(1)} %get-tuple-element.20), channel_id=1, source_target_pairs={{0,1},{1,0},{2,3},{3,2},{4,5},{5,4},{6,7},{7,6},{8,9},{9,8},{10,11... | collective-permute-start | bytes 589832 | tf_op jit(solution)/shard_map/ppermute | solution.py:288
  64.6 16.6 %collective-permute-start.9 = (bf16[256,384]{1,0:T(8,128)(2,1)S(1)}, bf16[256,384]{1,0:T(8,128)(2,1)S(1)}, u32[]{:S(2)}, u32[]{:S(2)}) collective-permute-start(bf16[256,384]{1,0:T(8,128)(2,1)S(1)} %add_convert_fusion), channel_id=1, source_target_pairs={{0,264},{8,256},{16,280},{24,272},{32,296},{40,288},{48,312},{56,3... | collective-permute-start | bytes 589832 | tf_op jit(solution)/shard_map/ppermute | solution.py:295

commit v4 on v3

--- a/solution.py
+++ b/solution.py
@@ -34,58 +34,73 @@
 
 
 def start_out(
-    place, order, band, count, q_ref, k_ref, v_ref, r_ref, w_ref, t_ref,
-    spread_ref, near_ref, cross_ref, along_ref, mine_ref, mask_ref,
-    q_in, k_in, v_in, sems, w_sems,
+    pair, odd, chip, core, order, band, count, q_ref, k_ref, v_ref, w_ref, t_ref,
+    spread_ref, near_ref, cross_ref, mine_ref, other_ref, mask_ref,
+    q_in, k_in, v_in, stage, near, cross, mine, other, mask, sems, stage_sems, out_sems,
 ):
-    odd, core = place[1], place[3]
+    odd, core = odd[0], core[0]
     depth, width = w_ref.shape[1], w_ref.shape[2] // (2 * CHIPS)
     slots = t_ref.shape[2]
     loads = [
         pltpu.make_async_copy(source.at[0], target, sems.at[i])
-        for i, (source, target) in enumerate((
-            (k_ref, k_in), (v_ref, v_in), (q_ref, q_in), (r_ref, along_ref.at[:, pl.ds(0, width)])
-        ))
+        for i, (source, target) in enumerate(((k_ref, k_in), (v_ref, v_in), (q_ref, q_in)))
     ]
-    copies = []
+    staged = []
     for target in range(CHIPS):
+        parts = []
         for half in range(2):
             side = target * 2 + (core if half == 0 else 1 - core)
             columns = pl.ds(pl.multiple_of(side * width, 128), width)
-            copies.append((
+            parts.append((
                 w_ref.at[0, :, columns],
-                spread_ref.at[target, pl.ds(0, depth), pl.ds(half * width, width)],
+                stage.at[target, pl.ds(0, depth), pl.ds(half * width, width)],
             ))
             columns = pl.ds(pl.multiple_of((side * 2 + odd) * HD, 128), HD)
             for kind in range(2):
-                copies.append((
+                parts.append((
                     t_ref.at[0, kind, :, columns],
-                    spread_ref.at[target, pl.ds(depth, slots), pl.ds((2 * half + kind) * HD, HD)],
+                    stage.at[target, pl.ds(depth, slots), pl.ds((2 * half + kind) * HD, HD)],
                 ))
-    copies = [
-        pltpu.make_async_copy(source, target, w_sems.at[i])
-        for i, (source, target) in enumerate(copies)
-    ]
-    for copy in loads + copies:
-        copy.start()
-    spread_ref[:, depth:, 4 * HD :] = jnp.zeros((CHIPS, slots, 2 * width - 4 * HD), BF16)
-    mask_ref[...] = mask_rows(place, order, band, count)
+        staged.append([
+            pltpu.make_async_copy(source, to, stage_sems.at[target, i])
+            for i, (source, to) in enumerate(parts)
+        ])
+    for load in loads:
+        load.start()
+    for parts in staged:
+        for part in parts:
+            part.start()
+    stage[:, depth:, 4 * HD :] = jnp.zeros((CHIPS, slots, 2 * width - 4 * HD), BF16)
+    sent = []
+
+    def send(source, target):
+        sent.append(pltpu.make_async_copy(source, target, out_sems.at[len(sent)]))
+        sent[-1].start()
+
+    mask[...] = mask_rows(pair[0], odd, core, order, band, count)
+    send(mask, mask_ref)
 
     def halves(load, ref, prepare):
         load.wait()
         a, b = prepare(ref[:, :HD]), prepare(ref[:, HD:])
         return jnp.where(odd == 0, a, b), jnp.where(odd == 0, b, a)
 
-    near_ref[0], cross_ref[0] = halves(loads[0], k_in, normed)
-    near_ref[1], cross_ref[1] = halves(loads[1], v_in, lambda x: x)
-    mine_ref[...], along_ref[:, width:] = halves(loads[2], q_in, normed)
-    loads[3].wait()
-    for copy in copies:
+    near[0], cross[0] = halves(loads[0], k_in, normed)
+    near[1], cross[1] = halves(loads[1], v_in, lambda x: x)
+    send(near, near_ref)
+    send(cross, cross_ref)
+    mine[...], other[...] = halves(loads[2], q_in, normed)
+    send(mine, mine_ref)
+    send(other, other_ref)
+    for target, parts in enumerate(staged):
+        for part in parts:
+            part.wait()
+        send(stage.at[target], spread_ref.at[target])
+    for copy in sent:
         copy.wait()
 
 
-def mask_rows(place, order, band, count):
-    own, odd = place[0], place[1]
+def mask_rows(own, odd, core, order, band, count):
     total = order.shape[0] // 4
 
     def tile_at(pair, slot):
@@ -97,8 +112,8 @@
     high = jnp.zeros((8, HD), jnp.int32)
     for slot in range(4):
         tile = tile_at(own, slot)
-        low = jnp.where(row == slot, band[tile, 0], low)
-        high = jnp.where(row == slot, band[tile, 1], high)
+        low = jnp.where(row == slot, band[0, tile], low)
+        high = jnp.where(row == slot, band[1, tile], high)
     held = jnp.full((8, HD), -1, jnp.int32)
     beside = own - 1 + 2 * lax.rem(own, 2)
     for piece, pair in enumerate((own, own ^ 1, own - 2, own + 2, beside)):
@@ -109,13 +124,13 @@
             held = jnp.where(lane == 4 * piece + slot, tile, held)
     seen = (held >= low) & (held <= high)
     result = jnp.where((lane <= TEXT_LANE) & jnp.logical_not(seen), F32(FAR), F32(0.0))
-    for at, value in ((COUNT_LANE, count[0]), (ODD_LANE, odd), (CORE_LANE, place[3])):
+    for at, value in ((COUNT_LANE, count[0]), (ODD_LANE, odd), (CORE_LANE, core)):
         result = jnp.where(lane == at, value.astype(F32), result)
     return result
 
 
-def masked_query(mask_ref, mine_ref, along_ref):
-    query = jnp.concatenate([mine_ref[...], along_ref[:, along_ref.shape[1] - HD :]], axis=0)
+def masked_query(mask_ref, mine_ref, query_ref):
+    query = jnp.concatenate([mine_ref[...], query_ref[...]], axis=0)
     lane = lax.broadcasted_iota(jnp.int32, (TILE, HD), 1)
     lanes = [
         jnp.where(lane <= TEXT_LANE, mask_ref[slot : slot + 1, :], F32(0.0)).astype(BF16)
@@ -162,10 +177,10 @@
 
 
 def first_keys(
-    mask_ref, mine_ref, along_ref, near_ref, pair_ref, far_ref, cross_ref, below_ref, above_ref,
+    mask_ref, mine_ref, query_ref, near_ref, pair_ref, far_ref, cross_ref, below_ref, above_ref,
     own_text, core_text, total_ref,
 ):
-    query = masked_query(mask_ref, mine_ref, along_ref)
+    query = masked_query(mask_ref, mine_ref, query_ref)
     total = add_keys(None, query, *piece_arrays(0, near_ref, pair_ref))
     total = add_keys(total, query, *piece_arrays(1, far_ref, cross_ref))
     total = add_keys(total, query, *piece_arrays(2, below_ref.at[0], below_ref.at[1]))
@@ -174,8 +189,8 @@
     total_ref[...] = add_keys(total, query, *text_arrays(mask_ref, core_text, True))
 
 
-def last_keys(mask_ref, mine_ref, along_ref, sum_ref, beside_ref, out_ref):
-    query = masked_query(mask_ref, mine_ref, along_ref)
+def last_keys(mask_ref, mine_ref, query_ref, sum_ref, beside_ref, out_ref):
+    query = masked_query(mask_ref, mine_ref, query_ref)
     pieces = piece_arrays(PIECES - 1, beside_ref.at[0], beside_ref.at[1])
     total = add_keys(sum_ref[...], query, *pieces)
     result = total[:, :HD] / total[:, HD:]
@@ -188,14 +203,14 @@
         out_ref[CHIPS + chip] = to_odd
 
 
-def project(heads_ref, weight_ref, along_ref, gate_ref, kept_ref, sent_ref):
+def project(heads_ref, weight_ref, rows_ref, gate_ref, kept_ref, sent_ref):
     total = None
     depth, width = 2 * HD, kept_ref.shape[1]
     for chip in range(CHIPS):
         heads = jnp.concatenate([heads_ref[chip], heads_ref[CHIPS + chip]], axis=1)
         part = jnp.dot(heads, weight_ref[chip, :depth], preferred_element_type=F32)
         total = part if total is None else total + part
-    kept_ref[...] = along_ref[:, :width].astype(F32) + gate_ref[...] * total[:, :width]
+    kept_ref[...] = rows_ref[...].astype(F32) + gate_ref[...] * total[:, :width]
     sent_ref[...] = total[:, width:].astype(BF16)
 
 
@@ -203,28 +218,26 @@
     seq_count = lax.axis_size("seq")
     seq = lax.axis_index("seq")
     grp = lax.axis_index("grp")
-    place = jnp.stack([seq >> 1, seq & 1, grp >> 1, grp & 1]).astype(jnp.int32)
+    place = [at.astype(jnp.int32).reshape(1) for at in (seq >> 1, seq & 1, grp >> 1, grp & 1)]
     shape = jax.ShapeDtypeStruct
     width = gate.shape[1]
     depth, slots = out_weight.shape[1], text_kv.shape[2]
 
-    spread, near, cross_out, along, mine, mask = pl.pallas_call(
+    spread_shape = (CHIPS, depth + slots, 2 * width)
+    token_shapes = [(2, BLOCK, HD)] * 2 + [(BLOCK, HD)] * 2
+    spread, near, cross_out, mine, query_out, mask = pl.pallas_call(
         start_out,
-        out_shape=(
-            shape((CHIPS, depth + slots, 2 * width), BF16),
-            shape((2, BLOCK, HD), BF16),
-            shape((2, BLOCK, HD), BF16),
-            shape((BLOCK, width + HD), BF16),
-            shape((BLOCK, HD), BF16),
-            shape((8, HD), F32),
-        ),
-        in_specs=[SMEM] * 4 + [HBM] * 6,
-        out_specs=(VMEM,) * 6,
+        out_shape=[shape(dims, BF16) for dims in [spread_shape, *token_shapes]]
+        + [shape((8, HD), F32)],
+        in_specs=[SMEM] * 7 + [HBM] * 5,
+        out_specs=[HBM] * 6,
         scratch_shapes=[pltpu.VMEM((BLOCK, 2 * HD), BF16)] * 3
-        + [pltpu.SemaphoreType.DMA((4,)), pltpu.SemaphoreType.DMA((6 * CHIPS,))],
+        + [pltpu.VMEM(dims, BF16) for dims in [spread_shape, *token_shapes]]
+        + [pltpu.VMEM((8, HD), F32)]
+        + [pltpu.SemaphoreType.DMA(dims) for dims in ((3,), (CHIPS, 6), (5 + CHIPS,))],
         compiler_params=params(60),
         cost_estimate=pl.CostEstimate(flops=10**6, bytes_accessed=4 * 10**6, transcendentals=0),
-    )(place, tile_order, band, text_count, queries, keys, values, rows, out_weight, text_kv)
+    )(*place, tile_order, band.T, text_count, queries, keys, values, out_weight, text_kv)
 
     by_core = [[2 * chip + core for chip in range(CHIPS)] for core in range(2)]
     spread = lax.all_to_all(spread, "grp", 0, 0, axis_index_groups=by_core)
@@ -235,10 +248,11 @@
     pair_in = swapped(cross_out, 1)
     far_in = swapped(near, 2)
     cross_in = swapped(cross_out, 3)
-    along_in = swapped(along, 1)
 
     own_pair = jnp.stack([near, pair_in])
     other_pair = jnp.stack([far_in, cross_in])
+    other_pair, query_out = lax.optimization_barrier((other_pair, query_out))
+    query_in = swapped(query_out, 1)
     up = [(i, i + 4) for i in range(seq_count - 4)]
     down = [(i + 4, i) for i in range(seq_count - 4)]
     below = lax.ppermute(own_pair, "seq", up)
@@ -261,14 +275,16 @@
         in_specs=[VMEM] * 11,
         compiler_params=params(),
         cost_estimate=cost(5),
-    )(mask, mine, along_in, near, pair_in, far_in, cross_in, below, above, own_text, core_text)
+    )(mask, mine, query_in, near, pair_in, far_in, cross_in, below, above, own_text, core_text)
+    total, rows_out = lax.optimization_barrier((total, rows[0]))
+    rows_in = swapped(rows_out, 1)
     attention = pl.pallas_call(
         last_keys,
         out_shape=shape((2 * CHIPS, BLOCK, HD), BF16),
         in_specs=[VMEM] * 5,
         compiler_params=params(),
         cost_estimate=cost(1),
-    )(mask, mine, along_in, total, beside)
+    )(mask, mine, query_in, total, beside)
 
     groups = [
         [(2 * pair + odd) * 2 * CHIPS + 2 * chip + core for odd in range(2) for chip in range(CHIPS)]
@@ -284,7 +300,7 @@
         cost_estimate=pl.CostEstimate(
             flops=2 * BLOCK * 1024 * 768, bytes_accessed=3 * 10**6, transcendentals=0
         ),
-    )(heads, spread, along_in, gate)
+    )(heads, spread, rows_in, gate)
     other = lax.ppermute(sent, "grp", [(g, g ^ 1) for g in range(2 * CHIPS)])
     result = (kept + gate * other.astype(F32)).astype(BF16)
     across = [

time: 82.4 us -> 83.7 us (1.016)
  the two profiles are of different devices: /device:TPU:24 before, /device:TPU:26 now
where the time goes in v4:
time: 83.7 us; the launch traced here: 83.1 us
  starting transfers between devices  51.8 us (62%)
  waiting for transfers between devices  20.5 us (24%)
  Pallas kernels  8.35 us (10%)
  between operations  0.9 us (1%)
  other arithmetic  0.86 us (1%)
    ppermute x5, starting transfers between devices, swapped(): return lax.ppermute(block, 'seq', [(i, i ^ mask) for i in range(seq_count)])  17.6 us
    ppermute x5, waiting for transfers between devices, swapped(): return lax.ppermute(block, 'seq', [(i, i ^ mask) for i in range(seq_count)])  9.75 us
    ppermute x1, waiting for transfers between devices, body(): handed = lax.ppermute(result, ('section', 'seq'), across)  8.15 us
    ppermute x1, starting transfers between devices, body(): handed = lax.ppermute(result, ('section', 'seq'), across)  7.47 us
    all_to_all x1, starting transfers between devices, body(): lax.all_to_all(attention, ('seq', 'grp'), 0, 0, axis_index_groups=groups)  6.25 us
    all_to_all x1, starting transfers between devices, body(): spread = lax.all_to_all(spread, 'grp', 0, 0, axis_index_groups=by_core)  4.97 us
    ppermute x1, starting transfers between devices, body(): beside = lax.ppermute(other_pair, 'seq', mixed)  4.7 us
    ppermute x1, starting transfers between devices, body(): below = lax.ppermute(own_pair, 'seq', up)  4.69 us
  transfers between devices with their start and end apart: 13, of which 5 were waited for; matrix products, arithmetic and copies ran while one was open for 1% of the time, Pallas kernels for 3%

profile of v4, /device:TPU:26, one launch (start us, length us, event | category | flops | bytes accessed | tf_op | source)
XLA Modules:
  0.0 83.1 jit_solution(7604948006937544826)
XLA Ops:
  0.7 4.2 %shard_map.100 = (bf16[4,288,768]{2,1,0:T(8,128)(2,1)}, bf16[2,256,128]{2,1,0:T(8,128)(2,1)}, bf16[2,256,128]{2,1,0:T(8,128)(2,1)}, bf16[256,128]{1,0:T(8,128)(2...) custom-call(s32[1]{0:T(128)} %bitcast.pair, s32[1]{0:T(128)} %bitcast.1.odd, s32[1]{0:T(128)} %bitcast.2.chip, ...), custom_call_target="tpu_custom_call" | custom-call | flops 1000000 | bytes 4000000 | tf_op jit(solution)/shard_map/pallas_call | solution.py:228
  4.9 0.0 copy-start.4
  4.9 0.0 copy-start
  4.9 0.0 copy-start.5
  4.9 0.0 copy-start.1
  4.9 0.0 copy-start.3
  5.0 5.0 %all-to-all-start = ((bf16[4,288,768]{2,1,0:T(8,128)(2,1)}), bf16[4,288,768]{2,1,0:T(8,128)(2,1)S(1)}, u32[]{:S(2)}, u32[]{:S(2)}) async-start(bf16[4,288,768]{2,1,0:T(8,128)(2,1)} %get-tuple-element.23), calls=%async_computation | async-start | bytes 3538944 | tf_op jit(solution)/shard_map/all_to_all | solution.py:243
  9.9 0.0 copy-done.4
  9.9 4.3 %collective-permute-start.3 = (bf16[2,256,128]{2,1,0:T(8,128)(2,1)S(1)}, bf16[2,256,128]{2,1,0:T(8,128)(2,1)S(1)}, u32[]{:S(2)}, u32[]{:S(2)}) collective-permute-start(bf16[2,256,128]{2,1,0:T(8,128)(2,1)S(1)} %copy-done.4), channel_id=1, source_target_pairs={{0,8},{8,0},{16,24},{24,16},{32,40},{40,32},{48,56},{56,48},{64,72... | collective-permute-start | bytes 393224 | tf_op jit(solution)/shard_map/ppermute | solution.py:246
  14.2 5.5 %collective-permute-start.1 = (bf16[2,256,128]{2,1,0:T(8,128)(2,1)S(1)}, bf16[2,256,128]{2,1,0:T(8,128)(2,1)S(1)}, u32[]{:S(2)}, u32[]{:S(2)}) collective-permute-start(bf16[2,256,128]{2,1,0:T(8,128)(2,1)S(1)} %copy-done.4), channel_id=1, source_target_pairs={{0,24},{8,16},{16,8},{24,0},{32,56},{40,48},{48,40},{56,32},{64,88... | collective-permute-start | bytes 393224 | tf_op jit(solution)/shard_map/ppermute | solution.py:246
  19.7 0.0 copy-done
  19.8 2.5 %collective-permute-start = (bf16[2,256,128]{2,1,0:T(8,128)(2,1)S(1)}, bf16[2,256,128]{2,1,0:T(8,128)(2,1)S(1)}, u32[]{:S(2)}, u32[]{:S(2)}) collective-permute-start(bf16[2,256,128]{2,1,0:T(8,128)(2,1)S(1)} %copy-done), channel_id=1, source_target_pairs={{0,16},{8,24},{16,0},{24,8},{32,48},{40,56},{48,32},{56,40},{64,80... | collective-permute-start | bytes 393224 | tf_op jit(solution)/shard_map/ppermute | solution.py:246
  22.2 0.0 collective-permute-done.3.pair_ref
  22.2 0.8 pad_maximum_fusion.1
  23.0 2.3 %collective-permute-start.5 = (bf16[2,2,256,128]{3,2,1,0:T(8,128)(2,1)}, bf16[2,2,256,128]{3,2,1,0:T(8,128)(2,1)S(1)}, u32[]{:S(2)}, u32[]{:S(2)}) collective-permute-start(bf16[2,2,256,128]{3,2,1,0:T(8,128)(2,1)} %pad_maximum_fusion.1), channel_id=1, source_target_pairs={{32,0},{40,8},{48,16},{56,24},{64,32},{72,40},{80,48},{88,56},{96,... | collective-permute-start | bytes 786440 | tf_op jit(solution)/shard_map/ppermute | solution.py:259
  25.4 4.7 %collective-permute-start.4 = (bf16[2,2,256,128]{3,2,1,0:T(8,128)(2,1)}, bf16[2,2,256,128]{3,2,1,0:T(8,128)(2,1)S(1)}, u32[]{:S(2)}, u32[]{:S(2)}) collective-permute-start(bf16[2,2,256,128]{3,2,1,0:T(8,128)(2,1)} %pad_maximum_fusion.1), channel_id=1, source_target_pairs={{0,32},{8,40},{16,48},{24,56},{32,64},{40,72},{48,80},{56,88},{64,... | collective-permute-start | bytes 786440 | tf_op jit(solution)/shard_map/ppermute | solution.py:258
  30.1 0.0 collective-permute-done.1.cross_ref
  30.1 1.1 %collective-permute-done.far_ref = bf16[2,256,128]{2,1,0:T(8,128)(2,1)S(1)} collective-permute-done((bf16[2,256,128]{2,1,0:T(8,128)(2,1)S(1)}, bf16[2,256,128]{2,1,0:T(8,128)(2,1)S(1)}, u32[]{:S(2)}, u32[]{:S(2)}) %collective-permute-start) | collective-permute-done | bytes 131104 | tf_op jit(solution)/shard_map/ppermute | solution.py:246
  31.2 0.0 copy-done.5
  31.2 1.9 %collective-permute-start.2 = (bf16[256,128]{1,0:T(8,128)(2,1)S(1)}, bf16[256,128]{1,0:T(8,128)(2,1)S(1)}, u32[]{:S(2)}, u32[]{:S(2)}) collective-permute-start(bf16[256,128]{1,0:T(8,128)(2,1)S(1)} %copy-done.5), channel_id=1, source_target_pairs={{0,8},{8,0},{16,24},{24,16},{32,40},{40,32},{48,56},{56,48},{64,72... | collective-permute-start | bytes 196616 | tf_op jit(solution)/shard_map/ppermute | solution.py:246
  33.2 4.7 %collective-permute-start.7 = (bf16[2,2,256,128]{3,2,1,0:T(8,128)(2,1)S(1)}, bf16[2,2,256,128]{3,2,1,0:T(8,128)(2,1)S(1)}, u32[]{:S(2)}, u32[]{:S(2)}) collective-permute-start(bf16[2,2,256,128]{3,2,1,0:T(8,128)(2,1)S(1)} %pad_maximum_fusion), channel_id=1, source_target_pairs={{0,32},{8,40},{32,64},{40,72},{64,96},{72,104},{96,128},{104,136},... | collective-permute-start | bytes 786440 | tf_op jit(solution)/shard_map/ppermute | solution.py:261
  37.9 0.0 all-to-all-done.weight_ref
  37.9 1.9 %collective-permute-start.6 = (bf16[4,32,256]{2,1,0:T(8,128)(2,1)S(1)}, bf16[4,32,256]{2,1,0:T(8,128)(2,1)S(1)}, u32[]{:S(2)}, u32[]{:S(2)}) collective-permute-start(bf16[4,32,256]{2,1,0:T(8,128)(2,1)S(1)} %get-tuple-element.29), channel_id=1, source_target_pairs={{0,1},{1,0},{2,3},{3,2},{4,5},{5,4},{6,7},{7,6},{8,9},{9,8},{10,11... | collective-permute-start | bytes 196616 | tf_op jit(solution)/shard_map/ppermute | solution.py:264
  39.8 0.0 collective-permute-done.2.query_ref
  39.8 0.0 collective-permute-done.5.above_ref
  39.8 0.0 collective-permute-done.4.below_ref
  39.9 1.2 %collective-permute-done.6.core_text = bf16[4,32,256]{2,1,0:T(8,128)(2,1)S(1)} collective-permute-done((bf16[4,32,256]{2,1,0:T(8,128)(2,1)S(1)}, bf16[4,32,256]{2,1,0:T(8,128)(2,1)S(1)}, u32[]{:S(2)}, u32[]{:S(2)}) %collective-permute-start.6) | collective-permute-done | bytes 65568 | tf_op jit(solution)/shard_map/ppermute | solution.py:264
  41.0 0.0 copy-done.1
  41.0 0.0 copy-done.3
  41.1 2.1 %shard_map.101.sum_ref = f32[512,256]{1,0:T(8,128)S(1)} custom-call(f32[8,128]{1,0:T(8,128)S(1)} %copy-done.3, bf16[256,128]{1,0:T(8,128)(2,1)S(1)} %copy-done.1, bf16[256,128]{1,0:T(8,128)(2,1)S(1)} %collective-permute-done.2.query_ref, bf16[2,256,128]{2,1,0:T(8,128)(2,1)S(1)} %copy-done, bf16[2,256,128]{2,1,0:T(8,128)(2,1)S(1)} %collective-permute-done.3.pair_ref, ...), custom_call_target="tpu_custom_call" | custom-call | flops 1342177280 | bytes 1000000 | tf_op jit(solution)/shard_map/pallas_call | solution.py:272
  43.2 0.0 copy-start.2
  43.2 0.0 collective-permute-done.7.beside_ref
  43.2 1.4 %shard_map.102 = bf16[8,256,128]{2,1,0:T(8,128)(2,1)} custom-call(f32[8,128]{1,0:T(8,128)S(1)} %copy-done.3, bf16[256,128]{1,0:T(8,128)(2,1)S(1)} %copy-done.1, bf16[256,128]{1,0:T(8,128)(2,1)S(1)} %collective-permute-done.2.query_ref, f32[512,256]{1,0:T(8,128)S(1)} %shard_map.101.sum_ref, bf16[2,2,256,128]{3,2,1,0:T(8,128)(2,1)S(1)} %collective-permute-done.7.beside_ref), custom_call_target="tpu_custom_call" | custom-call | flops 268435456 | bytes 1000000 | tf_op jit(solution)/shard_map/pallas_call | solution.py:281
  44.6 6.3 %all-to-all-start.1 = ((bf16[8,256,128]{2,1,0:T(8,128)(2,1)}), bf16[8,256,128]{2,1,0:T(8,128)(2,1)S(1)}, u32[]{:S(2)}, u32[]{:S(2)}) async-start(bf16[8,256,128]{2,1,0:T(8,128)(2,1)} %shard_map.102), calls=%async_computation.1 | async-start | bytes 1048576 | tf_op jit(solution)/shard_map/all_to_all | solution.py:294
  50.9 3.4 %collective-permute-start.8 = (bf16[256,384]{1,0:T(8,128)(2,1)}, bf16[256,384]{1,0:T(8,128)(2,1)S(1)}, u32[]{:S(2)}, u32[]{:S(2)}) collective-permute-start(bf16[256,384]{1,0:T(8,128)(2,1)} %bitcast.17), channel_id=1, source_target_pairs={{0,8},{8,0},{16,24},{24,16},{32,40},{40,32},{48,56},{56,48},{64,72... | collective-permute-start | bytes 589832 | tf_op jit(solution)/shard_map/ppermute | solution.py:246
  54.2 8.6 %collective-permute-done.8.rows_ref = bf16[256,384]{1,0:T(8,128)(2,1)S(1)} collective-permute-done((bf16[256,384]{1,0:T(8,128)(2,1)}, bf16[256,384]{1,0:T(8,128)(2,1)S(1)}, u32[]{:S(2)}, u32[]{:S(2)}) %collective-permute-start.8) | collective-permute-done | bytes 196640 | tf_op jit(solution)/shard_map/ppermute | solution.py:246
  62.9 0.0 all-to-all-done.1.heads_ref
  62.9 0.0 copy-done.2
  62.9 0.6 shard_map.103
  63.5 1.9 %collective-permute-start.9 = (bf16[256,384]{1,0:T(8,128)(2,1)S(1)}, bf16[256,384]{1,0:T(8,128)(2,1)S(1)}, u32[]{:S(2)}, u32[]{:S(2)}) collective-permute-start(bf16[256,384]{1,0:T(8,128)(2,1)S(1)} %get-tuple-element.28), channel_id=1, source_target_pairs={{0,1},{1,0},{2,3},{3,2},{4,5},{5,4},{6,7},{7,6},{8,9},{9,8},{10,11... | collective-permute-start | bytes 589832 | tf_op jit(solution)/shard_map/ppermute | solution.py:304
  65.4 1.4 %collective-permute-done.9 = bf16[256,384]{1,0:T(8,128)(2,1)S(1)} collective-permute-done((bf16[256,384]{1,0:T(8,128)(2,1)S(1)}, bf16[256,384]{1,0:T(8,128)(2,1)S(1)}, u32[]{:S(2)}, u32[]{:S(2)}) %collective-permute-start.9) | collective-permute-done | bytes 196640 | tf_op jit(solution)/shard_map/ppermute | solution.py:304
  66.8 0.1 add_convert_fusion
  66.8 7.5 %collective-permute-start.10 = (bf16[256,384]{1,0:T(8,128)(2,1)S(1)}, bf16[256,384]{1,0:T(8,128)(2,1)S(1)}, u32[]{:S(2)}, u32[]{:S(2)}) collective-permute-start(bf16[256,384]{1,0:T(8,128)(2,1)S(1)} %add_convert_fusion), channel_id=1, source_target_pairs={{0,264},{8,256},{16,280},{24,272},{32,296},{40,288},{48,312},{56,3... | collective-permute-start | bytes 589832 | tf_op jit(solution)/shard_map/ppermute | solution.py:311
  74.3 8.1 %collective-permute-done.10 = bf16[256,384]{1,0:T(8,128)(2,1)S(1)} collective-permute-done((bf16[256,384]{1,0:T(8,128)(2,1)S(1)}, bf16[256,384]{1,0:T(8,128)(2,1)S(1)}, u32[]{:S(2)}, u32[]{:S(2)}) %collective-permute-start.10) | collective-permute-done | bytes 196640 | tf_op jit(solution)/shard_map/ppermute | solution.py:311
  82.5 0.7 copy.13
  (3 shorter events, 0.1 us)
Async XLA Ops:
  4.9 5.0 %copy-start.4 = (bf16[2,256,128]{2,1,0:T(8,128)(2,1)S(1)}, bf16[2,256,128]{2,1,0:T(8,128)(2,1)}, u32[]{:S(2)}) copy-start(bf16[2,256,128]{2,1,0:T(8,128)(2,1)} %get-tuple-element.20) | copy-start | bytes 393220
  4.9 14.8 %copy-start = (bf16[2,256,128]{2,1,0:T(8,128)(2,1)S(1)}, bf16[2,256,128]{2,1,0:T(8,128)(2,1)}, u32[]{:S(2)}) copy-start(bf16[2,256,128]{2,1,0:T(8,128)(2,1)} %get-tuple-element.19.near_ref) | copy-start | bytes 393220
  4.9 26.3 %copy-start.5 = (bf16[256,128]{1,0:T(8,128)(2,1)S(1)}, bf16[256,128]{1,0:T(8,128)(2,1)}, u32[]{:S(2)}) copy-start(bf16[256,128]{1,0:T(8,128)(2,1)} %get-tuple-element.22) | copy-start | bytes 196612
  4.9 36.1 %copy-start.1 = (bf16[256,128]{1,0:T(8,128)(2,1)S(1)}, bf16[256,128]{1,0:T(8,128)(2,1)}, u32[]{:S(2)}) copy-start(bf16[256,128]{1,0:T(8,128)(2,1)} %get-tuple-element.18.mine_ref) | copy-start | bytes 196612
  4.9 36.1 %copy-start.3 = (f32[8,128]{1,0:T(8,128)S(1)}, f32[8,128]{1,0:T(8,128)}, u32[]{:S(2)}) copy-start(f32[8,128]{1,0:T(8,128)} %get-tuple-element.17.mask_ref) | copy-start | bytes 12292
  5.0 32.9 %all-to-all-start = ((bf16[4,288,768]{2,1,0:T(8,128)(2,1)}), bf16[4,288,768]{2,1,0:T(8,128)(2,1)S(1)}, u32[]{:S(2)}, u32[]{:S(2)}) async-start(bf16[4,288,768]{2,1,0:T(8,128)(2,1)} %get-tuple-element.23), calls=%async_computation | async-start | bytes 3538944 | tf_op jit(solution)/shard_map/all_to_all | solution.py:243
  9.9 12.3 %collective-permute-start.3 = (bf16[2,256,128]{2,1,0:T(8,128)(2,1)S(1)}, bf16[2,256,128]{2,1,0:T(8,128)(2,1)S(1)}, u32[]{:S(2)}, u32[]{:S(2)}) collective-permute-start(bf16[2,256,128]{2,1,0:T(8,128)(2,1)S(1)} %copy-done.4), channel_id=1, source_target_pairs={{0,8},{8,0},{16,24},{24,16},{32,40},{40,32},{48,56},{56,48},{64,72... | collective-permute-start | bytes 393224 | tf_op jit(solution)/shard_map/ppermute | solution.py:246
  14.2 15.9 %collective-permute-start.1 = (bf16[2,256,128]{2,1,0:T(8,128)(2,1)S(1)}, bf16[2,256,128]{2,1,0:T(8,128)(2,1)S(1)}, u32[]{:S(2)}, u32[]{:S(2)}) collective-permute-start(bf16[2,256,128]{2,1,0:T(8,128)(2,1)S(1)} %copy-done.4), channel_id=1, source_target_pairs={{0,24},{8,16},{16,8},{24,0},{32,56},{40,48},{48,40},{56,32},{64,88... | collective-permute-start | bytes 393224 | tf_op jit(solution)/shard_map/ppermute | solution.py:246
  19.8 11.4 %collective-permute-start = (bf16[2,256,128]{2,1,0:T(8,128)(2,1)S(1)}, bf16[2,256,128]{2,1,0:T(8,128)(2,1)S(1)}, u32[]{:S(2)}, u32[]{:S(2)}) collective-permute-start(bf16[2,256,128]{2,1,0:T(8,128)(2,1)S(1)} %copy-done), channel_id=1, source_target_pairs={{0,16},{8,24},{16,0},{24,8},{32,48},{40,56},{48,32},{56,40},{64,80... | collective-permute-start | bytes 393224 | tf_op jit(solution)/shard_map/ppermute | solution.py:246
  23.0 16.8 %collective-permute-start.5 = (bf16[2,2,256,128]{3,2,1,0:T(8,128)(2,1)}, bf16[2,2,256,128]{3,2,1,0:T(8,128)(2,1)S(1)}, u32[]{:S(2)}, u32[]{:S(2)}) collective-permute-start(bf16[2,2,256,128]{3,2,1,0:T(8,128)(2,1)} %pad_maximum_fusion.1), channel_id=1, source_target_pairs={{32,0},{40,8},{48,16},{56,24},{64,32},{72,40},{80,48},{88,56},{96,... | collective-permute-start | bytes 786440 | tf_op jit(solution)/shard_map/ppermute | solution.py:259
  25.4 14.5 %collective-permute-start.4 = (bf16[2,2,256,128]{3,2,1,0:T(8,128)(2,1)}, bf16[2,2,256,128]{3,2,1,0:T(8,128)(2,1)S(1)}, u32[]{:S(2)}, u32[]{:S(2)}) collective-permute-start(bf16[2,2,256,128]{3,2,1,0:T(8,128)(2,1)} %pad_maximum_fusion.1), channel_id=1, source_target_pairs={{0,32},{8,40},{16,48},{24,56},{32,64},{40,72},{48,80},{56,88},{64,... | collective-permute-start | bytes 786440 | tf_op jit(solution)/shard_map/ppermute | solution.py:258
  31.2 8.6 %collective-permute-start.2 = (bf16[256,128]{1,0:T(8,128)(2,1)S(1)}, bf16[256,128]{1,0:T(8,128)(2,1)S(1)}, u32[]{:S(2)}, u32[]{:S(2)}) collective-permute-start(bf16[256,128]{1,0:T(8,128)(2,1)S(1)} %copy-done.5), channel_id=1, source_target_pairs={{0,8},{8,0},{16,24},{24,16},{32,40},{40,32},{48,56},{56,48},{64,72... | collective-permute-start | bytes 196616 | tf_op jit(solution)/shard_map/ppermute | solution.py:246
  33.2 10.0 %collective-permute-start.7 = (bf16[2,2,256,128]{3,2,1,0:T(8,128)(2,1)S(1)}, bf16[2,2,256,128]{3,2,1,0:T(8,128)(2,1)S(1)}, u32[]{:S(2)}, u32[]{:S(2)}) collective-permute-start(bf16[2,2,256,128]{3,2,1,0:T(8,128)(2,1)S(1)} %pad_maximum_fusion), channel_id=1, source_target_pairs={{0,32},{8,40},{32,64},{40,72},{64,96},{72,104},{96,128},{104,136},... | collective-permute-start | bytes 786440 | tf_op jit(solution)/shard_map/ppermute | solution.py:261
  37.9 3.1 %collective-permute-start.6 = (bf16[4,32,256]{2,1,0:T(8,128)(2,1)S(1)}, bf16[4,32,256]{2,1,0:T(8,128)(2,1)S(1)}, u32[]{:S(2)}, u32[]{:S(2)}) collective-permute-start(bf16[4,32,256]{2,1,0:T(8,128)(2,1)S(1)} %get-tuple-element.29), channel_id=1, source_target_pairs={{0,1},{1,0},{2,3},{3,2},{4,5},{5,4},{6,7},{7,6},{8,9},{9,8},{10,11... | collective-permute-start | bytes 196616 | tf_op jit(solution)/shard_map/ppermute | solution.py:264
  43.2 19.7 %copy-start.2 = (f32[1,384]{1,0:T(1,128)S(1)}, f32[1,384]{1,0:T(1,128)}, u32[]{:S(2)}) copy-start(f32[1,384]{1,0:T(1,128)} %gate_ref.1) | copy-start | bytes 4612
  44.6 18.3 %all-to-all-start.1 = ((bf16[8,256,128]{2,1,0:T(8,128)(2,1)}), bf16[8,256,128]{2,1,0:T(8,128)(2,1)S(1)}, u32[]{:S(2)}, u32[]{:S(2)}) async-start(bf16[8,256,128]{2,1,0:T(8,128)(2,1)} %shard_map.102), calls=%async_computation.1 | async-start | bytes 1048576 | tf_op jit(solution)/shard_map/all_to_all | solution.py:294
  50.9 12.0 %collective-permute-start.8 = (bf16[256,384]{1,0:T(8,128)(2,1)}, bf16[256,384]{1,0:T(8,128)(2,1)S(1)}, u32[]{:S(2)}, u32[]{:S(2)}) collective-permute-start(bf16[256,384]{1,0:T(8,128)(2,1)} %bitcast.17), channel_id=1, source_target_pairs={{0,8},{8,0},{16,24},{24,16},{32,40},{40,32},{48,56},{56,48},{64,72... | collective-permute-start | bytes 589832 | tf_op jit(solution)/shard_map/ppermute | solution.py:246
  63.5 3.3 %collective-permute-start.9 = (bf16[256,384]{1,0:T(8,128)(2,1)S(1)}, bf16[256,384]{1,0:T(8,128)(2,1)S(1)}, u32[]{:S(2)}, u32[]{:S(2)}) collective-permute-start(bf16[256,384]{1,0:T(8,128)(2,1)S(1)} %get-tuple-element.28), channel_id=1, source_target_pairs={{0,1},{1,0},{2,3},{3,2},{4,5},{5,4},{6,7},{7,6},{8,9},{9,8},{10,11... | collective-permute-start | bytes 589832 | tf_op jit(solution)/shard_map/ppermute | solution.py:304
  66.8 15.6 %collective-permute-start.10 = (bf16[256,384]{1,0:T(8,128)(2,1)S(1)}, bf16[256,384]{1,0:T(8,128)(2,1)S(1)}, u32[]{:S(2)}, u32[]{:S(2)}) collective-permute-start(bf16[256,384]{1,0:T(8,128)(2,1)S(1)} %add_convert_fusion), channel_id=1, source_target_pairs={{0,264},{8,256},{16,280},{24,272},{32,296},{40,288},{48,312},{56,3... | collective-permute-start | bytes 589832 | tf_op jit(solution)/shard_map/ppermute | solution.py:311

commit v5 on v4

--- a/solution.py
+++ b/solution.py
@@ -34,43 +34,30 @@
 
 
 def start_out(
-    pair, odd, chip, core, order, band, count, q_ref, k_ref, v_ref, w_ref, t_ref,
-    spread_ref, near_ref, cross_ref, mine_ref, other_ref, mask_ref,
-    q_in, k_in, v_in, stage, near, cross, mine, other, mask, sems, stage_sems, out_sems,
+    pair, odd, chip, core, order, band, count, q_ref, k_ref, v_ref, r_ref, w_ref, t_ref,
+    spread_ref, near_ref, cross_ref, mine_ref, along_ref, mask_ref,
+    q_in, k_in, v_in, t_in, stage, near, cross, mine, along, mask, sems, out_sems,
 ):
     odd, core = odd[0], core[0]
-    depth, width = w_ref.shape[1], w_ref.shape[2] // (2 * CHIPS)
-    slots = t_ref.shape[2]
+    depth, slots = w_ref.shape[1], t_ref.shape[2]
+    width = w_ref.shape[2] // CHIPS
     loads = [
-        pltpu.make_async_copy(source.at[0], target, sems.at[i])
-        for i, (source, target) in enumerate(((k_ref, k_in), (v_ref, v_in), (q_ref, q_in)))
-    ]
-    staged = []
-    for target in range(CHIPS):
-        parts = []
-        for half in range(2):
-            side = target * 2 + (core if half == 0 else 1 - core)
-            columns = pl.ds(pl.multiple_of(side * width, 128), width)
-            parts.append((
-                w_ref.at[0, :, columns],
-                stage.at[target, pl.ds(0, depth), pl.ds(half * width, width)],
-            ))
-            columns = pl.ds(pl.multiple_of((side * 2 + odd) * HD, 128), HD)
-            for kind in range(2):
-                parts.append((
-                    t_ref.at[0, kind, :, columns],
-                    stage.at[target, pl.ds(depth, slots), pl.ds((2 * half + kind) * HD, HD)],
-                ))
-        staged.append([
-            pltpu.make_async_copy(source, to, stage_sems.at[target, i])
-            for i, (source, to) in enumerate(parts)
-        ])
+        (k_ref.at[0], k_in),
+        (v_ref.at[0], v_in),
+        (q_ref.at[0], q_in),
+        (t_ref.at[0], t_in),
+        (r_ref.at[0], along.at[:, pl.ds(0, r_ref.shape[2])]),
+    ]
+    loads += [
+        (w_ref.at[0, :, pl.ds(target * width, width)], stage.at[target, pl.ds(0, depth)])
+        for target in range(CHIPS)
+    ]
+    loads = [
+        pltpu.make_async_copy(source, target, sems.at[i])
+        for i, (source, target) in enumerate(loads)
+    ]
     for load in loads:
         load.start()
-    for parts in staged:
-        for part in parts:
-            part.start()
-    stage[:, depth:, 4 * HD :] = jnp.zeros((CHIPS, slots, 2 * width - 4 * HD), BF16)
     sent = []
 
     def send(source, target):
@@ -89,13 +76,25 @@
     near[1], cross[1] = halves(loads[1], v_in, lambda x: x)
     send(near, near_ref)
     send(cross, cross_ref)
-    mine[...], other[...] = halves(loads[2], q_in, normed)
+    mine[...], along[:, r_ref.shape[2] :] = halves(loads[2], q_in, normed)
     send(mine, mine_ref)
-    send(other, other_ref)
-    for target, parts in enumerate(staged):
-        for part in parts:
-            part.wait()
+    loads[3].wait()
+    for target in range(CHIPS):
+        panels = []
+        for kind in range(2):
+            one, two = (
+                jnp.where(odd == 0, t_in[kind, :, at : at + HD], t_in[kind, :, at + HD : at + 2 * HD])
+                for at in (4 * target * HD, (4 * target + 2) * HD)
+            )
+            panels.append((jnp.where(core == 0, one, two), jnp.where(core == 0, two, one)))
+        for at, panel in enumerate((panels[0][0], panels[1][0], panels[0][1], panels[1][1])):
+            stage[target, depth:, at * HD : (at + 1) * HD] = panel
+        stage[target, depth:, 4 * HD :] = jnp.zeros((slots, width - 4 * HD), BF16)
+    for target, load in enumerate(loads[5:]):
+        load.wait()
         send(stage.at[target], spread_ref.at[target])
+    loads[4].wait()
+    send(along, along_ref)
     for copy in sent:
         copy.wait()
 
@@ -129,8 +128,8 @@
     return result
 
 
-def masked_query(mask_ref, mine_ref, query_ref):
-    query = jnp.concatenate([mine_ref[...], query_ref[...]], axis=0)
+def masked_query(mask_ref, mine_ref, along_ref):
+    query = jnp.concatenate([mine_ref[...], along_ref[:, along_ref.shape[1] - HD :]], axis=0)
     lane = lax.broadcasted_iota(jnp.int32, (TILE, HD), 1)
     lanes = [
         jnp.where(lane <= TEXT_LANE, mask_ref[slot : slot + 1, :], F32(0.0)).astype(BF16)
@@ -177,10 +176,10 @@
 
 
 def first_keys(
-    mask_ref, mine_ref, query_ref, near_ref, pair_ref, far_ref, cross_ref, below_ref, above_ref,
+    mask_ref, mine_ref, along_ref, near_ref, pair_ref, far_ref, cross_ref, below_ref, above_ref,
     own_text, core_text, total_ref,
 ):
-    query = masked_query(mask_ref, mine_ref, query_ref)
+    query = masked_query(mask_ref, mine_ref, along_ref)
     total = add_keys(None, query, *piece_arrays(0, near_ref, pair_ref))
     total = add_keys(total, query, *piece_arrays(1, far_ref, cross_ref))
     total = add_keys(total, query, *piece_arrays(2, below_ref.at[0], below_ref.at[1]))
@@ -189,8 +188,8 @@
     total_ref[...] = add_keys(total, query, *text_arrays(mask_ref, core_text, True))
 
 
-def last_keys(mask_ref, mine_ref, query_ref, sum_ref, beside_ref, out_ref):
-    query = masked_query(mask_ref, mine_ref, query_ref)
+def last_keys(mask_ref, mine_ref, along_ref, sum_ref, beside_ref, out_ref):
+    query = masked_query(mask_ref, mine_ref, along_ref)
     pieces = piece_arrays(PIECES - 1, beside_ref.at[0], beside_ref.at[1])
     total = add_keys(sum_ref[...], query, *pieces)
     result = total[:, :HD] / total[:, HD:]
@@ -203,15 +202,18 @@
         out_ref[CHIPS + chip] = to_odd
 
 
-def project(heads_ref, weight_ref, rows_ref, gate_ref, kept_ref, sent_ref):
+def project(core, heads_ref, weight_ref, along_ref, gate_ref, kept_ref, sent_ref):
     total = None
     depth, width = 2 * HD, kept_ref.shape[1]
     for chip in range(CHIPS):
         heads = jnp.concatenate([heads_ref[chip], heads_ref[CHIPS + chip]], axis=1)
         part = jnp.dot(heads, weight_ref[chip, :depth], preferred_element_type=F32)
         total = part if total is None else total + part
-    kept_ref[...] = rows_ref[...].astype(F32) + gate_ref[...] * total[:, :width]
-    sent_ref[...] = total[:, width:].astype(BF16)
+    low, high = total[:, :width], total[:, width:]
+    first = core[0] == 0
+    kept = jnp.where(first, low, high)
+    kept_ref[...] = along_ref[:, :width].astype(F32) + gate_ref[...] * kept
+    sent_ref[...] = jnp.where(first, high, low).astype(BF16)
 
 
 def body(rows, queries, keys, values, text_kv, text_count, out_weight, gate, band, tile_order):
@@ -224,20 +226,20 @@
     depth, slots = out_weight.shape[1], text_kv.shape[2]
 
     spread_shape = (CHIPS, depth + slots, 2 * width)
-    token_shapes = [(2, BLOCK, HD)] * 2 + [(BLOCK, HD)] * 2
-    spread, near, cross_out, mine, query_out, mask = pl.pallas_call(
+    token_shapes = [(2, BLOCK, HD)] * 2 + [(BLOCK, HD), (BLOCK, width + HD)]
+    spread, near, cross_out, mine, along, mask = pl.pallas_call(
         start_out,
         out_shape=[shape(dims, BF16) for dims in [spread_shape, *token_shapes]]
         + [shape((8, HD), F32)],
-        in_specs=[SMEM] * 7 + [HBM] * 5,
+        in_specs=[SMEM] * 7 + [HBM] * 6,
         out_specs=[HBM] * 6,
         scratch_shapes=[pltpu.VMEM((BLOCK, 2 * HD), BF16)] * 3
-        + [pltpu.VMEM(dims, BF16) for dims in [spread_shape, *token_shapes]]
+        + [pltpu.VMEM(dims, BF16) for dims in [text_kv.shape[1:], spread_shape, *token_shapes]]
         + [pltpu.VMEM((8, HD), F32)]
-        + [pltpu.SemaphoreType.DMA(dims) for dims in ((3,), (CHIPS, 6), (5 + CHIPS,))],
+        + [pltpu.SemaphoreType.DMA(dims) for dims in ((5 + CHIPS,), (5 + CHIPS,))],
         compiler_params=params(60),
         cost_estimate=pl.CostEstimate(flops=10**6, bytes_accessed=4 * 10**6, transcendentals=0),
-    )(*place, tile_order, band.T, text_count, queries, keys, values, out_weight, text_kv)
+    )(*place, tile_order, band.T, text_count, queries, keys, values, rows, out_weight, text_kv)
 
     by_core = [[2 * chip + core for chip in range(CHIPS)] for core in range(2)]
     spread = lax.all_to_all(spread, "grp", 0, 0, axis_index_groups=by_core)
@@ -251,8 +253,8 @@
 
     own_pair = jnp.stack([near, pair_in])
     other_pair = jnp.stack([far_in, cross_in])
-    other_pair, query_out = lax.optimization_barrier((other_pair, query_out))
-    query_in = swapped(query_out, 1)
+    own_pair, along = lax.optimization_barrier((own_pair, along))
+    along_in = swapped(along, 1)
     up = [(i, i + 4) for i in range(seq_count - 4)]
     down = [(i + 4, i) for i in range(seq_count - 4)]
     below = lax.ppermute(own_pair, "seq", up)
@@ -275,16 +277,14 @@
         in_specs=[VMEM] * 11,
         compiler_params=params(),
         cost_estimate=cost(5),
-    )(mask, mine, query_in, near, pair_in, far_in, cross_in, below, above, own_text, core_text)
-    total, rows_out = lax.optimization_barrier((total, rows[0]))
-    rows_in = swapped(rows_out, 1)
+    )(mask, mine, along_in, near, pair_in, far_in, cross_in, below, above, own_text, core_text)
     attention = pl.pallas_call(
         last_keys,
         out_shape=shape((2 * CHIPS, BLOCK, HD), BF16),
         in_specs=[VMEM] * 5,
         compiler_params=params(),
         cost_estimate=cost(1),
-    )(mask, mine, query_in, total, beside)
+    )(mask, mine, along_in, total, beside)
 
     groups = [
         [(2 * pair + odd) * 2 * CHIPS + 2 * chip + core for odd in range(2) for chip in range(CHIPS)]
@@ -295,12 +295,12 @@
     kept, sent = pl.pallas_call(
         project,
         out_shape=(shape((BLOCK, width), F32), shape((BLOCK, width), BF16)),
-        in_specs=[VMEM] * 4,
+        in_specs=[SMEM] + [VMEM] * 4,
         compiler_params=params(),
         cost_estimate=pl.CostEstimate(
             flops=2 * BLOCK * 1024 * 768, bytes_accessed=3 * 10**6, transcendentals=0
         ),
-    )(heads, spread, rows_in, gate)
+    )(place[3], heads, spread, along_in, gate)
     other = lax.ppermute(sent, "grp", [(g, g ^ 1) for g in range(2 * CHIPS)])
     result = (kept + gate * other.astype(F32)).astype(BF16)
     across = [

time: 83.7 us -> 79 us (0.944)
  the two profiles are of different devices: /device:TPU:26 before, /device:TPU:24 now
where the time goes in v5:
time: 79 us; the launch traced here: 78.5 us
  starting transfers between devices  41.6 us (53%)
  blocking collectives  15.6 us (20%)
  waiting for transfers between devices  11.3 us (14%)
  Pallas kernels  6.82 us (9%)
  other arithmetic  1.51 us (2%)
  between operations  0.87 us (1%)
    all_to_all x1, blocking collectives, body(): lax.all_to_all(attention, ('seq', 'grp'), 0, 0, axis_index_groups=groups)  15.6 us
    ppermute x4, starting transfers between devices, swapped(): return lax.ppermute(block, 'seq', [(i, i ^ mask) for i in range(seq_count)])  14.8 us
    ppermute x1, waiting for transfers between devices, body(): handed = lax.ppermute(result, ('section', 'seq'), across)  8.69 us
    ppermute x1, starting transfers between devices, body(): handed = lax.ppermute(result, ('section', 'seq'), across)  7.91 us
    ppermute x1, starting transfers between devices, body(): below = lax.ppermute(own_pair, 'seq', up)  4.69 us
    all_to_all x1, starting transfers between devices, body(): spread = lax.all_to_all(spread, 'grp', 0, 0, axis_index_groups=by_core)  4.44 us
    ppermute x1, starting transfers between devices, body(): beside = lax.ppermute(other_pair, 'seq', mixed)  3.65 us
    pallas_call x1, Pallas kernels, body(): pl.pallas_call(start_out, out_shape=[shape(dims, BF16) for dims in [sprea...  3.5 us
  transfers between devices with their start and end apart: 11, of which 4 were waited for; matrix products, arithmetic and copies ran while one was open for 2% of the time, Pallas kernels for 3%

profile of v5, /device:TPU:24, one launch (start us, length us, event | category | flops | bytes accessed | tf_op | source)
XLA Modules:
  0.0 78.5 jit_solution(9727901788589115038)
XLA Ops:
  0.7 3.5 %shard_map.100 = (bf16[4,288,768]{2,1,0:T(8,128)(2,1)}, bf16[2,256,128]{2,1,0:T(8,128)(2,1)}, bf16[2,256,128]{2,1,0:T(8,128)(2,1)}, bf16[256,128]{1,0:T(8,128)(2...) custom-call(s32[1]{0:T(128)} %bitcast.1.pair, s32[1]{0:T(128)} %bitcast.2.odd, s32[1]{0:T(128)} %bitcast.3.chip, ...), custom_call_target="tpu_custom_call" | custom-call | flops 1000000 | bytes 4000000 | tf_op jit(solution)/shard_map/pallas_call | solution.py:230
  4.2 0.0 copy-start.4
  4.2 0.0 copy-start
  4.2 0.0 copy-start.1
  4.2 0.0 copy-start.3
  4.2 4.4 %all-to-all-start = ((bf16[4,288,768]{2,1,0:T(8,128)(2,1)}), bf16[4,288,768]{2,1,0:T(8,128)(2,1)S(1)}, u32[]{:S(2)}, u32[]{:S(2)}) async-start(bf16[4,288,768]{2,1,0:T(8,128)(2,1)} %get-tuple-element.22), calls=%async_computation | async-start | bytes 3538944 | tf_op jit(solution)/shard_map/all_to_all | solution.py:245
  8.6 0.0 copy-done.4
  8.6 4.3 %collective-permute-start = (bf16[2,256,128]{2,1,0:T(8,128)(2,1)S(1)}, bf16[2,256,128]{2,1,0:T(8,128)(2,1)S(1)}, u32[]{:S(2)}, u32[]{:S(2)}) collective-permute-start(bf16[2,256,128]{2,1,0:T(8,128)(2,1)S(1)} %copy-done.4), channel_id=1, source_target_pairs={{0,8},{8,0},{16,24},{24,16},{32,40},{40,32},{48,56},{56,48},{64,72... | collective-permute-start | bytes 393224 | tf_op jit(solution)/shard_map/ppermute | solution.py:248
  12.9 5.5 %collective-permute-start.3 = (bf16[2,256,128]{2,1,0:T(8,128)(2,1)S(1)}, bf16[2,256,128]{2,1,0:T(8,128)(2,1)S(1)}, u32[]{:S(2)}, u32[]{:S(2)}) collective-permute-start(bf16[2,256,128]{2,1,0:T(8,128)(2,1)S(1)} %copy-done.4), channel_id=1, source_target_pairs={{0,24},{8,16},{16,8},{24,0},{32,56},{40,48},{48,40},{56,32},{64,88... | collective-permute-start | bytes 393224 | tf_op jit(solution)/shard_map/ppermute | solution.py:248
  18.5 0.0 copy-done
  18.5 2.5 %collective-permute-start.2 = (bf16[2,256,128]{2,1,0:T(8,128)(2,1)S(1)}, bf16[2,256,128]{2,1,0:T(8,128)(2,1)S(1)}, u32[]{:S(2)}, u32[]{:S(2)}) collective-permute-start(bf16[2,256,128]{2,1,0:T(8,128)(2,1)S(1)} %copy-done), channel_id=1, source_target_pairs={{0,16},{8,24},{16,0},{24,8},{32,48},{40,56},{48,32},{56,40},{64,80... | collective-permute-start | bytes 393224 | tf_op jit(solution)/shard_map/ppermute | solution.py:248
  21.0 0.0 collective-permute-done.pair_ref
  21.0 0.7 pad_maximum_fusion
  21.7 2.3 %collective-permute-start.5 = (bf16[2,2,256,128]{3,2,1,0:T(8,128)(2,1)}, bf16[2,2,256,128]{3,2,1,0:T(8,128)(2,1)S(1)}, u32[]{:S(2)}, u32[]{:S(2)}) collective-permute-start(bf16[2,2,256,128]{3,2,1,0:T(8,128)(2,1)} %pad_maximum_fusion), channel_id=1, source_target_pairs={{32,0},{40,8},{48,16},{56,24},{64,32},{72,40},{80,48},{88,56},{96,... | collective-permute-start | bytes 786440 | tf_op jit(solution)/shard_map/ppermute | solution.py:261
  24.0 4.7 %collective-permute-start.4 = (bf16[2,2,256,128]{3,2,1,0:T(8,128)(2,1)}, bf16[2,2,256,128]{3,2,1,0:T(8,128)(2,1)S(1)}, u32[]{:S(2)}, u32[]{:S(2)}) collective-permute-start(bf16[2,2,256,128]{3,2,1,0:T(8,128)(2,1)} %pad_maximum_fusion), channel_id=1, source_target_pairs={{0,32},{8,40},{16,48},{24,56},{32,64},{40,72},{48,80},{56,88},{64,... | collective-permute-start | bytes 786440 | tf_op jit(solution)/shard_map/ppermute | solution.py:260
  28.7 2.5 %collective-permute-start.1 = (bf16[256,512]{1,0:T(8,128)(2,1)}, bf16[256,512]{1,0:T(8,128)(2,1)S(1)}, u32[]{:S(2)}, u32[]{:S(2)}) collective-permute-start(bf16[256,512]{1,0:T(8,128)(2,1)} %get-tuple-element.20), channel_id=1, source_target_pairs={{0,8},{8,0},{16,24},{24,16},{32,40},{40,32},{48,56},{56,48},{64,72... | collective-permute-start | bytes 786440 | tf_op jit(solution)/shard_map/ppermute | solution.py:248
  31.2 0.0 collective-permute-done.3.cross_ref
  31.2 0.0 collective-permute-done.2.far_ref
  31.2 0.7 pad_maximum_fusion.1
  32.0 3.6 %collective-permute-start.7 = (bf16[2,2,256,128]{3,2,1,0:T(8,128)(2,1)}, bf16[2,2,256,128]{3,2,1,0:T(8,128)(2,1)S(1)}, u32[]{:S(2)}, u32[]{:S(2)}) collective-permute-start(bf16[2,2,256,128]{3,2,1,0:T(8,128)(2,1)} %pad_maximum_fusion.1), channel_id=1, source_target_pairs={{0,32},{8,40},{32,64},{40,72},{64,96},{72,104},{96,128},{104,136},... | collective-permute-start | bytes 786440 | tf_op jit(solution)/shard_map/ppermute | solution.py:263
  35.6 0.0 all-to-all-done.weight_ref
  35.6 1.9 %collective-permute-start.6 = (bf16[4,32,256]{2,1,0:T(8,128)(2,1)S(1)}, bf16[4,32,256]{2,1,0:T(8,128)(2,1)S(1)}, u32[]{:S(2)}, u32[]{:S(2)}) collective-permute-start(bf16[4,32,256]{2,1,0:T(8,128)(2,1)S(1)} %get-tuple-element.25), channel_id=1, source_target_pairs={{0,1},{1,0},{2,3},{3,2},{4,5},{5,4},{6,7},{7,6},{8,9},{9,8},{10,11... | collective-permute-start | bytes 196616 | tf_op jit(solution)/shard_map/ppermute | solution.py:266
  37.6 0.0 collective-permute-done.1.along_ref
  37.6 0.0 collective-permute-done.5.above_ref
  37.6 0.0 collective-permute-done.4.below_ref
  37.6 1.2 %collective-permute-done.6.core_text = bf16[4,32,256]{2,1,0:T(8,128)(2,1)S(1)} collective-permute-done((bf16[4,32,256]{2,1,0:T(8,128)(2,1)S(1)}, bf16[4,32,256]{2,1,0:T(8,128)(2,1)S(1)}, u32[]{:S(2)}, u32[]{:S(2)}) %collective-permute-start.6) | collective-permute-done | bytes 65568 | tf_op jit(solution)/shard_map/ppermute | solution.py:266
  38.8 0.0 copy-done.1
  38.8 0.0 copy-done.3
  38.8 2.1 %shard_map.101.sum_ref = f32[512,256]{1,0:T(8,128)S(1)} custom-call(f32[8,128]{1,0:T(8,128)S(1)} %copy-done.3, bf16[256,128]{1,0:T(8,128)(2,1)S(1)} %copy-done.1, bf16[256,512]{1,0:T(8,128)(2,1)S(1)} %collective-permute-done.1.along_ref, bf16[2,256,128]{2,1,0:T(8,128)(2,1)S(1)} %copy-done, bf16[2,256,128]{2,1,0:T(8,128)(2,1)S(1)} %collective-permute-done.pair_ref, ...), custom_call_target="tpu_custom_call" | custom-call | flops 1342177280 | bytes 1000000 | tf_op jit(solution)/shard_map/pallas_call | solution.py:274
  40.9 0.0 copy-start.2
  40.9 0.1 collective-permute-done.7.beside_ref
  41.0 0.6 shard_map.102
  41.6 15.6 %all_to_all.10.heads_ref = bf16[8,256,128]{2,1,0:T(8,128)(2,1)S(1)} all-to-all(bf16[8,256,128]{2,1,0:T(8,128)(2,1)S(1)} %shard_map.102), channel_id=1, replica_groups={{0,2,4,6,8,10,12,14},{1,3,5,7,9,11,13,15},{16,18,20,22,24,26,28,30},{17..., dimensions={0} | all-to-all | bytes 1048576 | tf_op jit(solution)/shard_map/all_to_all | solution.py:294
  57.2 0.0 copy-done.2
  57.2 0.6 shard_map.103
  57.8 1.9 %collective-permute-start.8 = (bf16[256,384]{1,0:T(8,128)(2,1)S(1)}, bf16[256,384]{1,0:T(8,128)(2,1)S(1)}, u32[]{:S(2)}, u32[]{:S(2)}) collective-permute-start(bf16[256,384]{1,0:T(8,128)(2,1)S(1)} %get-tuple-element.24), channel_id=1, source_target_pairs={{0,1},{1,0},{2,3},{3,2},{4,5},{5,4},{6,7},{7,6},{8,9},{9,8},{10,11... | collective-permute-start | bytes 589832 | tf_op jit(solution)/shard_map/ppermute | solution.py:304
  59.8 1.4 %collective-permute-done.8 = bf16[256,384]{1,0:T(8,128)(2,1)S(1)} collective-permute-done((bf16[256,384]{1,0:T(8,128)(2,1)S(1)}, bf16[256,384]{1,0:T(8,128)(2,1)S(1)}, u32[]{:S(2)}, u32[]{:S(2)}) %collective-permute-start.8) | collective-permute-done | bytes 196640 | tf_op jit(solution)/shard_map/ppermute | solution.py:304
  61.2 0.1 add_convert_fusion
  61.2 7.9 %collective-permute-start.9 = (bf16[256,384]{1,0:T(8,128)(2,1)S(1)}, bf16[256,384]{1,0:T(8,128)(2,1)S(1)}, u32[]{:S(2)}, u32[]{:S(2)}) collective-permute-start(bf16[256,384]{1,0:T(8,128)(2,1)S(1)} %add_convert_fusion), channel_id=1, source_target_pairs={{0,264},{8,256},{16,280},{24,272},{32,296},{40,288},{48,312},{56,3... | collective-permute-start | bytes 589832 | tf_op jit(solution)/shard_map/ppermute | solution.py:311
  69.1 8.7 %collective-permute-done.9 = bf16[256,384]{1,0:T(8,128)(2,1)S(1)} collective-permute-done((bf16[256,384]{1,0:T(8,128)(2,1)S(1)}, bf16[256,384]{1,0:T(8,128)(2,1)S(1)}, u32[]{:S(2)}, u32[]{:S(2)}) %collective-permute-start.9) | collective-permute-done | bytes 196640 | tf_op jit(solution)/shard_map/ppermute | solution.py:311
  77.8 0.7 copy.13
  (2 shorter events, 0.0 us)
Async XLA Ops:
  4.2 4.5 %copy-start.4 = (bf16[2,256,128]{2,1,0:T(8,128)(2,1)S(1)}, bf16[2,256,128]{2,1,0:T(8,128)(2,1)}, u32[]{:S(2)}) copy-start(bf16[2,256,128]{2,1,0:T(8,128)(2,1)} %get-tuple-element.18) | copy-start | bytes 393220
  4.2 14.3 %copy-start = (bf16[2,256,128]{2,1,0:T(8,128)(2,1)S(1)}, bf16[2,256,128]{2,1,0:T(8,128)(2,1)}, u32[]{:S(2)}) copy-start(bf16[2,256,128]{2,1,0:T(8,128)(2,1)} %get-tuple-element.17.near_ref) | copy-start | bytes 393220
  4.2 34.6 %copy-start.1 = (bf16[256,128]{1,0:T(8,128)(2,1)S(1)}, bf16[256,128]{1,0:T(8,128)(2,1)}, u32[]{:S(2)}) copy-start(bf16[256,128]{1,0:T(8,128)(2,1)} %get-tuple-element.16.mine_ref) | copy-start | bytes 196612
  4.2 34.6 %copy-start.3 = (f32[8,128]{1,0:T(8,128)S(1)}, f32[8,128]{1,0:T(8,128)}, u32[]{:S(2)}) copy-start(f32[8,128]{1,0:T(8,128)} %get-tuple-element.15.mask_ref) | copy-start | bytes 12292
  4.2 31.4 %all-to-all-start = ((bf16[4,288,768]{2,1,0:T(8,128)(2,1)}), bf16[4,288,768]{2,1,0:T(8,128)(2,1)S(1)}, u32[]{:S(2)}, u32[]{:S(2)}) async-start(bf16[4,288,768]{2,1,0:T(8,128)(2,1)} %get-tuple-element.22), calls=%async_computation | async-start | bytes 3538944 | tf_op jit(solution)/shard_map/all_to_all | solution.py:245
  8.6 12.3 %collective-permute-start = (bf16[2,256,128]{2,1,0:T(8,128)(2,1)S(1)}, bf16[2,256,128]{2,1,0:T(8,128)(2,1)S(1)}, u32[]{:S(2)}, u32[]{:S(2)}) collective-permute-start(bf16[2,256,128]{2,1,0:T(8,128)(2,1)S(1)} %copy-done.4), channel_id=1, source_target_pairs={{0,8},{8,0},{16,24},{24,16},{32,40},{40,32},{48,56},{56,48},{64,72... | collective-permute-start | bytes 393224 | tf_op jit(solution)/shard_map/ppermute | solution.py:248
  12.9 18.3 %collective-permute-start.3 = (bf16[2,256,128]{2,1,0:T(8,128)(2,1)S(1)}, bf16[2,256,128]{2,1,0:T(8,128)(2,1)S(1)}, u32[]{:S(2)}, u32[]{:S(2)}) collective-permute-start(bf16[2,256,128]{2,1,0:T(8,128)(2,1)S(1)} %copy-done.4), channel_id=1, source_target_pairs={{0,24},{8,16},{16,8},{24,0},{32,56},{40,48},{48,40},{56,32},{64,88... | collective-permute-start | bytes 393224 | tf_op jit(solution)/shard_map/ppermute | solution.py:248
  18.5 12.8 %collective-permute-start.2 = (bf16[2,256,128]{2,1,0:T(8,128)(2,1)S(1)}, bf16[2,256,128]{2,1,0:T(8,128)(2,1)S(1)}, u32[]{:S(2)}, u32[]{:S(2)}) collective-permute-start(bf16[2,256,128]{2,1,0:T(8,128)(2,1)S(1)} %copy-done), channel_id=1, source_target_pairs={{0,16},{8,24},{16,0},{24,8},{32,48},{40,56},{48,32},{56,40},{64,80... | collective-permute-start | bytes 393224 | tf_op jit(solution)/shard_map/ppermute | solution.py:248
  21.7 15.9 %collective-permute-start.5 = (bf16[2,2,256,128]{3,2,1,0:T(8,128)(2,1)}, bf16[2,2,256,128]{3,2,1,0:T(8,128)(2,1)S(1)}, u32[]{:S(2)}, u32[]{:S(2)}) collective-permute-start(bf16[2,2,256,128]{3,2,1,0:T(8,128)(2,1)} %pad_maximum_fusion), channel_id=1, source_target_pairs={{32,0},{40,8},{48,16},{56,24},{64,32},{72,40},{80,48},{88,56},{96,... | collective-permute-start | bytes 786440 | tf_op jit(solution)/shard_map/ppermute | solution.py:261
  24.0 13.6 %collective-permute-start.4 = (bf16[2,2,256,128]{3,2,1,0:T(8,128)(2,1)}, bf16[2,2,256,128]{3,2,1,0:T(8,128)(2,1)S(1)}, u32[]{:S(2)}, u32[]{:S(2)}) collective-permute-start(bf16[2,2,256,128]{3,2,1,0:T(8,128)(2,1)} %pad_maximum_fusion), channel_id=1, source_target_pairs={{0,32},{8,40},{16,48},{24,56},{32,64},{40,72},{48,80},{56,88},{64,... | collective-permute-start | bytes 786440 | tf_op jit(solution)/shard_map/ppermute | solution.py:260
  28.7 8.8 %collective-permute-start.1 = (bf16[256,512]{1,0:T(8,128)(2,1)}, bf16[256,512]{1,0:T(8,128)(2,1)S(1)}, u32[]{:S(2)}, u32[]{:S(2)}) collective-permute-start(bf16[256,512]{1,0:T(8,128)(2,1)} %get-tuple-element.20), channel_id=1, source_target_pairs={{0,8},{8,0},{16,24},{24,16},{32,40},{40,32},{48,56},{56,48},{64,72... | collective-permute-start | bytes 786440 | tf_op jit(solution)/shard_map/ppermute | solution.py:248
  32.0 9.0 %collective-permute-start.7 = (bf16[2,2,256,128]{3,2,1,0:T(8,128)(2,1)}, bf16[2,2,256,128]{3,2,1,0:T(8,128)(2,1)S(1)}, u32[]{:S(2)}, u32[]{:S(2)}) collective-permute-start(bf16[2,2,256,128]{3,2,1,0:T(8,128)(2,1)} %pad_maximum_fusion.1), channel_id=1, source_target_pairs={{0,32},{8,40},{32,64},{40,72},{64,96},{72,104},{96,128},{104,136},... | collective-permute-start | bytes 786440 | tf_op jit(solution)/shard_map/ppermute | solution.py:263
  35.6 3.1 %collective-permute-start.6 = (bf16[4,32,256]{2,1,0:T(8,128)(2,1)S(1)}, bf16[4,32,256]{2,1,0:T(8,128)(2,1)S(1)}, u32[]{:S(2)}, u32[]{:S(2)}) collective-permute-start(bf16[4,32,256]{2,1,0:T(8,128)(2,1)S(1)} %get-tuple-element.25), channel_id=1, source_target_pairs={{0,1},{1,0},{2,3},{3,2},{4,5},{5,4},{6,7},{7,6},{8,9},{9,8},{10,11... | collective-permute-start | bytes 196616 | tf_op jit(solution)/shard_map/ppermute | solution.py:266
  40.9 16.3 %copy-start.2 = (f32[1,384]{1,0:T(1,128)S(1)}, f32[1,384]{1,0:T(1,128)}, u32[]{:S(2)}) copy-start(f32[1,384]{1,0:T(1,128)} %gate_ref.1) | copy-start | bytes 4612
  57.8 3.3 %collective-permute-start.8 = (bf16[256,384]{1,0:T(8,128)(2,1)S(1)}, bf16[256,384]{1,0:T(8,128)(2,1)S(1)}, u32[]{:S(2)}, u32[]{:S(2)}) collective-permute-start(bf16[256,384]{1,0:T(8,128)(2,1)S(1)} %get-tuple-element.24), channel_id=1, source_target_pairs={{0,1},{1,0},{2,3},{3,2},{4,5},{5,4},{6,7},{7,6},{8,9},{9,8},{10,11... | collective-permute-start | bytes 589832 | tf_op jit(solution)/shard_map/ppermute | solution.py:304
  61.2 16.6 %collective-permute-start.9 = (bf16[256,384]{1,0:T(8,128)(2,1)S(1)}, bf16[256,384]{1,0:T(8,128)(2,1)S(1)}, u32[]{:S(2)}, u32[]{:S(2)}) collective-permute-start(bf16[256,384]{1,0:T(8,128)(2,1)S(1)} %add_convert_fusion), channel_id=1, source_target_pairs={{0,264},{8,256},{16,280},{24,272},{32,296},{40,288},{48,312},{56,3... | collective-permute-start | bytes 589832 | tf_op jit(solution)/shard_map/ppermute | solution.py:311

commit v6 on v5

--- a/solution.py
+++ b/solution.py
@@ -21,6 +21,7 @@
 F32 = jnp.float32
 SMEM = pl.BlockSpec(memory_space=pltpu.SMEM)
 VMEM = pl.BlockSpec(memory_space=pltpu.VMEM)
+ANY = pl.BlockSpec(memory_space=pl.ANY)
 HBM = pl.BlockSpec(memory_space=pltpu.HBM)
 
 
@@ -34,9 +35,9 @@
 
 
 def start_out(
-    pair, odd, chip, core, order, band, count, q_ref, k_ref, v_ref, r_ref, w_ref, t_ref,
-    spread_ref, near_ref, cross_ref, mine_ref, along_ref, mask_ref,
-    q_in, k_in, v_in, t_in, stage, near, cross, mine, along, mask, sems, out_sems,
+    pair, odd, core, order_ref, band_ref, count_ref, q_ref, k_ref, v_ref, w_ref, t_ref,
+    spread_ref, near_ref, cross_ref, pair_out_ref, mine_ref, mask_ref,
+    q_in, k_in, v_in, t_in, stage, near, mixed, mine, mask, order, band, count, sems, out_sems,
 ):
     odd, core = odd[0], core[0]
     depth, slots = w_ref.shape[1], t_ref.shape[2]
@@ -46,12 +47,12 @@
         (v_ref.at[0], v_in),
         (q_ref.at[0], q_in),
         (t_ref.at[0], t_in),
-        (r_ref.at[0], along.at[:, pl.ds(0, r_ref.shape[2])]),
     ]
     loads += [
         (w_ref.at[0, :, pl.ds(target * width, width)], stage.at[target, pl.ds(0, depth)])
         for target in range(CHIPS)
     ]
+    loads += [(order_ref, order), (band_ref, band), (count_ref, count)]
     loads = [
         pltpu.make_async_copy(source, target, sems.at[i])
         for i, (source, target) in enumerate(loads)
@@ -63,20 +64,18 @@
     def send(source, target):
         sent.append(pltpu.make_async_copy(source, target, out_sems.at[len(sent)]))
         sent[-1].start()
-
-    mask[...] = mask_rows(pair[0], odd, core, order, band, count)
-    send(mask, mask_ref)
 
     def halves(load, ref, prepare):
         load.wait()
         a, b = prepare(ref[:, :HD]), prepare(ref[:, HD:])
         return jnp.where(odd == 0, a, b), jnp.where(odd == 0, b, a)
 
-    near[0], cross[0] = halves(loads[0], k_in, normed)
-    near[1], cross[1] = halves(loads[1], v_in, lambda x: x)
+    near[0], mixed[0] = halves(loads[0], k_in, normed)
+    near[1], mixed[1] = halves(loads[1], v_in, lambda x: x)
     send(near, near_ref)
-    send(cross, cross_ref)
-    mine[...], along[:, r_ref.shape[2] :] = halves(loads[2], q_in, normed)
+    send(mixed.at[pl.ds(0, 2)], cross_ref)
+    mine[...], mixed[2] = halves(loads[2], q_in, normed)
+    send(mixed, pair_out_ref)
     send(mine, mine_ref)
     loads[3].wait()
     for target in range(CHIPS):
@@ -90,11 +89,13 @@
         for at, panel in enumerate((panels[0][0], panels[1][0], panels[0][1], panels[1][1])):
             stage[target, depth:, at * HD : (at + 1) * HD] = panel
         stage[target, depth:, 4 * HD :] = jnp.zeros((slots, width - 4 * HD), BF16)
-    for target, load in enumerate(loads[5:]):
+    for load in loads[4 + CHIPS :]:
+        load.wait()
+    mask[...] = mask_rows(pair[0], odd, core, order, band, count)
+    send(mask, mask_ref)
+    for target, load in enumerate(loads[4 : 4 + CHIPS]):
         load.wait()
         send(stage.at[target], spread_ref.at[target])
-    loads[4].wait()
-    send(along, along_ref)
     for copy in sent:
         copy.wait()
 
@@ -128,8 +129,8 @@
     return result
 
 
-def masked_query(mask_ref, mine_ref, along_ref):
-    query = jnp.concatenate([mine_ref[...], along_ref[:, along_ref.shape[1] - HD :]], axis=0)
+def masked_query(mask_ref, mine_ref, pair_ref):
+    query = jnp.concatenate([mine_ref[...], pair_ref[2]], axis=0)
     lane = lax.broadcasted_iota(jnp.int32, (TILE, HD), 1)
     lanes = [
         jnp.where(lane <= TEXT_LANE, mask_ref[slot : slot + 1, :], F32(0.0)).astype(BF16)
@@ -176,20 +177,28 @@
 
 
 def first_keys(
-    mask_ref, mine_ref, along_ref, near_ref, pair_ref, far_ref, cross_ref, below_ref, above_ref,
-    own_text, core_text, total_ref,
+    mask_ref, mine_ref, near_ref, pair_ref, far_ref, cross_ref, below_ref, above_ref,
+    own_text, core_text, total_ref, below, above, sems,
 ):
-    query = masked_query(mask_ref, mine_ref, along_ref)
+    loads = [
+        pltpu.make_async_copy(source, target, sems.at[i])
+        for i, (source, target) in enumerate(((below_ref, below), (above_ref, above)))
+    ]
+    for load in loads:
+        load.start()
+    query = masked_query(mask_ref, mine_ref, pair_ref)
     total = add_keys(None, query, *piece_arrays(0, near_ref, pair_ref))
     total = add_keys(total, query, *piece_arrays(1, far_ref, cross_ref))
-    total = add_keys(total, query, *piece_arrays(2, below_ref.at[0], below_ref.at[1]))
-    total = add_keys(total, query, *piece_arrays(3, above_ref.at[0], above_ref.at[1]))
     total = add_keys(total, query, *text_arrays(mask_ref, own_text, False))
-    total_ref[...] = add_keys(total, query, *text_arrays(mask_ref, core_text, True))
-
-
-def last_keys(mask_ref, mine_ref, along_ref, sum_ref, beside_ref, out_ref):
-    query = masked_query(mask_ref, mine_ref, along_ref)
+    total = add_keys(total, query, *text_arrays(mask_ref, core_text, True))
+    loads[0].wait()
+    total = add_keys(total, query, *piece_arrays(2, below.at[0], below.at[1]))
+    loads[1].wait()
+    total_ref[...] = add_keys(total, query, *piece_arrays(3, above.at[0], above.at[1]))
+
+
+def last_keys(mask_ref, mine_ref, pair_ref, sum_ref, beside_ref, out_ref):
+    query = masked_query(mask_ref, mine_ref, pair_ref)
     pieces = piece_arrays(PIECES - 1, beside_ref.at[0], beside_ref.at[1])
     total = add_keys(sum_ref[...], query, *pieces)
     result = total[:, :HD] / total[:, HD:]
@@ -202,7 +211,12 @@
         out_ref[CHIPS + chip] = to_odd
 
 
-def project(core, heads_ref, weight_ref, along_ref, gate_ref, kept_ref, sent_ref):
+def join(low_ref, high_ref, out_ref):
+    out_ref[0] = low_ref[...]
+    out_ref[1] = high_ref[:2]
+
+
+def project(core, heads_ref, weight_ref, rows_ref, gate_ref, kept_ref, sent_ref):
     total = None
     depth, width = 2 * HD, kept_ref.shape[1]
     for chip in range(CHIPS):
@@ -212,7 +226,7 @@
     low, high = total[:, :width], total[:, width:]
     first = core[0] == 0
     kept = jnp.where(first, low, high)
-    kept_ref[...] = along_ref[:, :width].astype(F32) + gate_ref[...] * kept
+    kept_ref[...] = rows_ref[...].astype(F32) + gate_ref[...] * kept
     sent_ref[...] = jnp.where(first, high, low).astype(BF16)
 
 
@@ -220,26 +234,27 @@
     seq_count = lax.axis_size("seq")
     seq = lax.axis_index("seq")
     grp = lax.axis_index("grp")
-    place = [at.astype(jnp.int32).reshape(1) for at in (seq >> 1, seq & 1, grp >> 1, grp & 1)]
+    place = [at.astype(jnp.int32).reshape(1) for at in (seq >> 1, seq & 1, grp & 1)]
     shape = jax.ShapeDtypeStruct
     width = gate.shape[1]
     depth, slots = out_weight.shape[1], text_kv.shape[2]
 
     spread_shape = (CHIPS, depth + slots, 2 * width)
-    token_shapes = [(2, BLOCK, HD)] * 2 + [(BLOCK, HD), (BLOCK, width + HD)]
-    spread, near, cross_out, mine, along, mask = pl.pallas_call(
+    token_shapes = [(2, BLOCK, HD)] * 2 + [(3, BLOCK, HD), (BLOCK, HD)]
+    spread, near, cross_out, pair_out, mine, mask = pl.pallas_call(
         start_out,
         out_shape=[shape(dims, BF16) for dims in [spread_shape, *token_shapes]]
         + [shape((8, HD), F32)],
-        in_specs=[SMEM] * 7 + [HBM] * 6,
+        in_specs=[SMEM] * 3 + [HBM] * 8,
         out_specs=[HBM] * 6,
         scratch_shapes=[pltpu.VMEM((BLOCK, 2 * HD), BF16)] * 3
-        + [pltpu.VMEM(dims, BF16) for dims in [text_kv.shape[1:], spread_shape, *token_shapes]]
+        + [pltpu.VMEM(dims, BF16) for dims in [text_kv.shape[1:], spread_shape, *token_shapes[1:]]]
         + [pltpu.VMEM((8, HD), F32)]
-        + [pltpu.SemaphoreType.DMA(dims) for dims in ((5 + CHIPS,), (5 + CHIPS,))],
+        + [pltpu.SMEM(array.shape, jnp.int32) for array in (tile_order, band.T, text_count)]
+        + [pltpu.SemaphoreType.DMA(dims) for dims in ((7 + CHIPS,), (5 + CHIPS,))],
         compiler_params=params(60),
         cost_estimate=pl.CostEstimate(flops=10**6, bytes_accessed=4 * 10**6, transcendentals=0),
-    )(*place, tile_order, band.T, text_count, queries, keys, values, rows, out_weight, text_kv)
+    )(*place, tile_order, band.T, text_count, queries, keys, values, out_weight, text_kv)
 
     by_core = [[2 * chip + core for chip in range(CHIPS)] for core in range(2)]
     spread = lax.all_to_all(spread, "grp", 0, 0, axis_index_groups=by_core)
@@ -247,14 +262,24 @@
     def swapped(block, mask):
         return lax.ppermute(block, "seq", [(i, i ^ mask) for i in range(seq_count)])
 
-    pair_in = swapped(cross_out, 1)
+    pair_in = swapped(pair_out, 1)
     far_in = swapped(near, 2)
     cross_in = swapped(cross_out, 3)
 
-    own_pair = jnp.stack([near, pair_in])
-    other_pair = jnp.stack([far_in, cross_in])
-    own_pair, along = lax.optimization_barrier((own_pair, along))
-    along_in = swapped(along, 1)
+    def joined(low, high):
+        return pl.pallas_call(
+            join,
+            out_shape=shape((2, 2, BLOCK, HD), BF16),
+            in_specs=[VMEM] * 2,
+            compiler_params=params(),
+            cost_estimate=pl.CostEstimate(flops=0, bytes_accessed=2**19, transcendentals=0),
+        )(low, high)
+
+    own_pair = joined(near, pair_in)
+    rows_out, _ = lax.optimization_barrier((rows[0], own_pair))
+    after, _ = lax.optimization_barrier((far_in, own_pair))
+    rows_in = swapped(rows_out, 1)
+    other_pair = joined(after, cross_in)
     up = [(i, i + 4) for i in range(seq_count - 4)]
     down = [(i + 4, i) for i in range(seq_count - 4)]
     below = lax.ppermute(own_pair, "seq", up)
@@ -274,17 +299,19 @@
     total = pl.pallas_call(
         first_keys,
         out_shape=shape((PAIR, 2 * HD), F32),
-        in_specs=[VMEM] * 11,
+        in_specs=[VMEM] * 6 + [ANY] * 2 + [VMEM] * 2,
+        scratch_shapes=[pltpu.VMEM((2, 2, BLOCK, HD), BF16)] * 2 + [pltpu.SemaphoreType.DMA((2,))],
         compiler_params=params(),
         cost_estimate=cost(5),
-    )(mask, mine, along_in, near, pair_in, far_in, cross_in, below, above, own_text, core_text)
+    )(mask, mine, near, pair_in, far_in, cross_in, below, above, own_text, core_text)
+    total, rows_in = lax.optimization_barrier((total, rows_in))
     attention = pl.pallas_call(
         last_keys,
         out_shape=shape((2 * CHIPS, BLOCK, HD), BF16),
         in_specs=[VMEM] * 5,
         compiler_params=params(),
         cost_estimate=cost(1),
-    )(mask, mine, along_in, total, beside)
+    )(mask, mine, pair_in, total, beside)
 
     groups = [
         [(2 * pair + odd) * 2 * CHIPS + 2 * chip + core for odd in range(2) for chip in range(CHIPS)]
@@ -300,7 +327,7 @@
         cost_estimate=pl.CostEstimate(
             flops=2 * BLOCK * 1024 * 768, bytes_accessed=3 * 10**6, transcendentals=0
         ),
-    )(place[3], heads, spread, along_in, gate)
+    )(place[2], heads, spread, rows_in, gate)
     other = lax.ppermute(sent, "grp", [(g, g ^ 1) for g in range(2 * CHIPS)])
     result = (kept + gate * other.astype(F32)).astype(BF16)
     across = [
@@ -308,8 +335,7 @@
         for part in range(2)
         for i in range(seq_count)
     ]
-    handed = lax.ppermute(result, ("section", "seq"), across)
-    return handed[None]
+    return lax.ppermute(result[None], ("section", "seq"), across)
 
 
 def solution(mesh):

time: 79 us -> 79.4 us (level)
  the two profiles are of different devices: /device:TPU:24 before, /device:TPU:26 now
where the time goes in v6:
time: 79.4 us; the launch traced here: 78.9 us
  starting transfers between devices  43.2 us (54%)
  blocking collectives  14.6 us (18%)
  waiting for transfers between devices  12.1 us (15%)
  Pallas kernels  7.25 us (9%)
  between operations  0.91 us (1%)
    ppermute x4, starting transfers between devices, swapped(): return lax.ppermute(block, 'seq', [(i, i ^ mask) for i in range(seq_count)])  14.6 us
    all_to_all x1, blocking collectives, body(): lax.all_to_all(attention, ('seq', 'grp'), 0, 0, axis_index_groups=groups)  14.6 us
    ppermute x1, waiting for transfers between devices, body(): return lax.ppermute(result[None], ('section', 'seq'), across)  9.4 us
    ppermute x1, starting transfers between devices, body(): return lax.ppermute(result[None], ('section', 'seq'), across)  8.43 us
    all_to_all x1, starting transfers between devices, body(): spread = lax.all_to_all(spread, 'grp', 0, 0, axis_index_groups=by_core)  4.97 us
    ppermute x1, starting transfers between devices, body(): below = lax.ppermute(own_pair, 'seq', up)  4.7 us
    ppermute x1, starting transfers between devices, body(): beside = lax.ppermute(other_pair, 'seq', mixed)  4.26 us
    pallas_call x1, Pallas kernels, body(): pl.pallas_call(first_keys, out_shape=shape((PAIR, 2 * HD), F32), in_specs...  3.25 us
  transfers between devices with their start and end apart: 11, of which 4 were waited for; matrix products, arithmetic and copies ran while one was open for 0% of the time, Pallas kernels for 4%

profile of v6, /device:TPU:26, one launch (start us, length us, event | category | flops | bytes accessed | tf_op | source)
XLA Modules:
  0.0 78.9 jit_solution(12247979113886757411)
XLA Ops:
  0.7 2.8 %shard_map.100 = (bf16[4,288,768]{2,1,0:T(8,128)(2,1)}, bf16[2,256,128]{2,1,0:T(8,128)(2,1)}, bf16[2,256,128]{2,1,0:T(8,128)(2,1)}, bf16[3,256,128]{2,1,0:T(8,12...) custom-call(s32[1]{0:T(128)} %bitcast.1.pair, s32[1]{0:T(128)} %bitcast.2.odd, s32[1]{0:T(128)} %bitcast.core, ...), custom_call_target="tpu_custom_call" | custom-call | flops 1000000 | bytes 4000000 | tf_op jit(solution)/shard_map/pallas_call | solution.py:244
  3.4 0.0 copy-start.4
  3.4 0.0 copy-start
  3.4 0.0 copy-start.5
  3.5 0.0 copy-start.1
  3.5 0.0 copy-start.3
  3.5 5.0 %all-to-all-start = ((bf16[4,288,768]{2,1,0:T(8,128)(2,1)}), bf16[4,288,768]{2,1,0:T(8,128)(2,1)S(1)}, u32[]{:S(2)}, u32[]{:S(2)}) async-start(bf16[4,288,768]{2,1,0:T(8,128)(2,1)} %get-tuple-element.22), calls=%async_computation | async-start | bytes 3538944 | tf_op jit(solution)/shard_map/all_to_all | solution.py:260
  8.4 0.0 copy-done.4
  8.4 4.3 %collective-permute-start = (bf16[3,256,128]{2,1,0:T(8,128)(2,1)S(1)}, bf16[3,256,128]{2,1,0:T(8,128)(2,1)S(1)}, u32[]{:S(2)}, u32[]{:S(2)}) collective-permute-start(bf16[3,256,128]{2,1,0:T(8,128)(2,1)S(1)} %copy-done.4), channel_id=1, source_target_pairs={{0,8},{8,0},{16,24},{24,16},{32,40},{40,32},{48,56},{56,48},{64,72... | collective-permute-start | bytes 589832 | tf_op jit(solution)/shard_map/ppermute | solution.py:263
  12.7 0.0 copy-done
  12.7 6.1 %collective-permute-start.1 = (bf16[2,256,128]{2,1,0:T(8,128)(2,1)S(1)}, bf16[2,256,128]{2,1,0:T(8,128)(2,1)S(1)}, u32[]{:S(2)}, u32[]{:S(2)}) collective-permute-start(bf16[2,256,128]{2,1,0:T(8,128)(2,1)S(1)} %copy-done), channel_id=1, source_target_pairs={{0,16},{8,24},{16,0},{24,8},{32,48},{40,56},{48,32},{56,40},{64,80... | collective-permute-start | bytes 393224 | tf_op jit(solution)/shard_map/ppermute | solution.py:263
  18.8 0.0 copy-done.5
  18.8 1.9 %collective-permute-start.2 = (bf16[2,256,128]{2,1,0:T(8,128)(2,1)S(1)}, bf16[2,256,128]{2,1,0:T(8,128)(2,1)S(1)}, u32[]{:S(2)}, u32[]{:S(2)}) collective-permute-start(bf16[2,256,128]{2,1,0:T(8,128)(2,1)S(1)} %copy-done.5), channel_id=1, source_target_pairs={{0,24},{8,16},{16,8},{24,0},{32,56},{40,48},{48,40},{56,32},{64,88... | collective-permute-start | bytes 393224 | tf_op jit(solution)/shard_map/ppermute | solution.py:263
  20.8 0.0 collective-permute-done.high_ref.pair_ref
  20.8 2.4 %collective-permute-start.4 = (bf16[2,2,256,128]{3,2,1,0:T(8,128)(2,1)S(1)}, bf16[2,2,256,128]{3,2,1,0:T(8,128)(2,1)}, u32[]{:S(2)}, u32[]{:S(2)}) collective-permute-start(bf16[2,2,256,128]{3,2,1,0:T(8,128)(2,1)S(1)} %shard_map.101), channel_id=1, source_target_pairs={{32,0},{40,8},{48,16},{56,24},{64,32},{72,40},{80,48},{88,56},{96,... | collective-permute-start | bytes 786440 | tf_op jit(solution)/shard_map/ppermute | solution.py:286
  23.2 4.7 %collective-permute-start.3 = (bf16[2,2,256,128]{3,2,1,0:T(8,128)(2,1)S(1)}, bf16[2,2,256,128]{3,2,1,0:T(8,128)(2,1)}, u32[]{:S(2)}, u32[]{:S(2)}) collective-permute-start(bf16[2,2,256,128]{3,2,1,0:T(8,128)(2,1)S(1)} %shard_map.101), channel_id=1, source_target_pairs={{0,32},{8,40},{16,48},{24,56},{32,64},{40,72},{48,80},{56,88},{64,... | collective-permute-start | bytes 786440 | tf_op jit(solution)/shard_map/ppermute | solution.py:285
  27.9 0.1 collective-permute-done.1.far_ref.low_ref
  28.0 2.3 %collective-permute-start.6 = (bf16[256,384]{1,0:T(8,128)(2,1)}, bf16[256,384]{1,0:T(8,128)(2,1)S(1)}, u32[]{:S(2)}, u32[]{:S(2)}) collective-permute-start(bf16[256,384]{1,0:T(8,128)(2,1)} %bitcast.4), channel_id=1, source_target_pairs={{0,8},{8,0},{16,24},{24,16},{32,40},{40,32},{48,56},{56,48},{64,72... | collective-permute-start | bytes 589832 | tf_op jit(solution)/shard_map/ppermute | solution.py:263
  30.4 0.0 collective-permute-done.2.cross_ref.high_ref
  30.4 4.3 %collective-permute-start.7 = (bf16[2,2,256,128]{3,2,1,0:T(8,128)(2,1)S(1)}, bf16[2,2,256,128]{3,2,1,0:T(8,128)(2,1)S(1)}, u32[]{:S(2)}, u32[]{:S(2)}) collective-permute-start(bf16[2,2,256,128]{3,2,1,0:T(8,128)(2,1)S(1)} %shard_map.103), channel_id=1, source_target_pairs={{0,32},{8,40},{32,64},{40,72},{64,96},{72,104},{96,128},{104,136},... | collective-permute-start | bytes 786440 | tf_op jit(solution)/shard_map/ppermute | solution.py:288
  34.7 0.0 all-to-all-done.weight_ref
  34.7 1.9 %collective-permute-start.5 = (bf16[4,32,256]{2,1,0:T(8,128)(2,1)S(1)}, bf16[4,32,256]{2,1,0:T(8,128)(2,1)S(1)}, u32[]{:S(2)}, u32[]{:S(2)}) collective-permute-start(bf16[4,32,256]{2,1,0:T(8,128)(2,1)S(1)} %get-tuple-element.29), channel_id=1, source_target_pairs={{0,1},{1,0},{2,3},{3,2},{4,5},{5,4},{6,7},{7,6},{8,9},{9,8},{10,11... | collective-permute-start | bytes 196616 | tf_op jit(solution)/shard_map/ppermute | solution.py:291
  36.6 0.0 collective-permute-done.4.above_ref
  36.6 0.0 collective-permute-done.3.below_ref
  36.7 1.2 %collective-permute-done.5.core_text = bf16[4,32,256]{2,1,0:T(8,128)(2,1)S(1)} collective-permute-done((bf16[4,32,256]{2,1,0:T(8,128)(2,1)S(1)}, bf16[4,32,256]{2,1,0:T(8,128)(2,1)S(1)}, u32[]{:S(2)}, u32[]{:S(2)}) %collective-permute-start.5) | collective-permute-done | bytes 65568 | tf_op jit(solution)/shard_map/ppermute | solution.py:291
  37.9 0.0 copy-done.1
  37.9 0.0 copy-done.3
  37.9 3.2 %shard_map.102.sum_ref = f32[512,256]{1,0:T(8,128)S(1)} custom-call(f32[8,128]{1,0:T(8,128)S(1)} %copy-done.3, bf16[256,128]{1,0:T(8,128)(2,1)S(1)} %copy-done.1, bf16[2,256,128]{2,1,0:T(8,128)(2,1)S(1)} %copy-done, bf16[3,256,128]{2,1,0:T(8,128)(2,1)S(1)} %collective-permute-done.high_ref.pair_ref, ...), custom_call_target="tpu_custom_call" | custom-call | flops 1342177280 | bytes 1000000 | tf_op jit(solution)/shard_map/pallas_call | solution.py:299
  41.1 0.0 copy-start.2
  41.1 0.0 collective-permute-done.6.rows_ref
  41.1 0.0 collective-permute-done.7.beside_ref
  41.2 0.6 shard_map.104
  41.8 14.6 %all_to_all.10.heads_ref = bf16[8,256,128]{2,1,0:T(8,128)(2,1)S(1)} all-to-all(bf16[8,256,128]{2,1,0:T(8,128)(2,1)S(1)} %shard_map.104), channel_id=1, replica_groups={{0,2,4,6,8,10,12,14},{1,3,5,7,9,11,13,15},{16,18,20,22,24,26,28,30},{17..., dimensions={0} | all-to-all | bytes 1048576 | tf_op jit(solution)/shard_map/all_to_all | solution.py:321
  56.4 0.0 copy-done.2
  56.4 0.6 shard_map.105
  57.0 1.9 %collective-permute-start.8 = (bf16[256,384]{1,0:T(8,128)(2,1)S(1)}, bf16[256,384]{1,0:T(8,128)(2,1)S(1)}, u32[]{:S(2)}, u32[]{:S(2)}) collective-permute-start(bf16[256,384]{1,0:T(8,128)(2,1)S(1)} %get-tuple-element.28), channel_id=1, source_target_pairs={{0,1},{1,0},{2,3},{3,2},{4,5},{5,4},{6,7},{7,6},{8,9},{9,8},{10,11... | collective-permute-start | bytes 589832 | tf_op jit(solution)/shard_map/ppermute | solution.py:331
  58.9 1.4 %collective-permute-done.8 = bf16[256,384]{1,0:T(8,128)(2,1)S(1)} collective-permute-done((bf16[256,384]{1,0:T(8,128)(2,1)S(1)}, bf16[256,384]{1,0:T(8,128)(2,1)S(1)}, u32[]{:S(2)}, u32[]{:S(2)}) %collective-permute-start.8) | collective-permute-done | bytes 196640 | tf_op jit(solution)/shard_map/ppermute | solution.py:331
  60.3 0.1 fusion
  60.3 8.4 %collective-permute-start.9 = (bf16[1,256,384]{2,1,0:T(8,128)(2,1)S(1)}, bf16[1,256,384]{2,1,0:T(8,128)(2,1)S(1)}, u32[]{:S(2)}, u32[]{:S(2)}) collective-permute-start(bf16[1,256,384]{2,1,0:T(8,128)(2,1)S(1)} %fusion), channel_id=1, source_target_pairs={{0,264},{8,256},{16,280},{24,272},{32,296},{40,288},{48,312},{56,3... | collective-permute-start | bytes 589832 | tf_op jit(solution)/shard_map/ppermute | solution.py:338
  68.8 9.4 %collective-permute-done.9 = bf16[1,256,384]{2,1,0:T(8,128)(2,1)S(1)} collective-permute-done((bf16[1,256,384]{2,1,0:T(8,128)(2,1)S(1)}, bf16[1,256,384]{2,1,0:T(8,128)(2,1)S(1)}, u32[]{:S(2)}, u32[]{:S(2)}) %collective-permute-start.9) | collective-permute-done | bytes 196640 | tf_op jit(solution)/shard_map/ppermute | solution.py:338
  78.2 0.7 copy.13
  (4 shorter events, 0.1 us)
Async XLA Ops:
  3.4 5.0 %copy-start.4 = (bf16[3,256,128]{2,1,0:T(8,128)(2,1)S(1)}, bf16[3,256,128]{2,1,0:T(8,128)(2,1)}, u32[]{:S(2)}) copy-start(bf16[3,256,128]{2,1,0:T(8,128)(2,1)} %get-tuple-element.19) | copy-start | bytes 589828
  3.4 9.3 %copy-start = (bf16[2,256,128]{2,1,0:T(8,128)(2,1)S(1)}, bf16[2,256,128]{2,1,0:T(8,128)(2,1)}, u32[]{:S(2)}) copy-start(bf16[2,256,128]{2,1,0:T(8,128)(2,1)} %get-tuple-element.20.low_ref.near_ref) | copy-start | bytes 393220
  3.4 15.4 %copy-start.5 = (bf16[2,256,128]{2,1,0:T(8,128)(2,1)S(1)}, bf16[2,256,128]{2,1,0:T(8,128)(2,1)}, u32[]{:S(2)}) copy-start(bf16[2,256,128]{2,1,0:T(8,128)(2,1)} %get-tuple-element.21) | copy-start | bytes 393220
  3.5 34.4 %copy-start.1 = (bf16[256,128]{1,0:T(8,128)(2,1)S(1)}, bf16[256,128]{1,0:T(8,128)(2,1)}, u32[]{:S(2)}) copy-start(bf16[256,128]{1,0:T(8,128)(2,1)} %get-tuple-element.18.mine_ref) | copy-start | bytes 196612
  3.5 34.4 %copy-start.3 = (f32[8,128]{1,0:T(8,128)S(1)}, f32[8,128]{1,0:T(8,128)}, u32[]{:S(2)}) copy-start(f32[8,128]{1,0:T(8,128)} %get-tuple-element.17.mask_ref) | copy-start | bytes 12292
  3.5 31.2 %all-to-all-start = ((bf16[4,288,768]{2,1,0:T(8,128)(2,1)}), bf16[4,288,768]{2,1,0:T(8,128)(2,1)S(1)}, u32[]{:S(2)}, u32[]{:S(2)}) async-start(bf16[4,288,768]{2,1,0:T(8,128)(2,1)} %get-tuple-element.22), calls=%async_computation | async-start | bytes 3538944 | tf_op jit(solution)/shard_map/all_to_all | solution.py:260
  8.4 12.3 %collective-permute-start = (bf16[3,256,128]{2,1,0:T(8,128)(2,1)S(1)}, bf16[3,256,128]{2,1,0:T(8,128)(2,1)S(1)}, u32[]{:S(2)}, u32[]{:S(2)}) collective-permute-start(bf16[3,256,128]{2,1,0:T(8,128)(2,1)S(1)} %copy-done.4), channel_id=1, source_target_pairs={{0,8},{8,0},{16,24},{24,16},{32,40},{40,32},{48,56},{56,48},{64,72... | collective-permute-start | bytes 589832 | tf_op jit(solution)/shard_map/ppermute | solution.py:263
  12.7 15.3 %collective-permute-start.1 = (bf16[2,256,128]{2,1,0:T(8,128)(2,1)S(1)}, bf16[2,256,128]{2,1,0:T(8,128)(2,1)S(1)}, u32[]{:S(2)}, u32[]{:S(2)}) collective-permute-start(bf16[2,256,128]{2,1,0:T(8,128)(2,1)S(1)} %copy-done), channel_id=1, source_target_pairs={{0,16},{8,24},{16,0},{24,8},{32,48},{40,56},{48,32},{56,40},{64,80... | collective-permute-start | bytes 393224 | tf_op jit(solution)/shard_map/ppermute | solution.py:263
  18.8 11.5 %collective-permute-start.2 = (bf16[2,256,128]{2,1,0:T(8,128)(2,1)S(1)}, bf16[2,256,128]{2,1,0:T(8,128)(2,1)S(1)}, u32[]{:S(2)}, u32[]{:S(2)}) collective-permute-start(bf16[2,256,128]{2,1,0:T(8,128)(2,1)S(1)} %copy-done.5), channel_id=1, source_target_pairs={{0,24},{8,16},{16,8},{24,0},{32,56},{40,48},{48,40},{56,32},{64,88... | collective-permute-start | bytes 393224 | tf_op jit(solution)/shard_map/ppermute | solution.py:263
  20.8 15.8 %collective-permute-start.4 = (bf16[2,2,256,128]{3,2,1,0:T(8,128)(2,1)S(1)}, bf16[2,2,256,128]{3,2,1,0:T(8,128)(2,1)}, u32[]{:S(2)}, u32[]{:S(2)}) collective-permute-start(bf16[2,2,256,128]{3,2,1,0:T(8,128)(2,1)S(1)} %shard_map.101), channel_id=1, source_target_pairs={{32,0},{40,8},{48,16},{56,24},{64,32},{72,40},{80,48},{88,56},{96,... | collective-permute-start | bytes 786440 | tf_op jit(solution)/shard_map/ppermute | solution.py:286
  23.2 13.5 %collective-permute-start.3 = (bf16[2,2,256,128]{3,2,1,0:T(8,128)(2,1)S(1)}, bf16[2,2,256,128]{3,2,1,0:T(8,128)(2,1)}, u32[]{:S(2)}, u32[]{:S(2)}) collective-permute-start(bf16[2,2,256,128]{3,2,1,0:T(8,128)(2,1)S(1)} %shard_map.101), channel_id=1, source_target_pairs={{0,32},{8,40},{16,48},{24,56},{32,64},{40,72},{48,80},{56,88},{64,... | collective-permute-start | bytes 786440 | tf_op jit(solution)/shard_map/ppermute | solution.py:285
  28.0 13.1 %collective-permute-start.6 = (bf16[256,384]{1,0:T(8,128)(2,1)}, bf16[256,384]{1,0:T(8,128)(2,1)S(1)}, u32[]{:S(2)}, u32[]{:S(2)}) collective-permute-start(bf16[256,384]{1,0:T(8,128)(2,1)} %bitcast.4), channel_id=1, source_target_pairs={{0,8},{8,0},{16,24},{24,16},{32,40},{40,32},{48,56},{56,48},{64,72... | collective-permute-start | bytes 589832 | tf_op jit(solution)/shard_map/ppermute | solution.py:263
  30.4 10.7 %collective-permute-start.7 = (bf16[2,2,256,128]{3,2,1,0:T(8,128)(2,1)S(1)}, bf16[2,2,256,128]{3,2,1,0:T(8,128)(2,1)S(1)}, u32[]{:S(2)}, u32[]{:S(2)}) collective-permute-start(bf16[2,2,256,128]{3,2,1,0:T(8,128)(2,1)S(1)} %shard_map.103), channel_id=1, source_target_pairs={{0,32},{8,40},{32,64},{40,72},{64,96},{72,104},{96,128},{104,136},... | collective-permute-start | bytes 786440 | tf_op jit(solution)/shard_map/ppermute | solution.py:288
  34.7 3.1 %collective-permute-start.5 = (bf16[4,32,256]{2,1,0:T(8,128)(2,1)S(1)}, bf16[4,32,256]{2,1,0:T(8,128)(2,1)S(1)}, u32[]{:S(2)}, u32[]{:S(2)}) collective-permute-start(bf16[4,32,256]{2,1,0:T(8,128)(2,1)S(1)} %get-tuple-element.29), channel_id=1, source_target_pairs={{0,1},{1,0},{2,3},{3,2},{4,5},{5,4},{6,7},{7,6},{8,9},{9,8},{10,11... | collective-permute-start | bytes 196616 | tf_op jit(solution)/shard_map/ppermute | solution.py:291
  41.1 15.2 %copy-start.2 = (f32[1,384]{1,0:T(1,128)S(1)}, f32[1,384]{1,0:T(1,128)}, u32[]{:S(2)}) copy-start(f32[1,384]{1,0:T(1,128)} %gate_ref.1) | copy-start | bytes 4612
  57.0 3.3 %collective-permute-start.8 = (bf16[256,384]{1,0:T(8,128)(2,1)S(1)}, bf16[256,384]{1,0:T(8,128)(2,1)S(1)}, u32[]{:S(2)}, u32[]{:S(2)}) collective-permute-start(bf16[256,384]{1,0:T(8,128)(2,1)S(1)} %get-tuple-element.28), channel_id=1, source_target_pairs={{0,1},{1,0},{2,3},{3,2},{4,5},{5,4},{6,7},{7,6},{8,9},{9,8},{10,11... | collective-permute-start | bytes 589832 | tf_op jit(solution)/shard_map/ppermute | solution.py:331
  60.3 17.8 %collective-permute-start.9 = (bf16[1,256,384]{2,1,0:T(8,128)(2,1)S(1)}, bf16[1,256,384]{2,1,0:T(8,128)(2,1)S(1)}, u32[]{:S(2)}, u32[]{:S(2)}) collective-permute-start(bf16[1,256,384]{2,1,0:T(8,128)(2,1)S(1)} %fusion), channel_id=1, source_target_pairs={{0,264},{8,256},{16,280},{24,272},{32,296},{40,288},{48,312},{56,3... | collective-permute-start | bytes 589832 | tf_op jit(solution)/shard_map/ppermute | solution.py:338

commit v7 on v6

--- a/solution.py
+++ b/solution.py
@@ -21,7 +21,6 @@
 F32 = jnp.float32
 SMEM = pl.BlockSpec(memory_space=pltpu.SMEM)
 VMEM = pl.BlockSpec(memory_space=pltpu.VMEM)
-ANY = pl.BlockSpec(memory_space=pl.ANY)
 HBM = pl.BlockSpec(memory_space=pltpu.HBM)
 
 
@@ -178,23 +177,15 @@
 
 def first_keys(
     mask_ref, mine_ref, near_ref, pair_ref, far_ref, cross_ref, below_ref, above_ref,
-    own_text, core_text, total_ref, below, above, sems,
+    own_text, core_text, total_ref,
 ):
-    loads = [
-        pltpu.make_async_copy(source, target, sems.at[i])
-        for i, (source, target) in enumerate(((below_ref, below), (above_ref, above)))
-    ]
-    for load in loads:
-        load.start()
     query = masked_query(mask_ref, mine_ref, pair_ref)
     total = add_keys(None, query, *piece_arrays(0, near_ref, pair_ref))
     total = add_keys(total, query, *piece_arrays(1, far_ref, cross_ref))
     total = add_keys(total, query, *text_arrays(mask_ref, own_text, False))
     total = add_keys(total, query, *text_arrays(mask_ref, core_text, True))
-    loads[0].wait()
-    total = add_keys(total, query, *piece_arrays(2, below.at[0], below.at[1]))
-    loads[1].wait()
-    total_ref[...] = add_keys(total, query, *piece_arrays(3, above.at[0], above.at[1]))
+    total = add_keys(total, query, *piece_arrays(2, below_ref.at[0], below_ref.at[1]))
+    total_ref[...] = add_keys(total, query, *piece_arrays(3, above_ref.at[0], above_ref.at[1]))
 
 
 def last_keys(mask_ref, mine_ref, pair_ref, sum_ref, beside_ref, out_ref):
@@ -275,10 +266,10 @@
             cost_estimate=pl.CostEstimate(flops=0, bytes_accessed=2**19, transcendentals=0),
         )(low, high)
 
+    pair_in, rows_out = lax.optimization_barrier((pair_in, rows[0]))
     own_pair = joined(near, pair_in)
-    rows_out, _ = lax.optimization_barrier((rows[0], own_pair))
+    rows_in = swapped(rows_out, 1)
     after, _ = lax.optimization_barrier((far_in, own_pair))
-    rows_in = swapped(rows_out, 1)
     other_pair = joined(after, cross_in)
     up = [(i, i + 4) for i in range(seq_count - 4)]
     down = [(i + 4, i) for i in range(seq_count - 4)]
@@ -296,15 +287,14 @@
         size = 4 * PAIR * pieces * PAIR * 256
         return pl.CostEstimate(flops=size, bytes_accessed=10**6, transcendentals=PAIR * pieces * PAIR)
 
+    mask, rows_in = lax.optimization_barrier((mask, rows_in))
     total = pl.pallas_call(
         first_keys,
         out_shape=shape((PAIR, 2 * HD), F32),
-        in_specs=[VMEM] * 6 + [ANY] * 2 + [VMEM] * 2,
-        scratch_shapes=[pltpu.VMEM((2, 2, BLOCK, HD), BF16)] * 2 + [pltpu.SemaphoreType.DMA((2,))],
+        in_specs=[VMEM] * 10,
         compiler_params=params(),
         cost_estimate=cost(5),
     )(mask, mine, near, pair_in, far_in, cross_in, below, above, own_text, core_text)
-    total, rows_in = lax.optimization_barrier((total, rows_in))
     attention = pl.pallas_call(
         last_keys,
         out_shape=shape((2 * CHIPS, BLOCK, HD), BF16),

time: 79.4 us -> 77.9 us (0.981)
  the two profiles are of different devices: /device:TPU:26 before, /device:TPU:24 now
where the time goes in v7:
time: 77.9 us; the launch traced here: 77.4 us
  starting transfers between devices  41.5 us (53%)
  blocking collectives  15.8 us (20%)
  waiting for transfers between devices  11.3 us (15%)
  Pallas kernels  7.16 us (9%)
  between operations  0.91 us (1%)
    all_to_all x1, blocking collectives, body(): lax.all_to_all(attention, ('seq', 'grp'), 0, 0, axis_index_groups=groups)  15.8 us
    ppermute x4, starting transfers between devices, swapped(): return lax.ppermute(block, 'seq', [(i, i ^ mask) for i in range(seq_count)])  14.8 us
    ppermute x1, waiting for transfers between devices, body(): return lax.ppermute(result[None], ('section', 'seq'), across)  8.65 us
    ppermute x1, starting transfers between devices, body(): return lax.ppermute(result[None], ('section', 'seq'), across)  7.89 us
    ppermute x1, starting transfers between devices, body(): below = lax.ppermute(own_pair, 'seq', up)  4.7 us
    all_to_all x1, starting transfers between devices, body(): spread = lax.all_to_all(spread, 'grp', 0, 0, axis_index_groups=by_core)  4.44 us
    ppermute x1, starting transfers between devices, body(): beside = lax.ppermute(other_pair, 'seq', mixed)  3.48 us
    pallas_call x1, Pallas kernels, body(): pl.pallas_call(first_keys, out_shape=shape((PAIR, 2 * HD), F32), in_specs...  3.15 us
  transfers between devices with their start and end apart: 11, of which 3 were waited for; matrix products, arithmetic and copies ran while one was open for 0% of the time, Pallas kernels for 4%

profile of v7, /device:TPU:24, one launch (start us, length us, event | category | flops | bytes accessed | tf_op | source)
XLA Modules:
  0.0 77.4 jit_solution(6432622256201871662)
XLA Ops:
  0.7 2.8 %shard_map.100 = (bf16[4,288,768]{2,1,0:T(8,128)(2,1)}, bf16[2,256,128]{2,1,0:T(8,128)(2,1)}, bf16[2,256,128]{2,1,0:T(8,128)(2,1)}, bf16[3,256,128]{2,1,0:T(8,12...) custom-call(s32[1]{0:T(128)} %bitcast.1.pair, s32[1]{0:T(128)} %bitcast.2.odd, s32[1]{0:T(128)} %bitcast.core, ...), custom_call_target="tpu_custom_call" | custom-call | flops 1000000 | bytes 4000000 | tf_op jit(solution)/shard_map/pallas_call | solution.py:235
  3.4 0.0 copy-start.4
  3.4 0.0 copy-start
  3.4 0.0 copy-start.5
  3.5 0.0 copy-start.1
  3.5 0.0 copy-start.3
  3.5 4.4 %all-to-all-start = ((bf16[4,288,768]{2,1,0:T(8,128)(2,1)}), bf16[4,288,768]{2,1,0:T(8,128)(2,1)S(1)}, u32[]{:S(2)}, u32[]{:S(2)}) async-start(bf16[4,288,768]{2,1,0:T(8,128)(2,1)} %get-tuple-element.26), calls=%async_computation | async-start | bytes 3538944 | tf_op jit(solution)/shard_map/all_to_all | solution.py:251
  7.9 0.0 copy-done.4
  7.9 4.3 %collective-permute-start = (bf16[3,256,128]{2,1,0:T(8,128)(2,1)S(1)}, bf16[3,256,128]{2,1,0:T(8,128)(2,1)S(1)}, u32[]{:S(2)}, u32[]{:S(2)}) collective-permute-start(bf16[3,256,128]{2,1,0:T(8,128)(2,1)S(1)} %copy-done.4), channel_id=1, source_target_pairs={{0,8},{8,0},{16,24},{24,16},{32,40},{40,32},{48,56},{56,48},{64,72... | collective-permute-start | bytes 589832 | tf_op jit(solution)/shard_map/ppermute | solution.py:254
  12.2 0.0 copy-done
  12.2 6.1 %collective-permute-start.2 = (bf16[2,256,128]{2,1,0:T(8,128)(2,1)S(1)}, bf16[2,256,128]{2,1,0:T(8,128)(2,1)S(1)}, u32[]{:S(2)}, u32[]{:S(2)}) collective-permute-start(bf16[2,256,128]{2,1,0:T(8,128)(2,1)S(1)} %copy-done), channel_id=1, source_target_pairs={{0,16},{8,24},{16,0},{24,8},{32,48},{40,56},{48,32},{56,40},{64,80... | collective-permute-start | bytes 393224 | tf_op jit(solution)/shard_map/ppermute | solution.py:254
  18.3 0.0 copy-done.5
  18.3 1.9 %collective-permute-start.3 = (bf16[2,256,128]{2,1,0:T(8,128)(2,1)S(1)}, bf16[2,256,128]{2,1,0:T(8,128)(2,1)S(1)}, u32[]{:S(2)}, u32[]{:S(2)}) collective-permute-start(bf16[2,256,128]{2,1,0:T(8,128)(2,1)S(1)} %copy-done.5), channel_id=1, source_target_pairs={{0,24},{8,16},{16,8},{24,0},{32,56},{40,48},{48,40},{56,32},{64,88... | collective-permute-start | bytes 393224 | tf_op jit(solution)/shard_map/ppermute | solution.py:254
  20.2 0.0 collective-permute-done.high_ref.pair_ref
  20.3 2.4 %collective-permute-start.5 = (bf16[2,2,256,128]{3,2,1,0:T(8,128)(2,1)S(1)}, bf16[2,2,256,128]{3,2,1,0:T(8,128)(2,1)}, u32[]{:S(2)}, u32[]{:S(2)}) collective-permute-start(bf16[2,2,256,128]{3,2,1,0:T(8,128)(2,1)S(1)} %shard_map.101), channel_id=1, source_target_pairs={{32,0},{40,8},{48,16},{56,24},{64,32},{72,40},{80,48},{88,56},{96,... | collective-permute-start | bytes 786440 | tf_op jit(solution)/shard_map/ppermute | solution.py:277
  22.6 4.7 %collective-permute-start.4 = (bf16[2,2,256,128]{3,2,1,0:T(8,128)(2,1)S(1)}, bf16[2,2,256,128]{3,2,1,0:T(8,128)(2,1)}, u32[]{:S(2)}, u32[]{:S(2)}) collective-permute-start(bf16[2,2,256,128]{3,2,1,0:T(8,128)(2,1)S(1)} %shard_map.101), channel_id=1, source_target_pairs={{0,32},{8,40},{16,48},{24,56},{32,64},{40,72},{48,80},{56,88},{64,... | collective-permute-start | bytes 786440 | tf_op jit(solution)/shard_map/ppermute | solution.py:276
  27.3 2.5 %collective-permute-start.1 = (bf16[256,384]{1,0:T(8,128)(2,1)}, bf16[256,384]{1,0:T(8,128)(2,1)S(1)}, u32[]{:S(2)}, u32[]{:S(2)}) collective-permute-start(bf16[256,384]{1,0:T(8,128)(2,1)} %bitcast.4), channel_id=1, source_target_pairs={{0,8},{8,0},{16,24},{24,16},{32,40},{40,32},{48,56},{56,48},{64,72... | collective-permute-start | bytes 589832 | tf_op jit(solution)/shard_map/ppermute | solution.py:254
  29.8 0.0 collective-permute-done.2.far_ref.low_ref
  29.8 0.0 collective-permute-done.3.cross_ref.high_ref
  29.9 3.5 %collective-permute-start.7 = (bf16[2,2,256,128]{3,2,1,0:T(8,128)(2,1)S(1)}, bf16[2,2,256,128]{3,2,1,0:T(8,128)(2,1)S(1)}, u32[]{:S(2)}, u32[]{:S(2)}) collective-permute-start(bf16[2,2,256,128]{3,2,1,0:T(8,128)(2,1)S(1)} %shard_map.103), channel_id=1, source_target_pairs={{0,32},{8,40},{32,64},{40,72},{64,96},{72,104},{96,128},{104,136},... | collective-permute-start | bytes 786440 | tf_op jit(solution)/shard_map/ppermute | solution.py:279
  33.4 0.0 all-to-all-done.weight_ref
  33.4 1.9 %collective-permute-start.6 = (bf16[4,32,256]{2,1,0:T(8,128)(2,1)S(1)}, bf16[4,32,256]{2,1,0:T(8,128)(2,1)S(1)}, u32[]{:S(2)}, u32[]{:S(2)}) collective-permute-start(bf16[4,32,256]{2,1,0:T(8,128)(2,1)S(1)} %get-tuple-element.31), channel_id=1, source_target_pairs={{0,1},{1,0},{2,3},{3,2},{4,5},{5,4},{6,7},{7,6},{8,9},{9,8},{10,11... | collective-permute-start | bytes 196616 | tf_op jit(solution)/shard_map/ppermute | solution.py:282
  35.3 0.0 collective-permute-done.1.rows_ref
  35.3 0.0 collective-permute-done.5.above_ref
  35.4 0.0 collective-permute-done.4.below_ref
  35.4 1.2 %collective-permute-done.6.core_text = bf16[4,32,256]{2,1,0:T(8,128)(2,1)S(1)} collective-permute-done((bf16[4,32,256]{2,1,0:T(8,128)(2,1)S(1)}, bf16[4,32,256]{2,1,0:T(8,128)(2,1)S(1)}, u32[]{:S(2)}, u32[]{:S(2)}) %collective-permute-start.6) | collective-permute-done | bytes 65568 | tf_op jit(solution)/shard_map/ppermute | solution.py:282
  36.6 0.0 copy-done.1
  36.6 0.0 copy-done.3
  36.6 3.1 %shard_map.102.sum_ref = f32[512,256]{1,0:T(8,128)S(1)} custom-call(f32[8,128]{1,0:T(8,128)S(1)} %copy-done.3, bf16[256,128]{1,0:T(8,128)(2,1)S(1)} %copy-done.1, bf16[2,256,128]{2,1,0:T(8,128)(2,1)S(1)} %copy-done, bf16[3,256,128]{2,1,0:T(8,128)(2,1)S(1)} %collective-permute-done.high_ref.pair_ref, ...), custom_call_target="tpu_custom_call" | custom-call | flops 1342177280 | bytes 1000000 | tf_op jit(solution)/shard_map/pallas_call | solution.py:291
  39.7 0.0 copy-start.2
  39.7 0.0 collective-permute-done.7.beside_ref
  39.7 0.6 shard_map.104
  40.3 15.8 %all_to_all.10.heads_ref = bf16[8,256,128]{2,1,0:T(8,128)(2,1)S(1)} all-to-all(bf16[8,256,128]{2,1,0:T(8,128)(2,1)S(1)} %shard_map.104), channel_id=1, replica_groups={{0,2,4,6,8,10,12,14},{1,3,5,7,9,11,13,15},{16,18,20,22,24,26,28,30},{17..., dimensions={0} | all-to-all | bytes 1048576 | tf_op jit(solution)/shard_map/all_to_all | solution.py:311
  56.2 0.0 copy-done.2
  56.2 0.6 shard_map.105
  56.8 1.9 %collective-permute-start.8 = (bf16[256,384]{1,0:T(8,128)(2,1)S(1)}, bf16[256,384]{1,0:T(8,128)(2,1)S(1)}, u32[]{:S(2)}, u32[]{:S(2)}) collective-permute-start(bf16[256,384]{1,0:T(8,128)(2,1)S(1)} %get-tuple-element.30), channel_id=1, source_target_pairs={{0,1},{1,0},{2,3},{3,2},{4,5},{5,4},{6,7},{7,6},{8,9},{9,8},{10,11... | collective-permute-start | bytes 589832 | tf_op jit(solution)/shard_map/ppermute | solution.py:321
  58.7 1.4 %collective-permute-done.8 = bf16[256,384]{1,0:T(8,128)(2,1)S(1)} collective-permute-done((bf16[256,384]{1,0:T(8,128)(2,1)S(1)}, bf16[256,384]{1,0:T(8,128)(2,1)S(1)}, u32[]{:S(2)}, u32[]{:S(2)}) %collective-permute-start.8) | collective-permute-done | bytes 196640 | tf_op jit(solution)/shard_map/ppermute | solution.py:321
  60.1 0.1 fusion
  60.2 7.9 %collective-permute-start.9 = (bf16[1,256,384]{2,1,0:T(8,128)(2,1)S(1)}, bf16[1,256,384]{2,1,0:T(8,128)(2,1)S(1)}, u32[]{:S(2)}, u32[]{:S(2)}) collective-permute-start(bf16[1,256,384]{2,1,0:T(8,128)(2,1)S(1)} %fusion), channel_id=1, source_target_pairs={{0,264},{8,256},{16,280},{24,272},{32,296},{40,288},{48,312},{56,3... | collective-permute-start | bytes 589832 | tf_op jit(solution)/shard_map/ppermute | solution.py:328
  68.1 8.7 %collective-permute-done.9 = bf16[1,256,384]{2,1,0:T(8,128)(2,1)S(1)} collective-permute-done((bf16[1,256,384]{2,1,0:T(8,128)(2,1)S(1)}, bf16[1,256,384]{2,1,0:T(8,128)(2,1)S(1)}, u32[]{:S(2)}, u32[]{:S(2)}) %collective-permute-start.9) | collective-permute-done | bytes 196640 | tf_op jit(solution)/shard_map/ppermute | solution.py:328
  76.7 0.7 copy.13
  (4 shorter events, 0.1 us)
Async XLA Ops:
  3.4 4.5 %copy-start.4 = (bf16[3,256,128]{2,1,0:T(8,128)(2,1)S(1)}, bf16[3,256,128]{2,1,0:T(8,128)(2,1)}, u32[]{:S(2)}) copy-start(bf16[3,256,128]{2,1,0:T(8,128)(2,1)} %get-tuple-element.19) | copy-start | bytes 589828
  3.4 8.8 %copy-start = (bf16[2,256,128]{2,1,0:T(8,128)(2,1)S(1)}, bf16[2,256,128]{2,1,0:T(8,128)(2,1)}, u32[]{:S(2)}) copy-start(bf16[2,256,128]{2,1,0:T(8,128)(2,1)} %get-tuple-element.24.low_ref.near_ref) | copy-start | bytes 393220
  3.4 14.9 %copy-start.5 = (bf16[2,256,128]{2,1,0:T(8,128)(2,1)S(1)}, bf16[2,256,128]{2,1,0:T(8,128)(2,1)}, u32[]{:S(2)}) copy-start(bf16[2,256,128]{2,1,0:T(8,128)(2,1)} %get-tuple-element.25) | copy-start | bytes 393220
  3.5 33.1 %copy-start.1 = (bf16[256,128]{1,0:T(8,128)(2,1)S(1)}, bf16[256,128]{1,0:T(8,128)(2,1)}, u32[]{:S(2)}) copy-start(bf16[256,128]{1,0:T(8,128)(2,1)} %get-tuple-element.22.mine_ref) | copy-start | bytes 196612
  3.5 33.1 %copy-start.3 = (f32[8,128]{1,0:T(8,128)S(1)}, f32[8,128]{1,0:T(8,128)}, u32[]{:S(2)}) copy-start(f32[8,128]{1,0:T(8,128)} %get-tuple-element.21.mask_ref) | copy-start | bytes 12292
  3.5 29.9 %all-to-all-start = ((bf16[4,288,768]{2,1,0:T(8,128)(2,1)}), bf16[4,288,768]{2,1,0:T(8,128)(2,1)S(1)}, u32[]{:S(2)}, u32[]{:S(2)}) async-start(bf16[4,288,768]{2,1,0:T(8,128)(2,1)} %get-tuple-element.26), calls=%async_computation | async-start | bytes 3538944 | tf_op jit(solution)/shard_map/all_to_all | solution.py:251
  7.9 12.3 %collective-permute-start = (bf16[3,256,128]{2,1,0:T(8,128)(2,1)S(1)}, bf16[3,256,128]{2,1,0:T(8,128)(2,1)S(1)}, u32[]{:S(2)}, u32[]{:S(2)}) collective-permute-start(bf16[3,256,128]{2,1,0:T(8,128)(2,1)S(1)} %copy-done.4), channel_id=1, source_target_pairs={{0,8},{8,0},{16,24},{24,16},{32,40},{40,32},{48,56},{56,48},{64,72... | collective-permute-start | bytes 589832 | tf_op jit(solution)/shard_map/ppermute | solution.py:254
  12.2 17.6 %collective-permute-start.2 = (bf16[2,256,128]{2,1,0:T(8,128)(2,1)S(1)}, bf16[2,256,128]{2,1,0:T(8,128)(2,1)S(1)}, u32[]{:S(2)}, u32[]{:S(2)}) collective-permute-start(bf16[2,256,128]{2,1,0:T(8,128)(2,1)S(1)} %copy-done), channel_id=1, source_target_pairs={{0,16},{8,24},{16,0},{24,8},{32,48},{40,56},{48,32},{56,40},{64,80... | collective-permute-start | bytes 393224 | tf_op jit(solution)/shard_map/ppermute | solution.py:254
  18.3 11.5 %collective-permute-start.3 = (bf16[2,256,128]{2,1,0:T(8,128)(2,1)S(1)}, bf16[2,256,128]{2,1,0:T(8,128)(2,1)S(1)}, u32[]{:S(2)}, u32[]{:S(2)}) collective-permute-start(bf16[2,256,128]{2,1,0:T(8,128)(2,1)S(1)} %copy-done.5), channel_id=1, source_target_pairs={{0,24},{8,16},{16,8},{24,0},{32,56},{40,48},{48,40},{56,32},{64,88... | collective-permute-start | bytes 393224 | tf_op jit(solution)/shard_map/ppermute | solution.py:254
  20.3 15.1 %collective-permute-start.5 = (bf16[2,2,256,128]{3,2,1,0:T(8,128)(2,1)S(1)}, bf16[2,2,256,128]{3,2,1,0:T(8,128)(2,1)}, u32[]{:S(2)}, u32[]{:S(2)}) collective-permute-start(bf16[2,2,256,128]{3,2,1,0:T(8,128)(2,1)S(1)} %shard_map.101), channel_id=1, source_target_pairs={{32,0},{40,8},{48,16},{56,24},{64,32},{72,40},{80,48},{88,56},{96,... | collective-permute-start | bytes 786440 | tf_op jit(solution)/shard_map/ppermute | solution.py:277
  22.6 12.7 %collective-permute-start.4 = (bf16[2,2,256,128]{3,2,1,0:T(8,128)(2,1)S(1)}, bf16[2,2,256,128]{3,2,1,0:T(8,128)(2,1)}, u32[]{:S(2)}, u32[]{:S(2)}) collective-permute-start(bf16[2,2,256,128]{3,2,1,0:T(8,128)(2,1)S(1)} %shard_map.101), channel_id=1, source_target_pairs={{0,32},{8,40},{16,48},{24,56},{32,64},{40,72},{48,80},{56,88},{64,... | collective-permute-start | bytes 786440 | tf_op jit(solution)/shard_map/ppermute | solution.py:276
  27.3 8.0 %collective-permute-start.1 = (bf16[256,384]{1,0:T(8,128)(2,1)}, bf16[256,384]{1,0:T(8,128)(2,1)S(1)}, u32[]{:S(2)}, u32[]{:S(2)}) collective-permute-start(bf16[256,384]{1,0:T(8,128)(2,1)} %bitcast.4), channel_id=1, source_target_pairs={{0,8},{8,0},{16,24},{24,16},{32,40},{40,32},{48,56},{56,48},{64,72... | collective-permute-start | bytes 589832 | tf_op jit(solution)/shard_map/ppermute | solution.py:254
  29.9 9.8 %collective-permute-start.7 = (bf16[2,2,256,128]{3,2,1,0:T(8,128)(2,1)S(1)}, bf16[2,2,256,128]{3,2,1,0:T(8,128)(2,1)S(1)}, u32[]{:S(2)}, u32[]{:S(2)}) collective-permute-start(bf16[2,2,256,128]{3,2,1,0:T(8,128)(2,1)S(1)} %shard_map.103), channel_id=1, source_target_pairs={{0,32},{8,40},{32,64},{40,72},{64,96},{72,104},{96,128},{104,136},... | collective-permute-start | bytes 786440 | tf_op jit(solution)/shard_map/ppermute | solution.py:279
  33.4 3.1 %collective-permute-start.6 = (bf16[4,32,256]{2,1,0:T(8,128)(2,1)S(1)}, bf16[4,32,256]{2,1,0:T(8,128)(2,1)S(1)}, u32[]{:S(2)}, u32[]{:S(2)}) collective-permute-start(bf16[4,32,256]{2,1,0:T(8,128)(2,1)S(1)} %get-tuple-element.31), channel_id=1, source_target_pairs={{0,1},{1,0},{2,3},{3,2},{4,5},{5,4},{6,7},{7,6},{8,9},{9,8},{10,11... | collective-permute-start | bytes 196616 | tf_op jit(solution)/shard_map/ppermute | solution.py:282
  39.7 16.5 %copy-start.2 = (f32[1,384]{1,0:T(1,128)S(1)}, f32[1,384]{1,0:T(1,128)}, u32[]{:S(2)}) copy-start(f32[1,384]{1,0:T(1,128)} %gate_ref.1) | copy-start | bytes 4612
  56.8 3.3 %collective-permute-start.8 = (bf16[256,384]{1,0:T(8,128)(2,1)S(1)}, bf16[256,384]{1,0:T(8,128)(2,1)S(1)}, u32[]{:S(2)}, u32[]{:S(2)}) collective-permute-start(bf16[256,384]{1,0:T(8,128)(2,1)S(1)} %get-tuple-element.30), channel_id=1, source_target_pairs={{0,1},{1,0},{2,3},{3,2},{4,5},{5,4},{6,7},{7,6},{8,9},{9,8},{10,11... | collective-permute-start | bytes 589832 | tf_op jit(solution)/shard_map/ppermute | solution.py:321
  60.2 16.6 %collective-permute-start.9 = (bf16[1,256,384]{2,1,0:T(8,128)(2,1)S(1)}, bf16[1,256,384]{2,1,0:T(8,128)(2,1)S(1)}, u32[]{:S(2)}, u32[]{:S(2)}) collective-permute-start(bf16[1,256,384]{2,1,0:T(8,128)(2,1)S(1)} %fusion), channel_id=1, source_target_pairs={{0,264},{8,256},{16,280},{24,272},{32,296},{40,288},{48,312},{56,3... | collective-permute-start | bytes 589832 | tf_op jit(solution)/shard_map/ppermute | solution.py:328

commit v8 on v7

--- a/solution.py
+++ b/solution.py
@@ -16,7 +16,7 @@
 EXP2_SCALE = HD ** (-0.5) * math.log2(math.e)
 PIECES = 5
 TEXT_LANE = 4 * PIECES
-COUNT_LANE, ODD_LANE, CORE_LANE = 32, 33, 34
+ODD_LANE, CORE_LANE = 32, 33
 BF16 = jnp.bfloat16
 F32 = jnp.float32
 SMEM = pl.BlockSpec(memory_space=pltpu.SMEM)
@@ -34,9 +34,9 @@
 
 
 def start_out(
-    pair, odd, core, order_ref, band_ref, count_ref, q_ref, k_ref, v_ref, w_ref, t_ref,
+    pair, odd, core, order_ref, band_ref, q_ref, k_ref, v_ref, w_ref, t_ref,
     spread_ref, near_ref, cross_ref, pair_out_ref, mine_ref, mask_ref,
-    q_in, k_in, v_in, t_in, stage, near, mixed, mine, mask, order, band, count, sems, out_sems,
+    q_in, k_in, v_in, t_in, order, band, sems,
 ):
     odd, core = odd[0], core[0]
     depth, slots = w_ref.shape[1], t_ref.shape[2]
@@ -46,36 +46,31 @@
         (v_ref.at[0], v_in),
         (q_ref.at[0], q_in),
         (t_ref.at[0], t_in),
+        (order_ref, order),
+        (band_ref, band),
     ]
     loads += [
-        (w_ref.at[0, :, pl.ds(target * width, width)], stage.at[target, pl.ds(0, depth)])
+        (w_ref.at[0, :, pl.ds(target * width, width)], spread_ref.at[target, pl.ds(0, depth)])
         for target in range(CHIPS)
     ]
-    loads += [(order_ref, order), (band_ref, band), (count_ref, count)]
     loads = [
         pltpu.make_async_copy(source, target, sems.at[i])
         for i, (source, target) in enumerate(loads)
     ]
     for load in loads:
         load.start()
-    sent = []
-
-    def send(source, target):
-        sent.append(pltpu.make_async_copy(source, target, out_sems.at[len(sent)]))
-        sent[-1].start()
 
     def halves(load, ref, prepare):
         load.wait()
         a, b = prepare(ref[:, :HD]), prepare(ref[:, HD:])
         return jnp.where(odd == 0, a, b), jnp.where(odd == 0, b, a)
 
-    near[0], mixed[0] = halves(loads[0], k_in, normed)
-    near[1], mixed[1] = halves(loads[1], v_in, lambda x: x)
-    send(near, near_ref)
-    send(mixed.at[pl.ds(0, 2)], cross_ref)
-    mine[...], mixed[2] = halves(loads[2], q_in, normed)
-    send(mixed, pair_out_ref)
-    send(mine, mine_ref)
+    near_ref[0], key_other = halves(loads[0], k_in, normed)
+    near_ref[1], value_other = halves(loads[1], v_in, lambda x: x)
+    mine_ref[...], pair_out_ref[2] = halves(loads[2], q_in, normed)
+    for ref in (cross_ref, pair_out_ref):
+        ref[0] = key_other
+        ref[1] = value_other
     loads[3].wait()
     for target in range(CHIPS):
         panels = []
@@ -86,20 +81,16 @@
             )
             panels.append((jnp.where(core == 0, one, two), jnp.where(core == 0, two, one)))
         for at, panel in enumerate((panels[0][0], panels[1][0], panels[0][1], panels[1][1])):
-            stage[target, depth:, at * HD : (at + 1) * HD] = panel
-        stage[target, depth:, 4 * HD :] = jnp.zeros((slots, width - 4 * HD), BF16)
-    for load in loads[4 + CHIPS :]:
+            spread_ref[target, depth:, at * HD : (at + 1) * HD] = panel
+        spread_ref[target, depth:, 4 * HD :] = jnp.zeros((slots, width - 4 * HD), BF16)
+    for load in loads[4:6]:
         load.wait()
-    mask[...] = mask_rows(pair[0], odd, core, order, band, count)
-    send(mask, mask_ref)
-    for target, load in enumerate(loads[4 : 4 + CHIPS]):
+    mask_ref[...] = mask_rows(pair[0], odd, core, order, band)
+    for load in loads[6:]:
         load.wait()
-        send(stage.at[target], spread_ref.at[target])
-    for copy in sent:
-        copy.wait()
-
-
-def mask_rows(own, odd, core, order, band, count):
+
+
+def mask_rows(own, odd, core, order, band):
     total = order.shape[0] // 4
 
     def tile_at(pair, slot):
@@ -123,7 +114,7 @@
             held = jnp.where(lane == 4 * piece + slot, tile, held)
     seen = (held >= low) & (held <= high)
     result = jnp.where((lane <= TEXT_LANE) & jnp.logical_not(seen), F32(FAR), F32(0.0))
-    for at, value in ((COUNT_LANE, count[0]), (ODD_LANE, odd), (CORE_LANE, core)):
+    for at, value in ((ODD_LANE, odd), (CORE_LANE, core)):
         result = jnp.where(lane == at, value.astype(F32), result)
     return result
 
@@ -161,7 +152,7 @@
     return key, lanes, value
 
 
-def text_arrays(mask_ref, text_ref, other_core):
+def text_arrays(count, mask_ref, text_ref, other_core):
     text = text_ref[...]
     chips, held, _ = text.shape
     key = normed(text[:, :, :HD].reshape(chips * held, HD))
@@ -171,27 +162,30 @@
     core = mask_ref[0:1, CORE_LANE : CORE_LANE + 1]
     side = 1.0 - core if other_core else core
     slot = (2 * (row // held) * held + row % held).astype(F32) + side * held
-    dead = (lane == TEXT_LANE) & (slot >= mask_ref[0:1, COUNT_LANE : COUNT_LANE + 1])
+    dead = (lane == TEXT_LANE) & (slot >= count[0].astype(F32))
     return key, jnp.where(dead, F32(1.0), F32(0.0)).astype(BF16), value
 
 
 def first_keys(
-    mask_ref, mine_ref, near_ref, pair_ref, far_ref, cross_ref, below_ref, above_ref,
-    own_text, core_text, total_ref,
+    mask_ref, mine_ref, near_ref, pair_ref, far_ref, cross_ref, below_ref, above_ref, total_ref
 ):
     query = masked_query(mask_ref, mine_ref, pair_ref)
     total = add_keys(None, query, *piece_arrays(0, near_ref, pair_ref))
     total = add_keys(total, query, *piece_arrays(1, far_ref, cross_ref))
-    total = add_keys(total, query, *text_arrays(mask_ref, own_text, False))
-    total = add_keys(total, query, *text_arrays(mask_ref, core_text, True))
     total = add_keys(total, query, *piece_arrays(2, below_ref.at[0], below_ref.at[1]))
     total_ref[...] = add_keys(total, query, *piece_arrays(3, above_ref.at[0], above_ref.at[1]))
 
 
-def last_keys(mask_ref, mine_ref, pair_ref, sum_ref, beside_ref, out_ref):
+def last_keys(
+    count, mask_ref, mine_ref, pair_ref, sum_ref, own_text, core_text, beside_ref, out_ref
+):
     query = masked_query(mask_ref, mine_ref, pair_ref)
+    texts = zip(
+        text_arrays(count, mask_ref, own_text, False), text_arrays(count, mask_ref, core_text, True)
+    )
+    total = add_keys(sum_ref[...], query, *(jnp.concatenate(both, axis=0) for both in texts))
     pieces = piece_arrays(PIECES - 1, beside_ref.at[0], beside_ref.at[1])
-    total = add_keys(sum_ref[...], query, *pieces)
+    total = add_keys(total, query, *pieces)
     result = total[:, :HD] / total[:, HD:]
     odd = mask_ref[0:1, ODD_LANE : ODD_LANE + 1] > 0.5
     own, other = result[:BLOCK], result[BLOCK:]
@@ -232,20 +226,20 @@
 
     spread_shape = (CHIPS, depth + slots, 2 * width)
     token_shapes = [(2, BLOCK, HD)] * 2 + [(3, BLOCK, HD), (BLOCK, HD)]
+    loaded = (tile_order, band.T, queries, keys, values, out_weight, text_kv)
     spread, near, cross_out, pair_out, mine, mask = pl.pallas_call(
         start_out,
-        out_shape=[shape(dims, BF16) for dims in [spread_shape, *token_shapes]]
-        + [shape((8, HD), F32)],
-        in_specs=[SMEM] * 3 + [HBM] * 8,
-        out_specs=[HBM] * 6,
+        out_shape=[pltpu.VMEM(dims, BF16) for dims in [spread_shape, *token_shapes]]
+        + [pltpu.VMEM((8, HD), F32)],
+        in_specs=[SMEM] * 3 + [HBM] * 7,
+        out_specs=[VMEM] * 6,
         scratch_shapes=[pltpu.VMEM((BLOCK, 2 * HD), BF16)] * 3
-        + [pltpu.VMEM(dims, BF16) for dims in [text_kv.shape[1:], spread_shape, *token_shapes[1:]]]
-        + [pltpu.VMEM((8, HD), F32)]
-        + [pltpu.SMEM(array.shape, jnp.int32) for array in (tile_order, band.T, text_count)]
-        + [pltpu.SemaphoreType.DMA(dims) for dims in ((7 + CHIPS,), (5 + CHIPS,))],
-        compiler_params=params(60),
+        + [pltpu.VMEM(text_kv.shape[1:], BF16)]
+        + [pltpu.SMEM(array.shape, jnp.int32) for array in loaded[:2]]
+        + [pltpu.SemaphoreType.DMA((6 + CHIPS,))],
+        compiler_params=params(),
         cost_estimate=pl.CostEstimate(flops=10**6, bytes_accessed=4 * 10**6, transcendentals=0),
-    )(*place, tile_order, band.T, text_count, queries, keys, values, out_weight, text_kv)
+    )(*place, *(pltpu.with_memory_space_constraint(a, pltpu.HBM) for a in loaded))
 
     by_core = [[2 * chip + core for chip in range(CHIPS)] for core in range(2)]
     spread = lax.all_to_all(spread, "grp", 0, 0, axis_index_groups=by_core)
@@ -287,21 +281,21 @@
         size = 4 * PAIR * pieces * PAIR * 256
         return pl.CostEstimate(flops=size, bytes_accessed=10**6, transcendentals=PAIR * pieces * PAIR)
 
-    mask, rows_in = lax.optimization_barrier((mask, rows_in))
     total = pl.pallas_call(
         first_keys,
         out_shape=shape((PAIR, 2 * HD), F32),
-        in_specs=[VMEM] * 10,
+        in_specs=[VMEM] * 8,
         compiler_params=params(),
         cost_estimate=cost(5),
-    )(mask, mine, near, pair_in, far_in, cross_in, below, above, own_text, core_text)
+    )(mask, mine, near, pair_in, far_in, cross_in, below, above)
+    total, rows_in = lax.optimization_barrier((total, rows_in))
     attention = pl.pallas_call(
         last_keys,
         out_shape=shape((2 * CHIPS, BLOCK, HD), BF16),
-        in_specs=[VMEM] * 5,
+        in_specs=[SMEM] + [VMEM] * 7,
         compiler_params=params(),
         cost_estimate=cost(1),
-    )(mask, mine, pair_in, total, beside)
+    )(text_count, mask, mine, pair_in, total, own_text, core_text, beside)
 
     groups = [
         [(2 * pair + odd) * 2 * CHIPS + 2 * chip + core for odd in range(2) for chip in range(CHIPS)]

time: 77.9 us -> 76.9 us (0.987)
  waiting for transfers between devices: 11.3 us -> 10.2 us
    ppermute x1, waiting for transfers between devices: 1.19 us -> 0.01 us  [body(): lax.ppermute(spread[:, depth:, 2 * HD:4 * HD], 'grp', [(g, g ^ 1) for g i...]
where the time goes in v8:
time: 76.9 us; the launch traced here: 76.4 us
  starting transfers between devices  41.5 us (54%)
  blocking collectives  16 us (21%)
  waiting for transfers between devices  10.2 us (13%)
  Pallas kernels  7.16 us (9%)
  between operations  0.84 us (1%)
    all_to_all x1, blocking collectives, body(): lax.all_to_all(attention, ('seq', 'grp'), 0, 0, axis_index_groups=groups)  16 us
    ppermute x4, starting transfers between devices, swapped(): return lax.ppermute(block, 'seq', [(i, i ^ mask) for i in range(seq_count)])  14.8 us
    ppermute x1, waiting for transfers between devices, body(): return lax.ppermute(result[None], ('section', 'seq'), across)  8.69 us
    ppermute x1, starting transfers between devices, body(): return lax.ppermute(result[None], ('section', 'seq'), across)  8.02 us
    ppermute x1, starting transfers between devices, body(): below = lax.ppermute(own_pair, 'seq', up)  4.7 us
    all_to_all x1, starting transfers between devices, body(): spread = lax.all_to_all(spread, 'grp', 0, 0, axis_index_groups=by_core)  4.3 us
    ppermute x1, starting transfers between devices, body(): beside = lax.ppermute(other_pair, 'seq', mixed)  3.48 us
    pallas_call x1, Pallas kernels, body(): pl.pallas_call(start_out, out_shape=[pltpu.VMEM(dims, BF16) for dims in [...  2.95 us
  transfers between devices with their start and end apart: 11, of which 3 were waited for; matrix products, arithmetic and copies ran while one was open for 0% of the time, Pallas kernels for 4%

profile of v8, /device:TPU:24, one launch (start us, length us, event | category | flops | bytes accessed | tf_op | source)
XLA Modules:
  0.0 76.4 jit_solution(15176917116037407918)
XLA Ops:
  0.0 2.9 %shard_map.100 = (bf16[4,288,768]{2,1,0:T(8,128)(2,1)}, bf16[2,256,128]{2,1,0:T(8,128)(2,1)S(1)}, bf16[2,256,128]{2,1,0:T(8,128)(2,1)S(1)}, bf16[3,256,128]{2,1,...) custom-call(s32[1]{0:T(128)} %bitcast.1.pair, s32[1]{0:T(128)} %bitcast.2.odd, s32[1]{0:T(128)} %bitcast.core, ...), custom_call_target="tpu_custom_call" | custom-call | flops 1000000 | bytes 4000000 | tf_op jit(solution)/shard_map/pallas_call | solution.py:230
  3.0 4.3 %all-to-all-start = ((bf16[4,288,768]{2,1,0:T(8,128)(2,1)}), bf16[4,288,768]{2,1,0:T(8,128)(2,1)S(1)}, u32[]{:S(2)}, u32[]{:S(2)}) async-start(bf16[4,288,768]{2,1,0:T(8,128)(2,1)} %get-tuple-element.26), calls=%async_computation | async-start | bytes 3538944 | tf_op jit(solution)/shard_map/all_to_all | solution.py:245
  7.3 4.3 %collective-permute-start = (bf16[3,256,128]{2,1,0:T(8,128)(2,1)S(1)}, bf16[3,256,128]{2,1,0:T(8,128)(2,1)S(1)}, u32[]{:S(2)}, u32[]{:S(2)}) collective-permute-start(bf16[3,256,128]{2,1,0:T(8,128)(2,1)S(1)} %get-tuple-element.20), channel_id=1, source_target_pairs={{0,8},{8,0},{16,24},{24,16},{32,40},{40,32},{48,56},{56,48},{64,72... | collective-permute-start | bytes 589832 | tf_op jit(solution)/shard_map/ppermute | solution.py:248
  11.5 6.1 %collective-permute-start.1 = (bf16[2,256,128]{2,1,0:T(8,128)(2,1)S(1)}, bf16[2,256,128]{2,1,0:T(8,128)(2,1)S(1)}, u32[]{:S(2)}, u32[]{:S(2)}) collective-permute-start(bf16[2,256,128]{2,1,0:T(8,128)(2,1)S(1)} %get-tuple-element.22.low_ref.near_ref), channel_id=1, source_target_pairs={{0,16},{8,24},{16,0},{24,8},{32,48},{40,56},{48,32},{56,40},{64,80... | collective-permute-start | bytes 393224 | tf_op jit(solution)/shard_map/ppermute | solution.py:248
  17.6 1.9 %collective-permute-start.2 = (bf16[2,256,128]{2,1,0:T(8,128)(2,1)S(1)}, bf16[2,256,128]{2,1,0:T(8,128)(2,1)S(1)}, u32[]{:S(2)}, u32[]{:S(2)}) collective-permute-start(bf16[2,256,128]{2,1,0:T(8,128)(2,1)S(1)} %get-tuple-element.23), channel_id=1, source_target_pairs={{0,24},{8,16},{16,8},{24,0},{32,56},{40,48},{48,40},{56,32},{64,88... | collective-permute-start | bytes 393224 | tf_op jit(solution)/shard_map/ppermute | solution.py:248
  19.6 0.0 collective-permute-done.high_ref.pair_ref
  19.6 2.4 %collective-permute-start.4 = (bf16[2,2,256,128]{3,2,1,0:T(8,128)(2,1)S(1)}, bf16[2,2,256,128]{3,2,1,0:T(8,128)(2,1)}, u32[]{:S(2)}, u32[]{:S(2)}) collective-permute-start(bf16[2,2,256,128]{3,2,1,0:T(8,128)(2,1)S(1)} %shard_map.101), channel_id=1, source_target_pairs={{32,0},{40,8},{48,16},{56,24},{64,32},{72,40},{80,48},{88,56},{96,... | collective-permute-start | bytes 786440 | tf_op jit(solution)/shard_map/ppermute | solution.py:271
  22.0 4.7 %collective-permute-start.3 = (bf16[2,2,256,128]{3,2,1,0:T(8,128)(2,1)S(1)}, bf16[2,2,256,128]{3,2,1,0:T(8,128)(2,1)}, u32[]{:S(2)}, u32[]{:S(2)}) collective-permute-start(bf16[2,2,256,128]{3,2,1,0:T(8,128)(2,1)S(1)} %shard_map.101), channel_id=1, source_target_pairs={{0,32},{8,40},{16,48},{24,56},{32,64},{40,72},{48,80},{56,88},{64,... | collective-permute-start | bytes 786440 | tf_op jit(solution)/shard_map/ppermute | solution.py:270
  27.3 2.5 %collective-permute-start.5 = (bf16[256,384]{1,0:T(8,128)(2,1)}, bf16[256,384]{1,0:T(8,128)(2,1)S(1)}, u32[]{:S(2)}, u32[]{:S(2)}) collective-permute-start(bf16[256,384]{1,0:T(8,128)(2,1)} %bitcast.4), channel_id=1, source_target_pairs={{0,8},{8,0},{16,24},{24,16},{32,40},{40,32},{48,56},{56,48},{64,72... | collective-permute-start | bytes 589832 | tf_op jit(solution)/shard_map/ppermute | solution.py:248
  29.8 0.0 collective-permute-done.1.far_ref.low_ref
  29.8 0.0 collective-permute-done.2.cross_ref.high_ref
  29.8 3.5 %collective-permute-start.7 = (bf16[2,2,256,128]{3,2,1,0:T(8,128)(2,1)S(1)}, bf16[2,2,256,128]{3,2,1,0:T(8,128)(2,1)S(1)}, u32[]{:S(2)}, u32[]{:S(2)}) collective-permute-start(bf16[2,2,256,128]{3,2,1,0:T(8,128)(2,1)S(1)} %shard_map.103), channel_id=1, source_target_pairs={{0,32},{8,40},{32,64},{40,72},{64,96},{72,104},{96,128},{104,136},... | collective-permute-start | bytes 786440 | tf_op jit(solution)/shard_map/ppermute | solution.py:273
  33.3 0.0 all-to-all-done.weight_ref
  33.4 1.9 %collective-permute-start.6 = (bf16[4,32,256]{2,1,0:T(8,128)(2,1)S(1)}, bf16[4,32,256]{2,1,0:T(8,128)(2,1)S(1)}, u32[]{:S(2)}, u32[]{:S(2)}) collective-permute-start(bf16[4,32,256]{2,1,0:T(8,128)(2,1)S(1)} %get-tuple-element.31), channel_id=1, source_target_pairs={{0,1},{1,0},{2,3},{3,2},{4,5},{5,4},{6,7},{7,6},{8,9},{9,8},{10,11... | collective-permute-start | bytes 196616 | tf_op jit(solution)/shard_map/ppermute | solution.py:276
  35.3 0.0 collective-permute-done.4.above_ref
  35.3 0.0 collective-permute-done.3.below_ref
  35.3 2.7 %shard_map.102.sum_ref = f32[512,256]{1,0:T(8,128)S(1)} custom-call(f32[8,128]{1,0:T(8,128)S(1)} %get-tuple-element.18.mask_ref, bf16[256,128]{1,0:T(8,128)(2,1)S(1)} %get-tuple-element.19.mine_ref, bf16[2,256,128]{2,1,0:T(8,128)(2,1)S(1)} %get-tuple-element.22.low_ref.near_ref, bf16[3,256,128]{2,1,0:T(8,128)(2,1)S(1)} %collective-permute-done.high_ref.pair_ref, ...), custom_call_target="tpu_custom_call" | custom-call | flops 1342177280 | bytes 1000000 | tf_op jit(solution)/shard_map/pallas_call | solution.py:284
  38.0 0.0 copy-start
  38.0 0.0 collective-permute-done.5.rows_ref
  38.1 0.1 collective-permute-done.7.beside_ref
  38.1 0.0 collective-permute-done.6.core_text
  38.1 0.9 %shard_map.104 = bf16[8,256,128]{2,1,0:T(8,128)(2,1)S(1)} custom-call(s32[1]{0:T(128)S(6)} %copy.12.count, f32[8,128]{1,0:T(8,128)S(1)} %get-tuple-element.18.mask_ref, bf16[256,128]{1,0:T(8,128)(2,1)S(1)} %get-tuple-element.19.mine_ref, bf16[3,256,128]{2,1,0:T(8,128)(2,1)S(1)} %collective-permute-done.high_ref.pair_ref, f32[512,256]{1,0:T(8,128)S(1)} %shard_map.102.sum_ref, ...), custom_call_target="tpu_custom_call" | custom-call | flops 268435456 | bytes 1000000 | tf_op jit(solution)/shard_map/pallas_call | solution.py:292
  39.0 16.0 %all_to_all.10.heads_ref = bf16[8,256,128]{2,1,0:T(8,128)(2,1)S(1)} all-to-all(bf16[8,256,128]{2,1,0:T(8,128)(2,1)S(1)} %shard_map.104), channel_id=1, replica_groups={{0,2,4,6,8,10,12,14},{1,3,5,7,9,11,13,15},{16,18,20,22,24,26,28,30},{17..., dimensions={0} | all-to-all | bytes 1048576 | tf_op jit(solution)/shard_map/all_to_all | solution.py:305
  55.0 0.0 copy-done
  55.0 0.6 shard_map.105
  55.6 1.9 %collective-permute-start.8 = (bf16[256,384]{1,0:T(8,128)(2,1)S(1)}, bf16[256,384]{1,0:T(8,128)(2,1)S(1)}, u32[]{:S(2)}, u32[]{:S(2)}) collective-permute-start(bf16[256,384]{1,0:T(8,128)(2,1)S(1)} %get-tuple-element.30), channel_id=1, source_target_pairs={{0,1},{1,0},{2,3},{3,2},{4,5},{5,4},{6,7},{7,6},{8,9},{9,8},{10,11... | collective-permute-start | bytes 589832 | tf_op jit(solution)/shard_map/ppermute | solution.py:315
  57.6 1.4 %collective-permute-done.8 = bf16[256,384]{1,0:T(8,128)(2,1)S(1)} collective-permute-done((bf16[256,384]{1,0:T(8,128)(2,1)S(1)}, bf16[256,384]{1,0:T(8,128)(2,1)S(1)}, u32[]{:S(2)}, u32[]{:S(2)}) %collective-permute-start.8) | collective-permute-done | bytes 196640 | tf_op jit(solution)/shard_map/ppermute | solution.py:315
  59.0 0.1 fusion
  59.0 8.0 %collective-permute-start.9 = (bf16[1,256,384]{2,1,0:T(8,128)(2,1)S(1)}, bf16[1,256,384]{2,1,0:T(8,128)(2,1)S(1)}, u32[]{:S(2)}, u32[]{:S(2)}) collective-permute-start(bf16[1,256,384]{2,1,0:T(8,128)(2,1)S(1)} %fusion), channel_id=1, source_target_pairs={{0,264},{8,256},{16,280},{24,272},{32,296},{40,288},{48,312},{56,3... | collective-permute-start | bytes 589832 | tf_op jit(solution)/shard_map/ppermute | solution.py:322
  67.0 8.7 %collective-permute-done.9 = bf16[1,256,384]{2,1,0:T(8,128)(2,1)S(1)} collective-permute-done((bf16[1,256,384]{2,1,0:T(8,128)(2,1)S(1)}, bf16[1,256,384]{2,1,0:T(8,128)(2,1)S(1)}, u32[]{:S(2)}, u32[]{:S(2)}) %collective-permute-start.9) | collective-permute-done | bytes 196640 | tf_op jit(solution)/shard_map/ppermute | solution.py:322
  75.7 0.7 copy.13
  (4 shorter events, 0.1 us)
Async XLA Ops:
  3.0 30.4 %all-to-all-start = ((bf16[4,288,768]{2,1,0:T(8,128)(2,1)}), bf16[4,288,768]{2,1,0:T(8,128)(2,1)S(1)}, u32[]{:S(2)}, u32[]{:S(2)}) async-start(bf16[4,288,768]{2,1,0:T(8,128)(2,1)} %get-tuple-element.26), calls=%async_computation | async-start | bytes 3538944 | tf_op jit(solution)/shard_map/all_to_all | solution.py:245
  7.3 12.3 %collective-permute-start = (bf16[3,256,128]{2,1,0:T(8,128)(2,1)S(1)}, bf16[3,256,128]{2,1,0:T(8,128)(2,1)S(1)}, u32[]{:S(2)}, u32[]{:S(2)}) collective-permute-start(bf16[3,256,128]{2,1,0:T(8,128)(2,1)S(1)} %get-tuple-element.20), channel_id=1, source_target_pairs={{0,8},{8,0},{16,24},{24,16},{32,40},{40,32},{48,56},{56,48},{64,72... | collective-permute-start | bytes 589832 | tf_op jit(solution)/shard_map/ppermute | solution.py:248
  11.5 18.3 %collective-permute-start.1 = (bf16[2,256,128]{2,1,0:T(8,128)(2,1)S(1)}, bf16[2,256,128]{2,1,0:T(8,128)(2,1)S(1)}, u32[]{:S(2)}, u32[]{:S(2)}) collective-permute-start(bf16[2,256,128]{2,1,0:T(8,128)(2,1)S(1)} %get-tuple-element.22.low_ref.near_ref), channel_id=1, source_target_pairs={{0,16},{8,24},{16,0},{24,8},{32,48},{40,56},{48,32},{56,40},{64,80... | collective-permute-start | bytes 393224 | tf_op jit(solution)/shard_map/ppermute | solution.py:248
  17.6 12.2 %collective-permute-start.2 = (bf16[2,256,128]{2,1,0:T(8,128)(2,1)S(1)}, bf16[2,256,128]{2,1,0:T(8,128)(2,1)S(1)}, u32[]{:S(2)}, u32[]{:S(2)}) collective-permute-start(bf16[2,256,128]{2,1,0:T(8,128)(2,1)S(1)} %get-tuple-element.23), channel_id=1, source_target_pairs={{0,24},{8,16},{16,8},{24,0},{32,56},{40,48},{48,40},{56,32},{64,88... | collective-permute-start | bytes 393224 | tf_op jit(solution)/shard_map/ppermute | solution.py:248
  19.6 15.7 %collective-permute-start.4 = (bf16[2,2,256,128]{3,2,1,0:T(8,128)(2,1)S(1)}, bf16[2,2,256,128]{3,2,1,0:T(8,128)(2,1)}, u32[]{:S(2)}, u32[]{:S(2)}) collective-permute-start(bf16[2,2,256,128]{3,2,1,0:T(8,128)(2,1)S(1)} %shard_map.101), channel_id=1, source_target_pairs={{32,0},{40,8},{48,16},{56,24},{64,32},{72,40},{80,48},{88,56},{96,... | collective-permute-start | bytes 786440 | tf_op jit(solution)/shard_map/ppermute | solution.py:271
  22.0 13.3 %collective-permute-start.3 = (bf16[2,2,256,128]{3,2,1,0:T(8,128)(2,1)S(1)}, bf16[2,2,256,128]{3,2,1,0:T(8,128)(2,1)}, u32[]{:S(2)}, u32[]{:S(2)}) collective-permute-start(bf16[2,2,256,128]{3,2,1,0:T(8,128)(2,1)S(1)} %shard_map.101), channel_id=1, source_target_pairs={{0,32},{8,40},{16,48},{24,56},{32,64},{40,72},{48,80},{56,88},{64,... | collective-permute-start | bytes 786440 | tf_op jit(solution)/shard_map/ppermute | solution.py:270
  27.3 10.7 %collective-permute-start.5 = (bf16[256,384]{1,0:T(8,128)(2,1)}, bf16[256,384]{1,0:T(8,128)(2,1)S(1)}, u32[]{:S(2)}, u32[]{:S(2)}) collective-permute-start(bf16[256,384]{1,0:T(8,128)(2,1)} %bitcast.4), channel_id=1, source_target_pairs={{0,8},{8,0},{16,24},{24,16},{32,40},{40,32},{48,56},{56,48},{64,72... | collective-permute-start | bytes 589832 | tf_op jit(solution)/shard_map/ppermute | solution.py:248
  29.8 8.3 %collective-permute-start.7 = (bf16[2,2,256,128]{3,2,1,0:T(8,128)(2,1)S(1)}, bf16[2,2,256,128]{3,2,1,0:T(8,128)(2,1)S(1)}, u32[]{:S(2)}, u32[]{:S(2)}) collective-permute-start(bf16[2,2,256,128]{3,2,1,0:T(8,128)(2,1)S(1)} %shard_map.103), channel_id=1, source_target_pairs={{0,32},{8,40},{32,64},{40,72},{64,96},{72,104},{96,128},{104,136},... | collective-permute-start | bytes 786440 | tf_op jit(solution)/shard_map/ppermute | solution.py:273
  33.4 4.7 %collective-permute-start.6 = (bf16[4,32,256]{2,1,0:T(8,128)(2,1)S(1)}, bf16[4,32,256]{2,1,0:T(8,128)(2,1)S(1)}, u32[]{:S(2)}, u32[]{:S(2)}) collective-permute-start(bf16[4,32,256]{2,1,0:T(8,128)(2,1)S(1)} %get-tuple-element.31), channel_id=1, source_target_pairs={{0,1},{1,0},{2,3},{3,2},{4,5},{5,4},{6,7},{7,6},{8,9},{9,8},{10,11... | collective-permute-start | bytes 196616 | tf_op jit(solution)/shard_map/ppermute | solution.py:276
  38.0 17.0 %copy-start = (f32[1,384]{1,0:T(1,128)S(1)}, f32[1,384]{1,0:T(1,128)}, u32[]{:S(2)}) copy-start(f32[1,384]{1,0:T(1,128)} %gate_ref.1) | copy-start | bytes 4612
  55.6 3.3 %collective-permute-start.8 = (bf16[256,384]{1,0:T(8,128)(2,1)S(1)}, bf16[256,384]{1,0:T(8,128)(2,1)S(1)}, u32[]{:S(2)}, u32[]{:S(2)}) collective-permute-start(bf16[256,384]{1,0:T(8,128)(2,1)S(1)} %get-tuple-element.30), channel_id=1, source_target_pairs={{0,1},{1,0},{2,3},{3,2},{4,5},{5,4},{6,7},{7,6},{8,9},{9,8},{10,11... | collective-permute-start | bytes 589832 | tf_op jit(solution)/shard_map/ppermute | solution.py:315
  59.0 16.7 %collective-permute-start.9 = (bf16[1,256,384]{2,1,0:T(8,128)(2,1)S(1)}, bf16[1,256,384]{2,1,0:T(8,128)(2,1)S(1)}, u32[]{:S(2)}, u32[]{:S(2)}) collective-permute-start(bf16[1,256,384]{2,1,0:T(8,128)(2,1)S(1)} %fusion), channel_id=1, source_target_pairs={{0,264},{8,256},{16,280},{24,272},{32,296},{40,288},{48,312},{56,3... | collective-permute-start | bytes 589832 | tf_op jit(solution)/shard_map/ppermute | solution.py:322

commit v9 on v8

v9 whole, which is shorter than its diff:
```python
import math

import jax
import jax.numpy as jnp
from jax import lax
from jax.experimental import pallas as pl
from jax.experimental.pallas import tpu as pltpu
from jax.sharding import PartitionSpec as P

HD = 128
TILE = 128
BLOCK = 256
PAIR = 2 * BLOCK
CHIPS = 4
FAR = -30000.0
EXP2_SCALE = HD ** (-0.5) * math.log2(math.e)
PIECES = 5
TEXT_LANE = 4 * PIECES
ODD_LANE = 32

BF16 = jnp.bfloat16
F32 = jnp.float32
SMEM = pl.BlockSpec(memory_space=pltpu.SMEM)
VMEM = pl.BlockSpec(memory_space=pltpu.VMEM)
HBM = pl.BlockSpec(memory_space=pltpu.HBM)


def params(mib=16):
    return pltpu.CompilerParams(vmem_limit_bytes=mib * 1024 * 1024)


def normed(block):
    wide = block.astype(F32)
    return (wide * lax.rsqrt(jnp.mean(wide * wide, axis=-1, keepdims=True) + 1e-06)).astype(BF16)


def start_out(
    pair, odd, order_ref, band_ref, q_ref, k_ref, v_ref, r_ref, w_ref, t_ref,
    spread_ref, near_ref, cross_ref, along_ref, mine_ref, rows_ref, mask_ref,
    q_in, k_in, v_in, t_in, order, band, sems,
):
    odd = odd[0]
    depth, slots = w_ref.shape[1], t_ref.shape[2]
    targets, width = spread_ref.shape[0], spread_ref.shape[2]
    loads = [
        (k_ref.at[0], k_in),
        (v_ref.at[0], v_in),
        (q_ref.at[0], q_in),
        (t_ref.at[0], t_in),
        (order_ref, order),
        (band_ref, band),
        (r_ref.at[0], rows_ref),
    ]
    loads += [
        (w_ref.at[0, :, pl.ds(target * width, width)], spread_ref.at[target, pl.ds(0, depth)])
        for target in range(targets)
    ]
    loads = [
        pltpu.make_async_copy(source, target, sems.at[i])
        for i, (source, target) in enumerate(loads)
    ]
    for load in loads:
        load.start()

    def own_first(a, b):
        return jnp.where(odd == 0, a, b), jnp.where(odd == 0, b, a)

    def halves(load, ref, prepare):
        load.wait()
        return own_first(prepare(ref[:, :HD]), prepare(ref[:, HD:]))

    near_ref[0], key_other = halves(loads[0], k_in, normed)
    near_ref[1], value_other = halves(loads[1], v_in, lambda x: x)
    mine_ref[...], query_other = halves(loads[2], q_in, normed)
    cross_ref[0] = key_other
    cross_ref[1] = value_other
    for at, block in enumerate((key_other, value_other, query_other)):
        along_ref[:, at * HD : (at + 1) * HD] = block
    loads[3].wait()
    for target in range(targets):
        at = 2 * target * HD
        for kind in range(2):
            panel, _ = own_first(t_in[kind, :, at : at + HD], t_in[kind, :, at + HD : at + 2 * HD])
            spread_ref[target, depth:, kind * HD : (kind + 1) * HD] = panel
        spread_ref[target, depth:, 2 * HD :] = jnp.zeros((slots, width - 2 * HD), BF16)
    for load in loads[4:6]:
        load.wait()
    mask_ref[...] = mask_rows(pair[0], odd, order, band)
    for load in loads[6:]:
        load.wait()


def mask_rows(own, odd, order, band):
    total = order.shape[0] // 4

    def tile_at(pair, slot):
        return order[pair * 4 + ((slot // 2) ^ odd) * 2 + slot % 2]

    lane = lax.broadcasted_iota(jnp.int32, (8, HD), 1)
    row = lax.broadcasted_iota(jnp.int32, (8, HD), 0)
    low = jnp.zeros((8, HD), jnp.int32)
    high = jnp.zeros((8, HD), jnp.int32)
    for slot in range(4):
        tile = tile_at(own, slot)
        low = jnp.where(row == slot, band[0, tile], low)
        high = jnp.where(row == slot, band[1, tile], high)
    held = jnp.full((8, HD), -1, jnp.int32)
    beside = own - 1 + 2 * lax.rem(own, 2)
    for piece, pair in enumerate((own, own ^ 1, own - 2, own + 2, beside)):
        inside = (pair >= 0) & (pair < total)
        kept = jnp.clip(pair, 0, total - 1)
        for slot in range(4):
            tile = jnp.where(inside, tile_at(kept, slot), -1)
            held = jnp.where(lane == 4 * piece + slot, tile, held)
    seen = (held >= low) & (held <= high)
    result = jnp.where((lane <= TEXT_LANE) & jnp.logical_not(seen), F32(FAR), F32(0.0))
    return jnp.where(lane == ODD_LANE, odd.astype(F32), result)


def masked_query(mask_ref, mine_ref, along_ref):
    query = jnp.concatenate([mine_ref[...], along_ref[:, 2 * HD : 3 * HD]], axis=0)
    lane = lax.broadcasted_iota(jnp.int32, (TILE, HD), 1)
    lanes = [
        jnp.where(lane <= TEXT_LANE, mask_ref[slot : slot + 1, :], F32(0.0)).astype(BF16)
        for slot in range(4)
    ]
    return jnp.concatenate([query, jnp.concatenate(lanes, axis=0)], axis=1)


def add_keys(total, query, key, key_lanes, value):
    scores = lax.dot_general(
        query,
        jnp.concatenate([key, key_lanes], axis=1),
        (((1,), (1,)), ((), ())),
        preferred_element_type=F32,
    )
    weights = jnp.exp2(scores * EXP2_SCALE).astype(BF16)
    wide = jnp.concatenate([value, jnp.ones_like(value)], axis=1)
    part = lax.dot_general(weights, wide, (((1,), (0,)), ((), ())), preferred_element_type=F32)
    return part if total is None else total + part


def piece_arrays(index, low_ref, high_ref):
    shape = (PAIR, HD)
    row = lax.broadcasted_iota(jnp.int32, shape, 0)
    lane = lax.broadcasted_iota(jnp.int32, shape, 1)
    lanes = jnp.where(lane == 4 * index + row // TILE, F32(1.0), F32(0.0)).astype(BF16)
    key = jnp.concatenate([low_ref[0], high_ref[0]], axis=0)
    value = jnp.concatenate([low_ref[1], high_ref[1]], axis=0)
    return key, lanes, value


def text_arrays(count, text_ref):
    groups, held, _ = text_ref.shape
    text = text_ref[...].reshape(groups * held, 2 * HD)
    shape = (groups * held, HD)
    slot = lax.broadcasted_iota(jnp.int32, shape, 0)
    lane = lax.broadcasted_iota(jnp.int32, shape, 1)
    dead = jnp.where((lane == TEXT_LANE) & (slot >= count[0]), F32(1.0), F32(0.0))
    return normed(text[:, :HD]), dead.astype(BF16), text[:, HD:]


def first_keys(
    mask_ref, mine_ref, along_ref, own_ref, other_ref, below_ref, above_ref, total_ref
):
    query = masked_query(mask_ref, mine_ref, along_ref)
    total = None
    for piece, ref in enumerate((own_ref, other_ref, below_ref, above_ref)):
        total = add_keys(total, query, *piece_arrays(piece, ref.at[0], ref.at[1]))
    total_ref[...] = total


def last_keys(count, mask_ref, mine_ref, along_ref, sum_ref, text_ref, beside_ref, out_ref):
    query = masked_query(mask_ref, mine_ref, along_ref)
    total = add_keys(sum_ref[...], query, *text_arrays(count, text_ref))
    pieces = piece_arrays(PIECES - 1, beside_ref.at[0], beside_ref.at[1])
    total = add_keys(total, query, *pieces)
    result = total[:, :HD] / total[:, HD:]
    odd = mask_ref[0:1, ODD_LANE : ODD_LANE + 1] > 0.5
    own, other = result[:BLOCK], result[BLOCK:]
    to_even = jnp.where(odd, own, other).astype(BF16)
    to_odd = jnp.where(odd, other, own).astype(BF16)
    for chip in range(CHIPS):
        out_ref[chip] = to_even
        out_ref[CHIPS + chip] = to_odd


def join(low_ref, high_ref, out_ref):
    out_ref[0] = low_ref[...]
    out_ref[1] = high_ref[...]


def join_pair(low_ref, along_ref, out_ref):
    out_ref[0] = low_ref[...]
    for kind in range(2):
        out_ref[1, kind] = along_ref[:, kind * HD : (kind + 1) * HD]


def projected(core, heads_ref, weight_ref):
    total = None
    for chip in range(CHIPS):
        heads = jnp.concatenate([heads_ref[chip], heads_ref[CHIPS + chip]], axis=1)
        weight = weight_ref[2 * chip + core, : 2 * HD]
        part = jnp.dot(heads, weight, preferred_element_type=F32)
        total = part if total is None else total + part
    return total


def project_own(core, heads_ref, weight_ref, kept_ref):
    kept_ref[...] = projected(core[0], heads_ref, weight_ref)


def project_other(core, heads_ref, weight_ref, kept_ref, rows_ref, gate_ref, out_ref):
    share = kept_ref[...] + projected(1 - core[0], heads_ref, weight_ref)
    rows = rows_ref[...].astype(F32)
    out_ref[...] = (rows + gate_ref[...] * share).astype(BF16)


def body(rows, queries, keys, values, text_kv, text_count, out_weight, gate, band, tile_order):
    seq_count = lax.axis_size("seq")
    seq = lax.axis_index("seq")
    grp = lax.axis_index("grp")
    place = [at.astype(jnp.int32).reshape(1) for at in (seq >> 1, seq & 1, grp & 1)]
    shape = jax.ShapeDtypeStruct
    width = gate.shape[1]
    depth, slots = out_weight.shape[1], text_kv.shape[2]

    spread_shape = (2 * CHIPS, depth + slots, width)
    token_shapes = [(2, BLOCK, HD)] * 2 + [(BLOCK, 3 * HD), (BLOCK, HD), (BLOCK, width)]
    loaded = (tile_order, band.T, queries, keys, values, rows, out_weight, text_kv)
    spread, near, cross_out, along, mine, rows_out, mask = pl.pallas_call(
        start_out,
        out_shape=[pltpu.VMEM(dims, BF16) for dims in [spread_shape, *token_shapes]]
        + [pltpu.VMEM((8, HD), F32)],
        in_specs=[SMEM] * 2 + [HBM] * 8,
        out_specs=[VMEM] * 7,
        scratch_shapes=[pltpu.VMEM((BLOCK, 2 * HD), BF16)] * 3
        + [pltpu.VMEM(text_kv.shape[1:], BF16)]
        + [pltpu.SMEM(array.shape, jnp.int32) for array in loaded[:2]]
        + [pltpu.SemaphoreType.DMA((7 + 2 * CHIPS,))],
        compiler_params=params(),
        cost_estimate=pl.CostEstimate(flops=10**6, bytes_accessed=4 * 10**6, transcendentals=0),
    )(*place[:2], *(pltpu.with_memory_space_constraint(a, pltpu.HBM) for a in loaded))

    spread = lax.all_to_all(spread, "grp", 0, 0)

    def swapped(block, mask):
        return lax.ppermute(block, "seq", [(i, i ^ mask) for i in range(seq_count)])

    along_in = swapped(along, 1)
    far_in = swapped(near, 2)
    cross_in = swapped(cross_out, 3)

    def joined(kernel, low, high):
        return pl.pallas_call(
            kernel,
            out_shape=shape((2, 2, BLOCK, HD), BF16),
            in_specs=[VMEM] * 2,
            compiler_params=params(),
            cost_estimate=pl.CostEstimate(flops=0, bytes_accessed=2**19, transcendentals=0),
        )(low, high)

    along_in, rows_out = lax.optimization_barrier((along_in, rows_out))
    own_pair = joined(join_pair, near, along_in)
    rows_in = swapped(rows_out, 1)
    after, _ = lax.optimization_barrier((far_in, own_pair))
    other_pair = joined(join, after, cross_in)
    up = [(i, i + 4) for i in range(seq_count - 4)]
    down = [(i + 4, i) for i in range(seq_count - 4)]
    below = lax.ppermute(own_pair, "seq", up)
    above = lax.ppermute(own_pair, "seq", down)
    mixed = [(i, j) for i, j in up if i % 4 < 2] + [(i, j) for i, j in down if i % 4 >= 2]
    beside = lax.ppermute(other_pair, "seq", mixed)
    text = spread[:, depth:, : 2 * HD]

    def cost(pieces):
        size = 4 * PAIR * pieces * PAIR * 256
        return pl.CostEstimate(flops=size, bytes_accessed=10**6, transcendentals=PAIR * pieces * PAIR)

    mask, rows_in = lax.optimization_barrier((mask, rows_in))
    total = pl.pallas_call(
        first_keys,
        out_shape=shape((PAIR, 2 * HD), F32),
        in_specs=[VMEM] * 7,
        compiler_params=params(),
        cost_estimate=cost(5),
    )(mask, mine, along_in, own_pair, other_pair, below, above)
    attention = pl.pallas_call(
        last_keys,
        out_shape=shape((2 * CHIPS, BLOCK, HD), BF16),
        in_specs=[SMEM] + [VMEM] * 6,
        compiler_params=params(),
        cost_estimate=cost(1),
    )(text_count, mask, mine, along_in, total, text, beside)

    groups = [
        [(2 * pair + odd) * 2 * CHIPS + 2 * chip + core for odd in range(2) for chip in range(CHIPS)]
        for pair in range(seq_count // 2)
        for core in range(2)
    ]
    heads = lax.all_to_all(attention, ("seq", "grp"), 0, 0, axis_index_groups=groups)
    other_heads = lax.ppermute(heads, "grp", [(g, g ^ 1) for g in range(2 * CHIPS)])
    half = pl.CostEstimate(flops=2 * BLOCK * 1024 * 384, bytes_accessed=10**6, transcendentals=0)
    kept = pl.pallas_call(
        project_own,
        out_shape=shape((BLOCK, width), F32),
        in_specs=[SMEM] + [VMEM] * 2,
        compiler_params=params(),
        cost_estimate=half,
    )(place[2], heads, spread)
    result = pl.pallas_call(
        project_other,
        out_shape=shape((BLOCK, width), BF16),
        in_specs=[SMEM] + [VMEM] * 5,
        compiler_params=params(),
        cost_estimate=half,
    )(place[2], other_heads, spread, kept, rows_in, gate)
    across = [
        (part * seq_count + i, (1 - part) * seq_count + (i ^ 1))
        for part in range(2)
        for i in range(seq_count)
    ]
    return lax.ppermute(result[None], ("section", "seq"), across)


def solution(mesh):
    placed = (
        P("section", "seq", "grp"),
        P("section", "seq", "grp"),
        P("section", "seq", "grp"),
        P("section", "seq", "grp"),
        P("section", None, "grp", None),
        P("section"),
        P("section", "grp", None),
        P("section", "grp"),
        P(),
        P(),
    )
    return jax.shard_map(
        body, mesh=mesh, in_specs=placed, out_specs=P("section", "seq", "grp"), check_vma=False
    )
```

time: 76.9 us -> 76.5 us (level)
  the two profiles are of different devices: /device:TPU:24 before, /device:TPU:34 now
where the time goes in v9:
time: 76.5 us; the launch traced here: 76 us
  starting transfers between devices  38.2 us (50%)
  waiting for transfers between devices  16.1 us (21%)
  blocking collectives  13.7 us (18%)
  Pallas kernels  6.49 us (8%)
  between operations  0.82 us (1%)
    ppermute x4, starting transfers between devices, swapped(): return lax.ppermute(block, 'seq', [(i, i ^ mask) for i in range(seq_count)])  14.7 us
    all_to_all x1, blocking collectives, body(): lax.all_to_all(attention, ('seq', 'grp'), 0, 0, axis_index_groups=groups)  13.7 us
    ppermute x1, waiting for transfers between devices, body(): return lax.ppermute(result[None], ('section', 'seq'), across)  9.4 us
    ppermute x1, starting transfers between devices, body(): return lax.ppermute(result[None], ('section', 'seq'), across)  8.25 us
    all_to_all x1, starting transfers between devices, body(): spread = lax.all_to_all(spread, 'grp', 0, 0)  4.84 us
    ppermute x1, starting transfers between devices, body(): below = lax.ppermute(own_pair, 'seq', up)  3.48 us
    ppermute x1, waiting for transfers between devices, body(): beside = lax.ppermute(other_pair, 'seq', mixed)  3.3 us
    pallas_call x1, Pallas kernels, body(): pl.pallas_call(start_out, out_shape=[pltpu.VMEM(dims, BF16) for dims in [...  3.03 us
  transfers between devices with their start and end apart: 10, of which 4 were waited for; matrix products, arithmetic and copies ran while one was open for 0% of the time, Pallas kernels for 3%

profile of v9, /device:TPU:34, one launch (start us, length us, event | category | flops | bytes accessed | tf_op | source)
XLA Modules:
  0.0 76.0 jit_solution(15012612596057869732)
XLA Ops:
  0.0 3.0 %shard_map.100 = (bf16[8,288,384]{2,1,0:T(8,128)(2,1)}, bf16[2,256,128]{2,1,0:T(8,128)(2,1)S(1)}, bf16[2,256,128]{2,1,0:T(8,128)(2,1)S(1)}, bf16[256,384]{1,0:T(...) custom-call(s32[1]{0:T(128)} %bitcast.1.pair, s32[1]{0:T(128)} %bitcast.2.odd, ...), custom_call_target="tpu_custom_call" | custom-call | flops 1000000 | bytes 4000000 | tf_op jit(solution)/shard_map/pallas_call | solution.py:231
  3.0 4.8 %all-to-all-start = ((bf16[8,288,384]{2,1,0:T(8,128)(2,1)}), bf16[8,288,384]{2,1,0:T(8,128)(2,1)S(1)}, u32[]{:S(2)}, u32[]{:S(2)}) async-start(bf16[8,288,384]{2,1,0:T(8,128)(2,1)} %get-tuple-element.27), calls=%async_computation | async-start | bytes 3538944 | tf_op jit(solution)/shard_map/all_to_all | solution.py:245
  7.9 4.3 %collective-permute-start = (bf16[256,384]{1,0:T(8,128)(2,1)S(1)}, bf16[256,384]{1,0:T(8,128)(2,1)S(1)}, u32[]{:S(2)}, u32[]{:S(2)}) collective-permute-start(bf16[256,384]{1,0:T(8,128)(2,1)S(1)} %get-tuple-element.18), channel_id=1, source_target_pairs={{0,8},{8,0},{16,24},{24,16},{32,40},{40,32},{48,56},{56,48},{64,72... | collective-permute-start | bytes 589832 | tf_op jit(solution)/shard_map/ppermute | solution.py:248
  12.2 6.1 %collective-permute-start.2 = (bf16[2,256,128]{2,1,0:T(8,128)(2,1)S(1)}, bf16[2,256,128]{2,1,0:T(8,128)(2,1)S(1)}, u32[]{:S(2)}, u32[]{:S(2)}) collective-permute-start(bf16[2,256,128]{2,1,0:T(8,128)(2,1)S(1)} %get-tuple-element.24.low_ref), channel_id=1, source_target_pairs={{0,16},{8,24},{16,0},{24,8},{32,48},{40,56},{48,32},{56,40},{64,80... | collective-permute-start | bytes 393224 | tf_op jit(solution)/shard_map/ppermute | solution.py:248
  18.3 1.9 %collective-permute-start.3 = (bf16[2,256,128]{2,1,0:T(8,128)(2,1)S(1)}, bf16[2,256,128]{2,1,0:T(8,128)(2,1)S(1)}, u32[]{:S(2)}, u32[]{:S(2)}) collective-permute-start(bf16[2,256,128]{2,1,0:T(8,128)(2,1)S(1)} %get-tuple-element.26), channel_id=1, source_target_pairs={{0,24},{8,16},{16,8},{24,0},{32,56},{40,48},{48,40},{56,32},{64,88... | collective-permute-start | bytes 393224 | tf_op jit(solution)/shard_map/ppermute | solution.py:248
  20.2 0.0 collective-permute-done.along_ref
  20.2 2.4 %collective-permute-start.5 = (bf16[2,2,256,128]{3,2,1,0:T(8,128)(2,1)S(1)}, bf16[2,2,256,128]{3,2,1,0:T(8,128)(2,1)S(1)}, u32[]{:S(2)}, u32[]{:S(2)}) collective-permute-start(bf16[2,2,256,128]{3,2,1,0:T(8,128)(2,1)S(1)} %shard_map.101.own_ref), channel_id=1, source_target_pairs={{32,0},{40,8},{48,16},{56,24},{64,32},{72,40},{80,48},{88,56},{96,... | collective-permute-start | bytes 786440 | tf_op jit(solution)/shard_map/ppermute | solution.py:271
  22.6 3.5 %collective-permute-start.4 = (bf16[2,2,256,128]{3,2,1,0:T(8,128)(2,1)S(1)}, bf16[2,2,256,128]{3,2,1,0:T(8,128)(2,1)S(1)}, u32[]{:S(2)}, u32[]{:S(2)}) collective-permute-start(bf16[2,2,256,128]{3,2,1,0:T(8,128)(2,1)S(1)} %shard_map.101.own_ref), channel_id=1, source_target_pairs={{0,32},{8,40},{16,48},{24,56},{32,64},{40,72},{48,80},{56,88},{64,... | collective-permute-start | bytes 786440 | tf_op jit(solution)/shard_map/ppermute | solution.py:270
  26.1 2.5 %collective-permute-start.1 = (bf16[256,384]{1,0:T(8,128)(2,1)S(1)}, bf16[256,384]{1,0:T(8,128)(2,1)S(1)}, u32[]{:S(2)}, u32[]{:S(2)}) collective-permute-start(bf16[256,384]{1,0:T(8,128)(2,1)S(1)} %get-tuple-element.20), channel_id=1, source_target_pairs={{0,8},{8,0},{16,24},{24,16},{32,40},{40,32},{48,56},{56,48},{64,72... | collective-permute-start | bytes 589832 | tf_op jit(solution)/shard_map/ppermute | solution.py:248
  28.6 0.0 collective-permute-done.2.low_ref
  28.6 0.0 collective-permute-done.3.high_ref
  28.6 2.6 %collective-permute-start.6 = (bf16[2,2,256,128]{3,2,1,0:T(8,128)(2,1)S(1)}, bf16[2,2,256,128]{3,2,1,0:T(8,128)(2,1)S(1)}, u32[]{:S(2)}, u32[]{:S(2)}) collective-permute-start(bf16[2,2,256,128]{3,2,1,0:T(8,128)(2,1)S(1)} %shard_map.102.other_ref), channel_id=1, source_target_pairs={{0,32},{8,40},{32,64},{40,72},{64,96},{72,104},{96,128},{104,136},... | collective-permute-start | bytes 786440 | tf_op jit(solution)/shard_map/ppermute | solution.py:273
  31.9 2.0 %collective-permute-done.1.rows_ref = bf16[256,384]{1,0:T(8,128)(2,1)S(1)} collective-permute-done((bf16[256,384]{1,0:T(8,128)(2,1)S(1)}, bf16[256,384]{1,0:T(8,128)(2,1)S(1)}, u32[]{:S(2)}, u32[]{:S(2)}) %collective-permute-start.1) | collective-permute-done | bytes 196640 | tf_op jit(solution)/shard_map/ppermute | solution.py:248
  33.8 0.0 collective-permute-done.5.above_ref
  33.8 0.0 collective-permute-done.4.below_ref
  33.8 1.7 %shard_map.103.sum_ref = f32[512,256]{1,0:T(8,128)S(1)} custom-call(f32[8,128]{1,0:T(8,128)S(1)} %get-tuple-element.21.mask_ref, bf16[256,128]{1,0:T(8,128)(2,1)S(1)} %get-tuple-element.22.mine_ref, bf16[256,384]{1,0:T(8,128)(2,1)S(1)} %collective-permute-done.along_ref, bf16[2,2,256,128]{3,2,1,0:T(8,128)(2,1)S(1)} %shard_map.101.own_ref, ...), custom_call_target="tpu_custom_call" | custom-call | flops 1342177280 | bytes 1000000 | tf_op jit(solution)/shard_map/pallas_call | solution.py:281
  35.5 0.0 all-to-all-done.weight_ref
  35.5 3.3 %collective-permute-done.6.beside_ref = bf16[2,2,256,128]{3,2,1,0:T(8,128)(2,1)S(1)} collective-permute-done((bf16[2,2,256,128]{3,2,1,0:T(8,128)(2,1)S(1)}, bf16[2,2,256,128]{3,2,1,0:T(8,128)(2,1)S(1)}, u32[]{:S(2)}, u32[]{:S(2)}) %collective-permute-start.6) | collective-permute-done | bytes 262176 | tf_op jit(solution)/shard_map/ppermute | solution.py:273
  38.8 0.8 %shard_map.104 = bf16[8,256,128]{2,1,0:T(8,128)(2,1)S(1)} custom-call(s32[1]{0:T(128)S(6)} %copy.12.count, f32[8,128]{1,0:T(8,128)S(1)} %get-tuple-element.21.mask_ref, bf16[256,128]{1,0:T(8,128)(2,1)S(1)} %get-tuple-element.22.mine_ref, bf16[256,384]{1,0:T(8,128)(2,1)S(1)} %collective-permute-done.along_ref, f32[512,256]{1,0:T(8,128)S(1)} %shard_map.103.sum_ref, ...), custom_call_target="tpu_custom_call" | custom-call | flops 268435456 | bytes 1000000 | tf_op jit(solution)/shard_map/pallas_call | solution.py:288
  39.7 0.0 copy-start
  39.7 13.7 %all_to_all.10.heads_ref = bf16[8,256,128]{2,1,0:T(8,128)(2,1)S(1)} all-to-all(bf16[8,256,128]{2,1,0:T(8,128)(2,1)S(1)} %shard_map.104), channel_id=1, replica_groups={{0,2,4,6,8,10,12,14},{1,3,5,7,9,11,13,15},{16,18,20,22,24,26,28,30},{17..., dimensions={0} | all-to-all | bytes 1048576 | tf_op jit(solution)/shard_map/all_to_all | solution.py:301
  53.4 1.9 %collective-permute-start.7 = (bf16[8,256,128]{2,1,0:T(8,128)(2,1)S(1)}, bf16[8,256,128]{2,1,0:T(8,128)(2,1)S(1)}, u32[]{:S(2)}, u32[]{:S(2)}) collective-permute-start(bf16[8,256,128]{2,1,0:T(8,128)(2,1)S(1)} %all_to_all.10.heads_ref), channel_id=1, source_target_pairs={{0,1},{1,0},{2,3},{3,2},{4,5},{5,4},{6,7},{7,6},{8,9},{9,8},{10,11... | collective-permute-start | bytes 1572872 | tf_op jit(solution)/shard_map/ppermute | solution.py:302
  55.3 0.4 shard_map.105.kept_ref
  55.8 1.4 %collective-permute-done.7.heads_ref = bf16[8,256,128]{2,1,0:T(8,128)(2,1)S(1)} collective-permute-done((bf16[8,256,128]{2,1,0:T(8,128)(2,1)S(1)}, bf16[8,256,128]{2,1,0:T(8,128)(2,1)S(1)}, u32[]{:S(2)}, u32[]{:S(2)}) %collective-permute-start.7) | collective-permute-done | bytes 524320 | tf_op jit(solution)/shard_map/ppermute | solution.py:302
  57.2 0.0 copy-done
  57.2 0.4 shard_map.106
  57.7 8.2 %collective-permute-start.8 = (bf16[1,256,384]{2,1,0:T(8,128)(2,1)S(1)}, bf16[1,256,384]{2,1,0:T(8,128)(2,1)S(1)}, u32[]{:S(2)}, u32[]{:S(2)}) collective-permute-start(bf16[1,256,384]{2,1,0:T(8,128)(2,1)S(1)} %bitcast.5), channel_id=1, source_target_pairs={{0,264},{8,256},{16,280},{24,272},{32,296},{40,288},{48,312},{56,3... | collective-permute-start | bytes 589832 | tf_op jit(solution)/shard_map/ppermute | solution.py:323
  65.9 9.4 %collective-permute-done.8 = bf16[1,256,384]{2,1,0:T(8,128)(2,1)S(1)} collective-permute-done((bf16[1,256,384]{2,1,0:T(8,128)(2,1)S(1)}, bf16[1,256,384]{2,1,0:T(8,128)(2,1)S(1)}, u32[]{:S(2)}, u32[]{:S(2)}) %collective-permute-start.8) | collective-permute-done | bytes 196640 | tf_op jit(solution)/shard_map/ppermute | solution.py:323
  75.3 0.7 copy.13
  (3 shorter events, 0.1 us)
Async XLA Ops:
  3.0 32.5 %all-to-all-start = ((bf16[8,288,384]{2,1,0:T(8,128)(2,1)}), bf16[8,288,384]{2,1,0:T(8,128)(2,1)S(1)}, u32[]{:S(2)}, u32[]{:S(2)}) async-start(bf16[8,288,384]{2,1,0:T(8,128)(2,1)} %get-tuple-element.27), calls=%async_computation | async-start | bytes 3538944 | tf_op jit(solution)/shard_map/all_to_all | solution.py:245
  7.9 12.3 %collective-permute-start = (bf16[256,384]{1,0:T(8,128)(2,1)S(1)}, bf16[256,384]{1,0:T(8,128)(2,1)S(1)}, u32[]{:S(2)}, u32[]{:S(2)}) collective-permute-start(bf16[256,384]{1,0:T(8,128)(2,1)S(1)} %get-tuple-element.18), channel_id=1, source_target_pairs={{0,8},{8,0},{16,24},{24,16},{32,40},{40,32},{48,56},{56,48},{64,72... | collective-permute-start | bytes 589832 | tf_op jit(solution)/shard_map/ppermute | solution.py:248
  12.2 16.4 %collective-permute-start.2 = (bf16[2,256,128]{2,1,0:T(8,128)(2,1)S(1)}, bf16[2,256,128]{2,1,0:T(8,128)(2,1)S(1)}, u32[]{:S(2)}, u32[]{:S(2)}) collective-permute-start(bf16[2,256,128]{2,1,0:T(8,128)(2,1)S(1)} %get-tuple-element.24.low_ref), channel_id=1, source_target_pairs={{0,16},{8,24},{16,0},{24,8},{32,48},{40,56},{48,32},{56,40},{64,80... | collective-permute-start | bytes 393224 | tf_op jit(solution)/shard_map/ppermute | solution.py:248
  18.3 10.3 %collective-permute-start.3 = (bf16[2,256,128]{2,1,0:T(8,128)(2,1)S(1)}, bf16[2,256,128]{2,1,0:T(8,128)(2,1)S(1)}, u32[]{:S(2)}, u32[]{:S(2)}) collective-permute-start(bf16[2,256,128]{2,1,0:T(8,128)(2,1)S(1)} %get-tuple-element.26), channel_id=1, source_target_pairs={{0,24},{8,16},{16,8},{24,0},{32,56},{40,48},{48,40},{56,32},{64,88... | collective-permute-start | bytes 393224 | tf_op jit(solution)/shard_map/ppermute | solution.py:248
  20.2 13.6 %collective-permute-start.5 = (bf16[2,2,256,128]{3,2,1,0:T(8,128)(2,1)S(1)}, bf16[2,2,256,128]{3,2,1,0:T(8,128)(2,1)S(1)}, u32[]{:S(2)}, u32[]{:S(2)}) collective-permute-start(bf16[2,2,256,128]{3,2,1,0:T(8,128)(2,1)S(1)} %shard_map.101.own_ref), channel_id=1, source_target_pairs={{32,0},{40,8},{48,16},{56,24},{64,32},{72,40},{80,48},{88,56},{96,... | collective-permute-start | bytes 786440 | tf_op jit(solution)/shard_map/ppermute | solution.py:271
  22.6 11.2 %collective-permute-start.4 = (bf16[2,2,256,128]{3,2,1,0:T(8,128)(2,1)S(1)}, bf16[2,2,256,128]{3,2,1,0:T(8,128)(2,1)S(1)}, u32[]{:S(2)}, u32[]{:S(2)}) collective-permute-start(bf16[2,2,256,128]{3,2,1,0:T(8,128)(2,1)S(1)} %shard_map.101.own_ref), channel_id=1, source_target_pairs={{0,32},{8,40},{16,48},{24,56},{32,64},{40,72},{48,80},{56,88},{64,... | collective-permute-start | bytes 786440 | tf_op jit(solution)/shard_map/ppermute | solution.py:270
  26.1 7.7 %collective-permute-start.1 = (bf16[256,384]{1,0:T(8,128)(2,1)S(1)}, bf16[256,384]{1,0:T(8,128)(2,1)S(1)}, u32[]{:S(2)}, u32[]{:S(2)}) collective-permute-start(bf16[256,384]{1,0:T(8,128)(2,1)S(1)} %get-tuple-element.20), channel_id=1, source_target_pairs={{0,8},{8,0},{16,24},{24,16},{32,40},{40,32},{48,56},{56,48},{64,72... | collective-permute-start | bytes 589832 | tf_op jit(solution)/shard_map/ppermute | solution.py:248
  28.6 10.2 %collective-permute-start.6 = (bf16[2,2,256,128]{3,2,1,0:T(8,128)(2,1)S(1)}, bf16[2,2,256,128]{3,2,1,0:T(8,128)(2,1)S(1)}, u32[]{:S(2)}, u32[]{:S(2)}) collective-permute-start(bf16[2,2,256,128]{3,2,1,0:T(8,128)(2,1)S(1)} %shard_map.102.other_ref), channel_id=1, source_target_pairs={{0,32},{8,40},{32,64},{40,72},{64,96},{72,104},{96,128},{104,136},... | collective-permute-start | bytes 786440 | tf_op jit(solution)/shard_map/ppermute | solution.py:273
  39.7 17.5 %copy-start = (f32[1,384]{1,0:T(1,128)S(1)}, f32[1,384]{1,0:T(1,128)}, u32[]{:S(2)}) copy-start(f32[1,384]{1,0:T(1,128)} %gate_ref.1) | copy-start | bytes 4612
  53.4 3.8 %collective-permute-start.7 = (bf16[8,256,128]{2,1,0:T(8,128)(2,1)S(1)}, bf16[8,256,128]{2,1,0:T(8,128)(2,1)S(1)}, u32[]{:S(2)}, u32[]{:S(2)}) collective-permute-start(bf16[8,256,128]{2,1,0:T(8,128)(2,1)S(1)} %all_to_all.10.heads_ref), channel_id=1, source_target_pairs={{0,1},{1,0},{2,3},{3,2},{4,5},{5,4},{6,7},{7,6},{8,9},{9,8},{10,11... | collective-permute-start | bytes 1572872 | tf_op jit(solution)/shard_map/ppermute | solution.py:302
  57.7 17.7 %collective-permute-start.8 = (bf16[1,256,384]{2,1,0:T(8,128)(2,1)S(1)}, bf16[1,256,384]{2,1,0:T(8,128)(2,1)S(1)}, u32[]{:S(2)}, u32[]{:S(2)}) collective-permute-start(bf16[1,256,384]{2,1,0:T(8,128)(2,1)S(1)} %bitcast.5), channel_id=1, source_target_pairs={{0,264},{8,256},{16,280},{24,272},{32,296},{40,288},{48,312},{56,3... | collective-permute-start | bytes 589832 | tf_op jit(solution)/shard_map/ppermute | solution.py:323

commit v10 on v8

--- a/solution.py
+++ b/solution.py
@@ -36,7 +36,7 @@
 def start_out(
     pair, odd, core, order_ref, band_ref, q_ref, k_ref, v_ref, w_ref, t_ref,
     spread_ref, near_ref, cross_ref, pair_out_ref, mine_ref, mask_ref,
-    q_in, k_in, v_in, t_in, order, band, sems,
+    q_in, k_in, v_in, t_in, stage, order, band, sems, out_sems,
 ):
     odd, core = odd[0], core[0]
     depth, slots = w_ref.shape[1], t_ref.shape[2]
@@ -50,7 +50,7 @@
         (band_ref, band),
     ]
     loads += [
-        (w_ref.at[0, :, pl.ds(target * width, width)], spread_ref.at[target, pl.ds(0, depth)])
+        (w_ref.at[0, :, pl.ds(target * width, width)], stage.at[target, pl.ds(0, depth)])
         for target in range(CHIPS)
     ]
     loads = [
@@ -67,10 +67,11 @@
 
     near_ref[0], key_other = halves(loads[0], k_in, normed)
     near_ref[1], value_other = halves(loads[1], v_in, lambda x: x)
-    mine_ref[...], pair_out_ref[2] = halves(loads[2], q_in, normed)
-    for ref in (cross_ref, pair_out_ref):
-        ref[0] = key_other
-        ref[1] = value_other
+    mine_ref[...], query_other = halves(loads[2], q_in, normed)
+    cross_ref[0] = key_other
+    cross_ref[1] = value_other
+    for at, block in enumerate((key_other, value_other, query_other)):
+        pair_out_ref[:, at * HD : (at + 1) * HD] = block
     loads[3].wait()
     for target in range(CHIPS):
         panels = []
@@ -81,13 +82,20 @@
             )
             panels.append((jnp.where(core == 0, one, two), jnp.where(core == 0, two, one)))
         for at, panel in enumerate((panels[0][0], panels[1][0], panels[0][1], panels[1][1])):
-            spread_ref[target, depth:, at * HD : (at + 1) * HD] = panel
-        spread_ref[target, depth:, 4 * HD :] = jnp.zeros((slots, width - 4 * HD), BF16)
+            stage[target, depth:, at * HD : (at + 1) * HD] = panel
+        stage[target, depth:, 4 * HD :] = jnp.zeros((slots, width - 4 * HD), BF16)
+    sent = []
+    for target, load in enumerate(loads[6:]):
+        load.wait()
+        sent.append(
+            pltpu.make_async_copy(stage.at[target], spread_ref.at[target], out_sems.at[target])
+        )
+        sent[-1].start()
     for load in loads[4:6]:
         load.wait()
     mask_ref[...] = mask_rows(pair[0], odd, core, order, band)
-    for load in loads[6:]:
-        load.wait()
+    for copy in sent:
+        copy.wait()
 
 
 def mask_rows(own, odd, core, order, band):
@@ -120,7 +128,7 @@
 
 
 def masked_query(mask_ref, mine_ref, pair_ref):
-    query = jnp.concatenate([mine_ref[...], pair_ref[2]], axis=0)
+    query = jnp.concatenate([mine_ref[...], pair_ref[:, 2 * HD :]], axis=0)
     lane = lax.broadcasted_iota(jnp.int32, (TILE, HD), 1)
     lanes = [
         jnp.where(lane <= TEXT_LANE, mask_ref[slot : slot + 1, :], F32(0.0)).astype(BF16)
@@ -167,13 +175,13 @@
 
 
 def first_keys(
-    mask_ref, mine_ref, near_ref, pair_ref, far_ref, cross_ref, below_ref, above_ref, total_ref
+    mask_ref, mine_ref, pair_ref, own_ref, other_ref, below_ref, above_ref, total_ref
 ):
     query = masked_query(mask_ref, mine_ref, pair_ref)
-    total = add_keys(None, query, *piece_arrays(0, near_ref, pair_ref))
-    total = add_keys(total, query, *piece_arrays(1, far_ref, cross_ref))
-    total = add_keys(total, query, *piece_arrays(2, below_ref.at[0], below_ref.at[1]))
-    total_ref[...] = add_keys(total, query, *piece_arrays(3, above_ref.at[0], above_ref.at[1]))
+    total = None
+    for piece, ref in enumerate((own_ref, other_ref, below_ref, above_ref)):
+        total = add_keys(total, query, *piece_arrays(piece, ref.at[0], ref.at[1]))
+    total_ref[...] = total
 
 
 def last_keys(
@@ -189,8 +197,8 @@
     result = total[:, :HD] / total[:, HD:]
     odd = mask_ref[0:1, ODD_LANE : ODD_LANE + 1] > 0.5
     own, other = result[:BLOCK], result[BLOCK:]
-    to_even = jnp.where(odd, own, other).astype(BF16)
-    to_odd = jnp.where(odd, other, own).astype(BF16)
+    to_even = jnp.where(odd, other, own).astype(BF16)
+    to_odd = jnp.where(odd, own, other).astype(BF16)
     for chip in range(CHIPS):
         out_ref[chip] = to_even
         out_ref[CHIPS + chip] = to_odd
@@ -198,7 +206,13 @@
 
 def join(low_ref, high_ref, out_ref):
     out_ref[0] = low_ref[...]
-    out_ref[1] = high_ref[:2]
+    out_ref[1] = high_ref[...]
+
+
+def join_pair(low_ref, pair_ref, out_ref):
+    out_ref[0] = low_ref[...]
+    for kind in range(2):
+        out_ref[1, kind] = pair_ref[:, kind * HD : (kind + 1) * HD]
 
 
 def project(core, heads_ref, weight_ref, rows_ref, gate_ref, kept_ref, sent_ref):
@@ -225,18 +239,19 @@
     depth, slots = out_weight.shape[1], text_kv.shape[2]
 
     spread_shape = (CHIPS, depth + slots, 2 * width)
-    token_shapes = [(2, BLOCK, HD)] * 2 + [(3, BLOCK, HD), (BLOCK, HD)]
+    token_shapes = [(2, BLOCK, HD)] * 2 + [(BLOCK, 3 * HD), (BLOCK, HD)]
     loaded = (tile_order, band.T, queries, keys, values, out_weight, text_kv)
     spread, near, cross_out, pair_out, mine, mask = pl.pallas_call(
         start_out,
-        out_shape=[pltpu.VMEM(dims, BF16) for dims in [spread_shape, *token_shapes]]
+        out_shape=[shape(spread_shape, BF16)]
+        + [pltpu.VMEM(dims, BF16) for dims in token_shapes]
         + [pltpu.VMEM((8, HD), F32)],
         in_specs=[SMEM] * 3 + [HBM] * 7,
-        out_specs=[VMEM] * 6,
+        out_specs=[HBM] + [VMEM] * 5,
         scratch_shapes=[pltpu.VMEM((BLOCK, 2 * HD), BF16)] * 3
-        + [pltpu.VMEM(text_kv.shape[1:], BF16)]
+        + [pltpu.VMEM(dims, BF16) for dims in (text_kv.shape[1:], spread_shape)]
         + [pltpu.SMEM(array.shape, jnp.int32) for array in loaded[:2]]
-        + [pltpu.SemaphoreType.DMA((6 + CHIPS,))],
+        + [pltpu.SemaphoreType.DMA((count,)) for count in (6 + CHIPS, CHIPS)],
         compiler_params=params(),
         cost_estimate=pl.CostEstimate(flops=10**6, bytes_accessed=4 * 10**6, transcendentals=0),
     )(*place, *(pltpu.with_memory_space_constraint(a, pltpu.HBM) for a in loaded))
@@ -251,20 +266,18 @@
     far_in = swapped(near, 2)
     cross_in = swapped(cross_out, 3)
 
-    def joined(low, high):
+    def joined(kernel, low, high):
         return pl.pallas_call(
-            join,
+            kernel,
             out_shape=shape((2, 2, BLOCK, HD), BF16),
             in_specs=[VMEM] * 2,
             compiler_params=params(),
             cost_estimate=pl.CostEstimate(flops=0, bytes_accessed=2**19, transcendentals=0),
         )(low, high)
 
-    pair_in, rows_out = lax.optimization_barrier((pair_in, rows[0]))
-    own_pair = joined(near, pair_in)
-    rows_in = swapped(rows_out, 1)
+    own_pair = joined(join_pair, near, pair_in)
     after, _ = lax.optimization_barrier((far_in, own_pair))
-    other_pair = joined(after, cross_in)
+    other_pair = joined(join, after, cross_in)
     up = [(i, i + 4) for i in range(seq_count - 4)]
     down = [(i + 4, i) for i in range(seq_count - 4)]
     below = lax.ppermute(own_pair, "seq", up)
@@ -284,11 +297,10 @@
     total = pl.pallas_call(
         first_keys,
         out_shape=shape((PAIR, 2 * HD), F32),
-        in_specs=[VMEM] * 8,
+        in_specs=[VMEM] * 7,
         compiler_params=params(),
         cost_estimate=cost(5),
-    )(mask, mine, near, pair_in, far_in, cross_in, below, above)
-    total, rows_in = lax.optimization_barrier((total, rows_in))
+    )(mask, mine, pair_in, own_pair, other_pair, below, above)
     attention = pl.pallas_call(
         last_keys,
         out_shape=shape((2 * CHIPS, BLOCK, HD), BF16),
@@ -311,15 +323,10 @@
         cost_estimate=pl.CostEstimate(
             flops=2 * BLOCK * 1024 * 768, bytes_accessed=3 * 10**6, transcendentals=0
         ),
-    )(place[2], heads, spread, rows_in, gate)
+    )(place[2], heads, spread, rows[0], gate)
     other = lax.ppermute(sent, "grp", [(g, g ^ 1) for g in range(2 * CHIPS)])
     result = (kept + gate * other.astype(F32)).astype(BF16)
-    across = [
-        (part * seq_count + i, (1 - part) * seq_count + (i ^ 1))
-        for part in range(2)
-        for i in range(seq_count)
-    ]
-    return lax.ppermute(result[None], ("section", "seq"), across)
+    return lax.ppermute(result, "section", [(0, 1), (1, 0)])[None]
 
 
 def solution(mesh):

time: 76.9 us -> 74.4 us (0.967)
  the two profiles are of different devices: /device:TPU:24 before, /device:TPU:88 now
where the time goes in v10:
time: 74.4 us; the launch traced here: 74 us
  starting transfers between devices  38.9 us (52%)
  waiting for transfers between devices  14 us (19%)
  blocking collectives  13.7 us (18%)
  Pallas kernels  5.84 us (8%)
  between operations  0.82 us (1%)
    all_to_all x1, blocking collectives, body(): lax.all_to_all(attention, ('seq', 'grp'), 0, 0, axis_index_groups=groups)  13.7 us
    ppermute x3, starting transfers between devices, swapped(): return lax.ppermute(block, 'seq', [(i, i ^ mask) for i in range(seq_count)])  10.5 us
    ppermute x1, waiting for transfers between devices, body(): return lax.ppermute(result, 'section', [(0, 1), (1, 0)])[None]  9.55 us
    ppermute x1, starting transfers between devices, body(): return lax.ppermute(result, 'section', [(0, 1), (1, 0)])[None]  8.5 us
    ppermute x1, starting transfers between devices, body(): below = lax.ppermute(own_pair, 'seq', up)  4.7 us
    ppermute x1, starting transfers between devices, body(): beside = lax.ppermute(other_pair, 'seq', mixed)  4.7 us
    all_to_all x1, starting transfers between devices, body(): spread = lax.all_to_all(spread, 'grp', 0, 0, axis_index_groups=by_core)  4.3 us
    pallas_call x1, Pallas kernels, body(): pl.pallas_call(start_out, out_shape=[shape(spread_shape, BF16)] + [pltpu....  2.64 us
  transfers between devices with their start and end apart: 10, of which 4 were waited for; matrix products, arithmetic and copies ran while one was open for 0% of the time, Pallas kernels for 2%

profile of v10, /device:TPU:88, one launch (start us, length us, event | category | flops | bytes accessed | tf_op | source)
XLA Modules:
  0.0 74.0 jit_solution(17979493975898928771)
XLA Ops:
  0.0 2.6 %shard_map.100 = (bf16[4,288,768]{2,1,0:T(8,128)(2,1)}, bf16[2,256,128]{2,1,0:T(8,128)(2,1)S(1)}, bf16[2,256,128]{2,1,0:T(8,128)(2,1)S(1)}, bf16[256,384]{1,0:T(...) custom-call(s32[1]{0:T(128)} %bitcast.1.pair, s32[1]{0:T(128)} %bitcast.2.odd, s32[1]{0:T(128)} %bitcast.core, ...), custom_call_target="tpu_custom_call" | custom-call | flops 1000000 | bytes 4000000 | tf_op jit(solution)/shard_map/pallas_call | solution.py:244
  2.6 4.3 %all-to-all-start = ((bf16[4,288,768]{2,1,0:T(8,128)(2,1)}), bf16[4,288,768]{2,1,0:T(8,128)(2,1)S(1)}, u32[]{:S(2)}, u32[]{:S(2)}) async-start(bf16[4,288,768]{2,1,0:T(8,128)(2,1)} %get-tuple-element.20), calls=%async_computation | async-start | bytes 3538944 | tf_op jit(solution)/shard_map/all_to_all | solution.py:260
  7.0 1.9 %collective-permute-start = (bf16[256,384]{1,0:T(8,128)(2,1)S(1)}, bf16[256,384]{1,0:T(8,128)(2,1)S(1)}, u32[]{:S(2)}, u32[]{:S(2)}) collective-permute-start(bf16[256,384]{1,0:T(8,128)(2,1)S(1)} %get-tuple-element.16), channel_id=1, source_target_pairs={{0,8},{8,0},{16,24},{24,16},{32,40},{40,32},{48,56},{56,48},{64,72... | collective-permute-start | bytes 589832 | tf_op jit(solution)/shard_map/ppermute | solution.py:263
  8.9 6.1 %collective-permute-start.1 = (bf16[2,256,128]{2,1,0:T(8,128)(2,1)S(1)}, bf16[2,256,128]{2,1,0:T(8,128)(2,1)S(1)}, u32[]{:S(2)}, u32[]{:S(2)}) collective-permute-start(bf16[2,256,128]{2,1,0:T(8,128)(2,1)S(1)} %get-tuple-element.17.low_ref), channel_id=1, source_target_pairs={{0,16},{8,24},{16,0},{24,8},{32,48},{40,56},{48,32},{56,40},{64,80... | collective-permute-start | bytes 393224 | tf_op jit(solution)/shard_map/ppermute | solution.py:263
  15.0 2.5 %collective-permute-start.2 = (bf16[2,256,128]{2,1,0:T(8,128)(2,1)S(1)}, bf16[2,256,128]{2,1,0:T(8,128)(2,1)S(1)}, u32[]{:S(2)}, u32[]{:S(2)}) collective-permute-start(bf16[2,256,128]{2,1,0:T(8,128)(2,1)S(1)} %get-tuple-element.19), channel_id=1, source_target_pairs={{0,24},{8,16},{16,8},{24,0},{32,56},{40,48},{48,40},{56,32},{64,88... | collective-permute-start | bytes 393224 | tf_op jit(solution)/shard_map/ppermute | solution.py:263
  17.4 0.0 collective-permute-done.pair_ref
  17.5 2.4 %collective-permute-start.4 = (bf16[2,2,256,128]{3,2,1,0:T(8,128)(2,1)S(1)}, bf16[2,2,256,128]{3,2,1,0:T(8,128)(2,1)S(1)}, u32[]{:S(2)}, u32[]{:S(2)}) collective-permute-start(bf16[2,2,256,128]{3,2,1,0:T(8,128)(2,1)S(1)} %shard_map.101.own_ref), channel_id=1, source_target_pairs={{32,0},{40,8},{48,16},{56,24},{64,32},{72,40},{80,48},{88,56},{96,... | collective-permute-start | bytes 786440 | tf_op jit(solution)/shard_map/ppermute | solution.py:284
  19.9 4.7 %collective-permute-start.3 = (bf16[2,2,256,128]{3,2,1,0:T(8,128)(2,1)S(1)}, bf16[2,2,256,128]{3,2,1,0:T(8,128)(2,1)S(1)}, u32[]{:S(2)}, u32[]{:S(2)}) collective-permute-start(bf16[2,2,256,128]{3,2,1,0:T(8,128)(2,1)S(1)} %shard_map.101.own_ref), channel_id=1, source_target_pairs={{0,32},{8,40},{16,48},{24,56},{32,64},{40,72},{48,80},{56,88},{64,... | collective-permute-start | bytes 786440 | tf_op jit(solution)/shard_map/ppermute | solution.py:283
  25.2 0.0 collective-permute-done.1.low_ref
  25.2 1.6 %collective-permute-done.2.high_ref = bf16[2,256,128]{2,1,0:T(8,128)(2,1)S(1)} collective-permute-done((bf16[2,256,128]{2,1,0:T(8,128)(2,1)S(1)}, bf16[2,256,128]{2,1,0:T(8,128)(2,1)S(1)}, u32[]{:S(2)}, u32[]{:S(2)}) %collective-permute-start.2) | collective-permute-done | bytes 131104 | tf_op jit(solution)/shard_map/ppermute | solution.py:263
  26.9 4.7 %collective-permute-start.6 = (bf16[2,2,256,128]{3,2,1,0:T(8,128)(2,1)S(1)}, bf16[2,2,256,128]{3,2,1,0:T(8,128)(2,1)S(1)}, u32[]{:S(2)}, u32[]{:S(2)}) collective-permute-start(bf16[2,2,256,128]{3,2,1,0:T(8,128)(2,1)S(1)} %shard_map.102.other_ref), channel_id=1, source_target_pairs={{0,32},{8,40},{32,64},{40,72},{64,96},{72,104},{96,128},{104,136},... | collective-permute-start | bytes 786440 | tf_op jit(solution)/shard_map/ppermute | solution.py:286
  31.6 0.0 all-to-all-done.weight_ref
  31.6 1.9 %collective-permute-start.5 = (bf16[4,32,256]{2,1,0:T(8,128)(2,1)S(1)}, bf16[4,32,256]{2,1,0:T(8,128)(2,1)S(1)}, u32[]{:S(2)}, u32[]{:S(2)}) collective-permute-start(bf16[4,32,256]{2,1,0:T(8,128)(2,1)S(1)} %get-tuple-element.23), channel_id=1, source_target_pairs={{0,1},{1,0},{2,3},{3,2},{4,5},{5,4},{6,7},{7,6},{8,9},{9,8},{10,11... | collective-permute-start | bytes 196616 | tf_op jit(solution)/shard_map/ppermute | solution.py:289
  33.5 0.0 collective-permute-done.4.above_ref
  33.6 0.0 collective-permute-done.3.below_ref
  33.6 1.7 %shard_map.103.sum_ref = f32[512,256]{1,0:T(8,128)S(1)} custom-call(f32[8,128]{1,0:T(8,128)S(1)} %get-tuple-element.14.mask_ref, bf16[256,128]{1,0:T(8,128)(2,1)S(1)} %get-tuple-element.15.mine_ref, bf16[256,384]{1,0:T(8,128)(2,1)S(1)} %collective-permute-done.pair_ref, bf16[2,2,256,128]{3,2,1,0:T(8,128)(2,1)S(1)} %shard_map.101.own_ref, ...), custom_call_target="tpu_custom_call" | custom-call | flops 1342177280 | bytes 1000000 | tf_op jit(solution)/shard_map/pallas_call | solution.py:297
  35.3 0.0 copy-start
  35.3 0.0 copy-start.1
  35.3 1.4 %collective-permute-done.6.beside_ref = bf16[2,2,256,128]{3,2,1,0:T(8,128)(2,1)S(1)} collective-permute-done((bf16[2,2,256,128]{3,2,1,0:T(8,128)(2,1)S(1)}, bf16[2,2,256,128]{3,2,1,0:T(8,128)(2,1)S(1)}, u32[]{:S(2)}, u32[]{:S(2)}) %collective-permute-start.6) | collective-permute-done | bytes 262176 | tf_op jit(solution)/shard_map/ppermute | solution.py:286
  36.6 0.0 collective-permute-done.5.core_text
  36.6 0.9 %shard_map.104 = bf16[8,256,128]{2,1,0:T(8,128)(2,1)S(1)} custom-call(s32[1]{0:T(128)S(6)} %copy.12.count, f32[8,128]{1,0:T(8,128)S(1)} %get-tuple-element.14.mask_ref, bf16[256,128]{1,0:T(8,128)(2,1)S(1)} %get-tuple-element.15.mine_ref, bf16[256,384]{1,0:T(8,128)(2,1)S(1)} %collective-permute-done.pair_ref, f32[512,256]{1,0:T(8,128)S(1)} %shard_map.103.sum_ref, ...), custom_call_target="tpu_custom_call" | custom-call | flops 268435456 | bytes 1000000 | tf_op jit(solution)/shard_map/pallas_call | solution.py:304
  37.5 13.7 %all_to_all.10.heads_ref = bf16[8,256,128]{2,1,0:T(8,128)(2,1)S(1)} all-to-all(bf16[8,256,128]{2,1,0:T(8,128)(2,1)S(1)} %shard_map.104), channel_id=1, replica_groups={{0,2,4,6,8,10,12,14},{1,3,5,7,9,11,13,15},{16,18,20,22,24,26,28,30},{17..., dimensions={0} | all-to-all | bytes 1048576 | tf_op jit(solution)/shard_map/all_to_all | solution.py:317
  51.2 0.0 copy-done
  51.2 0.0 copy-done.1
  51.2 0.6 shard_map.105
  51.9 1.9 %collective-permute-start.7 = (bf16[256,384]{1,0:T(8,128)(2,1)S(1)}, bf16[256,384]{1,0:T(8,128)(2,1)S(1)}, u32[]{:S(2)}, u32[]{:S(2)}) collective-permute-start(bf16[256,384]{1,0:T(8,128)(2,1)S(1)} %get-tuple-element.22), channel_id=1, source_target_pairs={{0,1},{1,0},{2,3},{3,2},{4,5},{5,4},{6,7},{7,6},{8,9},{9,8},{10,11... | collective-permute-start | bytes 589832 | tf_op jit(solution)/shard_map/ppermute | solution.py:327
  53.8 1.4 %collective-permute-done.7 = bf16[256,384]{1,0:T(8,128)(2,1)S(1)} collective-permute-done((bf16[256,384]{1,0:T(8,128)(2,1)S(1)}, bf16[256,384]{1,0:T(8,128)(2,1)S(1)}, u32[]{:S(2)}, u32[]{:S(2)}) %collective-permute-start.7) | collective-permute-done | bytes 196640 | tf_op jit(solution)/shard_map/ppermute | solution.py:327
  55.2 0.1 add_convert_fusion
  55.2 8.5 %collective-permute-start.8 = (bf16[256,384]{1,0:T(8,128)(2,1)S(1)}, bf16[256,384]{1,0:T(8,128)(2,1)S(1)}, u32[]{:S(2)}, u32[]{:S(2)}) collective-permute-start(bf16[256,384]{1,0:T(8,128)(2,1)S(1)} %add_convert_fusion), channel_id=1, source_target_pairs={{0,256},{256,0},{1,257},{257,1},{2,258},{258,2},{3,259},{259,3},{4... | collective-permute-start | bytes 589832 | tf_op jit(solution)/shard_map/ppermute | solution.py:329
  63.7 9.6 %collective-permute-done.8 = bf16[256,384]{1,0:T(8,128)(2,1)S(1)} collective-permute-done((bf16[256,384]{1,0:T(8,128)(2,1)S(1)}, bf16[256,384]{1,0:T(8,128)(2,1)S(1)}, u32[]{:S(2)}, u32[]{:S(2)}) %collective-permute-start.8) | collective-permute-done | bytes 196640 | tf_op jit(solution)/shard_map/ppermute | solution.py:329
  73.3 0.7 copy.13
  (4 shorter events, 0.1 us)
Async XLA Ops:
  2.6 28.9 %all-to-all-start = ((bf16[4,288,768]{2,1,0:T(8,128)(2,1)}), bf16[4,288,768]{2,1,0:T(8,128)(2,1)S(1)}, u32[]{:S(2)}, u32[]{:S(2)}) async-start(bf16[4,288,768]{2,1,0:T(8,128)(2,1)} %get-tuple-element.20), calls=%async_computation | async-start | bytes 3538944 | tf_op jit(solution)/shard_map/all_to_all | solution.py:260
  7.0 10.5 %collective-permute-start = (bf16[256,384]{1,0:T(8,128)(2,1)S(1)}, bf16[256,384]{1,0:T(8,128)(2,1)S(1)}, u32[]{:S(2)}, u32[]{:S(2)}) collective-permute-start(bf16[256,384]{1,0:T(8,128)(2,1)S(1)} %get-tuple-element.16), channel_id=1, source_target_pairs={{0,8},{8,0},{16,24},{24,16},{32,40},{40,32},{48,56},{56,48},{64,72... | collective-permute-start | bytes 589832 | tf_op jit(solution)/shard_map/ppermute | solution.py:263
  8.9 16.3 %collective-permute-start.1 = (bf16[2,256,128]{2,1,0:T(8,128)(2,1)S(1)}, bf16[2,256,128]{2,1,0:T(8,128)(2,1)S(1)}, u32[]{:S(2)}, u32[]{:S(2)}) collective-permute-start(bf16[2,256,128]{2,1,0:T(8,128)(2,1)S(1)} %get-tuple-element.17.low_ref), channel_id=1, source_target_pairs={{0,16},{8,24},{16,0},{24,8},{32,48},{40,56},{48,32},{56,40},{64,80... | collective-permute-start | bytes 393224 | tf_op jit(solution)/shard_map/ppermute | solution.py:263
  15.0 11.9 %collective-permute-start.2 = (bf16[2,256,128]{2,1,0:T(8,128)(2,1)S(1)}, bf16[2,256,128]{2,1,0:T(8,128)(2,1)S(1)}, u32[]{:S(2)}, u32[]{:S(2)}) collective-permute-start(bf16[2,256,128]{2,1,0:T(8,128)(2,1)S(1)} %get-tuple-element.19), channel_id=1, source_target_pairs={{0,24},{8,16},{16,8},{24,0},{32,56},{40,48},{48,40},{56,32},{64,88... | collective-permute-start | bytes 393224 | tf_op jit(solution)/shard_map/ppermute | solution.py:263
  17.5 16.1 %collective-permute-start.4 = (bf16[2,2,256,128]{3,2,1,0:T(8,128)(2,1)S(1)}, bf16[2,2,256,128]{3,2,1,0:T(8,128)(2,1)S(1)}, u32[]{:S(2)}, u32[]{:S(2)}) collective-permute-start(bf16[2,2,256,128]{3,2,1,0:T(8,128)(2,1)S(1)} %shard_map.101.own_ref), channel_id=1, source_target_pairs={{32,0},{40,8},{48,16},{56,24},{64,32},{72,40},{80,48},{88,56},{96,... | collective-permute-start | bytes 786440 | tf_op jit(solution)/shard_map/ppermute | solution.py:284
  19.9 13.7 %collective-permute-start.3 = (bf16[2,2,256,128]{3,2,1,0:T(8,128)(2,1)S(1)}, bf16[2,2,256,128]{3,2,1,0:T(8,128)(2,1)S(1)}, u32[]{:S(2)}, u32[]{:S(2)}) collective-permute-start(bf16[2,2,256,128]{3,2,1,0:T(8,128)(2,1)S(1)} %shard_map.101.own_ref), channel_id=1, source_target_pairs={{0,32},{8,40},{16,48},{24,56},{32,64},{40,72},{48,80},{56,88},{64,... | collective-permute-start | bytes 786440 | tf_op jit(solution)/shard_map/ppermute | solution.py:283
  26.9 9.8 %collective-permute-start.6 = (bf16[2,2,256,128]{3,2,1,0:T(8,128)(2,1)S(1)}, bf16[2,2,256,128]{3,2,1,0:T(8,128)(2,1)S(1)}, u32[]{:S(2)}, u32[]{:S(2)}) collective-permute-start(bf16[2,2,256,128]{3,2,1,0:T(8,128)(2,1)S(1)} %shard_map.102.other_ref), channel_id=1, source_target_pairs={{0,32},{8,40},{32,64},{40,72},{64,96},{72,104},{96,128},{104,136},... | collective-permute-start | bytes 786440 | tf_op jit(solution)/shard_map/ppermute | solution.py:286
  31.6 5.0 %collective-permute-start.5 = (bf16[4,32,256]{2,1,0:T(8,128)(2,1)S(1)}, bf16[4,32,256]{2,1,0:T(8,128)(2,1)S(1)}, u32[]{:S(2)}, u32[]{:S(2)}) collective-permute-start(bf16[4,32,256]{2,1,0:T(8,128)(2,1)S(1)} %get-tuple-element.23), channel_id=1, source_target_pairs={{0,1},{1,0},{2,3},{3,2},{4,5},{5,4},{6,7},{7,6},{8,9},{9,8},{10,11... | collective-permute-start | bytes 196616 | tf_op jit(solution)/shard_map/ppermute | solution.py:289
  35.3 16.0 %copy-start = (bf16[1,256,384]{2,1,0:T(8,128)(2,1)S(1)}, bf16[1,256,384]{2,1,0:T(8,128)(2,1)}, u32[]{:S(2)}) copy-start(bf16[1,256,384]{2,1,0:T(8,128)(2,1)} %param.10) | copy-start | bytes 589828
  35.3 16.0 %copy-start.1 = (f32[1,384]{1,0:T(1,128)S(1)}, f32[1,384]{1,0:T(1,128)}, u32[]{:S(2)}) copy-start(f32[1,384]{1,0:T(1,128)} %gate_ref.1) | copy-start | bytes 4612
  51.9 3.3 %collective-permute-start.7 = (bf16[256,384]{1,0:T(8,128)(2,1)S(1)}, bf16[256,384]{1,0:T(8,128)(2,1)S(1)}, u32[]{:S(2)}, u32[]{:S(2)}) collective-permute-start(bf16[256,384]{1,0:T(8,128)(2,1)S(1)} %get-tuple-element.22), channel_id=1, source_target_pairs={{0,1},{1,0},{2,3},{3,2},{4,5},{5,4},{6,7},{7,6},{8,9},{9,8},{10,11... | collective-permute-start | bytes 589832 | tf_op jit(solution)/shard_map/ppermute | solution.py:327
  55.2 18.1 %collective-permute-start.8 = (bf16[256,384]{1,0:T(8,128)(2,1)S(1)}, bf16[256,384]{1,0:T(8,128)(2,1)S(1)}, u32[]{:S(2)}, u32[]{:S(2)}) collective-permute-start(bf16[256,384]{1,0:T(8,128)(2,1)S(1)} %add_convert_fusion), channel_id=1, source_target_pairs={{0,256},{256,0},{1,257},{257,1},{2,258},{258,2},{3,259},{259,3},{4... | collective-permute-start | bytes 589832 | tf_op jit(solution)/shard_map/ppermute | solution.py:329

commit v11 on v10

--- a/solution.py
+++ b/solution.py
@@ -215,18 +215,24 @@
         out_ref[1, kind] = pair_ref[:, kind * HD : (kind + 1) * HD]
 
 
-def project(core, heads_ref, weight_ref, rows_ref, gate_ref, kept_ref, sent_ref):
+def projected(core, heads_ref, weight_ref, width):
     total = None
-    depth, width = 2 * HD, kept_ref.shape[1]
+    columns = pl.ds(pl.multiple_of(core * width, 128), width)
     for chip in range(CHIPS):
         heads = jnp.concatenate([heads_ref[chip], heads_ref[CHIPS + chip]], axis=1)
-        part = jnp.dot(heads, weight_ref[chip, :depth], preferred_element_type=F32)
+        weight = weight_ref[chip, : 2 * HD, columns]
+        part = jnp.dot(heads, weight, preferred_element_type=F32)
         total = part if total is None else total + part
-    low, high = total[:, :width], total[:, width:]
-    first = core[0] == 0
-    kept = jnp.where(first, low, high)
-    kept_ref[...] = rows_ref[...].astype(F32) + gate_ref[...] * kept
-    sent_ref[...] = jnp.where(first, high, low).astype(BF16)
+    return total
+
+
+def project_other(core, heads_ref, weight_ref, out_ref):
+    out_ref[...] = projected(1 - core[0], heads_ref, weight_ref, out_ref.shape[1]).astype(BF16)
+
+
+def project_own(core, heads_ref, weight_ref, rows_ref, gate_ref, out_ref):
+    share = projected(core[0], heads_ref, weight_ref, out_ref.shape[1])
+    out_ref[...] = rows_ref[...].astype(F32) + gate_ref[...] * share
 
 
 def body(rows, queries, keys, values, text_kv, text_count, out_weight, gate, band, tile_order):
@@ -315,14 +321,20 @@
         for core in range(2)
     ]
     heads = lax.all_to_all(attention, ("seq", "grp"), 0, 0, axis_index_groups=groups)
-    kept, sent = pl.pallas_call(
-        project,
-        out_shape=(shape((BLOCK, width), F32), shape((BLOCK, width), BF16)),
+    half = pl.CostEstimate(flops=2 * BLOCK * 1024 * 384, bytes_accessed=10**6, transcendentals=0)
+    sent = pl.pallas_call(
+        project_other,
+        out_shape=shape((BLOCK, width), BF16),
+        in_specs=[SMEM] + [VMEM] * 2,
+        compiler_params=params(),
+        cost_estimate=half,
+    )(place[2], heads, spread)
+    kept = pl.pallas_call(
+        project_own,
+        out_shape=shape((BLOCK, width), F32),
         in_specs=[SMEM] + [VMEM] * 4,
         compiler_params=params(),
-        cost_estimate=pl.CostEstimate(
-            flops=2 * BLOCK * 1024 * 768, bytes_accessed=3 * 10**6, transcendentals=0
-        ),
+        cost_estimate=half,
     )(place[2], heads, spread, rows[0], gate)
     other = lax.ppermute(sent, "grp", [(g, g ^ 1) for g in range(2 * CHIPS)])
     result = (kept + gate * other.astype(F32)).astype(BF16)

time: 74.4 us -> 74.4 us (level)
  transfers between devices with their start and end apart: 10 -> 10, of which waited for: 4 -> 4; matrix products, arithmetic and copies ran while one was open for 0% -> 0% of each run, Pallas kernels for 2% -> 3%
where the time goes in v11:
time: 74.4 us; the launch traced here: 73.9 us
  starting transfers between devices  38.9 us (52%)
  blocking collectives  13.8 us (19%)
  waiting for transfers between devices  13.5 us (18%)
  Pallas kernels  6.1 us (8%)
  between operations  0.84 us (1%)
    all_to_all x1, blocking collectives, body(): lax.all_to_all(attention, ('seq', 'grp'), 0, 0, axis_index_groups=groups)  13.8 us
    ppermute x3, starting transfers between devices, swapped(): return lax.ppermute(block, 'seq', [(i, i ^ mask) for i in range(seq_count)])  10.5 us
    ppermute x1, waiting for transfers between devices, body(): return lax.ppermute(result, 'section', [(0, 1), (1, 0)])[None]  9.55 us
    ppermute x1, starting transfers between devices, body(): return lax.ppermute(result, 'section', [(0, 1), (1, 0)])[None]  8.49 us
    ppermute x1, starting transfers between devices, body(): below = lax.ppermute(own_pair, 'seq', up)  4.7 us
    ppermute x1, starting transfers between devices, body(): beside = lax.ppermute(other_pair, 'seq', mixed)  4.7 us
    all_to_all x1, starting transfers between devices, body(): spread = lax.all_to_all(spread, 'grp', 0, 0, axis_index_groups=by_core)  4.3 us
    pallas_call x1, Pallas kernels, body(): pl.pallas_call(start_out, out_shape=[shape(spread_shape, BF16)] + [pltpu....  2.62 us
  transfers between devices with their start and end apart: 10, of which 4 were waited for; matrix products, arithmetic and copies ran while one was open for 0% of the time, Pallas kernels for 3%

profile of v11, /device:TPU:88, one launch (start us, length us, event | category | flops | bytes accessed | tf_op | source)
XLA Modules:
  0.0 73.9 jit_solution(177970826219168476)
XLA Ops:
  0.0 2.6 %shard_map.100 = (bf16[4,288,768]{2,1,0:T(8,128)(2,1)}, bf16[2,256,128]{2,1,0:T(8,128)(2,1)S(1)}, bf16[2,256,128]{2,1,0:T(8,128)(2,1)S(1)}, bf16[256,384]{1,0:T(...) custom-call(s32[1]{0:T(128)} %bitcast.1.pair, s32[1]{0:T(128)} %bitcast.2.odd, s32[1]{0:T(128)} %bitcast.core, ...), custom_call_target="tpu_custom_call" | custom-call | flops 1000000 | bytes 4000000 | tf_op jit(solution)/shard_map/pallas_call | solution.py:250
  2.6 4.3 %all-to-all-start = ((bf16[4,288,768]{2,1,0:T(8,128)(2,1)}), bf16[4,288,768]{2,1,0:T(8,128)(2,1)S(1)}, u32[]{:S(2)}, u32[]{:S(2)}) async-start(bf16[4,288,768]{2,1,0:T(8,128)(2,1)} %get-tuple-element.18), calls=%async_computation | async-start | bytes 3538944 | tf_op jit(solution)/shard_map/all_to_all | solution.py:266
  6.9 1.9 %collective-permute-start = (bf16[256,384]{1,0:T(8,128)(2,1)S(1)}, bf16[256,384]{1,0:T(8,128)(2,1)S(1)}, u32[]{:S(2)}, u32[]{:S(2)}) collective-permute-start(bf16[256,384]{1,0:T(8,128)(2,1)S(1)} %get-tuple-element.14), channel_id=1, source_target_pairs={{0,8},{8,0},{16,24},{24,16},{32,40},{40,32},{48,56},{56,48},{64,72... | collective-permute-start | bytes 589832 | tf_op jit(solution)/shard_map/ppermute | solution.py:269
  8.9 6.1 %collective-permute-start.1 = (bf16[2,256,128]{2,1,0:T(8,128)(2,1)S(1)}, bf16[2,256,128]{2,1,0:T(8,128)(2,1)S(1)}, u32[]{:S(2)}, u32[]{:S(2)}) collective-permute-start(bf16[2,256,128]{2,1,0:T(8,128)(2,1)S(1)} %get-tuple-element.15.low_ref), channel_id=1, source_target_pairs={{0,16},{8,24},{16,0},{24,8},{32,48},{40,56},{48,32},{56,40},{64,80... | collective-permute-start | bytes 393224 | tf_op jit(solution)/shard_map/ppermute | solution.py:269
  15.0 2.5 %collective-permute-start.2 = (bf16[2,256,128]{2,1,0:T(8,128)(2,1)S(1)}, bf16[2,256,128]{2,1,0:T(8,128)(2,1)S(1)}, u32[]{:S(2)}, u32[]{:S(2)}) collective-permute-start(bf16[2,256,128]{2,1,0:T(8,128)(2,1)S(1)} %get-tuple-element.17), channel_id=1, source_target_pairs={{0,24},{8,16},{16,8},{24,0},{32,56},{40,48},{48,40},{56,32},{64,88... | collective-permute-start | bytes 393224 | tf_op jit(solution)/shard_map/ppermute | solution.py:269
  17.4 0.0 collective-permute-done.pair_ref
  17.5 2.4 %collective-permute-start.4 = (bf16[2,2,256,128]{3,2,1,0:T(8,128)(2,1)S(1)}, bf16[2,2,256,128]{3,2,1,0:T(8,128)(2,1)S(1)}, u32[]{:S(2)}, u32[]{:S(2)}) collective-permute-start(bf16[2,2,256,128]{3,2,1,0:T(8,128)(2,1)S(1)} %shard_map.101.own_ref), channel_id=1, source_target_pairs={{32,0},{40,8},{48,16},{56,24},{64,32},{72,40},{80,48},{88,56},{96,... | collective-permute-start | bytes 786440 | tf_op jit(solution)/shard_map/ppermute | solution.py:290
  19.8 4.7 %collective-permute-start.3 = (bf16[2,2,256,128]{3,2,1,0:T(8,128)(2,1)S(1)}, bf16[2,2,256,128]{3,2,1,0:T(8,128)(2,1)S(1)}, u32[]{:S(2)}, u32[]{:S(2)}) collective-permute-start(bf16[2,2,256,128]{3,2,1,0:T(8,128)(2,1)S(1)} %shard_map.101.own_ref), channel_id=1, source_target_pairs={{0,32},{8,40},{16,48},{24,56},{32,64},{40,72},{48,80},{56,88},{64,... | collective-permute-start | bytes 786440 | tf_op jit(solution)/shard_map/ppermute | solution.py:289
  25.2 0.0 collective-permute-done.1.low_ref
  25.2 1.6 %collective-permute-done.2.high_ref = bf16[2,256,128]{2,1,0:T(8,128)(2,1)S(1)} collective-permute-done((bf16[2,256,128]{2,1,0:T(8,128)(2,1)S(1)}, bf16[2,256,128]{2,1,0:T(8,128)(2,1)S(1)}, u32[]{:S(2)}, u32[]{:S(2)}) %collective-permute-start.2) | collective-permute-done | bytes 131104 | tf_op jit(solution)/shard_map/ppermute | solution.py:269
  26.9 4.7 %collective-permute-start.6 = (bf16[2,2,256,128]{3,2,1,0:T(8,128)(2,1)S(1)}, bf16[2,2,256,128]{3,2,1,0:T(8,128)(2,1)S(1)}, u32[]{:S(2)}, u32[]{:S(2)}) collective-permute-start(bf16[2,2,256,128]{3,2,1,0:T(8,128)(2,1)S(1)} %shard_map.102.other_ref), channel_id=1, source_target_pairs={{0,32},{8,40},{32,64},{40,72},{64,96},{72,104},{96,128},{104,136},... | collective-permute-start | bytes 786440 | tf_op jit(solution)/shard_map/ppermute | solution.py:292
  31.6 0.0 all-to-all-done.weight_ref
  31.6 1.9 %collective-permute-start.5 = (bf16[4,32,256]{2,1,0:T(8,128)(2,1)S(1)}, bf16[4,32,256]{2,1,0:T(8,128)(2,1)S(1)}, u32[]{:S(2)}, u32[]{:S(2)}) collective-permute-start(bf16[4,32,256]{2,1,0:T(8,128)(2,1)S(1)} %get-tuple-element.19), channel_id=1, source_target_pairs={{0,1},{1,0},{2,3},{3,2},{4,5},{5,4},{6,7},{7,6},{8,9},{9,8},{10,11... | collective-permute-start | bytes 196616 | tf_op jit(solution)/shard_map/ppermute | solution.py:295
  33.5 0.0 collective-permute-done.4.above_ref
  33.5 0.0 collective-permute-done.3.below_ref
  33.6 1.7 %shard_map.103.sum_ref = f32[512,256]{1,0:T(8,128)S(1)} custom-call(f32[8,128]{1,0:T(8,128)S(1)} %get-tuple-element.12.mask_ref, bf16[256,128]{1,0:T(8,128)(2,1)S(1)} %get-tuple-element.13.mine_ref, bf16[256,384]{1,0:T(8,128)(2,1)S(1)} %collective-permute-done.pair_ref, bf16[2,2,256,128]{3,2,1,0:T(8,128)(2,1)S(1)} %shard_map.101.own_ref, ...), custom_call_target="tpu_custom_call" | custom-call | flops 1342177280 | bytes 1000000 | tf_op jit(solution)/shard_map/pallas_call | solution.py:303
  35.2 1.4 %collective-permute-done.6.beside_ref = bf16[2,2,256,128]{3,2,1,0:T(8,128)(2,1)S(1)} collective-permute-done((bf16[2,2,256,128]{3,2,1,0:T(8,128)(2,1)S(1)}, bf16[2,2,256,128]{3,2,1,0:T(8,128)(2,1)S(1)}, u32[]{:S(2)}, u32[]{:S(2)}) %collective-permute-start.6) | collective-permute-done | bytes 262176 | tf_op jit(solution)/shard_map/ppermute | solution.py:292
  36.6 0.0 collective-permute-done.5.core_text
  36.6 0.9 %shard_map.104 = bf16[8,256,128]{2,1,0:T(8,128)(2,1)S(1)} custom-call(s32[1]{0:T(128)S(6)} %copy.12.count, f32[8,128]{1,0:T(8,128)S(1)} %get-tuple-element.12.mask_ref, bf16[256,128]{1,0:T(8,128)(2,1)S(1)} %get-tuple-element.13.mine_ref, bf16[256,384]{1,0:T(8,128)(2,1)S(1)} %collective-permute-done.pair_ref, f32[512,256]{1,0:T(8,128)S(1)} %shard_map.103.sum_ref, ...), custom_call_target="tpu_custom_call" | custom-call | flops 268435456 | bytes 1000000 | tf_op jit(solution)/shard_map/pallas_call | solution.py:310
  37.5 0.0 copy-start.1
  37.5 0.0 copy-start
  37.5 13.8 %all_to_all.10.heads_ref = bf16[8,256,128]{2,1,0:T(8,128)(2,1)S(1)} all-to-all(bf16[8,256,128]{2,1,0:T(8,128)(2,1)S(1)} %shard_map.104), channel_id=1, replica_groups={{0,2,4,6,8,10,12,14},{1,3,5,7,9,11,13,15},{16,18,20,22,24,26,28,30},{17..., dimensions={0} | all-to-all | bytes 1048576 | tf_op jit(solution)/shard_map/all_to_all | solution.py:323
  51.4 0.4 shard_map.106
  51.8 1.9 %collective-permute-start.7 = (bf16[256,384]{1,0:T(8,128)(2,1)S(1)}, bf16[256,384]{1,0:T(8,128)(2,1)S(1)}, u32[]{:S(2)}, u32[]{:S(2)}) collective-permute-start(bf16[256,384]{1,0:T(8,128)(2,1)S(1)} %shard_map.106), channel_id=1, source_target_pairs={{0,1},{1,0},{2,3},{3,2},{4,5},{5,4},{6,7},{7,6},{8,9},{9,8},{10,11... | collective-permute-start | bytes 589832 | tf_op jit(solution)/shard_map/ppermute | solution.py:339
  53.7 0.0 copy-done.1
  53.8 0.0 copy-done
  53.8 0.4 shard_map.105
  54.2 0.9 %collective-permute-done.7 = bf16[256,384]{1,0:T(8,128)(2,1)S(1)} collective-permute-done((bf16[256,384]{1,0:T(8,128)(2,1)S(1)}, bf16[256,384]{1,0:T(8,128)(2,1)S(1)}, u32[]{:S(2)}, u32[]{:S(2)}) %collective-permute-start.7) | collective-permute-done | bytes 196640 | tf_op jit(solution)/shard_map/ppermute | solution.py:339
  55.1 0.1 add_convert_fusion
  55.2 8.5 %collective-permute-start.8 = (bf16[256,384]{1,0:T(8,128)(2,1)S(1)}, bf16[256,384]{1,0:T(8,128)(2,1)S(1)}, u32[]{:S(2)}, u32[]{:S(2)}) collective-permute-start(bf16[256,384]{1,0:T(8,128)(2,1)S(1)} %add_convert_fusion), channel_id=1, source_target_pairs={{0,256},{256,0},{1,257},{257,1},{2,258},{258,2},{3,259},{259,3},{4... | collective-permute-start | bytes 589832 | tf_op jit(solution)/shard_map/ppermute | solution.py:341
  63.7 9.5 %collective-permute-done.8 = bf16[256,384]{1,0:T(8,128)(2,1)S(1)} collective-permute-done((bf16[256,384]{1,0:T(8,128)(2,1)S(1)}, bf16[256,384]{1,0:T(8,128)(2,1)S(1)}, u32[]{:S(2)}, u32[]{:S(2)}) %collective-permute-start.8) | collective-permute-done | bytes 196640 | tf_op jit(solution)/shard_map/ppermute | solution.py:341
  73.2 0.7 copy.13
  (4 shorter events, 0.1 us)
Async XLA Ops:
  2.6 28.9 %all-to-all-start = ((bf16[4,288,768]{2,1,0:T(8,128)(2,1)}), bf16[4,288,768]{2,1,0:T(8,128)(2,1)S(1)}, u32[]{:S(2)}, u32[]{:S(2)}) async-start(bf16[4,288,768]{2,1,0:T(8,128)(2,1)} %get-tuple-element.18), calls=%async_computation | async-start | bytes 3538944 | tf_op jit(solution)/shard_map/all_to_all | solution.py:266
  6.9 10.5 %collective-permute-start = (bf16[256,384]{1,0:T(8,128)(2,1)S(1)}, bf16[256,384]{1,0:T(8,128)(2,1)S(1)}, u32[]{:S(2)}, u32[]{:S(2)}) collective-permute-start(bf16[256,384]{1,0:T(8,128)(2,1)S(1)} %get-tuple-element.14), channel_id=1, source_target_pairs={{0,8},{8,0},{16,24},{24,16},{32,40},{40,32},{48,56},{56,48},{64,72... | collective-permute-start | bytes 589832 | tf_op jit(solution)/shard_map/ppermute | solution.py:269
  8.9 16.3 %collective-permute-start.1 = (bf16[2,256,128]{2,1,0:T(8,128)(2,1)S(1)}, bf16[2,256,128]{2,1,0:T(8,128)(2,1)S(1)}, u32[]{:S(2)}, u32[]{:S(2)}) collective-permute-start(bf16[2,256,128]{2,1,0:T(8,128)(2,1)S(1)} %get-tuple-element.15.low_ref), channel_id=1, source_target_pairs={{0,16},{8,24},{16,0},{24,8},{32,48},{40,56},{48,32},{56,40},{64,80... | collective-permute-start | bytes 393224 | tf_op jit(solution)/shard_map/ppermute | solution.py:269
  15.0 11.9 %collective-permute-start.2 = (bf16[2,256,128]{2,1,0:T(8,128)(2,1)S(1)}, bf16[2,256,128]{2,1,0:T(8,128)(2,1)S(1)}, u32[]{:S(2)}, u32[]{:S(2)}) collective-permute-start(bf16[2,256,128]{2,1,0:T(8,128)(2,1)S(1)} %get-tuple-element.17), channel_id=1, source_target_pairs={{0,24},{8,16},{16,8},{24,0},{32,56},{40,48},{48,40},{56,32},{64,88... | collective-permute-start | bytes 393224 | tf_op jit(solution)/shard_map/ppermute | solution.py:269
  17.5 16.1 %collective-permute-start.4 = (bf16[2,2,256,128]{3,2,1,0:T(8,128)(2,1)S(1)}, bf16[2,2,256,128]{3,2,1,0:T(8,128)(2,1)S(1)}, u32[]{:S(2)}, u32[]{:S(2)}) collective-permute-start(bf16[2,2,256,128]{3,2,1,0:T(8,128)(2,1)S(1)} %shard_map.101.own_ref), channel_id=1, source_target_pairs={{32,0},{40,8},{48,16},{56,24},{64,32},{72,40},{80,48},{88,56},{96,... | collective-permute-start | bytes 786440 | tf_op jit(solution)/shard_map/ppermute | solution.py:290
  19.8 13.7 %collective-permute-start.3 = (bf16[2,2,256,128]{3,2,1,0:T(8,128)(2,1)S(1)}, bf16[2,2,256,128]{3,2,1,0:T(8,128)(2,1)S(1)}, u32[]{:S(2)}, u32[]{:S(2)}) collective-permute-start(bf16[2,2,256,128]{3,2,1,0:T(8,128)(2,1)S(1)} %shard_map.101.own_ref), channel_id=1, source_target_pairs={{0,32},{8,40},{16,48},{24,56},{32,64},{40,72},{48,80},{56,88},{64,... | collective-permute-start | bytes 786440 | tf_op jit(solution)/shard_map/ppermute | solution.py:289
  26.9 9.8 %collective-permute-start.6 = (bf16[2,2,256,128]{3,2,1,0:T(8,128)(2,1)S(1)}, bf16[2,2,256,128]{3,2,1,0:T(8,128)(2,1)S(1)}, u32[]{:S(2)}, u32[]{:S(2)}) collective-permute-start(bf16[2,2,256,128]{3,2,1,0:T(8,128)(2,1)S(1)} %shard_map.102.other_ref), channel_id=1, source_target_pairs={{0,32},{8,40},{32,64},{40,72},{64,96},{72,104},{96,128},{104,136},... | collective-permute-start | bytes 786440 | tf_op jit(solution)/shard_map/ppermute | solution.py:292
  31.6 5.0 %collective-permute-start.5 = (bf16[4,32,256]{2,1,0:T(8,128)(2,1)S(1)}, bf16[4,32,256]{2,1,0:T(8,128)(2,1)S(1)}, u32[]{:S(2)}, u32[]{:S(2)}) collective-permute-start(bf16[4,32,256]{2,1,0:T(8,128)(2,1)S(1)} %get-tuple-element.19), channel_id=1, source_target_pairs={{0,1},{1,0},{2,3},{3,2},{4,5},{5,4},{6,7},{7,6},{8,9},{9,8},{10,11... | collective-permute-start | bytes 196616 | tf_op jit(solution)/shard_map/ppermute | solution.py:295
  37.5 16.2 %copy-start.1 = (f32[1,384]{1,0:T(1,128)S(1)}, f32[1,384]{1,0:T(1,128)}, u32[]{:S(2)}) copy-start(f32[1,384]{1,0:T(1,128)} %gate_ref.1) | copy-start | bytes 4612
  37.5 16.2 %copy-start = (bf16[1,256,384]{2,1,0:T(8,128)(2,1)S(1)}, bf16[1,256,384]{2,1,0:T(8,128)(2,1)}, u32[]{:S(2)}) copy-start(bf16[1,256,384]{2,1,0:T(8,128)(2,1)} %param.10) | copy-start | bytes 589828
  51.8 3.3 %collective-permute-start.7 = (bf16[256,384]{1,0:T(8,128)(2,1)S(1)}, bf16[256,384]{1,0:T(8,128)(2,1)S(1)}, u32[]{:S(2)}, u32[]{:S(2)}) collective-permute-start(bf16[256,384]{1,0:T(8,128)(2,1)S(1)} %shard_map.106), channel_id=1, source_target_pairs={{0,1},{1,0},{2,3},{3,2},{4,5},{5,4},{6,7},{7,6},{8,9},{9,8},{10,11... | collective-permute-start | bytes 589832 | tf_op jit(solution)/shard_map/ppermute | solution.py:339
  55.2 18.0 %collective-permute-start.8 = (bf16[256,384]{1,0:T(8,128)(2,1)S(1)}, bf16[256,384]{1,0:T(8,128)(2,1)S(1)}, u32[]{:S(2)}, u32[]{:S(2)}) collective-permute-start(bf16[256,384]{1,0:T(8,128)(2,1)S(1)} %add_convert_fusion), channel_id=1, source_target_pairs={{0,256},{256,0},{1,257},{257,1},{2,258},{258,2},{3,259},{259,3},{4... | collective-permute-start | bytes 589832 | tf_op jit(solution)/shard_map/ppermute | solution.py:341

commit v12 on v11

--- a/solution.py
+++ b/solution.py
@@ -188,12 +188,13 @@
     count, mask_ref, mine_ref, pair_ref, sum_ref, own_text, core_text, beside_ref, out_ref
 ):
     query = masked_query(mask_ref, mine_ref, pair_ref)
-    texts = zip(
-        text_arrays(count, mask_ref, own_text, False), text_arrays(count, mask_ref, core_text, True)
-    )
-    total = add_keys(sum_ref[...], query, *(jnp.concatenate(both, axis=0) for both in texts))
+    texts = [
+        text_arrays(count, mask_ref, own_text, False),
+        text_arrays(count, mask_ref, core_text, True),
+    ]
     pieces = piece_arrays(PIECES - 1, beside_ref.at[0], beside_ref.at[1])
-    total = add_keys(total, query, *pieces)
+    together = (jnp.concatenate(three, axis=0) for three in zip(*texts, pieces))
+    total = add_keys(sum_ref[...], query, *together)
     result = total[:, :HD] / total[:, HD:]
     odd = mask_ref[0:1, ODD_LANE : ODD_LANE + 1] > 0.5
     own, other = result[:BLOCK], result[BLOCK:]

time: 74.4 us -> 74.4 us (level)
  no operation moved by 1% of the time
where the time goes in v12:
time: 74.4 us; the launch traced here: 73.9 us
  starting transfers between devices  38.9 us (52%)
  blocking collectives  13.8 us (19%)
  waiting for transfers between devices  13.5 us (18%)
  Pallas kernels  6.08 us (8%)
  between operations  0.84 us (1%)
    all_to_all x1, blocking collectives, body(): lax.all_to_all(attention, ('seq', 'grp'), 0, 0, axis_index_groups=groups)  13.8 us
    ppermute x3, starting transfers between devices, swapped(): return lax.ppermute(block, 'seq', [(i, i ^ mask) for i in range(seq_count)])  10.5 us
    ppermute x1, waiting for transfers between devices, body(): return lax.ppermute(result, 'section', [(0, 1), (1, 0)])[None]  9.55 us
    ppermute x1, starting transfers between devices, body(): return lax.ppermute(result, 'section', [(0, 1), (1, 0)])[None]  8.49 us
    ppermute x1, starting transfers between devices, body(): below = lax.ppermute(own_pair, 'seq', up)  4.7 us
    ppermute x1, starting transfers between devices, body(): beside = lax.ppermute(other_pair, 'seq', mixed)  4.7 us
    all_to_all x1, starting transfers between devices, body(): spread = lax.all_to_all(spread, 'grp', 0, 0, axis_index_groups=by_core)  4.3 us
    pallas_call x1, Pallas kernels, body(): pl.pallas_call(start_out, out_shape=[shape(spread_shape, BF16)] + [pltpu....  2.62 us
  transfers between devices with their start and end apart: 10, of which 4 were waited for; matrix products, arithmetic and copies ran while one was open for 0% of the time, Pallas kernels for 3%

profile of v12, /device:TPU:88, one launch (start us, length us, event | category | flops | bytes accessed | tf_op | source)
XLA Modules:
  0.0 73.9 jit_solution(7806109729786069532)
XLA Ops:
  0.0 2.6 %shard_map.100 = (bf16[4,288,768]{2,1,0:T(8,128)(2,1)}, bf16[2,256,128]{2,1,0:T(8,128)(2,1)S(1)}, bf16[2,256,128]{2,1,0:T(8,128)(2,1)S(1)}, bf16[256,384]{1,0:T(...) custom-call(s32[1]{0:T(128)} %bitcast.1.pair, s32[1]{0:T(128)} %bitcast.2.odd, s32[1]{0:T(128)} %bitcast.core, ...), custom_call_target="tpu_custom_call" | custom-call | flops 1000000 | bytes 4000000 | tf_op jit(solution)/shard_map/pallas_call | solution.py:251
  2.6 4.3 %all-to-all-start = ((bf16[4,288,768]{2,1,0:T(8,128)(2,1)}), bf16[4,288,768]{2,1,0:T(8,128)(2,1)S(1)}, u32[]{:S(2)}, u32[]{:S(2)}) async-start(bf16[4,288,768]{2,1,0:T(8,128)(2,1)} %get-tuple-element.18), calls=%async_computation | async-start | bytes 3538944 | tf_op jit(solution)/shard_map/all_to_all | solution.py:267
  6.9 1.9 %collective-permute-start = (bf16[256,384]{1,0:T(8,128)(2,1)S(1)}, bf16[256,384]{1,0:T(8,128)(2,1)S(1)}, u32[]{:S(2)}, u32[]{:S(2)}) collective-permute-start(bf16[256,384]{1,0:T(8,128)(2,1)S(1)} %get-tuple-element.14), channel_id=1, source_target_pairs={{0,8},{8,0},{16,24},{24,16},{32,40},{40,32},{48,56},{56,48},{64,72... | collective-permute-start | bytes 589832 | tf_op jit(solution)/shard_map/ppermute | solution.py:270
  8.9 6.1 %collective-permute-start.1 = (bf16[2,256,128]{2,1,0:T(8,128)(2,1)S(1)}, bf16[2,256,128]{2,1,0:T(8,128)(2,1)S(1)}, u32[]{:S(2)}, u32[]{:S(2)}) collective-permute-start(bf16[2,256,128]{2,1,0:T(8,128)(2,1)S(1)} %get-tuple-element.15.low_ref), channel_id=1, source_target_pairs={{0,16},{8,24},{16,0},{24,8},{32,48},{40,56},{48,32},{56,40},{64,80... | collective-permute-start | bytes 393224 | tf_op jit(solution)/shard_map/ppermute | solution.py:270
  15.0 2.5 %collective-permute-start.2 = (bf16[2,256,128]{2,1,0:T(8,128)(2,1)S(1)}, bf16[2,256,128]{2,1,0:T(8,128)(2,1)S(1)}, u32[]{:S(2)}, u32[]{:S(2)}) collective-permute-start(bf16[2,256,128]{2,1,0:T(8,128)(2,1)S(1)} %get-tuple-element.17), channel_id=1, source_target_pairs={{0,24},{8,16},{16,8},{24,0},{32,56},{40,48},{48,40},{56,32},{64,88... | collective-permute-start | bytes 393224 | tf_op jit(solution)/shard_map/ppermute | solution.py:270
  17.4 0.0 collective-permute-done.pair_ref
  17.5 2.4 %collective-permute-start.4 = (bf16[2,2,256,128]{3,2,1,0:T(8,128)(2,1)S(1)}, bf16[2,2,256,128]{3,2,1,0:T(8,128)(2,1)S(1)}, u32[]{:S(2)}, u32[]{:S(2)}) collective-permute-start(bf16[2,2,256,128]{3,2,1,0:T(8,128)(2,1)S(1)} %shard_map.101.own_ref), channel_id=1, source_target_pairs={{32,0},{40,8},{48,16},{56,24},{64,32},{72,40},{80,48},{88,56},{96,... | collective-permute-start | bytes 786440 | tf_op jit(solution)/shard_map/ppermute | solution.py:291
  19.8 4.7 %collective-permute-start.3 = (bf16[2,2,256,128]{3,2,1,0:T(8,128)(2,1)S(1)}, bf16[2,2,256,128]{3,2,1,0:T(8,128)(2,1)S(1)}, u32[]{:S(2)}, u32[]{:S(2)}) collective-permute-start(bf16[2,2,256,128]{3,2,1,0:T(8,128)(2,1)S(1)} %shard_map.101.own_ref), channel_id=1, source_target_pairs={{0,32},{8,40},{16,48},{24,56},{32,64},{40,72},{48,80},{56,88},{64,... | collective-permute-start | bytes 786440 | tf_op jit(solution)/shard_map/ppermute | solution.py:290
  25.2 0.0 collective-permute-done.1.low_ref
  25.2 1.6 %collective-permute-done.2.high_ref = bf16[2,256,128]{2,1,0:T(8,128)(2,1)S(1)} collective-permute-done((bf16[2,256,128]{2,1,0:T(8,128)(2,1)S(1)}, bf16[2,256,128]{2,1,0:T(8,128)(2,1)S(1)}, u32[]{:S(2)}, u32[]{:S(2)}) %collective-permute-start.2) | collective-permute-done | bytes 131104 | tf_op jit(solution)/shard_map/ppermute | solution.py:270
  26.9 4.7 %collective-permute-start.6 = (bf16[2,2,256,128]{3,2,1,0:T(8,128)(2,1)S(1)}, bf16[2,2,256,128]{3,2,1,0:T(8,128)(2,1)S(1)}, u32[]{:S(2)}, u32[]{:S(2)}) collective-permute-start(bf16[2,2,256,128]{3,2,1,0:T(8,128)(2,1)S(1)} %shard_map.102.other_ref), channel_id=1, source_target_pairs={{0,32},{8,40},{32,64},{40,72},{64,96},{72,104},{96,128},{104,136},... | collective-permute-start | bytes 786440 | tf_op jit(solution)/shard_map/ppermute | solution.py:293
  31.6 0.0 all-to-all-done.weight_ref
  31.6 1.9 %collective-permute-start.5 = (bf16[4,32,256]{2,1,0:T(8,128)(2,1)S(1)}, bf16[4,32,256]{2,1,0:T(8,128)(2,1)S(1)}, u32[]{:S(2)}, u32[]{:S(2)}) collective-permute-start(bf16[4,32,256]{2,1,0:T(8,128)(2,1)S(1)} %get-tuple-element.19), channel_id=1, source_target_pairs={{0,1},{1,0},{2,3},{3,2},{4,5},{5,4},{6,7},{7,6},{8,9},{9,8},{10,11... | collective-permute-start | bytes 196616 | tf_op jit(solution)/shard_map/ppermute | solution.py:296
  33.5 0.0 collective-permute-done.4.above_ref
  33.5 0.0 collective-permute-done.3.below_ref
  33.6 1.7 %shard_map.103.sum_ref = f32[512,256]{1,0:T(8,128)S(1)} custom-call(f32[8,128]{1,0:T(8,128)S(1)} %get-tuple-element.12.mask_ref, bf16[256,128]{1,0:T(8,128)(2,1)S(1)} %get-tuple-element.13.mine_ref, bf16[256,384]{1,0:T(8,128)(2,1)S(1)} %collective-permute-done.pair_ref, bf16[2,2,256,128]{3,2,1,0:T(8,128)(2,1)S(1)} %shard_map.101.own_ref, ...), custom_call_target="tpu_custom_call" | custom-call | flops 1342177280 | bytes 1000000 | tf_op jit(solution)/shard_map/pallas_call | solution.py:304
  35.2 1.4 %collective-permute-done.6.beside_ref = bf16[2,2,256,128]{3,2,1,0:T(8,128)(2,1)S(1)} collective-permute-done((bf16[2,2,256,128]{3,2,1,0:T(8,128)(2,1)S(1)}, bf16[2,2,256,128]{3,2,1,0:T(8,128)(2,1)S(1)}, u32[]{:S(2)}, u32[]{:S(2)}) %collective-permute-start.6) | collective-permute-done | bytes 262176 | tf_op jit(solution)/shard_map/ppermute | solution.py:293
  36.6 0.0 collective-permute-done.5.core_text
  36.6 0.9 %shard_map.104 = bf16[8,256,128]{2,1,0:T(8,128)(2,1)S(1)} custom-call(s32[1]{0:T(128)S(6)} %copy.12.count, f32[8,128]{1,0:T(8,128)S(1)} %get-tuple-element.12.mask_ref, bf16[256,128]{1,0:T(8,128)(2,1)S(1)} %get-tuple-element.13.mine_ref, bf16[256,384]{1,0:T(8,128)(2,1)S(1)} %collective-permute-done.pair_ref, f32[512,256]{1,0:T(8,128)S(1)} %shard_map.103.sum_ref, ...), custom_call_target="tpu_custom_call" | custom-call | flops 268435456 | bytes 1000000 | tf_op jit(solution)/shard_map/pallas_call | solution.py:311
  37.5 0.0 copy-start.1
  37.5 0.0 copy-start
  37.5 13.8 %all_to_all.10.heads_ref = bf16[8,256,128]{2,1,0:T(8,128)(2,1)S(1)} all-to-all(bf16[8,256,128]{2,1,0:T(8,128)(2,1)S(1)} %shard_map.104), channel_id=1, replica_groups={{0,2,4,6,8,10,12,14},{1,3,5,7,9,11,13,15},{16,18,20,22,24,26,28,30},{17..., dimensions={0} | all-to-all | bytes 1048576 | tf_op jit(solution)/shard_map/all_to_all | solution.py:324
  51.3 0.4 shard_map.106
  51.8 1.9 %collective-permute-start.7 = (bf16[256,384]{1,0:T(8,128)(2,1)S(1)}, bf16[256,384]{1,0:T(8,128)(2,1)S(1)}, u32[]{:S(2)}, u32[]{:S(2)}) collective-permute-start(bf16[256,384]{1,0:T(8,128)(2,1)S(1)} %shard_map.106), channel_id=1, source_target_pairs={{0,1},{1,0},{2,3},{3,2},{4,5},{5,4},{6,7},{7,6},{8,9},{9,8},{10,11... | collective-permute-start | bytes 589832 | tf_op jit(solution)/shard_map/ppermute | solution.py:340
  53.7 0.0 copy-done.1
  53.7 0.0 copy-done
  53.7 0.4 shard_map.105
  54.2 0.9 %collective-permute-done.7 = bf16[256,384]{1,0:T(8,128)(2,1)S(1)} collective-permute-done((bf16[256,384]{1,0:T(8,128)(2,1)S(1)}, bf16[256,384]{1,0:T(8,128)(2,1)S(1)}, u32[]{:S(2)}, u32[]{:S(2)}) %collective-permute-start.7) | collective-permute-done | bytes 196640 | tf_op jit(solution)/shard_map/ppermute | solution.py:340
  55.1 0.1 add_convert_fusion
  55.2 8.5 %collective-permute-start.8 = (bf16[256,384]{1,0:T(8,128)(2,1)S(1)}, bf16[256,384]{1,0:T(8,128)(2,1)S(1)}, u32[]{:S(2)}, u32[]{:S(2)}) collective-permute-start(bf16[256,384]{1,0:T(8,128)(2,1)S(1)} %add_convert_fusion), channel_id=1, source_target_pairs={{0,256},{256,0},{1,257},{257,1},{2,258},{258,2},{3,259},{259,3},{4... | collective-permute-start | bytes 589832 | tf_op jit(solution)/shard_map/ppermute | solution.py:342
  63.7 9.6 %collective-permute-done.8 = bf16[256,384]{1,0:T(8,128)(2,1)S(1)} collective-permute-done((bf16[256,384]{1,0:T(8,128)(2,1)S(1)}, bf16[256,384]{1,0:T(8,128)(2,1)S(1)}, u32[]{:S(2)}, u32[]{:S(2)}) %collective-permute-start.8) | collective-permute-done | bytes 196640 | tf_op jit(solution)/shard_map/ppermute | solution.py:342
  73.2 0.7 copy.13
  (4 shorter events, 0.1 us)
Async XLA Ops:
  2.6 28.9 %all-to-all-start = ((bf16[4,288,768]{2,1,0:T(8,128)(2,1)}), bf16[4,288,768]{2,1,0:T(8,128)(2,1)S(1)}, u32[]{:S(2)}, u32[]{:S(2)}) async-start(bf16[4,288,768]{2,1,0:T(8,128)(2,1)} %get-tuple-element.18), calls=%async_computation | async-start | bytes 3538944 | tf_op jit(solution)/shard_map/all_to_all | solution.py:267
  6.9 10.5 %collective-permute-start = (bf16[256,384]{1,0:T(8,128)(2,1)S(1)}, bf16[256,384]{1,0:T(8,128)(2,1)S(1)}, u32[]{:S(2)}, u32[]{:S(2)}) collective-permute-start(bf16[256,384]{1,0:T(8,128)(2,1)S(1)} %get-tuple-element.14), channel_id=1, source_target_pairs={{0,8},{8,0},{16,24},{24,16},{32,40},{40,32},{48,56},{56,48},{64,72... | collective-permute-start | bytes 589832 | tf_op jit(solution)/shard_map/ppermute | solution.py:270
  8.9 16.3 %collective-permute-start.1 = (bf16[2,256,128]{2,1,0:T(8,128)(2,1)S(1)}, bf16[2,256,128]{2,1,0:T(8,128)(2,1)S(1)}, u32[]{:S(2)}, u32[]{:S(2)}) collective-permute-start(bf16[2,256,128]{2,1,0:T(8,128)(2,1)S(1)} %get-tuple-element.15.low_ref), channel_id=1, source_target_pairs={{0,16},{8,24},{16,0},{24,8},{32,48},{40,56},{48,32},{56,40},{64,80... | collective-permute-start | bytes 393224 | tf_op jit(solution)/shard_map/ppermute | solution.py:270
  15.0 11.9 %collective-permute-start.2 = (bf16[2,256,128]{2,1,0:T(8,128)(2,1)S(1)}, bf16[2,256,128]{2,1,0:T(8,128)(2,1)S(1)}, u32[]{:S(2)}, u32[]{:S(2)}) collective-permute-start(bf16[2,256,128]{2,1,0:T(8,128)(2,1)S(1)} %get-tuple-element.17), channel_id=1, source_target_pairs={{0,24},{8,16},{16,8},{24,0},{32,56},{40,48},{48,40},{56,32},{64,88... | collective-permute-start | bytes 393224 | tf_op jit(solution)/shard_map/ppermute | solution.py:270
  17.5 16.1 %collective-permute-start.4 = (bf16[2,2,256,128]{3,2,1,0:T(8,128)(2,1)S(1)}, bf16[2,2,256,128]{3,2,1,0:T(8,128)(2,1)S(1)}, u32[]{:S(2)}, u32[]{:S(2)}) collective-permute-start(bf16[2,2,256,128]{3,2,1,0:T(8,128)(2,1)S(1)} %shard_map.101.own_ref), channel_id=1, source_target_pairs={{32,0},{40,8},{48,16},{56,24},{64,32},{72,40},{80,48},{88,56},{96,... | collective-permute-start | bytes 786440 | tf_op jit(solution)/shard_map/ppermute | solution.py:291
  19.8 13.7 %collective-permute-start.3 = (bf16[2,2,256,128]{3,2,1,0:T(8,128)(2,1)S(1)}, bf16[2,2,256,128]{3,2,1,0:T(8,128)(2,1)S(1)}, u32[]{:S(2)}, u32[]{:S(2)}) collective-permute-start(bf16[2,2,256,128]{3,2,1,0:T(8,128)(2,1)S(1)} %shard_map.101.own_ref), channel_id=1, source_target_pairs={{0,32},{8,40},{16,48},{24,56},{32,64},{40,72},{48,80},{56,88},{64,... | collective-permute-start | bytes 786440 | tf_op jit(solution)/shard_map/ppermute | solution.py:290
  26.9 9.8 %collective-permute-start.6 = (bf16[2,2,256,128]{3,2,1,0:T(8,128)(2,1)S(1)}, bf16[2,2,256,128]{3,2,1,0:T(8,128)(2,1)S(1)}, u32[]{:S(2)}, u32[]{:S(2)}) collective-permute-start(bf16[2,2,256,128]{3,2,1,0:T(8,128)(2,1)S(1)} %shard_map.102.other_ref), channel_id=1, source_target_pairs={{0,32},{8,40},{32,64},{40,72},{64,96},{72,104},{96,128},{104,136},... | collective-permute-start | bytes 786440 | tf_op jit(solution)/shard_map/ppermute | solution.py:293
  31.6 5.0 %collective-permute-start.5 = (bf16[4,32,256]{2,1,0:T(8,128)(2,1)S(1)}, bf16[4,32,256]{2,1,0:T(8,128)(2,1)S(1)}, u32[]{:S(2)}, u32[]{:S(2)}) collective-permute-start(bf16[4,32,256]{2,1,0:T(8,128)(2,1)S(1)} %get-tuple-element.19), channel_id=1, source_target_pairs={{0,1},{1,0},{2,3},{3,2},{4,5},{5,4},{6,7},{7,6},{8,9},{9,8},{10,11... | collective-permute-start | bytes 196616 | tf_op jit(solution)/shard_map/ppermute | solution.py:296
  37.5 16.2 %copy-start.1 = (f32[1,384]{1,0:T(1,128)S(1)}, f32[1,384]{1,0:T(1,128)}, u32[]{:S(2)}) copy-start(f32[1,384]{1,0:T(1,128)} %gate_ref.1) | copy-start | bytes 4612
  37.5 16.2 %copy-start = (bf16[1,256,384]{2,1,0:T(8,128)(2,1)S(1)}, bf16[1,256,384]{2,1,0:T(8,128)(2,1)}, u32[]{:S(2)}) copy-start(bf16[1,256,384]{2,1,0:T(8,128)(2,1)} %param.10) | copy-start | bytes 589828
  51.8 3.3 %collective-permute-start.7 = (bf16[256,384]{1,0:T(8,128)(2,1)S(1)}, bf16[256,384]{1,0:T(8,128)(2,1)S(1)}, u32[]{:S(2)}, u32[]{:S(2)}) collective-permute-start(bf16[256,384]{1,0:T(8,128)(2,1)S(1)} %shard_map.106), channel_id=1, source_target_pairs={{0,1},{1,0},{2,3},{3,2},{4,5},{5,4},{6,7},{7,6},{8,9},{9,8},{10,11... | collective-permute-start | bytes 589832 | tf_op jit(solution)/shard_map/ppermute | solution.py:340
  55.2 18.1 %collective-permute-start.8 = (bf16[256,384]{1,0:T(8,128)(2,1)S(1)}, bf16[256,384]{1,0:T(8,128)(2,1)S(1)}, u32[]{:S(2)}, u32[]{:S(2)}) collective-permute-start(bf16[256,384]{1,0:T(8,128)(2,1)S(1)} %add_convert_fusion), channel_id=1, source_target_pairs={{0,256},{256,0},{1,257},{257,1},{2,258},{258,2},{3,259},{259,3},{4... | collective-permute-start | bytes 589832 | tf_op jit(solution)/shard_map/ppermute | solution.py:342
